TPU v7x, 32 devices: a whole 2x2x4 slice. The times are simulated.
32 devices in a mesh: tok: 32 (over z, y, x, core).
Axes of the slice: x: 2, y: 2, z: 4, core: 2. Of those that a mesh axis runs over, the one named last changes fastest.
Arguments:
- block_input: bfloat16 [16384, 2048], P('tok'), may hold values from -6 to 6
- lengths: int32 [3], replicated, may hold values from 1 to 15999, as said below
- offsets: int32 [3], replicated, may hold values from 0 to 16383, as said below
- norm1_gain: bfloat16 [2048], P('tok'), may hold values from 0.099609375 to 1.8984375
- w_query: bfloat16 [2048, 256], P('tok'), may hold values from -0.125 to 0.125
- w_key: bfloat16 [2048, 256], P('tok'), may hold values from -0.125 to 0.125
- w_value: bfloat16 [2048, 2048], P('tok'), may hold values from -0.125 to 0.125
- w_out: bfloat16 [2048, 2048], P('tok'), may hold values from -1 to 1
- norm2_gain: bfloat16 [2048], P('tok'), may hold values from 0.099609375 to 1.8984375
- w_gate: bfloat16 [2048, 5504], P('tok'), may hold values from -0.125 to 0.125
- w_up: bfloat16 [2048, 5504], P('tok'), may hold values from -0.125 to 0.125
- w_down: bfloat16 [5504, 2048], P('tok'), may hold values from -0.078125 to 0.078125
- out_grad: bfloat16 [16384, 2048], P('tok'), may hold values from -6 to 6
Outputs:
- output: bfloat16 [16384, 2048], P('tok')
- input_grad: float32 [16384, 2048], P('tok')
- grad_norm1: float32 [2048], P('tok')
- grad_query: float32 [2048, 256], P('tok')
- grad_key: float32 [2048, 256], P('tok')
- grad_value: float32 [2048, 2048], P('tok')
- grad_out: float32 [2048, 2048], P('tok')
- grad_norm2: float32 [2048], P('tok')
- grad_gate: float32 [2048, 5504], P('tok')
- grad_up: float32 [2048, 5504], P('tok')
- grad_down: float32 [5504, 2048], P('tok')
Inputs may be any that keep to these rules, and one draw needn't show every extreme that they name: `lengths`: the rows cover the 16384 tokens without gaps or intersection, in the packed order: a row of exactly 384 tokens first, then the longest row, which starts among the first device's tokens and ends among the last device's, then a row of one token. offsets[r] is the first token of the row whose length is lengths[r]; the rows appear in the arrays in any order.
All inputs are finite; a program needn't handle non-finite values.
Results may differ from a plain program's by a relative error of at most 0.014.
Values may be sent and summed in bfloat16 or wider, within the bound.
A program may use at most 1.125 GiB of HBM per device.

v0:
```python
from functools import partial

import jax
import jax.numpy as jnp
from jax import lax
from jax.sharding import PartitionSpec as P

QK = 16
GROUP = 256


highest = lax.Precision.HIGHEST
eps = 1e-06


def entering(value, axis, join, neutral):
    count, mine = (lax.axis_size(axis), lax.axis_index(axis))
    pieces = jax.tree.map(lambda part: lax.all_gather(part, axis), value)
    subtotal = jax.tree.map(
        lambda part, zero: jnp.full_like(part, 0) + jnp.asarray(zero, part.dtype), value, neutral
    )

    def step(position, subtotal):
        longer = join(subtotal, jax.tree.map(lambda part: part[position], pieces))
        return jax.tree.map(lambda new, old: jnp.where(position < mine, new, old), longer, subtotal)

    return lax.fori_loop(0, count - 1, step, subtotal)


def entering_2(value, axis, join, neutral):
    count = lax.axis_size(axis)
    place = lax.axis_index(axis)
    ahead = count - 1 - place
    gathered = jax.tree.map(
        lambda a, kind: lax.all_gather(a.astype(kind), axis),
        value,
        jax.tree.map(lambda a: jnp.bfloat16 if a.dtype == jnp.float32 else a.dtype, value),
    )
    state = jax.tree.map(lambda a, e: jnp.zeros_like(a) + jnp.asarray(e, a.dtype), value, neutral)

    def one(step, state):
        source = count - 1 - step
        return join(
            state,
            jax.tree.map(
                lambda a, own: lax.dynamic_index_in_dim(a, source, 0, False).astype(own.dtype),
                gathered,
                value,
            ),
        )

    return lax.fori_loop(0, ahead, one, state)


def feature_map(values):
    width = values.shape[-1]
    ones = jnp.ones(values.shape[:-1] + (1,), jnp.float32)
    linear = values * width ** (-0.25)
    square = (values[..., :, None] * values[..., None, :]).reshape(
        values.shape[:-1] + (width * width,)
    )
    return jnp.concatenate([ones, linear, square * (0.5**0.5 * width ** (-0.5))], axis=-1)


def row_starts(positions, lengths, offsets):
    inside = (positions[:, None] >= offsets[None, :]) & (
        positions[:, None] < offsets[None, :] + lengths[None, :]
    )
    return jnp.sum(jnp.where(inside, offsets[None, :], 0), axis=1)


def block(carry, inputs):
    state, total = carry
    queries, keys_in, values, positions, row_start = inputs
    width = queries.shape[-1]
    phi_q = feature_map(queries)
    phi_k = feature_map(keys_in)
    score = jnp.einsum("ihd,jhd->hij", queries, keys_in, precision=highest) * width ** (-0.5)
    weight = 1.0 + score + 0.5 * score * score
    mask = (positions[None, :] <= positions[:, None]) & (positions[None, :] >= row_start[:, None])
    weight = jnp.where(mask[None], weight, 0.0)
    carried = (row_start < positions[0]).astype(jnp.float32)
    numer = jnp.einsum("hij,jhv->ihv", weight, values, precision=highest)
    numer = numer + carried[:, None, None] * jnp.einsum(
        "ihf,hfv->ihv", phi_q, state, precision=highest
    )
    denom = jnp.sum(weight, axis=2).T + carried[:, None] * jnp.einsum(
        "ihf,hf->ih", phi_q, total, precision=highest
    )
    last = row_start[-1]
    keep = (positions >= last).astype(jnp.float32)
    fresh = (last >= positions[0]).astype(jnp.float32)
    kept = phi_k * keep[:, None, None]
    state = (1.0 - fresh) * state + jnp.einsum("jhf,jhv->hfv", kept, values, precision=highest)
    total = (1.0 - fresh) * total + jnp.sum(kept, axis=0)
    return ((state, total), (numer, denom))


def attend(queries, keys_in, values, state_in, total_in, positions, row_start, first):
    tokens, heads, width = queries.shape
    count = tokens // GROUP

    def split(array):
        return array.reshape((count, GROUP) + array.shape[1:])

    init = (jnp.zeros_like(state_in), jnp.zeros_like(total_in))
    inputs = (split(queries), split(keys_in), split(values), split(positions), split(row_start))
    _, (numer, denom) = lax.scan(block, init, inputs)
    numer = numer.reshape(values.shape)
    denom = denom.reshape(tokens, heads)
    alive = (row_start < first).astype(jnp.float32)
    phi_q = feature_map(queries)
    numer = numer + alive[:, None, None] * jnp.einsum(
        "ihf,hfv->ihv", phi_q, state_in, precision=highest
    )
    denom = denom + alive[:, None] * jnp.einsum("ihf,hf->ih", phi_q, total_in, precision=highest)
    return numer / denom[..., None]


def local_state(keys_in, values, positions, row_start):
    phi_k = feature_map(keys_in)
    keep = (positions >= row_start[-1]).astype(jnp.float32)
    kept = phi_k * keep[:, None, None]
    return (jnp.einsum("jhf,jhv->hfv", kept, values, precision=highest), jnp.sum(kept, axis=0))


def carry_on(earlier, later):
    state_e, total_e, flag_e = earlier
    state_l, total_l, flag_l = later
    return (
        state_l + (1.0 - flag_l) * state_e,
        total_l + (1.0 - flag_l) * total_e,
        flag_l + flag_e - flag_l * flag_e,
    )


def contract_rows(left, right):
    return lax.dot_general(
        left, right, (((0,), (0,)), ((), ())), preferred_element_type=jnp.float32
    )


def contract_cols(left, right):
    return lax.dot_general(
        left, right, (((1,), (1,)), ((), ())), preferred_element_type=jnp.float32
    )


def shards(
    block_input,
    lengths,
    offsets,
    norm1_gain,
    w_query,
    w_key,
    w_value,
    w_out,
    norm2_gain,
    w_gate,
    w_up,
    w_down,
    out_grad,
):
    tokens = block_input.shape[0]
    first = lax.axis_index("tok") * tokens
    positions = first + jnp.arange(tokens, dtype=jnp.int32)
    row_start = row_starts(positions, lengths, offsets)
    gain_one, query_all, key_all, value_all, out_all = (
        lax.all_gather(norm1_gain, "tok", axis=0, tiled=True),
        lax.all_gather(w_query, "tok", axis=0, tiled=True),
        lax.all_gather(w_key, "tok", axis=0, tiled=True),
        lax.all_gather(w_value, "tok", axis=0, tiled=True),
        lax.all_gather(w_out, "tok", axis=0, tiled=True),
    )
    heads = query_all.shape[1] // QK
    width = value_all.shape[1]
    head_size = width // heads
    gain_one = gain_one.astype(jnp.float32)
    inputs32 = block_input.astype(jnp.float32)
    ratio_one = lax.rsqrt(jnp.mean(inputs32 * inputs32, axis=1, keepdims=True) + eps)
    normed_one = inputs32 * ratio_one
    hidden_one = (normed_one * gain_one).astype(jnp.bfloat16)
    queries = jnp.dot(hidden_one, query_all, preferred_element_type=jnp.float32).astype(
        jnp.bfloat16
    )
    keys_in = jnp.dot(hidden_one, key_all, preferred_element_type=jnp.float32).astype(jnp.bfloat16)
    values = jnp.dot(hidden_one, value_all, preferred_element_type=jnp.float32).astype(jnp.bfloat16)
    query_heads = queries.astype(jnp.float32).reshape(tokens, heads, QK)
    key_heads = keys_in.astype(jnp.float32).reshape(tokens, heads, QK)
    value_heads = values.astype(jnp.float32).reshape(tokens, heads, head_size)
    (state_dev, total_dev), state_back = jax.vjp(
        partial(local_state, positions=positions, row_start=row_start), key_heads, value_heads
    )
    flag = (row_start[-1] >= first).astype(jnp.float32)
    identity = (jnp.zeros_like(state_dev), jnp.zeros_like(total_dev), jnp.zeros((), jnp.float32))
    state_in, total_in, _ = entering((state_dev, total_dev, flag), "tok", carry_on, identity)
    mixed_heads, attend_back = jax.vjp(
        partial(attend, positions=positions, row_start=row_start, first=first),
        query_heads,
        key_heads,
        value_heads,
        state_in,
        total_in,
    )
    mixed = mixed_heads.reshape(tokens, width).astype(jnp.bfloat16)
    gain_two, gate_all, up_all, down_all = (
        lax.all_gather(norm2_gain, "tok", axis=0, tiled=True),
        lax.all_gather(w_gate, "tok", axis=0, tiled=True),
        lax.all_gather(w_up, "tok", axis=0, tiled=True),
        lax.all_gather(w_down, "tok", axis=0, tiled=True),
    )
    gain_two = gain_two.astype(jnp.float32)
    middle = inputs32 + jnp.dot(mixed, out_all, preferred_element_type=jnp.float32)
    ratio_two = lax.rsqrt(jnp.mean(middle * middle, axis=1, keepdims=True) + eps)
    normed_two = middle * ratio_two
    hidden_two = (normed_two * gain_two).astype(jnp.bfloat16)
    gate = jnp.dot(hidden_two, gate_all, preferred_element_type=jnp.float32)
    upper = jnp.dot(hidden_two, up_all, preferred_element_type=jnp.float32)
    sigma = jax.nn.sigmoid(gate)
    smooth = gate * sigma
    activation = (smooth * upper).astype(jnp.bfloat16)
    output = (middle + jnp.dot(activation, down_all, preferred_element_type=jnp.float32)).astype(
        jnp.bfloat16
    )
    d_act = contract_cols(out_grad, down_all)
    d_gate = (d_act * upper * sigma * (1.0 + gate * (1.0 - sigma))).astype(jnp.bfloat16)
    d_up = (d_act * smooth).astype(jnp.bfloat16)
    d_hidden_two = contract_cols(d_gate, gate_all) + contract_cols(d_up, up_all)
    term_norm_two = jnp.sum(d_hidden_two * normed_two, axis=0)
    scaled_two = d_hidden_two * gain_two
    d_middle = out_grad.astype(jnp.float32) + ratio_two * (
        scaled_two - normed_two * jnp.mean(scaled_two * normed_two, axis=1, keepdims=True)
    )
    term_gate = contract_rows(hidden_two, d_gate)
    term_up = contract_rows(hidden_two, d_up)
    term_down = contract_rows(activation, out_grad)
    grad_norm2, grad_gate, grad_up, grad_down = (
        lax.psum_scatter(term_norm_two, "tok", scatter_dimension=0, tiled=True),
        lax.psum_scatter(term_gate, "tok", scatter_dimension=0, tiled=True),
        lax.psum_scatter(term_up, "tok", scatter_dimension=0, tiled=True),
        lax.psum_scatter(term_down, "tok", scatter_dimension=0, tiled=True),
    )
    d_mixed = d_middle.astype(jnp.bfloat16)
    term_out = contract_rows(mixed, d_mixed)
    d_heads = contract_cols(d_mixed, out_all).reshape(tokens, heads, head_size)
    d_query, d_key, d_value, d_state_in, d_total_in = attend_back(d_heads)
    zero_id = (jnp.zeros_like(d_state_in), jnp.zeros_like(d_total_in), jnp.zeros((), jnp.float32))
    d_state_dev, d_total_dev, _ = entering_2(
        (d_state_in, d_total_in, flag), "tok", carry_on, zero_id
    )
    d_key_more, d_value_more = state_back((d_state_dev, d_total_dev))
    d_query_low = d_query.reshape(tokens, heads * QK).astype(jnp.bfloat16)
    d_key_low = (d_key + d_key_more).reshape(tokens, heads * QK).astype(jnp.bfloat16)
    d_value_low = (d_value + d_value_more).reshape(tokens, width).astype(jnp.bfloat16)
    term_query = contract_rows(hidden_one, d_query_low)
    term_key = contract_rows(hidden_one, d_key_low)
    term_value = contract_rows(hidden_one, d_value_low)
    d_hidden_one = (
        contract_cols(d_query_low, query_all)
        + contract_cols(d_key_low, key_all)
        + contract_cols(d_value_low, value_all)
    )
    term_norm_one = jnp.sum(d_hidden_one * normed_one, axis=0)
    scaled_one = d_hidden_one * gain_one
    input_grad = d_middle + ratio_one * (
        scaled_one - normed_one * jnp.mean(scaled_one * normed_one, axis=1, keepdims=True)
    )
    grad_norm1, grad_query, grad_key, grad_value, grad_out = (
        lax.psum_scatter(term_norm_one, "tok", scatter_dimension=0, tiled=True),
        lax.psum_scatter(term_query, "tok", scatter_dimension=0, tiled=True),
        lax.psum_scatter(term_key, "tok", scatter_dimension=0, tiled=True),
        lax.psum_scatter(term_value, "tok", scatter_dimension=0, tiled=True),
        lax.psum_scatter(term_out, "tok", scatter_dimension=0, tiled=True),
    )
    return (
        output,
        input_grad,
        grad_norm1,
        grad_query,
        grad_key,
        grad_value,
        grad_out,
        grad_norm2,
        grad_gate,
        grad_up,
        grad_down,
    )


def solution(mesh):
    return jax.shard_map(
        shards,
        mesh=mesh,
        in_specs=(
            P("tok", None),
            P(),
            P(),
            P("tok"),
            P("tok", None),
            P("tok", None),
            P("tok", None),
            P("tok", None),
            P("tok"),
            P("tok", None),
            P("tok", None),
            P("tok", None),
            P("tok", None),
        ),
        out_specs=(
            P("tok", None),
            P("tok", None),
            P("tok"),
            P("tok", None),
            P("tok", None),
            P("tok", None),
            P("tok", None),
            P("tok"),
            P("tok", None),
            P("tok", None),
            P("tok", None),
        ),
        check_vma=False,
    )
```

profile of v0, /device:TPU:0, one launch (start us, length us, event | category | flops | bytes accessed | tf_op | source)
XLA Modules:
  0.0 3677.2 jit_solution(5424058740255180745)
XLA Ops:
  14.5 42.2 %all-reduce.9 = (bf16[2048]{0:T(1024)(128)(2,1)S(1)}, bf16[2048]{0:T(1024)(128)(2,1)S(1)}, bf16[32]{0:T(256)(128)(2,1)}) all-reduce(bf16[2048]{0:T(1024)(128)(2,1)S(1)} %dynamic-update-slice, bf16[2048]{0:T(1024)(128)(2,1)S(1)} %dynamic-update-slice.2, bf16[32]{0:T(256)(128)(2,1)S(1)} %dynamic-update-slice.3), channel_id=1, replica_groups=mesh['tok'=32] {'tok'}, use_global_device_ids=true, to_apply=%add | all-reduce | flops 4128 | bytes 16512
  59.5 7.9 all-gather.15.cloned.1.call-done
  74.8 71.9 %all-gather.17.cloned.1.call-done = bf16[2048,2048]{1,0:T(8,128)(2,1)} async-done(((bf16[64,2048]{1,0:T(8,128)(2,1)}), bf16[2048,2048]{1,0:T(8,128)(2,1)}) %all-gather.17.cloned.1.call-update) | async-done | bytes 8388624 | tf_op jit(solution)/shard_map/all_gather | solution.py:172
  146.7 8.4 convolution_convert_fusion
  165.5 39.7 %all-reduce.1 = f32[32]{0:T(128)} all-reduce(f32[32]{0:T(128)S(1)} %dynamic-update-slice.1), channel_id=1, replica_groups=mesh['tok'=32] {'tok'}, use_global_device_ids=true, to_apply=%add.1 | all-reduce | flops 32 | bytes 256
  219.2 48.7 %all-gather.1 = f32[512,273]{1,0:T(8,128)} all-gather(f32[16,273]{1,0:T(8,128)S(1)} %fusion.159), channel_id=3, replica_groups=mesh['tok'=32] {'tok'}, dimensions={0}, use_global_device_ids=true | all-gather | bytes 576576 | tf_op jit(solution)/shard_map/all_gather | solution.py:18
  282.5 254.4 %while.111 = (s32[]{:T(128)}, f32[16,273,128]{2,1,0:T(8,128)S(1)}, f32[16,273]{1,0:T(8,128)S(1)}, f32[2,256,16,128]{1,0,3,2:T(2,128)}, f32[2,256,16]{1,0,2:T(2,1...) while((s32[]{:T(128)}, f32[16,273,128]{2,1,0:T(8,128)S(1)}, ...), condition=%wide.region_5.6_spmd.clone, body=%wide.region_2.5_spmd.clone.sunk | while | flops 5306758656 | bytes 188504304 | solution.py:108
  308.3 7.4 fusion.268
  323.2 9.1 multiply_add_fusion.7
  348.3 42.9 %dynamic_update_slice.267 = f32[2,256,16,128]{1,0,3,2:T(2,128)} dynamic-update-slice(f32[2,256,16,128]{1,0,3,2:T(2,128)} %get-tuple-element.2468, f32[1,256,16,128]{1,0,3,2:T(1,128)} %copy.250, s32[]{:T(128)S(6)} %copy.308, s32[]{:T(128)} %constant.319.clone.1..sunk.1, s32[]{:T(128)} %constant.319.clone.1..sunk.1, s32[]{:T(128)} %constant.319.clone.1..sunk.1) | dynamic-update-slice | bytes 4194308 | tf_op jit(solution)/shard_map/jvp()/while/body/jit(dynamic_update_index_in_dim)/dynamic_update_slice | solution.py:108
  400.1 7.4 bitcast_dynamic-update-slice_fusion.17
  409.1 6.3 fusion.273
  420.2 7.4 fusion.268
  435.1 9.1 multiply_add_fusion.7
  460.2 42.8 %dynamic_update_slice.267 = f32[2,256,16,128]{1,0,3,2:T(2,128)} dynamic-update-slice(f32[2,256,16,128]{1,0,3,2:T(2,128)} %get-tuple-element.2468, f32[1,256,16,128]{1,0,3,2:T(1,128)} %copy.250, s32[]{:T(128)S(6)} %copy.308, s32[]{:T(128)} %constant.319.clone.1..sunk.1, s32[]{:T(128)} %constant.319.clone.1..sunk.1, s32[]{:T(128)} %constant.319.clone.1..sunk.1) | dynamic-update-slice | bytes 4194308 | tf_op jit(solution)/shard_map/jvp()/while/body/jit(dynamic_update_index_in_dim)/dynamic_update_slice | solution.py:108
  511.9 7.4 bitcast_dynamic-update-slice_fusion.17
  520.9 6.3 fusion.273
  537.8 6.8 reshape.496
  544.7 22.5 reshape.527
  567.2 207.9 %all-gather.27.cloned.1.call-done = f32[512,273,128]{2,0,1:T(8,128)} async-done(((f32[16,273,128]{2,0,1:T(8,128)}), f32[512,273,128]{2,0,1:T(8,128)}) %all-gather.27.cloned.1.call-update) | async-done | bytes 71565328 | tf_op jit(solution)/shard_map/all_gather | solution.py:18
  775.2 236.2 %while.112 = (s32[]{:T(128)}, f32[16,273,128]{2,1,0:T(8,128)}, f32[16,273]{1,0:T(8,128)S(1)}, s32[]{:T(128)}, f32[32,16,273,128]{3,1,0,2:T(8,128)}, /*index=5*/f...) while((s32[]{:T(128)}, f32[16,273,128]{2,1,0:T(8,128)}, ...), condition=%wide.region_8.9_spmd.clone, body=%wide.region_7.8_spmd.clone.sunk | while | flops 2253893 | bytes 11234667 | solution.py:27
  1011.5 8.2 fusion.157
  1020.3 13.0 divide_convert_fusion
  1033.3 7.8 multiply_reduce_fusion.11
  1043.5 19.6 fusion.169
  1063.1 78.5 %all-gather.25.cloned.1.call-done = bf16[2048,5504]{1,0:T(8,128)(2,1)} async-done(((bf16[64,5504]{1,0:T(8,128)(2,1)}), bf16[2048,5504]{1,0:T(8,128)(2,1)}) %all-gather.25.cloned.1.call-update) | async-done | bytes 22544400 | tf_op jit(solution)/shard_map/all_gather | solution.py:209
  1141.6 19.1 fusion.170
  1160.7 26.9 multiply_convert_fusion
  1187.6 19.4 fusion.171
  1207.0 19.4 multiply_reduce_fusion.8
  1229.6 9.7 fusion.147
  1244.8 14.0 fusion.140
  1278.7 327.5 %while.113 = (s32[]{:T(128)}, f32[16,273,128]{2,1,0:T(8,128)S(1)}, f32[16,273]{1,0:T(8,128)S(1)}, f32[2,256,16,16]{1,0,3,2:T(2,128)}, f32[2,256,16,16]{1,0,3,2:T...) while((s32[]{:T(128)}, f32[16,273,128]{2,1,0:T(8,128)S(1)}, ...), condition=%wide.region_19.20_spmd.clone, body=%wide.region_14.19_spmd.clone.sunk | while | flops 10537659392 | bytes 360332672 | solution.py:108
  1279.0 8.4 fusion.299
  1287.3 13.9 fusion.300
  1346.1 10.6 fusion.296
  1364.3 6.4 dynamic_update_slice.270
  1384.0 6.2 dynamic_update_slice.271
  1396.3 42.9 %dynamic_update_slice.272 = f32[2,256,16,128]{1,0,3,2:T(2,128)} dynamic-update-slice(f32[2,256,16,128]{1,0,3,2:T(2,128)} %get-tuple-element.2591, f32[1,256,16,128]{1,0,3,2:T(1,128)} %copy.262, s32[]{:T(128)S(6)} %sub.84, s32[]{:T(128)} %constant.319.clone.1..sunk.3, s32[]{:T(128)} %constant.319.clone.1..sunk.3, s32[]{:T(128)} %constant.319.clone.1..sunk.3) | dynamic-update-slice | bytes 4194308 | tf_op jit(solution)/shard_map/transpose(jvp())/while/body/jit(dynamic_update_index_in_dim)/dynamic_update_slice | solution.py:108
  1439.6 8.0 fusion.299
  1447.6 13.6 fusion.300
  1505.6 10.0 fusion.296
  1523.2 6.3 dynamic_update_slice.270
  1554.9 42.8 %dynamic_update_slice.272 = f32[2,256,16,128]{1,0,3,2:T(2,128)} dynamic-update-slice(f32[2,256,16,128]{1,0,3,2:T(2,128)} %get-tuple-element.2591, f32[1,256,16,128]{1,0,3,2:T(1,128)} %copy.262, s32[]{:T(128)S(6)} %sub.84, s32[]{:T(128)} %constant.319.clone.1..sunk.3, s32[]{:T(128)} %constant.319.clone.1..sunk.3, s32[]{:T(128)} %constant.319.clone.1..sunk.3) | dynamic-update-slice | bytes 4194308 | tf_op jit(solution)/shard_map/transpose(jvp())/while/body/jit(dynamic_update_index_in_dim)/dynamic_update_slice | solution.py:108
  1607.7 10.6 add_bitcast_fusion.1
  1629.0 10.3 fusion.145
  1640.4 10.8 fusion.155
  1651.7 39.7 %all-gather.3 = bf16[512,273]{1,0:T(8,128)(2,1)S(1)} all-gather(bf16[16,273]{1,0:T(8,128)(2,1)S(1)} %bitcast.580), channel_id=5, replica_groups=mesh['tok'=32] {'tok'}, dimensions={0}, use_global_device_ids=true | all-gather | bytes 288288 | tf_op jit(solution)/shard_map/all_gather | solution.py:35
  1691.6 104.6 %while.110 = (s32[]{:T(128)}, f32[16,273,128]{2,1,0:T(8,128)S(1)}, f32[16,273]{1,0:T(8,128)S(1)}, s32[]{:T(128)}, bf16[32,16,273,128]{3,1,0,2:T(8,128)(2,1)}, /*...) while((s32[]{:T(128)}, f32[16,273,128]{2,1,0:T(8,128)S(1)}, ...), condition=%wide.region_21.22_spmd, body=%wide.region_20.21_spmd.sunk | while | flops 1690423 | bytes 7871341 | solution.py:52
  1813.0 23.8 fusion.174
  1836.8 23.4 fusion.175
  1860.3 6.8 reshape.507
  1867.1 12.1 fusion.128
  1880.6 8.4 fusion.160
  1890.5 20.7 fusion.176
  1911.3 706.8 %fusion = f32[176,2048]{1,0:T(8,128)S(1)} fusion(f32[5504,2048]{1,0:T(8,128)} %fusion.176), kind=kCustom, calls=%all-reduce-scatter | all-reduce-scatter fusion | flops 11534337 | bytes 46530560
  2618.2 73.7 %collective-permute-start = (f32[124,2048]{1,0:T(8,128)S(1)}, f32[124,2048]{1,0:T(8,128)S(1)}, u32[]{:S(2)}, u32[]{:S(2)}) collective-permute-start(f32[124,2048]{1,0:T(8,128)S(1)} %slice.28), channel_id=1, source_target_pairs={{0,1},{1,2},{2,3},{3,4},{4,5},{5,6},{6,7},{7,8},{8,9},{9,10},{10,1... | collective-permute-start | bytes 3047432
  2691.8 19.9 add_convert_fusion
  2723.4 7.9 fusion.173
  2735.3 123.0 %all-reduce.8 = (f32[2048]{0:T(1024)S(1)}, f32[2048]{0:T(1024)S(1)}) all-reduce(f32[2048]{0:T(1024)S(1)} %get-tuple-element.1766, f32[2048]{0:T(1024)S(1)} %copy-done.98), channel_id=6, replica_groups=mesh['tok'=32] {'tok'}, use_global_device_ids=true, to_apply=%region_26.27.clone | all-reduce | flops 4096 | bytes 32768
  2859.5 6.7 fusion.125
  2866.2 107.4 %reduce-scatter.17.cloned.1.call-done = f32[64,5504]{1,0:T(8,128)} async-done(((f32[2048,5504]{1,0:T(8,128)}), f32[64,5504]{1,0:T(8,128)}) %reduce-scatter.17.cloned.1.call-update) | async-done | bytes 1409040 | tf_op jit(solution)/shard_map/reduce_scatter | solution.py:239
  2973.6 503.0 %reduce-scatter.19.cloned.1.call-done = f32[64,5504]{1,0:T(8,128)} async-done(((f32[2048,5504]{1,0:T(8,128)}), f32[64,5504]{1,0:T(8,128)}) %reduce-scatter.19.cloned.1.call-update) | async-done | bytes 1409040 | tf_op jit(solution)/shard_map/reduce_scatter | solution.py:240
  3476.6 193.9 %reduce-scatter.13.cloned.1.call-done = f32[64,2048]{1,0:T(8,128)} async-done(((f32[2048,2048]{1,0:T(8,128)}), f32[64,2048]{1,0:T(8,128)}) %reduce-scatter.13.cloned.1.call-update) | async-done | bytes 524304 | tf_op jit(solution)/shard_map/reduce_scatter | solution.py:272
  (808 shorter events, 660.2 us)
Async XLA Ops:
  7.2 60.2 %all-gather.15.cloned.1.call-start = ((), (), s32[]{:S(2)}) async-start(), calls=%async_computation.6 | async-start | bytes 1081344 | tf_op jit(solution)/shard_map/all_gather | solution.py:171
  7.9 138.8 %all-gather.17.cloned.1.call-start = ((), (), s32[]{:S(2)}) async-start(), calls=%async_computation.7 | async-start | bytes 8650752 | tf_op jit(solution)/shard_map/all_gather | solution.py:172
  8.7 203.6 %all-gather.19.cloned.1.call-start = ((), (), s32[]{:S(2)}) async-start(), calls=%async_computation.8 | async-start | bytes 1081344 | tf_op jit(solution)/shard_map/all_gather | solution.py:170
  9.4 535.3 %all-gather.31.cloned.1.call-start = ((), (), s32[]{:S(2)}) async-start(), calls=%async_computation.20 | async-start | bytes 23789568 | tf_op jit(solution)/shard_map/all_gather | solution.py:210
  10.0 765.2 %all-gather.27.cloned.1.call-start = ((), (), s32[]{:S(2)}) async-start(), calls=%async_computation.18 | async-start | bytes 73801728 | tf_op jit(solution)/shard_map/all_gather | solution.py:18
  56.7 155.6 %copy-start.78 = (f32[2048]{0:T(1024)}, f32[2048]{0:T(1024)S(1)}, u32[]{:S(2)}) copy-start(f32[2048]{0:T(1024)S(1)} %convert_element_type.227) | copy-start | bytes 24580
  56.7 150.2 %copy-start.85 = (f32[273]{0:T(512)}, f32[273]{0:T(512)S(1)}, u32[]{:S(2)}) copy-start(f32[273]{0:T(512)S(1)} %pad.12.clone) | copy-start | bytes 3280
  57.4 149.6 %copy-start.81 = (f32[512]{0:T(512)}, f32[512]{0:T(512)S(1)}, u32[]{:S(2)}) copy-start(f32[512]{0:T(512)S(1)} %compare_convert_fusion.4) | copy-start | bytes 6148
  59.5 152.8 %copy-start.93 = (f32[512]{0:T(512)}, f32[512]{0:T(512)S(1)}, u32[]{:S(2)}) copy-start(f32[512]{0:T(512)S(1)} %add_rsqrt_fusion.1) | copy-start | bytes 6148
  70.1 135.7 %copy-start.37 = (f32[512,256]{0,1:T(8,128)}, f32[512,256]{0,1:T(8,128)S(1)}, u32[]{:S(2)}) copy-start(f32[512,256]{0,1:T(8,128)S(1)} %get-tuple-element.1954) | copy-start | bytes 1572868
  70.2 136.8 %copy-start.51 = (f32[512,16,16]{0,2,1:T(8,128)}, f32[512,16,16]{0,2,1:T(8,128)S(1)}, u32[]{:S(2)}) copy-start(f32[512,16,16]{0,2,1:T(8,128)S(1)} %get-tuple-element.1953) | copy-start | bytes 1572868
  70.2 76.6 %copy-start.27 = (bf16[512,2048]{1,0:T(8,128)(2,1)S(1)}, bf16[512,2048]{1,0:T(8,128)(2,1)}, u32[]{:S(2)}) copy-start(bf16[512,2048]{1,0:T(8,128)(2,1)} %param.21) | copy-start | bytes 6291460
  162.5 870.7 %all-gather.21.cloned.1.call-start = ((), (), s32[]{:S(2)}) async-start(), calls=%async_computation.9 | async-start | bytes 8650752 | tf_op jit(solution)/shard_map/all_gather | solution.py:173
  163.1 880.4 %all-gather.23.cloned.1.call-start = ((), (), s32[]{:S(2)}) async-start(), calls=%async_computation.10 | async-start | bytes 23248896 | tf_op jit(solution)/shard_map/all_gather | solution.py:208
  163.8 977.7 %all-gather.25.cloned.1.call-start = ((), (), s32[]{:S(2)}) async-start(), calls=%async_computation.11 | async-start | bytes 23248896 | tf_op jit(solution)/shard_map/all_gather | solution.py:209
  164.6 1526.8 %all-gather.29.cloned.1.call-start = ((), (), s32[]{:S(2)}) async-start(), calls=%async_computation.19 | async-start | bytes 36900864 | tf_op jit(solution)/shard_map/all_gather | solution.py:35
  304.5 15.0 copy-start.89
  304.6 28.9 copy-start.72
  323.1 9.2 copy-start
  323.2 9.2 copy-start.21
  416.6 14.8 copy-start.89
  416.6 28.8 copy-start.72
  435.1 9.2 copy-start
  435.1 9.2 copy-start.21
  544.7 230.5 %copy-start.64 = (f32[16,273]{1,0:T(8,128)S(1)}, f32[16,273]{1,0:T(8,128)}, u32[]{:S(2)}) copy-start(f32[16,273]{1,0:T(8,128)} %custom-call.3) | copy-start | bytes 52420
  544.7 230.5 %copy-start.101 = (f32[32]{0:T(128)S(1)}, f32[32]{0:T(128)}, u32[]{:S(2)}) copy-start(f32[32]{0:T(128)} %all-reduce.1) | copy-start | bytes 388
  775.2 236.3 %copy-start.67 = (f32[512,16,16]{0,2,1:T(8,128)S(1)}, f32[512,16,16]{0,2,1:T(8,128)}, u32[]{:S(2)}) copy-start(f32[512,16,16]{0,2,1:T(8,128)} %get-tuple-element.1955) | copy-start | bytes 1572868
  775.2 236.3 %copy-start.86 = (f32[273]{0:T(512)S(1)}, f32[273]{0:T(512)}, u32[]{:S(2)}) copy-start(f32[273]{0:T(512)} %copy-done.85) | copy-start | bytes 3280
  1011.4 8.9 copy-start.22
  1020.3 13.0 copy-start.75
  1020.3 13.0 copy-start.28
  1033.3 9.8 copy-start.80
  1043.4 98.1 %copy-start.49 = (bf16[512,2048]{1,0:T(8,128)(2,1)}, bf16[512,2048]{1,0:T(8,128)(2,1)S(1)}, u32[]{:S(2)}) copy-start(bf16[512,2048]{1,0:T(8,128)(2,1)S(1)} %multiply_convert_fusion.3) | copy-start | bytes 6291460
  1141.6 19.1 copy-start.55
  1207.0 19.4 copy-start.35
  1207.0 19.4 copy-start.56
  1260.0 1606.2 %reduce-scatter.9.cloned.1.call-start = ((), (), s32[]{:S(2)}) async-start(), calls=%async_computation.12 | async-start | bytes 2162688 | tf_op jit(solution)/shard_map/reduce_scatter | solution.py:270
  1278.7 329.0 %copy-start.66 = (f32[16,273]{1,0:T(8,128)S(1)}, f32[16,273]{1,0:T(8,128)}, u32[]{:S(2)}) copy-start(f32[16,273]{1,0:T(8,128)} %copy-done.65) | copy-start | bytes 52420
  1278.7 329.0 %copy-start.77 = (f32[512,16]{0,1:T(8,128)S(1)}, f32[512,16]{0,1:T(8,128)}, u32[]{:S(2)}) copy-start(f32[512,16]{0,1:T(8,128)} %copy-done.75) | copy-start | bytes 98308
  1278.7 329.0 %copy-start.84 = (f32[16,512]{1,0:T(8,128)S(1)}, f32[16,512]{1,0:T(8,128)}, u32[]{:S(2)}) copy-start(f32[16,512]{1,0:T(8,128)} %get-tuple-element.1950) | copy-start | bytes 98308
  1287.3 14.7 copy-start.97
  1287.3 14.8 copy-start.9
  1307.2 12.5 slice-start.4
  1319.8 9.6 slice-start.2
  1346.1 12.6 copy-start.23
  1346.1 12.6 copy-start.24
  1447.6 14.5 copy-start.97
  1447.6 14.5 copy-start.9
  1467.2 12.6 slice-start.4
  1479.8 9.8 slice-start.2
  1505.6 12.0 copy-start.23
  1505.6 12.0 copy-start.24
  1629.0 1237.2 %reduce-scatter.15.cloned.1.call-start = ((), (), s32[]{:S(2)}) async-start(), calls=%async_computation.15 | async-start | bytes 17301504 | tf_op jit(solution)/shard_map/reduce_scatter | solution.py:273
  1639.4 1226.8 %reduce-scatter.11.cloned.1.call-start = ((), (), s32[]{:S(2)}) async-start(), calls=%async_computation.13 | async-start | bytes 2162688 | tf_op jit(solution)/shard_map/reduce_scatter | solution.py:271
  1640.4 10.9 copy-start.53
  1640.4 51.2 %copy-start.99 = (bf16[32]{0:T(256)(128)(2,1)S(1)}, bf16[32]{0:T(256)(128)(2,1)}, u32[]{:S(2)}) copy-start(bf16[32]{0:T(256)(128)(2,1)} %get-tuple-element.2649) | copy-start | bytes 196
  1691.6 104.6 %copy-start.82 = (f32[512]{0:T(512)S(1)}, f32[512]{0:T(512)}, u32[]{:S(2)}) copy-start(f32[512]{0:T(512)} %copy-done.81) | copy-start | bytes 6148
  1812.9 1160.7 %reduce-scatter.17.cloned.1.call-start = ((), (), s32[]{:S(2)}) async-start(), calls=%async_computation.16 | async-start | bytes 46497792 | tf_op jit(solution)/shard_map/reduce_scatter | solution.py:239
  1836.8 1639.9 %reduce-scatter.19.cloned.1.call-start = ((), (), s32[]{:S(2)}) async-start(), calls=%async_computation.17 | async-start | bytes 46497792 | tf_op jit(solution)/shard_map/reduce_scatter | solution.py:240
  1860.2 1810.2 %reduce-scatter.13.cloned.1.call-start = ((), (), s32[]{:S(2)}) async-start(), calls=%async_computation.14 | async-start | bytes 17301504 | tf_op jit(solution)/shard_map/reduce_scatter | solution.py:272
  1867.1 13.4 copy-start.31
  2618.1 93.6 %copy-start.59 = (bf16[512,16,16]{0,2,1:T(8,128)(2,1)S(1)}, bf16[512,16,16]{0,2,1:T(8,128)(2,1)}, u32[]{:S(2)}) copy-start(bf16[512,16,16]{0,2,1:T(8,128)(2,1)} %copy-done.58) | copy-start | bytes 786436
  2618.2 93.6 %copy-start.60 = (bf16[2048,256]{1,0:T(8,128)(2,1)S(1)}, bf16[2048,256]{1,0:T(8,128)(2,1)}, u32[]{:S(2)}) copy-start(bf16[2048,256]{1,0:T(8,128)(2,1)} %all-gather.19.cloned.1.call-done) | copy-start | bytes 3145732
  2618.2 96.4 %collective-permute-start = (f32[124,2048]{1,0:T(8,128)S(1)}, f32[124,2048]{1,0:T(8,128)S(1)}, u32[]{:S(2)}, u32[]{:S(2)}) collective-permute-start(f32[124,2048]{1,0:T(8,128)S(1)} %slice.28), channel_id=1, source_target_pairs={{0,1},{1,2},{2,3},{3,4},{4,5},{5,6},{6,7},{7,8},{8,9},{9,10},{10,1... | collective-permute-start | bytes 3047432
  (103 other events, 489.8 us)
Sparse Core Ops, SparseCore 0:
  10.9 56.4 all-gather.14
  70.2 76.4 all-gather.16
  149.6 52.3 all-gather.18
  204.6 148.5 all-gather.30
  356.0 419.0 all-gather.26
  777.9 76.9 all-gather.20
  857.8 140.6 all-gather.22
  1001.3 140.1 all-gather.24
  1260.1 201.5 all-gather.28
  1629.1 135.4 reduce-scatter.8
  1767.5 363.9 reduce-scatter.14
  2134.3 169.5 reduce-scatter.10
  2306.8 666.7 reduce-scatter.16
  2976.4 500.1 reduce-scatter.18
  3479.3 191.1 reduce-scatter.12
where the time goes:
time: 3710 us; the launch traced here: 3680 us
  waiting for transfers between devices  1180 us (32%)
  blocking collectives  1000 us (27%)
  matrix products  526 us (14%)
  local copies, waits for them, and re-layouts  515 us (14%)
  other arithmetic  285 us (8%)
  loops' own time  85.4 us (2%)
  starting transfers between devices  74.3 us (2%)
    unnamed x4, blocking collectives  912 us
    reduce_scatter x1, waiting for transfers between devices, shards(): lax.psum_scatter(term_up, 'tok', scatter_dimension=0, tiled=True)  503 us
    dynamic_update_slice x28, local copies, waits for them, and re-layouts, attend(): _, (numer, denom) = lax.scan(block, init, inputs)  229 us
    all_gather x1, waiting for transfers between devices, entering(): pieces = jax.tree.map(lambda part: lax.all_gather(part, axis), value)  208 us
    reduce_scatter x1, waiting for transfers between devices, shards(): lax.psum_scatter(term_value, 'tok', scatter_dimension=0, tiled=True)  194 us
    select_n x62, other arithmetic, step(): jnp.where(position < mine, new, old)  140 us
    reduce_scatter x1, waiting for transfers between devices, shards(): lax.psum_scatter(term_gate, 'tok', scatter_dimension=0, tiled=True)  107 us
    dot_general x7, matrix products, contract_rows(): lax.dot_general(left, right, (((0,), (0,)), ((), ())), preferred_element_...  91.5 us
  transfers between devices with their start and end apart: 16, of which 7 were waited for; matrix products, arithmetic and copies ran while one was open for 51% of the time, Pallas kernels for 0%

commit v1 on v0

v1 whole, which is shorter than its diff:
```python
import jax
import jax.numpy as jnp
import numpy as np
from jax import lax
from jax.experimental import pallas as pl
from jax.experimental.pallas import tpu as pltpu
from jax.sharding import PartitionSpec as P

QK = 16
FEATS = 160
ROWS = 168
VMEM = 56 * 1024 * 1024
eps = 1e-06
f32 = jnp.float32
bf16 = jnp.bfloat16


def chip_dims(n):
    if n == 32:
        return [(8, 4), (4, 2), (2, 2)]
    if n == 128:
        return [(32, 4), (8, 4), (2, 4)]
    return [(2, n // 2)]


def quad_dims(n):
    if n == 32:
        return [(8, 4), (4, 2)]
    if n == 128:
        return [(32, 4), (8, 4), (4, 2)]
    return [(4, n // 4)]


def flip(x, bits):
    n = lax.axis_size("tok")
    return lax.ppermute(x, "tok", [(i, i ^ bits) for i in range(n)])


def shift(x, dim, k, wrap=True):
    stride, size = dim
    pairs = []
    for i in range(lax.axis_size("tok")):
        at = (i // stride) % size
        if wrap or 0 <= at + k < size:
            pairs.append((i, i + ((at + k) % size - at) * stride))
    return lax.ppermute(x, "tok", pairs)


def place(dim):
    return (lax.axis_index("tok") // dim[0]) % dim[1]


def pick(x, index, axis=0):
    return lax.dynamic_index_in_dim(x, index, axis, False)


def assemble(pieces):
    out = jnp.zeros((len(pieces),) + pieces[0][1].shape, pieces[0][1].dtype)
    for index, block in pieces:
        out = lax.dynamic_update_index_in_dim(out, block, index, 0)
    return out


def gather_stage(x, dim):
    at = place(dim)
    pieces = [(at, x)]
    for k in range(1, dim[1]):
        pieces.append((lax.rem(at + dim[1] - k, dim[1]), shift(x, dim, k)))
    return assemble(pieces)


def gather(x, dims):
    order = sorted(dims, key=lambda d: -d[0])
    done = []
    for dim in dims:
        x = gather_stage(x, dim)
        done.insert(0, dim)
    axes = [done.index(d) for d in order]
    rest = list(range(len(done), x.ndim))
    x = x.transpose(axes + rest)
    return x.reshape((-1,) + x.shape[len(done):])


def gather_blocks(x, dims):
    unit = min(d[0] for d in dims)
    blocks = [(jnp.int32(0), x)]
    for dim in dims:
        at, later = place(dim), []
        for k in range(dim[1]):
            step = lax.rem(at + dim[1] - k, dim[1]) * (dim[0] // unit)
            later += [(i + step, shift(b, dim, k) if k else b) for i, b in blocks]
        blocks = later
    return assemble(blocks)


def total(x, dims):
    for dim in dims:
        x = x + sum(shift(x, dim, k) for k in range(1, dim[1]))
    return x


def scatter(make, dims, grid):
    dim = dims[-1]
    at = place(dim)
    acc = None
    sent = []
    for k in range(1, dim[1]):
        sent.append(shift(make(lax.rem(at + k, dim[1])).astype(bf16), dim, k))
    acc = make(at).astype(f32) + sum(s.astype(f32) for s in sent)
    for dim in reversed(dims[:-1]):
        at = place(dim)
        low = acc.astype(bf16).reshape((-1, dim[1]) + acc.shape[1:])
        acc = acc.reshape((-1, dim[1]) + acc.shape[1:])
        own = pick(acc, at, 1)
        for k in range(1, dim[1]):
            own = own + shift(pick(low, lax.rem(at + k, dim[1]), 1), dim, k).astype(f32)
        acc = own
    return acc[0]


def feature_tables(heads):
    pairs = [(a, b) for a in range(QK + 1) for b in range(a, QK + 1)]
    one = np.zeros((heads, heads * QK, FEATS), np.float32)
    two = np.zeros((heads, heads * QK, FEATS), np.float32)
    rows = np.zeros((8, FEATS), np.float32)
    for f, (a, b) in enumerate(pairs):
        for h in range(heads):
            if a < QK:
                one[h, h * QK + a, f] = 1
            if b < QK:
                two[h, h * QK + b, f] = 1
        rows[0, f] = a == QK
        rows[1, f] = b == QK
        if a == QK:
            rows[2, f] = 1.0
        elif b == QK:
            rows[2, f] = QK**-0.5
        else:
            rows[2, f] = (0.5 if a == b else 1.0) / QK
    return jnp.asarray(one, bf16), jnp.asarray(two, bf16), jnp.asarray(rows)


def dot(a, b):
    return lax.dot_general(a, b, (((1,), (0,)), ((), ())), preferred_element_type=f32)


def dot_rows(a, b):
    return lax.dot_general(a, b, (((0,), (0,)), ((), ())), preferred_element_type=f32)


def dot_cols(a, b):
    return lax.dot_general(a, b, (((1,), (1,)), ((), ())), preferred_element_type=f32)


def halves(x):
    high = x.astype(bf16)
    return high, (x - high.astype(f32)).astype(bf16)


def features(x, one, two, rows):
    return dot(x, one) + rows[0:1], dot(x, two) + rows[1:2]


def total_row(state):
    return jnp.concatenate([state[FEATS : FEATS + 1], state[FEATS + 1 : FEATS + 2, : FEATS - 128]], axis=1)


def store_state(ref, state, row):
    ref[0, 0, :FEATS, :] = state
    ref[0, 0, FEATS:, :] = jnp.zeros((ROWS - FEATS, state.shape[1]), f32)
    ref[0, 0, FEATS : FEATS + 1, :] = row[:, :128]
    ref[0, 0, FEATS + 1 : FEATS + 2, : FEATS - 128] = row[:, 128:]


def kept_rows(scal, tile, tokens):
    index = lax.broadcasted_iota(jnp.int32, (tokens, 1), 0) + tile * tokens
    return index >= scal[tile]


def state_body(scal, k_ref, v_ref, one, two, rows, out_ref):
    tile = pl.program_id(0)
    a, b = features(k_ref[...], one[0], two[0], rows)
    phi = jnp.where(kept_rows(scal, tile, a.shape[0]), a * b, 0.0)
    high, low = halves(phi)
    v = v_ref[...]
    store_state(out_ref, dot_rows(high, v) + dot_rows(low, v), jnp.sum(phi, axis=0, keepdims=True))


def weights(q_ref, k_ref, lo_ref, tile, head):
    tokens, lanes = q_ref.shape
    lane = lax.broadcasted_iota(jnp.int32, (tokens, lanes), 1) // QK == head
    q = jnp.where(lane, q_ref[...], jnp.zeros((), bf16))
    score = dot_cols(q, k_ref[...]) * QK**-0.5
    row = lax.broadcasted_iota(jnp.int32, score.shape, 0)
    col = lax.broadcasted_iota(jnp.int32, score.shape, 1)
    lo = lo_ref[...] - tile * tokens
    mask = (col <= row) & (col >= lo)
    weight = jnp.where(mask, 1.0 + score + 0.5 * score * score, 0.0)
    return lane, score, mask, weight, lo < 0


def forward_body(q_ref, k_ref, v_ref, lo_ref, carry_ref, one, two, rows, y_ref, mixed_ref):
    tile, head = pl.program_id(0), pl.program_id(1)
    _, _, _, weight, alive = weights(q_ref, k_ref, lo_ref, tile, head)
    a, b = features(q_ref[...], one[0], two[0], rows)
    phi = jnp.where(alive, a * b * rows[2:3], 0.0)
    high, low = halves(phi)
    carry = carry_ref[0, 0]
    s_high, s_low = halves(carry[:FEATS])
    numer = dot(weight.astype(bf16), v_ref[...])
    numer = numer + (dot(high, s_high) + dot(high, s_low) + dot(low, s_high))
    denom = jnp.sum(weight, axis=1, keepdims=True) + jnp.sum(phi * total_row(carry), axis=1, keepdims=True)
    y = numer / denom
    y_ref[...] = y
    mixed_ref[...] = y.astype(bf16)


def spread(t, a, b, one, two):
    first_high, first_low = halves(t * b)
    second_high, second_low = halves(t * a)
    return (
        dot_cols(first_high, one) + dot_cols(first_low, one) + dot_cols(second_high, two) + dot_cols(second_low, two)
    )


def backward_body(
    q_ref, k_ref, v_ref, lo_ref, carry_ref, one, two, rows, y_ref, d_ref, dq_ref, dk_ref, dv_ref, ds_ref, dq_acc, dk_acc
):
    tile, head = pl.program_id(0), pl.program_id(1)
    lane, score, mask, weight, alive = weights(q_ref, k_ref, lo_ref, tile, head)
    a, b = features(q_ref[...], one[0], two[0], rows)
    phi = jnp.where(alive, a * b * rows[2:3], 0.0)
    high, low = halves(phi)
    carry = carry_ref[0, 0]
    s_high, s_low = halves(carry[:FEATS])
    row = total_row(carry)
    denom = jnp.sum(weight, axis=1, keepdims=True) + jnp.sum(phi * row, axis=1, keepdims=True)
    d = d_ref[...].astype(f32)
    g = d / denom
    c = -jnp.sum(d * y_ref[...], axis=1, keepdims=True) / denom
    g_high, g_low = halves(g)
    v = v_ref[...]
    dk = dot_cols(g_high, v) + dot_cols(g_low, v) + c
    ds = jnp.where(mask, dk * (1.0 + score) * QK**-0.5, 0.0).astype(bf16)
    dv_ref[...] = dot_rows(weight.astype(bf16), g_high)
    dphi = dot_cols(g_high, s_high) + dot_cols(g_high, s_low) + dot_cols(g_low, s_high) + c * row
    t = jnp.where(alive, dphi * rows[2:3], 0.0)
    dq = jnp.where(lane, dot(ds, k_ref[...]), 0.0) + spread(t, a, b, one[0], two[0])
    dkeys = jnp.where(lane, dot_rows(ds, q_ref[...]), 0.0)

    @pl.when(head == 0)
    def _():
        dq_acc[...] = dq
        dk_acc[...] = dkeys

    @pl.when(head > 0)
    def _():
        dq_acc[...] += dq
        dk_acc[...] += dkeys

    @pl.when(head == pl.num_programs(1) - 1)
    def _():
        dq_ref[...] = dq_acc[...].astype(bf16)
        dk_ref[...] = dk_acc[...]

    state = dot_rows(high, g_high) + dot_rows(high, g_low) + dot_rows(low, g_high)
    store_state(ds_ref, state, jnp.sum(phi * c, axis=0, keepdims=True))


def carried_body(scal, k_ref, v_ref, one, two, rows, grad_ref, dk_in, dv_in, dk_ref, dv_ref, acc):
    tile, head = pl.program_id(0), pl.program_id(1)
    a, b = features(k_ref[...], one[0], two[0], rows)
    keep = kept_rows(scal, tile, a.shape[0])
    high, low = halves(jnp.where(keep, a * b, 0.0))
    grad = grad_ref[0, 0]
    g_high, g_low = halves(grad[:FEATS])
    v = v_ref[...]
    dv = dv_in[...] + dot(high, g_high) + dot(high, g_low) + dot(low, g_high)
    dv_ref[...] = dv.astype(bf16)
    t = jnp.where(keep, dot_cols(v, g_high) + dot_cols(v, g_low) + total_row(grad), 0.0)
    dk = spread(t, a, b, one[0], two[0])

    @pl.when(head == 0)
    def _():
        acc[...] = dk_in[...] + dk

    @pl.when(head > 0)
    def _():
        acc[...] += dk

    @pl.when(head == pl.num_programs(1) - 1)
    def _():
        dk_ref[...] = acc[...].astype(bf16)


class Attention:
    def __init__(self, qkv, lo, heads, tokens):
        self.qkv, self.heads, self.tokens = qkv, heads, tokens
        self.lo = lo[:, None]
        self.scal = jnp.stack([lo[tokens - 1], lo[2 * tokens - 1]])
        self.tables = feature_tables(heads)
        lanes = heads * QK
        self.value = (qkv.shape[1] - 2 * lanes) // heads
        skip = 2 * lanes // self.value
        self.q = pl.BlockSpec((tokens, lanes), lambda t, h: (t, 0))
        self.k = pl.BlockSpec((tokens, lanes), lambda t, h: (t, 1))
        self.v = pl.BlockSpec((tokens, self.value), lambda t, h: (t, h + skip))
        self.o = pl.BlockSpec((tokens, self.value), lambda t, h: (t, h))
        self.l = pl.BlockSpec((tokens, 1), lambda t, h: (t, 0))
        self.s = pl.BlockSpec((1, 1, ROWS, self.value), lambda t, h: (h, t, 0, 0))
        self.e = pl.BlockSpec((1, lanes, FEATS), lambda t, h: (h, 0, 0))
        self.r = pl.BlockSpec((8, FEATS), lambda t, h: (0, 0))
        self.m = pl.BlockSpec(memory_space=pltpu.SMEM)
        self.table_specs = [self.e, self.e, self.r]
        self.acc = pltpu.VMEM((tokens, lanes), f32)
        self.state_shape = jax.ShapeDtypeStruct((heads, 2, ROWS, self.value), f32)

    def wide(self, kind):
        return jax.ShapeDtypeStruct((2 * self.tokens, self.heads * self.value), kind)

    def narrow(self, kind):
        return jax.ShapeDtypeStruct((2 * self.tokens, self.heads * QK), kind)

    def call(self, body, ins, outs, shapes, scratch, flops, args):
        size = sum(int(np.prod(a.shape)) * a.dtype.itemsize for a in list(args) + list(shapes))
        return pl.pallas_call(
            body,
            grid=(2, self.heads),
            in_specs=ins,
            out_specs=outs,
            out_shape=shapes,
            scratch_shapes=scratch,
            compiler_params=pltpu.CompilerParams(vmem_limit_bytes=VMEM),
            cost_estimate=pl.CostEstimate(flops=flops, bytes_accessed=size, transcendentals=0),
        )(*args)

    def states(self):
        (out,) = self.call(
            state_body,
            [self.m, self.k, self.v] + self.table_specs,
            [self.s],
            [self.state_shape],
            [],
            3 * 10**9,
            (self.scal, self.qkv, self.qkv, *self.tables),
        )
        return out

    def forward(self, carry):
        return self.call(
            forward_body,
            [self.q, self.k, self.v, self.l, self.s] + self.table_specs,
            [self.o, self.o],
            [self.wide(f32), self.wide(bf16)],
            [],
            10 * 10**9,
            (self.qkv, self.qkv, self.qkv, self.lo, carry, *self.tables),
        )

    def backward(self, carry, y, d_heads):
        return self.call(
            backward_body,
            [self.q, self.k, self.v, self.l, self.s] + self.table_specs + [self.o, self.o],
            [self.q, self.q, self.o, self.s],
            [self.narrow(bf16), self.narrow(f32), self.wide(f32), self.state_shape],
            [self.acc, self.acc],
            30 * 10**9,
            (self.qkv, self.qkv, self.qkv, self.lo, carry, *self.tables, y, d_heads),
        )

    def carried(self, grad, dk, dv):
        return self.call(
            carried_body,
            [self.m, self.k, self.v] + self.table_specs + [self.s, self.q, self.o],
            [self.q, self.o],
            [self.narrow(bf16), self.wide(bf16)],
            [self.acc],
            10 * 10**9,
            (self.scal, self.qkv, self.qkv, *self.tables, grad, dk, dv),
        )


def others(state, earlier, kind):
    n = lax.axis_size("tok")
    me = lax.axis_index("tok")
    sign = 1 if earlier else -1
    if n != 32:
        parts = lax.all_gather(state.astype(kind), "tok").astype(f32)
        index = jnp.arange(n)
        before = (sign * (me // 2 - index // 2) > 0) & (index % 2 == me % 2)
        return jnp.sum(jnp.where(before.reshape((n,) + (1,) * state.ndim), parts, 0.0), axis=0)
    plane = (me // 2) % 4
    slices = state.astype(kind).reshape((4, state.shape[0] // 4) + state.shape[1:])
    mine = [pick(slices, plane)]
    for k in range(1, 4):
        mine.append(flip(pick(slices, plane ^ k), 2 * k))
    mine = [part.astype(f32) for part in mine]
    whole = sum(mine).astype(kind)
    beyond = sum(shift(whole, (8, 4), sign * k, False).astype(f32) for k in range(1, 4))
    pieces = []
    for k in range(4):
        before = beyond
        for j in range(4):
            if j != k:
                before = before + jnp.where(sign * ((plane ^ k) - (plane ^ j)) > 0, mine[j], 0.0)
        before = before.astype(kind)
        pieces.append((plane ^ k, flip(before, 2 * k) if k else before))
    return assemble(pieces).reshape(state.shape).astype(f32)


def row_starts(positions, lengths, offsets):
    inside = (positions[:, None] >= offsets[None, :]) & (positions[:, None] < offsets[None, :] + lengths[None, :])
    return jnp.sum(jnp.where(inside, offsets[None, :], 0), axis=1)


def ordered(first, mine, theirs, axis=0):
    return jnp.concatenate([jnp.where(first, mine, theirs), jnp.where(first, theirs, mine)], axis=axis)


def shards(
    block_input,
    lengths,
    offsets,
    norm1_gain,
    w_query,
    w_key,
    w_value,
    w_out,
    norm2_gain,
    w_gate,
    w_up,
    w_down,
    out_grad,
):
    n = lax.axis_size("tok")
    me = lax.axis_index("tok")
    core, quad = me % 2, me % 4
    even = core == 0
    cdims, qdims = chip_dims(n), quad_dims(n)
    chips, quads = n // 2, n // 4
    tokens, width = block_input.shape
    rows = w_query.shape[0]
    heads = w_query.shape[1] // QK // 2
    half = width // 2
    lanes = heads * QK
    z_first = cdims
    x_last = [cdims[0]] + cdims[1:][::-1]

    def column_half(w, which):
        return lax.dynamic_slice_in_dim(w, which * (w.shape[1] // 2), w.shape[1] // 2, 1)

    def row_half(w, which):
        return lax.dynamic_slice_in_dim(w, which * (w.shape[0] // 2), w.shape[0] // 2, 0)

    gains = jnp.stack([norm1_gain, norm2_gain]).astype(f32)
    gains = gather(gather(gains, [(1, 2)]), cdims).reshape(n, 2, rows).transpose(1, 0, 2).reshape(2, 1, width)
    gain_one, gain_two = gains[0], gains[1]

    def by_core(which):
        return jnp.concatenate([column_half(w, which) for w in (w_query, w_key, w_value)], axis=1)

    chip_qkv = ordered(even, by_core(core), flip(by_core(1 - core), 1))
    cut = chip_qkv.shape[1] // 2
    qkv_all = jnp.concatenate(
        [gather(chip_qkv[:, :cut], z_first), gather(chip_qkv[:, cut:], x_last)], axis=2
    ).reshape(width, 2 * cut)

    inputs32 = block_input.astype(f32)
    ratio_one = lax.rsqrt(jnp.mean(inputs32 * inputs32, axis=1, keepdims=True) + eps)
    normed_one = inputs32 * ratio_one
    hidden_one = (normed_one * gain_one).astype(bf16)
    hidden_chip = ordered(even, hidden_one, flip(hidden_one, 1))
    qkv = dot(hidden_chip, qkv_all).astype(bf16)

    first = (me // 2) * 2 * tokens
    positions = first + jnp.arange(2 * tokens, dtype=jnp.int32)
    lo = row_starts(positions, lengths, offsets) - first
    attention = Attention(qkv, lo, heads, tokens)
    states = attention.states()
    fresh0 = (lo[tokens - 1] >= 0).astype(f32)
    fresh1 = (lo[2 * tokens - 1] >= tokens).astype(f32)
    entering = others(states[:, 1] + (1.0 - fresh1) * states[:, 0], True, f32)
    carry = jnp.stack([entering, states[:, 0] + (1.0 - fresh0) * entering], axis=1)
    y_heads, mixed_heads = attention.forward(carry)
    mixed = ordered(even, row_half(mixed_heads, core), flip(row_half(mixed_heads, 1 - core), 1), 1)

    chip_out = ordered(even, column_half(w_out, core), flip(column_half(w_out, 1 - core), 1))
    out_half = gather(chip_out, z_first).reshape(width, half)
    out_all = ordered(even, out_half, flip(out_half, 1), 1)
    middle = inputs32 + dot(mixed, out_all)
    ratio_two = lax.rsqrt(jnp.mean(middle * middle, axis=1, keepdims=True) + eps)
    normed_two = middle * ratio_two
    hidden_two = (normed_two * gain_two).astype(bf16)

    unit = w_down.shape[0]
    padded = -(-unit // 16) * 16
    cols = quads * padded

    def by_quad(w):
        w = w.reshape(rows, quads, 4, unit)
        w = jnp.pad(w, ((0, 0), (0, 0), (0, 0), (0, padded - unit)))
        return w.transpose(2, 0, 1, 3).reshape(4, rows, cols)

    gate_up = jnp.concatenate([by_quad(w_gate), by_quad(w_up)], axis=2)
    pieces = [(quad, pick(gate_up, quad))]
    for k in range(1, 4):
        pieces.append((quad ^ k, flip(pick(gate_up, quad ^ k), k)))
    gate_up = assemble(pieces).reshape(4 * rows, 2 * cols)
    gate_up = gather_blocks(gate_up, qdims).reshape(width, 2 * cols)
    down = jnp.pad(w_down, ((0, padded - unit), (0, 0)))
    down = gather_blocks(down, qdims).reshape(cols, width)

    def to_quad(x):
        near = jnp.concatenate([x, flip(x, 1)])
        far = flip(x, 2)
        return near, jnp.concatenate([far, flip(far, 1)])

    def from_quad(near, far):
        far_sum = far[:tokens] + flip(far[tokens:].astype(bf16), 1).astype(f32)
        near_sum = near[:tokens] + flip(near[tokens:].astype(bf16), 1).astype(f32)
        return near_sum + flip(far_sum.astype(bf16), 2).astype(f32)

    hidden_quad = to_quad(hidden_two)
    grad_quad = to_quad(out_grad)

    def ffn(hidden, grad):
        gate = dot(hidden, gate_up[:, :cols])
        upper = dot(hidden, gate_up[:, cols:])
        sigma = jax.nn.sigmoid(gate)
        smooth = gate * sigma
        activation = (smooth * upper).astype(bf16)
        out = dot(activation, down)
        d_act = dot_cols(grad, down)
        d_gate = (d_act * upper * sigma * (1.0 + gate * (1.0 - sigma))).astype(bf16)
        d_up = (d_act * smooth).astype(bf16)
        d_hidden = dot_cols(d_gate, gate_up[:, :cols]) + dot_cols(d_up, gate_up[:, cols:])
        return out, activation, d_gate, d_up, d_hidden

    near, far = ffn(hidden_quad[0], grad_quad[0]), ffn(hidden_quad[1], grad_quad[1])
    output = (middle + from_quad(near[0], far[0])).astype(bf16)
    d_hidden_two = from_quad(near[4], far[4])
    activation, d_gate, d_up = (jnp.concatenate([near[i], far[i]]) for i in (1, 2, 3))
    hidden_quad = jnp.concatenate(hidden_quad)
    grad_quad = jnp.concatenate(grad_quad)

    last = qdims[-1][1]

    def hidden_part(index):
        return pick(hidden_quad.reshape(4 * tokens, quads // last, last, width // quads), index, 2).reshape(
            4 * tokens, width // last
        )

    def scatter_gate(d):
        total = scatter(
            lambda index: dot_rows(hidden_part(index), d).reshape(quads // last, width // quads, cols), qdims, None
        )
        total = total.reshape(4, rows, cols)
        low = total.astype(bf16)
        parts = [(quad, pick(total, quad))]
        for k in range(1, 4):
            parts.append((quad ^ k, flip(pick(low, quad ^ k), k).astype(f32)))
        return assemble(parts).reshape(4, rows, quads, padded)[..., :unit].transpose(1, 2, 0, 3).reshape(rows, -1)

    term_down = dot_rows(activation, grad_quad).reshape(quads // last, last, padded, width)
    grad_down = scatter(lambda index: pick(term_down, index, 1), qdims, None)[:unit]
    grad_gate = scatter_gate(d_gate)
    grad_up = scatter_gate(d_up)

    term_norm_two = jnp.sum(d_hidden_two * normed_two, axis=0)
    scaled_two = d_hidden_two * gain_two
    d_middle = out_grad.astype(f32) + ratio_two * (
        scaled_two - normed_two * jnp.mean(scaled_two * normed_two, axis=1, keepdims=True)
    )
    d_mixed = d_middle.astype(bf16)
    d_mixed_chip = ordered(even, d_mixed, flip(d_mixed, 1))

    d_heads = dot_cols(d_mixed_chip, row_half(out_all, core)).astype(bf16)
    dq, dk, dv, d_states = attention.backward(carry, y_heads, d_heads)
    leaving = others(d_states[:, 0] + (1.0 - fresh0) * d_states[:, 1], False, bf16)
    d_states = jnp.stack([d_states[:, 1] + (1.0 - fresh1) * leaving, leaving], axis=1)
    dk, dv = attention.carried(d_states, dk, dv)
    d_qkv = jnp.concatenate([dq, dk, dv], axis=1)

    d_rows = row_half(d_qkv, 1 - core)
    theirs = flip(dot_cols(d_rows, qkv_all).astype(bf16), 1)
    d_hidden_one = dot_cols(row_half(d_qkv, core), qkv_all) + theirs.astype(f32)
    term_norm_one = jnp.sum(d_hidden_one * normed_one, axis=0)
    scaled_one = d_hidden_one * gain_one
    input_grad = d_middle + ratio_one * (
        scaled_one - normed_one * jnp.mean(scaled_one * normed_one, axis=1, keepdims=True)
    )

    last_chip = cdims[-1][1]

    def chip_part(x, index):
        return pick(x.reshape(2 * tokens, chips // last_chip, last_chip, 2 * rows), index, 2).reshape(
            2 * tokens, width // last_chip
        )

    def scatter_rows(x, d):
        total = scatter(
            lambda index: dot_rows(chip_part(x, index), d).reshape(chips // last_chip, 2 * rows, d.shape[1]),
            cdims,
            None,
        )
        return row_half(total, core), flip(row_half(total, 1 - core), 1)

    mine, theirs = scatter_rows(hidden_chip, d_qkv)
    spans = [(0, lanes), (lanes, 2 * lanes), (2 * lanes, 2 * lanes + half)]
    grad_query, grad_key, grad_value = (ordered(even, mine[:, a:b], theirs[:, a:b], 1) for a, b in spans)
    mixed_chip = jnp.concatenate(
        [
            ordered(even, mixed_heads[:tokens], flip(mixed_heads[:tokens], 1), 1),
            ordered(even, mixed_heads[tokens:], flip(mixed_heads[tokens:], 1), 1),
        ]
    )
    grad_out = ordered(even, *scatter_rows(mixed_chip, column_half(d_mixed_chip, core)), 1)

    def norm_shard(term):
        term = total(term.reshape(1, width), [(1, 2)] + cdims).reshape(n, rows)
        return pick(term, me)

    return (
        output,
        input_grad,
        norm_shard(term_norm_one),
        grad_query,
        grad_key,
        grad_value,
        grad_out,
        norm_shard(term_norm_two),
        grad_gate,
        grad_up,
        grad_down,
    )


def solution(mesh):
    return jax.shard_map(
        shards,
        mesh=mesh,
        in_specs=(
            P("tok", None),
            P(),
            P(),
            P("tok"),
            P("tok", None),
            P("tok", None),
            P("tok", None),
            P("tok", None),
            P("tok"),
            P("tok", None),
            P("tok", None),
            P("tok", None),
            P("tok", None),
        ),
        out_specs=(
            P("tok", None),
            P("tok", None),
            P("tok"),
            P("tok", None),
            P("tok", None),
            P("tok", None),
            P("tok", None),
            P("tok"),
            P("tok", None),
            P("tok", None),
            P("tok", None),
        ),
        check_vma=False,
    )
```

time: 3710 us -> 1600 us (0.43)
  blocking collectives: 1000 us -> 0 us
  waiting for transfers between devices: 1180 us -> 679 us
  matrix products: 526 us -> 251 us
  local copies, waits for them, and re-layouts: 515 us -> 294 us
  other arithmetic: 285 us -> 104 us
  Pallas kernels: 0 us -> 111 us
  loops' own time: 85.4 us -> 0 us
  starting transfers between devices: 74.3 us -> 148 us
    unnamed x4 -> x0, blocking collectives: 912 us -> none
    reduce_scatter x6 -> x0, waiting for transfers between devices: 804 us -> none  [the longest x1 503 us: shards(): lax.psum_scatter(term_up, 'tok', scatter_dimension=0, tiled=True)]
    ppermute x0 -> x119, waiting for transfers between devices: none -> 679 us  [the longest x75 587 us: shift(): return lax.ppermute(x, 'tok', pairs)]
    all_gather x9 -> x0, waiting for transfers between devices: 366 us -> none  [the longest x1 208 us: entering(): pieces = jax.tree.map(lambda part: lax.all_gather(part, axis), value)]
    dot_general x57 -> x26, matrix products: 526 us -> 251 us  [the longest x9 87.1 us: dot_cols(): lax.dot_general(a, b, (((1,), (1,)), ((), ())), preferred_element_type=f32)]
    dynamic_update_slice x28 -> x58, local copies, waits for them, and re-layouts: 229 us -> 38.4 us  [assemble(): out = lax.dynamic_update_index_in_dim(out, block, index, 0)]
    ppermute x0 -> x119, starting transfers between devices: none -> 148 us  [the longest x75 123 us: shift(): return lax.ppermute(x, 'tok', pairs)]
    select_n x62 -> x10, other arithmetic: 140 us -> 11.1 us  [ordered(): jnp.where(first, mine, theirs)]
  transfers between devices with their start and end apart: 16 -> 119, of which waited for: 7 -> 52; matrix products, arithmetic and copies ran while one was open for 51% -> 32% of each run, Pallas kernels for 0% -> 7%
where the time goes in v1:
time: 1600 us; the launch traced here: 1590 us
  waiting for transfers between devices  679 us (42%)
  local copies, waits for them, and re-layouts  294 us (18%)
  matrix products  251 us (16%)
  starting transfers between devices  148 us (9%)
  Pallas kernels  111 us (7%)
  other arithmetic  104 us (6%)
    ppermute x75, waiting for transfers between devices, shift(): return lax.ppermute(x, 'tok', pairs)  587 us
    ppermute x75, starting transfers between devices, shift(): return lax.ppermute(x, 'tok', pairs)  123 us
    pallas_call x4, Pallas kernels, call(): pl.pallas_call(body, grid=(2, self.heads), in_specs=ins, out_specs=outs,...  111 us
    unnamed x178, local copies, waits for them, and re-layouts  103 us
    ppermute x44, waiting for transfers between devices, flip(): return lax.ppermute(x, 'tok', [(i, i ^ bits) for i in range(n)])  92 us
    dot_general x9, matrix products, dot_cols(): lax.dot_general(a, b, (((1,), (1,)), ((), ())), preferred_element_type=f32)  87.1 us
    dot_general x8, matrix products, dot(): lax.dot_general(a, b, (((1,), (0,)), ((), ())), preferred_element_type=f32)  83 us
    dot_general x9, matrix products, dot_rows(): lax.dot_general(a, b, (((0,), (0,)), ((), ())), preferred_element_type=f32)  80.6 us
  transfers between devices with their start and end apart: 119, of which 52 were waited for; matrix products, arithmetic and copies ran while one was open for 32% of the time, Pallas kernels for 7%

profile of v1, /device:TPU:0, one launch (start us, length us, event | category | flops | bytes accessed | tf_op | source)
XLA Modules:
  0.0 1590.5 jit_solution(12385250046266245871)
XLA Ops:
  55.3 16.0 %collective-permute-start.2 = (f32[2,2,64]{2,0,1:T(2,128)S(1)}, f32[2,2,64]{2,0,1:T(2,128)S(1)}, u32[]{:S(2)}, u32[]{:S(2)}) collective-permute-start(f32[2,2,64]{2,0,1:T(2,128)S(1)} %dynamic_update_slice.227), channel_id=1, source_target_pairs={{0,16},{1,17},{2,18},{3,19},{4,20},{5,21},{6,22},{7,23},{8,24},{9,... | collective-permute-start | bytes 3080 | tf_op jit(solution)/shard_map/ppermute | solution.py:46
  100.9 7.6 collective-permute-done.14
  121.8 7.7 collective-permute-done.9
  186.9 45.7 %collective-permute-done.16 = bf16[4,128,640]{2,1,0:T(8,128)(2,1)S(1)} collective-permute-done((bf16[4,128,640]{2,1,0:T(8,128)(2,1)S(1)}, bf16[4,128,640]{2,1,0:T(8,128)(2,1)S(1)}, u32[]{:S(2)}, u32[]{:S(2)}) %collective-permute-start.16) | collective-permute-done | bytes 655392 | tf_op jit(solution)/shard_map/ppermute | solution.py:46
  238.1 11.9 collective-permute-done.50
  253.5 13.0 collective-permute-done.51
  274.6 7.6 collective-permute-done.52
  286.0 44.9 %collective-permute-done.40 = bf16[256,2816]{1,0:T(8,128)(2,1)S(1)} collective-permute-done((bf16[256,2816]{1,0:T(8,128)(2,1)S(1)}, bf16[256,2816]{1,0:T(8,128)(2,1)S(1)}, u32[]{:S(2)}, u32[]{:S(2)}) %collective-permute-start.40) | collective-permute-done | bytes 1441824 | tf_op jit(solution)/shard_map/ppermute | solution.py:46
  332.6 15.4 collective-permute-done.41
  350.8 14.6 collective-permute-done.42
  370.2 22.2 %collective-permute-done.17 = bf16[2,4,128,640]{3,2,0,1:T(8,128)(2,1)S(1)} collective-permute-done((bf16[2,4,128,640]{3,2,0,1:T(8,128)(2,1)S(1)}, bf16[2,4,128,640]{3,2,0,1:T(8,128)(2,1)S(1)}, u32[]{:S(2)}, u32[]{:S(2)}) %collective-permute-start.17) | collective-permute-done | bytes 1310752 | tf_op jit(solution)/shard_map/ppermute | solution.py:46
  399.1 7.2 convolution_convert_fusion.k_ref.v_ref.q_ref
  406.3 14.0 shard_map.239
  425.3 11.6 fusion.34
  436.8 7.9 collective-permute-done.20
  446.6 29.5 %collective-permute-start.23 = (f32[2,168,128]{2,1,0:T(8,128)S(1)}, f32[2,168,128]{2,1,0:T(8,128)}, u32[]{:S(2)}, u32[]{:S(2)}) collective-permute-start(f32[2,168,128]{2,1,0:T(8,128)S(1)} %fusion.125), channel_id=1, source_target_pairs={{0,24},{1,25},{2,26},{3,27},{4,28},{5,29},{6,30},{7,31}} | collective-permute-start | bytes 516104 | tf_op jit(solution)/shard_map/ppermute | solution.py:46
  482.7 7.7 reshape.345
  499.7 54.4 %collective-permute-done.25 = f32[2,168,128]{2,1,0:T(8,128)S(1)} collective-permute-done((f32[2,168,128]{2,1,0:T(8,128)S(1)}, f32[2,168,128]{2,1,0:T(8,128)S(1)}, u32[]{:S(2)}, u32[]{:S(2)}) %collective-permute-start.25) | collective-permute-done | bytes 172064 | tf_op jit(solution)/shard_map/ppermute | solution.py:36
  564.8 22.5 %shard_map.240 = (f32[1024,1024]{1,0:T(8,128)}, bf16[1024,1024]{1,0:T(8,128)(2,1)}) custom-call(bf16[1024,1280]{1,0:T(8,128)(2,1)} %convolution_convert_fusion.k_ref.v_ref.q_ref, bf16[1024,1280]{1,0:T(8,128)(2,1)} %convolution_convert_fusion.k_ref.v_ref.q_ref, bf16[1024,1280]{1,0:T(8,128)(2,1)} %convolution_convert_fusion.k_ref.v_ref.q_ref, ...), custom_call_target="tpu_custom_call" | custom-call | flops 10000000000 | bytes 16196608 | tf_op jit(solution)/shard_map/pallas_call | solution.py:326
  590.1 9.8 constant_dynamic-slice_fusion.21
  599.9 10.5 copy.114
  610.5 10.7 copy.113
  629.5 25.3 %collective-permute-done.45 = bf16[256,2816]{1,0:T(8,128)(2,1)S(1)} collective-permute-done((bf16[256,2816]{1,0:T(8,128)(2,1)S(1)}, bf16[256,2816]{1,0:T(8,128)(2,1)S(1)}, u32[]{:S(2)}, u32[]{:S(2)}) %collective-permute-start.45) | collective-permute-done | bytes 1441824 | tf_op jit(solution)/shard_map/ppermute | solution.py:46
  666.3 12.6 fusion.38
  678.9 19.0 %maximum_maximum_fusion = bf16[1024,2048]{1,0:T(8,128)(2,1)} fusion(bf16[512,1024]{1,0:T(8,128)(2,1)S(1)} %get-tuple-element.67, bf16[512,1024]{1,0:T(8,128)(2,1)S(1)} %get-tuple-element.66, bf16[512,1024]{1,0:T(8,128)(2,1)S(1)} %get-tuple-element.65, bf16[512,1024]{1,0:T(8,128)(2,1)S(1)} %get-tuple-element.64), kind=kLoop, calls=%fused_computation.77 | loop fusion | flops 16777216 | bytes 8388608 | tf_op jit(solution)/shard_map/concatenate | solution.py:611
  697.8 8.1 reshape.350
  705.9 11.2 constant_dynamic-slice_fusion.16
  717.1 10.5 copy.116
  727.6 10.6 copy.115
  739.0 11.4 fusion.66
  750.4 14.7 multiply_convert_fusion.3
  765.1 13.6 fusion.62
  778.8 10.2 convolution_add_fusion.1
  791.0 10.3 fusion.172
  805.3 10.3 fusion.64
  815.5 15.4 multiply_convert_fusion.1
  830.9 11.8 fusion.60
  848.4 14.4 reshape.357
  862.9 20.3 %constant_dynamic-slice_fusion.10 = (bf16[2048,4,1,256]{3,2,1,0:T(2,128)(2,1)}, bf16[2048,4,1,256]{3,2,1,0:T(2,128)(2,1)}) fusion(bf16[2048,4,2,256]{3,2,1,0:T(2,128)(2,1)} %reshape.357, s32[]{:T(128)S(6)} %select_n.656, s32[]{:T(128)S(6)} %select_n.657), kind=kLoop, calls=%fused_computation.326 | loop fusion | bytes 16777224 | tf_op jit(solution)/shard_map/jit(dynamic_index_in_dim)/dynamic_slice | solution.py:54
  883.2 20.2 %copy.118 = bf16[2048,4,1,256]{0,3,1,2:T(8,128)(2,1)} copy(bf16[2048,4,1,256]{3,2,1,0:T(2,128)(2,1)} %get-tuple-element.52) | data formatting | bytes 8388608
  903.4 10.6 fusion.57
  914.0 8.1 fusion.54
  922.1 8.8 convolution_add_fusion
  934.8 9.0 fusion.173
  948.4 20.1 %copy.117 = bf16[2048,4,1,256]{0,3,1,2:T(8,128)(2,1)} copy(bf16[2048,4,1,256]{3,2,1,0:T(2,128)(2,1)} %get-tuple-element.51) | data formatting | bytes 8388608
  969.9 18.8 %fusion.1 = f32[1408,2048]{1,0:T(8,128)} fusion(bf16[512,2048]{1,0:T(8,128)(2,1)} %collective-permute-done.61, bf16[512,2048]{1,0:T(8,128)(2,1)} %collective-permute-done.60, bf16[512,2048]{1,0:T(8,128)(2,1)} %collective-permute-done.58, bf16[512,2048]{1,0:T(8,128)(2,1)} %param.28, bf16[1024,1408]{1,0:T(8,128)(2,1)} %get-tuple-element.50, ...), kind=kOutput, calls=%fused_computation.5 | convolution fusion | flops 11856248832 | bytes 25690112 | tf_op jit(solution)/shard_map/dot_general | solution.py:148
  1001.5 11.9 collective-permute-done.108
  1013.4 11.1 fusion.171
  1026.7 48.5 %collective-permute-done.101 = bf16[4,256,1408]{2,1,0:T(8,128)(2,1)} collective-permute-done((bf16[4,256,1408]{2,1,0:T(8,128)(2,1)}, bf16[4,256,1408]{2,1,0:T(8,128)(2,1)}, u32[]{:S(2)}, u32[]{:S(2)}) %collective-permute-start.101) | collective-permute-done | bytes 2883616 | tf_op jit(solution)/shard_map/ppermute | solution.py:46
  1075.2 9.9 fusion.170
  1086.1 50.4 %collective-permute-done.115 = bf16[4,176,2048]{2,1,0:T(8,128)(2,1)S(1)} collective-permute-done((bf16[4,176,2048]{2,1,0:T(8,128)(2,1)S(1)}, bf16[4,176,2048]{2,1,0:T(8,128)(2,1)S(1)}, u32[]{:S(2)}, u32[]{:S(2)}) %collective-permute-start.115) | collective-permute-done | bytes 2883616 | tf_op jit(solution)/shard_map/ppermute | solution.py:46
  1145.1 39.6 %collective-permute-done.103 = bf16[1,256,1408]{2,1,0:T(8,128)(2,1)S(1)} collective-permute-done((bf16[1,256,1408]{2,1,0:T(8,128)(2,1)S(1)}, bf16[1,256,1408]{2,1,0:T(8,128)(2,1)S(1)}, u32[]{:S(2)}, u32[]{:S(2)}) %collective-permute-start.103) | collective-permute-done | bytes 720928 | tf_op jit(solution)/shard_map/ppermute | solution.py:46
  1188.3 15.8 collective-permute-done.118
  1205.3 26.2 %collective-permute-done.117 = bf16[1,176,2048]{2,1,0:T(8,128)(2,1)S(1)} collective-permute-done((bf16[1,176,2048]{2,1,0:T(8,128)(2,1)S(1)}, bf16[1,176,2048]{2,1,0:T(8,128)(2,1)S(1)}, u32[]{:S(2)}, u32[]{:S(2)}) %collective-permute-start.117) | collective-permute-done | bytes 720928 | tf_op jit(solution)/shard_map/ppermute | solution.py:46
  1234.8 17.5 %collective-permute-done.116 = bf16[1,176,2048]{2,1,0:T(8,128)(2,1)S(1)} collective-permute-done((bf16[1,176,2048]{2,1,0:T(8,128)(2,1)}, bf16[1,176,2048]{2,1,0:T(8,128)(2,1)S(1)}, u32[]{:S(2)}, u32[]{:S(2)}) %collective-permute-start.116) | collective-permute-done | bytes 720928 | tf_op jit(solution)/shard_map/ppermute | solution.py:46
  1262.5 8.1 fusion.164
  1283.2 45.9 %shard_map.241 = (bf16[1024,128]{1,0:T(8,128)(2,1)}, f32[1024,128]{1,0:T(8,128)}, f32[1024,1024]{1,0:T(8,128)}, f32[8,2,168,128]{3,2,1,0:T(8,128)}) custom-call(bf16[1024,1280]{1,0:T(8,128)(2,1)} %convolution_convert_fusion.k_ref.v_ref.q_ref, bf16[1024,1280]{1,0:T(8,128)(2,1)} %convolution_convert_fusion.k_ref.v_ref.q_ref, ...), custom_call_target="tpu_custom_call" | custom-call | flops 30000001024 | bytes 22553600 | tf_op jit(solution)/shard_map/pallas_call | solution.py:326
  1362.8 28.7 %shard_map.242 = (bf16[1024,128]{1,0:T(8,128)(2,1)}, bf16[1024,1024]{1,0:T(8,128)(2,1)}) custom-call(s32[2]{0:T(128)} %pad_add_fusion.scal, bf16[1024,1280]{1,0:T(8,128)(2,1)} %convolution_convert_fusion.k_ref.v_ref.q_ref, bf16[1024,1280]{1,0:T(8,128)(2,1)} %convolution_convert_fusion.k_ref.v_ref.q_ref, bf16[8,128,160]{2,1,0:T(8,128)(2,1)} %constant.623.clone.one, ...), custom_call_target="tpu_custom_call" | custom-call | flops 10000000000 | bytes 14357512 | tf_op jit(solution)/shard_map/pallas_call | solution.py:326
  1436.4 7.2 fusion.24
  1443.7 19.6 %collective-permute-done.89 = bf16[8,128,1024]{2,1,0:T(8,128)(2,1)} collective-permute-done((bf16[8,128,1024]{2,1,0:T(8,128)(2,1)}, bf16[8,128,1024]{2,1,0:T(8,128)(2,1)}, u32[]{:S(2)}, u32[]{:S(2)}) %collective-permute-start.89) | collective-permute-done | bytes 2097184 | tf_op jit(solution)/shard_map/ppermute | solution.py:46
  1479.2 17.6 %collective-permute-done.79 = f32[1,2048]{1,0:T(1,128)S(1)} collective-permute-done((f32[1,2048]{1,0:T(1,128)S(1)}, f32[1,2048]{1,0:T(1,128)S(1)}, u32[]{:S(2)}, u32[]{:S(2)}) %collective-permute-start.79) | collective-permute-done | bytes 8224 | tf_op jit(solution)/shard_map/ppermute | solution.py:46
  1497.3 21.3 %collective-permute-done.81 = bf16[8,128,1280]{2,1,0:T(8,128)(2,1)} collective-permute-done((bf16[8,128,1280]{2,1,0:T(8,128)(2,1)}, bf16[8,128,1280]{2,1,0:T(8,128)(2,1)}, u32[]{:S(2)}, u32[]{:S(2)}) %collective-permute-start.81) | collective-permute-done | bytes 2621472 | tf_op jit(solution)/shard_map/ppermute | solution.py:46
  1538.5 16.1 %collective-permute-done.82 = bf16[4,128,1280]{2,1,0:T(8,128)(2,1)} collective-permute-done((bf16[4,128,1280]{2,1,0:T(8,128)(2,1)S(1)}, bf16[4,128,1280]{2,1,0:T(8,128)(2,1)}, u32[]{:S(2)}, u32[]{:S(2)}) %collective-permute-start.82) | collective-permute-done | bytes 1310752 | tf_op jit(solution)/shard_map/ppermute | solution.py:46
  1567.8 19.0 %collective-permute-done.84 = bf16[1,128,1280]{2,1,0:T(8,128)(2,1)S(1)} collective-permute-done((bf16[1,128,1280]{2,1,0:T(8,128)(2,1)S(1)}, bf16[1,128,1280]{2,1,0:T(8,128)(2,1)S(1)}, u32[]{:S(2)}, u32[]{:S(2)}) %collective-permute-start.84) | collective-permute-done | bytes 327712 | tf_op jit(solution)/shard_map/ppermute | solution.py:46
  (598 shorter events, 454.5 us)
Async XLA Ops:
  2.8 171.0 %collective-permute-start.46 = (bf16[176,2048]{1,0:T(8,128)(2,1)}, bf16[176,2048]{1,0:T(8,128)(2,1)}, u32[]{:S(2)}, u32[]{:S(2)}) collective-permute-start(bf16[176,2048]{1,0:T(8,128)(2,1)} %pad.13), channel_id=1, source_target_pairs={{0,8},{1,9},{2,10},{3,11},{4,12},{5,13},{6,14},{7,15},{8,16},{9,17... | collective-permute-start | bytes 2162696 | tf_op jit(solution)/shard_map/ppermute | solution.py:46
  5.8 170.0 %collective-permute-start.47 = (bf16[176,2048]{1,0:T(8,128)(2,1)}, bf16[176,2048]{1,0:T(8,128)(2,1)}, u32[]{:S(2)}, u32[]{:S(2)}) collective-permute-start(bf16[176,2048]{1,0:T(8,128)(2,1)} %pad.13), channel_id=1, source_target_pairs={{0,16},{1,17},{2,18},{3,19},{4,20},{5,21},{6,22},{7,23},{8,24},{9,... | collective-permute-start | bytes 2162696 | tf_op jit(solution)/shard_map/ppermute | solution.py:46
  8.4 171.0 %collective-permute-start.48 = (bf16[176,2048]{1,0:T(8,128)(2,1)}, bf16[176,2048]{1,0:T(8,128)(2,1)}, u32[]{:S(2)}, u32[]{:S(2)}) collective-permute-start(bf16[176,2048]{1,0:T(8,128)(2,1)} %pad.13), channel_id=1, source_target_pairs={{0,24},{1,25},{2,26},{3,27},{4,28},{5,29},{6,30},{7,31},{8,0},{9,1... | collective-permute-start | bytes 2162696 | tf_op jit(solution)/shard_map/ppermute | solution.py:46
  11.3 76.6 %collective-permute-start.28 = (bf16[64,1024]{1,0:T(8,128)(2,1)}, bf16[64,1024]{1,0:T(8,128)(2,1)}, u32[]{:S(2)}, u32[]{:S(2)}) collective-permute-start(bf16[64,1024]{1,0:T(8,128)(2,1)} %constant_dynamic-slice_fusion.23), channel_id=1, source_target_pairs={{0,1},{1,0},{2,3},{3,2},{4,5},{5,4},{6,7},{7,6},{8,9},{9,8},{10,11... | collective-permute-start | bytes 393224 | tf_op jit(solution)/shard_map/ppermute | solution.py:36
  12.6 35.5 %collective-permute-start = (f32[2,64]{1,0:T(2,128)}, f32[2,64]{1,0:T(2,128)}, u32[]{:S(2)}, u32[]{:S(2)}) collective-permute-start(f32[2,64]{1,0:T(2,128)} %maximum_convert_fusion.1), channel_id=1, source_target_pairs={{0,1},{1,0},{2,3},{3,2},{4,5},{5,4},{6,7},{7,6},{8,9},{9,8},{10,11... | collective-permute-start | bytes 1544 | tf_op jit(solution)/shard_map/ppermute | solution.py:46
  88.0 50.4 %collective-permute-start.36 = (bf16[64,2816]{1,0:T(8,128)(2,1)}, bf16[64,2816]{1,0:T(8,128)(2,1)S(1)}, u32[]{:S(2)}, u32[]{:S(2)}) collective-permute-start(bf16[64,2816]{1,0:T(8,128)(2,1)} %get-tuple-element.85), channel_id=1, source_target_pairs={{0,1},{1,0},{2,3},{3,2},{4,5},{5,4},{6,7},{7,6},{8,9},{9,8},{10,11... | collective-permute-start | bytes 1081352 | tf_op jit(solution)/shard_map/ppermute | solution.py:36
  170.6 450.5 %collective-permute-start.60 = (bf16[512,2048]{1,0:T(8,128)(2,1)}, bf16[512,2048]{1,0:T(8,128)(2,1)}, u32[]{:S(2)}, u32[]{:S(2)}) collective-permute-start(bf16[512,2048]{1,0:T(8,128)(2,1)} %param.28), channel_id=1, source_target_pairs={{0,2},{1,3},{2,0},{3,1},{4,6},{5,7},{6,4},{7,5},{8,10},{9,11},{10,... | collective-permute-start | bytes 6291464 | tf_op jit(solution)/shard_map/ppermute | solution.py:36
  173.8 250.2 %collective-permute-start.58 = (bf16[512,2048]{1,0:T(8,128)(2,1)}, bf16[512,2048]{1,0:T(8,128)(2,1)}, u32[]{:S(2)}, u32[]{:S(2)}) collective-permute-start(bf16[512,2048]{1,0:T(8,128)(2,1)} %param.28), channel_id=1, source_target_pairs={{0,1},{1,0},{2,3},{3,2},{4,5},{5,4},{6,7},{7,6},{8,9},{9,8},{10,11... | collective-permute-start | bytes 6291464 | tf_op jit(solution)/shard_map/ppermute | solution.py:36
  175.9 56.6 %collective-permute-start.16 = (bf16[4,128,640]{2,1,0:T(8,128)(2,1)S(1)}, bf16[4,128,640]{2,1,0:T(8,128)(2,1)S(1)}, u32[]{:S(2)}, u32[]{:S(2)}) collective-permute-start(bf16[4,128,640]{2,1,0:T(8,128)(2,1)S(1)} %bitcast_dynamic-update-slice_fusion.39), channel_id=1, source_target_pairs={{0,2},{1,3},{2,0},{3,1},{4,6},{5,7},{6,4},{7,5},{8,10},{9,11},{10,... | collective-permute-start | bytes 1966088 | tf_op jit(solution)/shard_map/ppermute | solution.py:46
  179.5 55.2 %collective-permute-start.11 = (bf16[4,128,640]{2,1,0:T(8,128)(2,1)S(1)}, bf16[4,128,640]{2,1,0:T(8,128)(2,1)S(1)}, u32[]{:S(2)}, u32[]{:S(2)}) collective-permute-start(bf16[4,128,640]{2,1,0:T(8,128)(2,1)S(1)} %bitcast_dynamic-update-slice_fusion.43), channel_id=1, source_target_pairs={{0,4},{1,5},{2,6},{3,7},{4,0},{5,1},{6,2},{7,3},{8,12},{9,13},{10,... | collective-permute-start | bytes 1966088 | tf_op jit(solution)/shard_map/ppermute | solution.py:46
  184.3 68.2 %collective-permute-start.32 = (bf16[4,128,1024]{2,1,0:T(8,128)(2,1)S(1)}, bf16[4,128,1024]{2,1,0:T(8,128)(2,1)S(1)}, u32[]{:S(2)}, u32[]{:S(2)}) collective-permute-start(bf16[4,128,1024]{2,1,0:T(8,128)(2,1)S(1)} %bitcast_dynamic-update-slice_fusion.31), channel_id=1, source_target_pairs={{0,4},{1,5},{2,6},{3,7},{4,0},{5,1},{6,2},{7,3},{8,12},{9,13},{10,... | collective-permute-start | bytes 3145736 | tf_op jit(solution)/shard_map/ppermute | solution.py:46
  234.7 48.5 %collective-permute-start.39 = (bf16[256,2816]{1,0:T(8,128)(2,1)S(1)}, bf16[256,2816]{1,0:T(8,128)(2,1)S(1)}, u32[]{:S(2)}, u32[]{:S(2)}) collective-permute-start(bf16[256,2816]{1,0:T(8,128)(2,1)S(1)} %bitcast.434), channel_id=1, source_target_pairs={{0,8},{1,9},{2,10},{3,11},{4,12},{5,13},{6,14},{7,15},{8,16},{9,17... | collective-permute-start | bytes 4325384 | tf_op jit(solution)/shard_map/ppermute | solution.py:46
  252.5 78.4 %collective-permute-start.40 = (bf16[256,2816]{1,0:T(8,128)(2,1)S(1)}, bf16[256,2816]{1,0:T(8,128)(2,1)S(1)}, u32[]{:S(2)}, u32[]{:S(2)}) collective-permute-start(bf16[256,2816]{1,0:T(8,128)(2,1)S(1)} %bitcast.435), channel_id=1, source_target_pairs={{0,16},{1,17},{2,18},{3,19},{4,20},{5,21},{6,22},{7,23},{8,24},{9,... | collective-permute-start | bytes 4325384 | tf_op jit(solution)/shard_map/ppermute | solution.py:46
  282.2 85.1 %collective-permute-start.6 = (bf16[512,2048]{1,0:T(8,128)(2,1)S(1)}, bf16[512,2048]{1,0:T(8,128)(2,1)S(1)}, u32[]{:S(2)}, u32[]{:S(2)}) collective-permute-start(bf16[512,2048]{1,0:T(8,128)(2,1)S(1)} %copy-done.36), channel_id=1, source_target_pairs={{0,1},{1,0},{2,3},{3,2},{4,5},{5,4},{6,7},{7,6},{8,9},{9,8},{10,11... | collective-permute-start | bytes 6291464 | tf_op jit(solution)/shard_map/ppermute | solution.py:36
  283.2 64.8 %collective-permute-start.41 = (bf16[256,2816]{1,0:T(8,128)(2,1)S(1)}, bf16[256,2816]{1,0:T(8,128)(2,1)S(1)}, u32[]{:S(2)}, u32[]{:S(2)}) collective-permute-start(bf16[256,2816]{1,0:T(8,128)(2,1)S(1)} %bitcast.436), channel_id=1, source_target_pairs={{0,24},{1,25},{2,26},{3,27},{4,28},{5,29},{6,30},{7,31},{8,0},{9,1... | collective-permute-start | bytes 4325384 | tf_op jit(solution)/shard_map/ppermute | solution.py:46
  330.9 34.5 %collective-permute-start.42 = (bf16[256,2816]{1,0:T(8,128)(2,1)S(1)}, bf16[256,2816]{1,0:T(8,128)(2,1)S(1)}, u32[]{:S(2)}, u32[]{:S(2)}) collective-permute-start(bf16[256,2816]{1,0:T(8,128)(2,1)S(1)} %bitcast.437), channel_id=1, source_target_pairs={{0,4},{1,5},{2,6},{3,7},{4,0},{5,1},{6,2},{7,3},{8,12},{9,13},{10,... | collective-permute-start | bytes 4325384 | tf_op jit(solution)/shard_map/ppermute | solution.py:46
  348.0 44.4 %collective-permute-start.17 = (bf16[2,4,128,640]{3,2,0,1:T(8,128)(2,1)S(1)}, bf16[2,4,128,640]{3,2,0,1:T(8,128)(2,1)S(1)}, u32[]{:S(2)}, u32[]{:S(2)}) collective-permute-start(bf16[2,4,128,640]{3,2,0,1:T(8,128)(2,1)S(1)} %bitcast_dynamic-update-slice_fusion.24), channel_id=1, source_target_pairs={{0,4},{1,5},{2,6},{3,7},{4,0},{5,1},{6,2},{7,3},{8,12},{9,13},{10,... | collective-permute-start | bytes 3932168 | tf_op jit(solution)/shard_map/ppermute | solution.py:46
  365.4 31.9 %collective-permute-start.12 = (bf16[2,4,128,640]{3,2,0,1:T(8,128)(2,1)}, bf16[2,4,128,640]{3,2,0,1:T(8,128)(2,1)S(1)}, u32[]{:S(2)}, u32[]{:S(2)}) collective-permute-start(bf16[2,4,128,640]{3,2,0,1:T(8,128)(2,1)} %bitcast_dynamic-update-slice_fusion.27), channel_id=1, source_target_pairs={{0,2},{1,3},{2,0},{3,1},{4,6},{5,7},{6,4},{7,5},{8,10},{9,11},{10,... | collective-permute-start | bytes 3932168 | tf_op jit(solution)/shard_map/ppermute | solution.py:46
  367.4 194.4 %collective-permute-start.33 = (bf16[2,4,128,1024]{3,2,0,1:T(8,128)(2,1)}, bf16[2,4,128,1024]{3,2,0,1:T(8,128)(2,1)}, u32[]{:S(2)}, u32[]{:S(2)}) collective-permute-start(bf16[2,4,128,1024]{3,2,0,1:T(8,128)(2,1)} %bitcast_dynamic-update-slice_fusion.15), channel_id=1, source_target_pairs={{0,2},{1,3},{2,0},{3,1},{4,6},{5,7},{6,4},{7,5},{8,10},{9,11},{10,... | collective-permute-start | bytes 6291464 | tf_op jit(solution)/shard_map/ppermute | solution.py:46
  421.7 23.0 %collective-permute-start.20 = (f32[2,168,128]{2,1,0:T(8,128)S(1)}, f32[2,168,128]{2,1,0:T(8,128)S(1)}, u32[]{:S(2)}, u32[]{:S(2)}) collective-permute-start(f32[2,168,128]{2,1,0:T(8,128)S(1)} %get-tuple-element.107), channel_id=1, source_target_pairs={{0,6},{1,7},{2,4},{3,5},{4,2},{5,3},{6,0},{7,1},{8,14},{9,15},{10,... | collective-permute-start | bytes 516104 | tf_op jit(solution)/shard_map/ppermute | solution.py:36
  446.6 43.8 %collective-permute-start.23 = (f32[2,168,128]{2,1,0:T(8,128)S(1)}, f32[2,168,128]{2,1,0:T(8,128)}, u32[]{:S(2)}, u32[]{:S(2)}) collective-permute-start(f32[2,168,128]{2,1,0:T(8,128)S(1)} %fusion.125), channel_id=1, source_target_pairs={{0,24},{1,25},{2,26},{3,27},{4,28},{5,29},{6,30},{7,31}} | collective-permute-start | bytes 516104 | tf_op jit(solution)/shard_map/ppermute | solution.py:46
  490.5 131.3 %collective-permute-start.43 = (bf16[256,2816]{1,0:T(8,128)(2,1)}, bf16[256,2816]{1,0:T(8,128)(2,1)}, u32[]{:S(2)}, u32[]{:S(2)}) collective-permute-start(bf16[256,2816]{1,0:T(8,128)(2,1)} %copy-done.44), channel_id=1, source_target_pairs={{0,4},{1,5},{2,6},{3,7},{4,0},{5,1},{6,2},{7,3},{8,12},{9,13},{10,... | collective-permute-start | bytes 4325384 | tf_op jit(solution)/shard_map/ppermute | solution.py:46
  491.0 135.8 %collective-permute-start.44 = (bf16[256,2816]{1,0:T(8,128)(2,1)}, bf16[256,2816]{1,0:T(8,128)(2,1)}, u32[]{:S(2)}, u32[]{:S(2)}) collective-permute-start(bf16[256,2816]{1,0:T(8,128)(2,1)} %copy-done.43), channel_id=1, source_target_pairs={{0,4},{1,5},{2,6},{3,7},{4,0},{5,1},{6,2},{7,3},{8,12},{9,13},{10,... | collective-permute-start | bytes 4325384 | tf_op jit(solution)/shard_map/ppermute | solution.py:46
  499.2 54.9 %collective-permute-start.25 = (f32[2,168,128]{2,1,0:T(8,128)S(1)}, f32[2,168,128]{2,1,0:T(8,128)S(1)}, u32[]{:S(2)}, u32[]{:S(2)}) collective-permute-start(f32[2,168,128]{2,1,0:T(8,128)S(1)} %get-tuple-element.93), channel_id=1, source_target_pairs={{0,4},{1,5},{2,6},{3,7},{4,0},{5,1},{6,2},{7,3},{8,12},{9,13},{10,... | collective-permute-start | bytes 516104 | tf_op jit(solution)/shard_map/ppermute | solution.py:36
  564.8 92.3 %collective-permute-start.34 = (bf16[2048,1024]{1,0:T(8,128)(2,1)}, bf16[2048,1024]{1,0:T(8,128)(2,1)}, u32[]{:S(2)}, u32[]{:S(2)}) collective-permute-start(bf16[2048,1024]{1,0:T(8,128)(2,1)} %bitcast.73), channel_id=1, source_target_pairs={{0,1},{1,0},{2,3},{3,2},{4,5},{5,4},{6,7},{7,6},{8,9},{9,8},{10,11... | collective-permute-start | bytes 12582920 | tf_op jit(solution)/shard_map/ppermute | solution.py:36
  589.6 34.7 %collective-permute-start.87 = (bf16[512,1024]{1,0:T(8,128)(2,1)}, bf16[512,1024]{1,0:T(8,128)(2,1)}, u32[]{:S(2)}, u32[]{:S(2)}) collective-permute-start(bf16[512,1024]{1,0:T(8,128)(2,1)} %slice.140), channel_id=1, source_target_pairs={{0,1},{1,0},{2,3},{3,2},{4,5},{5,4},{6,7},{7,6},{8,9},{9,8},{10,11... | collective-permute-start | bytes 3145736 | tf_op jit(solution)/shard_map/ppermute | solution.py:36
  621.2 33.6 %collective-permute-start.45 = (bf16[256,2816]{1,0:T(8,128)(2,1)S(1)}, bf16[256,2816]{1,0:T(8,128)(2,1)S(1)}, u32[]{:S(2)}, u32[]{:S(2)}) collective-permute-start(bf16[256,2816]{1,0:T(8,128)(2,1)S(1)} %copy-done.46), channel_id=1, source_target_pairs={{0,4},{1,5},{2,6},{3,7},{4,0},{5,1},{6,2},{7,3},{8,12},{9,13},{10,... | collective-permute-start | bytes 4325384 | tf_op jit(solution)/shard_map/ppermute | solution.py:46
  621.7 44.5 %collective-permute-start.61 = (bf16[512,2048]{1,0:T(8,128)(2,1)}, bf16[512,2048]{1,0:T(8,128)(2,1)}, u32[]{:S(2)}, u32[]{:S(2)}) collective-permute-start(bf16[512,2048]{1,0:T(8,128)(2,1)} %collective-permute-done.60), channel_id=1, source_target_pairs={{0,1},{1,0},{2,3},{3,2},{4,5},{5,4},{6,7},{7,6},{8,9},{9,8},{10,11... | collective-permute-start | bytes 6291464 | tf_op jit(solution)/shard_map/ppermute | solution.py:36
  626.3 29.7 %collective-permute-start.88 = (bf16[512,1024]{1,0:T(8,128)(2,1)S(1)}, bf16[512,1024]{1,0:T(8,128)(2,1)S(1)}, u32[]{:S(2)}, u32[]{:S(2)}) collective-permute-start(bf16[512,1024]{1,0:T(8,128)(2,1)S(1)} %get-tuple-element.79), channel_id=1, source_target_pairs={{0,1},{1,0},{2,3},{3,2},{4,5},{5,4},{6,7},{7,6},{8,9},{9,8},{10,11... | collective-permute-start | bytes 3145736 | tf_op jit(solution)/shard_map/ppermute | solution.py:36
  626.8 29.1 %collective-permute-start.27 = (bf16[512,1024]{1,0:T(8,128)(2,1)S(1)}, bf16[512,1024]{1,0:T(8,128)(2,1)S(1)}, u32[]{:S(2)}, u32[]{:S(2)}) collective-permute-start(bf16[512,1024]{1,0:T(8,128)(2,1)S(1)} %get-tuple-element.80), channel_id=1, source_target_pairs={{0,1},{1,0},{2,3},{3,2},{4,5},{5,4},{6,7},{7,6},{8,9},{9,8},{10,11... | collective-permute-start | bytes 3145736 | tf_op jit(solution)/shard_map/ppermute | solution.py:36
  666.2 72.9 %collective-permute-start.35 = (bf16[512,2048]{1,0:T(8,128)(2,1)S(1)}, bf16[512,2048]{1,0:T(8,128)(2,1)}, u32[]{:S(2)}, u32[]{:S(2)}) collective-permute-start(bf16[512,2048]{1,0:T(8,128)(2,1)S(1)} %multiply_convert_fusion.6), channel_id=1, source_target_pairs={{0,1},{1,0},{2,3},{3,2},{4,5},{5,4},{6,7},{7,6},{8,9},{9,8},{10,11... | collective-permute-start | bytes 6291464 | tf_op jit(solution)/shard_map/ppermute | solution.py:36
  738.2 52.7 %collective-permute-start.54 = (bf16[512,2048]{1,0:T(8,128)(2,1)S(1)}, bf16[512,2048]{1,0:T(8,128)(2,1)S(1)}, u32[]{:S(2)}, u32[]{:S(2)}) collective-permute-start(bf16[512,2048]{1,0:T(8,128)(2,1)S(1)} %multiply_convert_fusion.6), channel_id=1, source_target_pairs={{0,2},{1,3},{2,0},{3,1},{4,6},{5,7},{6,4},{7,5},{8,10},{9,11},{10,... | collective-permute-start | bytes 6291464 | tf_op jit(solution)/shard_map/ppermute | solution.py:36
  931.2 61.2 %collective-permute-start.62 = (bf16[512,2048]{1,0:T(8,128)(2,1)S(1)}, bf16[512,2048]{1,0:T(8,128)(2,1)}, u32[]{:S(2)}, u32[]{:S(2)}) collective-permute-start(bf16[512,2048]{1,0:T(8,128)(2,1)S(1)} %slice.248), channel_id=1, source_target_pairs={{0,1},{1,0},{2,3},{3,2},{4,5},{5,4},{6,7},{7,6},{8,9},{9,8},{10,11... | collective-permute-start | bytes 6291464 | tf_op jit(solution)/shard_map/ppermute | solution.py:36
  947.8 49.8 %collective-permute-start.56 = (bf16[512,2048]{1,0:T(8,128)(2,1)}, bf16[512,2048]{1,0:T(8,128)(2,1)}, u32[]{:S(2)}, u32[]{:S(2)}) collective-permute-start(bf16[512,2048]{1,0:T(8,128)(2,1)} %slice.250), channel_id=1, source_target_pairs={{0,1},{1,0},{2,3},{3,2},{4,5},{5,4},{6,7},{7,6},{8,9},{9,8},{10,11... | collective-permute-start | bytes 6291464 | tf_op jit(solution)/shard_map/ppermute | solution.py:36
  947.8 65.6 %collective-permute-start.108 = (bf16[4,256,1408]{2,1,0:T(8,128)(2,1)}, bf16[4,256,1408]{2,1,0:T(8,128)(2,1)}, u32[]{:S(2)}, u32[]{:S(2)}) collective-permute-start(bf16[4,256,1408]{2,1,0:T(8,128)(2,1)} %fusion.57), channel_id=1, source_target_pairs={{0,4},{1,5},{2,6},{3,7},{4,0},{5,1},{6,2},{7,3},{8,12},{9,13},{10,... | collective-permute-start | bytes 8650760 | tf_op jit(solution)/shard_map/ppermute | solution.py:46
  968.5 106.7 %collective-permute-start.101 = (bf16[4,256,1408]{2,1,0:T(8,128)(2,1)}, bf16[4,256,1408]{2,1,0:T(8,128)(2,1)}, u32[]{:S(2)}, u32[]{:S(2)}) collective-permute-start(bf16[4,256,1408]{2,1,0:T(8,128)(2,1)} %fusion.54), channel_id=1, source_target_pairs={{0,4},{1,5},{2,6},{3,7},{4,0},{5,1},{6,2},{7,3},{8,12},{9,13},{10,... | collective-permute-start | bytes 8650760 | tf_op jit(solution)/shard_map/ppermute | solution.py:46
  991.8 144.7 %collective-permute-start.115 = (bf16[4,176,2048]{2,1,0:T(8,128)(2,1)S(1)}, bf16[4,176,2048]{2,1,0:T(8,128)(2,1)S(1)}, u32[]{:S(2)}, u32[]{:S(2)}) collective-permute-start(bf16[4,176,2048]{2,1,0:T(8,128)(2,1)S(1)} %fusion.74), channel_id=1, source_target_pairs={{0,4},{1,5},{2,6},{3,7},{4,0},{5,1},{6,2},{7,3},{8,12},{9,13},{10,... | collective-permute-start | bytes 8650760 | tf_op jit(solution)/shard_map/ppermute | solution.py:46
  1024.6 111.9 %collective-permute-start.111 = (bf16[1,256,1408]{2,1,0:T(8,128)(2,1)S(1)}, bf16[1,256,1408]{2,1,0:T(8,128)(2,1)S(1)}, u32[]{:S(2)}, u32[]{:S(2)}) collective-permute-start(bf16[1,256,1408]{2,1,0:T(8,128)(2,1)S(1)} %get-tuple-element.74), channel_id=1, source_target_pairs={{0,24},{1,25},{2,26},{3,27},{4,28},{5,29},{6,30},{7,31},{8,0},{9,1... | collective-permute-start | bytes 2162696 | tf_op jit(solution)/shard_map/ppermute | solution.py:46
  1024.7 117.8 %collective-permute-start.110 = (bf16[1,256,1408]{2,1,0:T(8,128)(2,1)S(1)}, bf16[1,256,1408]{2,1,0:T(8,128)(2,1)}, u32[]{:S(2)}, u32[]{:S(2)}) collective-permute-start(bf16[1,256,1408]{2,1,0:T(8,128)(2,1)S(1)} %get-tuple-element.75), channel_id=1, source_target_pairs={{0,16},{1,17},{2,18},{3,19},{4,20},{5,21},{6,22},{7,23},{8,24},{9,... | collective-permute-start | bytes 2162696 | tf_op jit(solution)/shard_map/ppermute | solution.py:46
  1025.4 117.8 %collective-permute-start.109 = (bf16[1,256,1408]{2,1,0:T(8,128)(2,1)S(1)}, bf16[1,256,1408]{2,1,0:T(8,128)(2,1)}, u32[]{:S(2)}, u32[]{:S(2)}) collective-permute-start(bf16[1,256,1408]{2,1,0:T(8,128)(2,1)S(1)} %get-tuple-element.73), channel_id=1, source_target_pairs={{0,8},{1,9},{2,10},{3,11},{4,12},{5,13},{6,14},{7,15},{8,16},{9,17... | collective-permute-start | bytes 2162696 | tf_op jit(solution)/shard_map/ppermute | solution.py:46
  1086.1 57.8 %collective-permute-start.104 = (bf16[1,256,1408]{2,1,0:T(8,128)(2,1)}, bf16[1,256,1408]{2,1,0:T(8,128)(2,1)S(1)}, u32[]{:S(2)}, u32[]{:S(2)}) collective-permute-start(bf16[1,256,1408]{2,1,0:T(8,128)(2,1)} %get-tuple-element.77), channel_id=1, source_target_pairs={{0,24},{1,25},{2,26},{3,27},{4,28},{5,29},{6,30},{7,31},{8,0},{9,1... | collective-permute-start | bytes 2162696 | tf_op jit(solution)/shard_map/ppermute | solution.py:46
  1136.5 48.2 %collective-permute-start.103 = (bf16[1,256,1408]{2,1,0:T(8,128)(2,1)S(1)}, bf16[1,256,1408]{2,1,0:T(8,128)(2,1)S(1)}, u32[]{:S(2)}, u32[]{:S(2)}) collective-permute-start(bf16[1,256,1408]{2,1,0:T(8,128)(2,1)S(1)} %get-tuple-element.78), channel_id=1, source_target_pairs={{0,16},{1,17},{2,18},{3,19},{4,20},{5,21},{6,22},{7,23},{8,24},{9,... | collective-permute-start | bytes 2162696 | tf_op jit(solution)/shard_map/ppermute | solution.py:46
  1137.4 47.4 %collective-permute-start.102 = (bf16[1,256,1408]{2,1,0:T(8,128)(2,1)S(1)}, bf16[1,256,1408]{2,1,0:T(8,128)(2,1)S(1)}, u32[]{:S(2)}, u32[]{:S(2)}) collective-permute-start(bf16[1,256,1408]{2,1,0:T(8,128)(2,1)S(1)} %get-tuple-element.76), channel_id=1, source_target_pairs={{0,8},{1,9},{2,10},{3,11},{4,12},{5,13},{6,14},{7,15},{8,16},{9,17... | collective-permute-start | bytes 2162696 | tf_op jit(solution)/shard_map/ppermute | solution.py:46
  1143.2 112.0 %collective-permute-start.59 = (bf16[512,2048]{1,0:T(8,128)(2,1)S(1)}, bf16[512,2048]{1,0:T(8,128)(2,1)S(1)}, u32[]{:S(2)}, u32[]{:S(2)}) collective-permute-start(bf16[512,2048]{1,0:T(8,128)(2,1)S(1)} %copy-done.35), channel_id=1, source_target_pairs={{0,1},{1,0},{2,3},{3,2},{4,5},{5,4},{6,7},{7,6},{8,9},{9,8},{10,11... | collective-permute-start | bytes 6291464 | tf_op jit(solution)/shard_map/ppermute | solution.py:36
  1143.9 115.4 %collective-permute-start.53 = (bf16[512,2048]{1,0:T(8,128)(2,1)S(1)}, bf16[512,2048]{1,0:T(8,128)(2,1)S(1)}, u32[]{:S(2)}, u32[]{:S(2)}) collective-permute-start(bf16[512,2048]{1,0:T(8,128)(2,1)S(1)} %copy-done.34), channel_id=1, source_target_pairs={{0,1},{1,0},{2,3},{3,2},{4,5},{5,4},{6,7},{7,6},{8,9},{9,8},{10,11... | collective-permute-start | bytes 6291464 | tf_op jit(solution)/shard_map/ppermute | solution.py:36
  1143.9 112.5 %collective-permute-start.63 = (bf16[512,2048]{1,0:T(8,128)(2,1)}, bf16[512,2048]{1,0:T(8,128)(2,1)S(1)}, u32[]{:S(2)}, u32[]{:S(2)}) collective-permute-start(bf16[512,2048]{1,0:T(8,128)(2,1)} %fusion.28), channel_id=1, source_target_pairs={{0,2},{1,3},{2,0},{3,1},{4,6},{5,7},{6,4},{7,5},{8,10},{9,11},{10,... | collective-permute-start | bytes 6291464 | tf_op jit(solution)/shard_map/ppermute | solution.py:36
  1184.8 46.8 %collective-permute-start.117 = (bf16[1,176,2048]{2,1,0:T(8,128)(2,1)S(1)}, bf16[1,176,2048]{2,1,0:T(8,128)(2,1)S(1)}, u32[]{:S(2)}, u32[]{:S(2)}) collective-permute-start(bf16[1,176,2048]{2,1,0:T(8,128)(2,1)S(1)} %get-tuple-element.72), channel_id=1, source_target_pairs={{0,16},{1,17},{2,18},{3,19},{4,20},{5,21},{6,22},{7,23},{8,24},{9,... | collective-permute-start | bytes 2162696 | tf_op jit(solution)/shard_map/ppermute | solution.py:46
  1204.1 55.5 %collective-permute-start.57 = (bf16[512,2048]{1,0:T(8,128)(2,1)S(1)}, bf16[512,2048]{1,0:T(8,128)(2,1)S(1)}, u32[]{:S(2)}, u32[]{:S(2)}) collective-permute-start(bf16[512,2048]{1,0:T(8,128)(2,1)S(1)} %copy-done.41), channel_id=1, source_target_pairs={{0,2},{1,3},{2,0},{3,1},{4,6},{5,7},{6,4},{7,5},{8,10},{9,11},{10,... | collective-permute-start | bytes 6291464 | tf_op jit(solution)/shard_map/ppermute | solution.py:36
  1271.6 63.2 %collective-permute-start.114 = (bf16[64,1408]{1,0:T(8,128)(2,1)S(1)}, bf16[64,1408]{1,0:T(8,128)(2,1)}, u32[]{:S(2)}, u32[]{:S(2)}) collective-permute-start(bf16[64,1408]{1,0:T(8,128)(2,1)S(1)} %get-tuple-element.97), channel_id=1, source_target_pairs={{0,3},{1,2},{2,1},{3,0},{4,7},{5,6},{6,5},{7,4},{8,11},{9,10},{10,... | collective-permute-start | bytes 540680 | tf_op jit(solution)/shard_map/ppermute | solution.py:36
  1338.4 66.3 %collective-permute-start.95 = (f32[1,2048]{1,0:T(1,128)S(1)}, f32[1,2048]{1,0:T(1,128)S(1)}, u32[]{:S(2)}, u32[]{:S(2)}) collective-permute-start(f32[1,2048]{1,0:T(1,128)S(1)} %bitcast.458), channel_id=1, source_target_pairs={{0,1},{1,0},{2,3},{3,2},{4,5},{5,4},{6,7},{7,6},{8,9},{9,8},{10,11... | collective-permute-start | bytes 24584 | tf_op jit(solution)/shard_map/ppermute | solution.py:46
  1401.9 34.5 %collective-permute-start.74 = (bf16[512,2048]{1,0:T(8,128)(2,1)}, bf16[512,2048]{1,0:T(8,128)(2,1)}, u32[]{:S(2)}, u32[]{:S(2)}) collective-permute-start(bf16[512,2048]{1,0:T(8,128)(2,1)} %convolution_convert_fusion.2), channel_id=1, source_target_pairs={{0,1},{1,0},{2,3},{3,2},{4,5},{5,4},{6,7},{7,6},{8,9},{9,8},{10,11... | collective-permute-start | bytes 6291464 | tf_op jit(solution)/shard_map/ppermute | solution.py:36
  1414.5 48.8 %collective-permute-start.89 = (bf16[8,128,1024]{2,1,0:T(8,128)(2,1)}, bf16[8,128,1024]{2,1,0:T(8,128)(2,1)}, u32[]{:S(2)}, u32[]{:S(2)}) collective-permute-start(bf16[8,128,1024]{2,1,0:T(8,128)(2,1)} %fusion.93), channel_id=1, source_target_pairs={{0,2},{1,3},{2,0},{3,1},{4,6},{5,7},{6,4},{7,5},{8,10},{9,11},{10,... | collective-permute-start | bytes 6291464 | tf_op jit(solution)/shard_map/ppermute | solution.py:46
  1420.5 98.2 %collective-permute-start.81 = (bf16[8,128,1280]{2,1,0:T(8,128)(2,1)}, bf16[8,128,1280]{2,1,0:T(8,128)(2,1)}, u32[]{:S(2)}, u32[]{:S(2)}) collective-permute-start(bf16[8,128,1280]{2,1,0:T(8,128)(2,1)} %convolution_convert_fusion.1), channel_id=1, source_target_pairs={{0,2},{1,3},{2,0},{3,1},{4,6},{5,7},{6,4},{7,5},{8,10},{9,11},{10,... | collective-permute-start | bytes 7864328 | tf_op jit(solution)/shard_map/ppermute | solution.py:46
  1435.9 95.4 %collective-permute-start.100 = (f32[1,2048]{1,0:T(1,128)S(1)}, f32[1,2048]{1,0:T(1,128)S(1)}, u32[]{:S(2)}, u32[]{:S(2)}) collective-permute-start(f32[1,2048]{1,0:T(1,128)S(1)} %add.847), channel_id=1, source_target_pairs={{0,2},{1,3},{2,0},{3,1},{4,6},{5,7},{6,4},{7,5},{8,10},{9,11},{10,... | collective-permute-start | bytes 24584 | tf_op jit(solution)/shard_map/ppermute | solution.py:46
  1443.6 25.7 %collective-permute-start.75 = (f32[1,2048]{1,0:T(1,128)S(1)}, f32[1,2048]{1,0:T(1,128)S(1)}, u32[]{:S(2)}, u32[]{:S(2)}) collective-permute-start(f32[1,2048]{1,0:T(1,128)S(1)} %bitcast.461), channel_id=1, source_target_pairs={{0,1},{1,0},{2,3},{3,2},{4,5},{5,4},{6,7},{7,6},{8,9},{9,8},{10,11... | collective-permute-start | bytes 24584 | tf_op jit(solution)/shard_map/ppermute | solution.py:46
  1474.2 58.3 %collective-permute-start.90 = (bf16[4,128,1024]{2,1,0:T(8,128)(2,1)}, bf16[4,128,1024]{2,1,0:T(8,128)(2,1)}, u32[]{:S(2)}, u32[]{:S(2)}) collective-permute-start(bf16[4,128,1024]{2,1,0:T(8,128)(2,1)} %dynamic-slice_bitcast_fusion.1), channel_id=1, source_target_pairs={{0,4},{1,5},{2,6},{3,7},{4,0},{5,1},{6,2},{7,3},{8,12},{9,13},{10,... | collective-permute-start | bytes 3145736 | tf_op jit(solution)/shard_map/ppermute | solution.py:46
  1496.9 34.4 %collective-permute-start.80 = (f32[1,2048]{1,0:T(1,128)S(1)}, f32[1,2048]{1,0:T(1,128)S(1)}, u32[]{:S(2)}, u32[]{:S(2)}) collective-permute-start(f32[1,2048]{1,0:T(1,128)S(1)} %add.828), channel_id=1, source_target_pairs={{0,2},{1,3},{2,0},{3,1},{4,6},{5,7},{6,4},{7,5},{8,10},{9,11},{10,... | collective-permute-start | bytes 24584 | tf_op jit(solution)/shard_map/ppermute | solution.py:46
  1524.9 29.8 %collective-permute-start.82 = (bf16[4,128,1280]{2,1,0:T(8,128)(2,1)S(1)}, bf16[4,128,1280]{2,1,0:T(8,128)(2,1)}, u32[]{:S(2)}, u32[]{:S(2)}) collective-permute-start(bf16[4,128,1280]{2,1,0:T(8,128)(2,1)S(1)} %dynamic-slice_bitcast_fusion), channel_id=1, source_target_pairs={{0,4},{1,5},{2,6},{3,7},{4,0},{5,1},{6,2},{7,3},{8,12},{9,13},{10,... | collective-permute-start | bytes 3932168 | tf_op jit(solution)/shard_map/ppermute | solution.py:46
  1534.9 24.7 %collective-permute-start.93 = (bf16[1,128,1024]{2,1,0:T(8,128)(2,1)S(1)}, bf16[1,128,1024]{2,1,0:T(8,128)(2,1)S(1)}, u32[]{:S(2)}, u32[]{:S(2)}) collective-permute-start(bf16[1,128,1024]{2,1,0:T(8,128)(2,1)S(1)} %get-tuple-element.91), channel_id=1, source_target_pairs={{0,24},{1,25},{2,26},{3,27},{4,28},{5,29},{6,30},{7,31},{8,0},{9,1... | collective-permute-start | bytes 786440 | tf_op jit(solution)/shard_map/ppermute | solution.py:46
  1537.6 23.2 %collective-permute-start.92 = (bf16[1,128,1024]{2,1,0:T(8,128)(2,1)S(1)}, bf16[1,128,1024]{2,1,0:T(8,128)(2,1)S(1)}, u32[]{:S(2)}, u32[]{:S(2)}) collective-permute-start(bf16[1,128,1024]{2,1,0:T(8,128)(2,1)S(1)} %get-tuple-element.92), channel_id=1, source_target_pairs={{0,16},{1,17},{2,18},{3,19},{4,20},{5,21},{6,22},{7,23},{8,24},{9,... | collective-permute-start | bytes 786440 | tf_op jit(solution)/shard_map/ppermute | solution.py:46
  1537.6 23.2 %collective-permute-start.91 = (bf16[1,128,1024]{2,1,0:T(8,128)(2,1)S(1)}, bf16[1,128,1024]{2,1,0:T(8,128)(2,1)S(1)}, u32[]{:S(2)}, u32[]{:S(2)}) collective-permute-start(bf16[1,128,1024]{2,1,0:T(8,128)(2,1)S(1)} %get-tuple-element.90), channel_id=1, source_target_pairs={{0,8},{1,9},{2,10},{3,11},{4,12},{5,13},{6,14},{7,15},{8,16},{9,17... | collective-permute-start | bytes 786440 | tf_op jit(solution)/shard_map/ppermute | solution.py:46
  1559.6 27.2 %collective-permute-start.84 = (bf16[1,128,1280]{2,1,0:T(8,128)(2,1)S(1)}, bf16[1,128,1280]{2,1,0:T(8,128)(2,1)S(1)}, u32[]{:S(2)}, u32[]{:S(2)}) collective-permute-start(bf16[1,128,1280]{2,1,0:T(8,128)(2,1)S(1)} %get-tuple-element.89), channel_id=1, source_target_pairs={{0,16},{1,17},{2,18},{3,19},{4,20},{5,21},{6,22},{7,23},{8,24},{9,... | collective-permute-start | bytes 983048 | tf_op jit(solution)/shard_map/ppermute | solution.py:46
  1559.6 27.2 %collective-permute-start.83 = (bf16[1,128,1280]{2,1,0:T(8,128)(2,1)S(1)}, bf16[1,128,1280]{2,1,0:T(8,128)(2,1)S(1)}, u32[]{:S(2)}, u32[]{:S(2)}) collective-permute-start(bf16[1,128,1280]{2,1,0:T(8,128)(2,1)S(1)} %get-tuple-element.87), channel_id=1, source_target_pairs={{0,8},{1,9},{2,10},{3,11},{4,12},{5,13},{6,14},{7,15},{8,16},{9,17... | collective-permute-start | bytes 983048 | tf_op jit(solution)/shard_map/ppermute | solution.py:46
  1561.0 26.1 %collective-permute-start.94 = (f32[64,1024]{1,0:T(8,128)S(1)}, f32[64,1024]{1,0:T(8,128)S(1)}, u32[]{:S(2)}, u32[]{:S(2)}) collective-permute-start(f32[64,1024]{1,0:T(8,128)S(1)} %dynamic-slice_bitcast_fusion.7), channel_id=1, source_target_pairs={{0,1},{1,0},{2,3},{3,2},{4,5},{5,4},{6,7},{7,6},{8,9},{9,8},{10,11... | collective-permute-start | bytes 786440 | tf_op jit(solution)/shard_map/ppermute | solution.py:36
  (139 other events, 3162.1 us)

commit v2 on v1

--- a/solution.py
+++ b/solution.py
@@ -61,6 +61,10 @@
     return out
 
 
+def after(x, *others):
+    return lax.optimization_barrier((x,) + others)[0]
+
+
 def gather_stage(x, dim):
     at = place(dim)
     pieces = [(at, x)]
@@ -69,28 +73,20 @@
     return assemble(pieces)
 
 
+def in_order(x, done):
+    axes = [done.index(d) for d in sorted(done, key=lambda d: -d[0])]
+    x = x.transpose(axes + list(range(len(done), x.ndim)))
+    return x.reshape((-1,) + x.shape[len(done) :])
+
+
 def gather(x, dims):
-    order = sorted(dims, key=lambda d: -d[0])
-    done = []
     for dim in dims:
         x = gather_stage(x, dim)
-        done.insert(0, dim)
-    axes = [done.index(d) for d in order]
-    rest = list(range(len(done), x.ndim))
-    x = x.transpose(axes + rest)
-    return x.reshape((-1,) + x.shape[len(done):])
-
-
-def gather_blocks(x, dims):
-    unit = min(d[0] for d in dims)
-    blocks = [(jnp.int32(0), x)]
-    for dim in dims:
-        at, later = place(dim), []
-        for k in range(dim[1]):
-            step = lax.rem(at + dim[1] - k, dim[1]) * (dim[0] // unit)
-            later += [(i + step, shift(b, dim, k) if k else b) for i, b in blocks]
-        blocks = later
-    return assemble(blocks)
+    return in_order(x, dims[::-1])
+
+
+def shift_order(size):
+    return [1, 3, 2] if size == 4 else list(range(1, size))
 
 
 def total(x, dims):
@@ -99,23 +95,168 @@
     return x
 
 
-def scatter(make, dims, grid):
-    dim = dims[-1]
-    at = place(dim)
-    acc = None
-    sent = []
-    for k in range(1, dim[1]):
-        sent.append(shift(make(lax.rem(at + k, dim[1])).astype(bf16), dim, k))
-    acc = make(at).astype(f32) + sum(s.astype(f32) for s in sent)
-    for dim in reversed(dims[:-1]):
-        at = place(dim)
-        low = acc.astype(bf16).reshape((-1, dim[1]) + acc.shape[1:])
-        acc = acc.reshape((-1, dim[1]) + acc.shape[1:])
-        own = pick(acc, at, 1)
-        for k in range(1, dim[1]):
-            own = own + shift(pick(low, lax.rem(at + k, dim[1]), 1), dim, k).astype(f32)
-        acc = own
-    return acc[0]
+class Scatter:
+    def __init__(self, make, dims):
+        self.make, self.dims, self.dim = make, dims, dims[-1]
+        self.at = place(self.dim)
+
+    def send(self):
+        sent = [(k, self.make(lax.rem(self.at + k, self.dim[1]))) for k in range(1, self.dim[1])]
+        self.here = [shift(s, self.dim, k) for k, s in sent]
+        return sent[0][1]
+
+    def keep(self, *gate):
+        self.kept = self.make(after(self.at, *gate) if gate else self.at)
+        return self.kept
+
+    def finish(self, *gates):
+        gates = list(gates) + [()] * len(self.dims)
+        acc = self.kept.astype(f32) + sum((after(h, *gates[0]) if gates[0] else h).astype(f32) for h in self.here)
+        for dim, gate in zip(reversed(self.dims[:-1]), gates[1:]):
+            at = place(dim)
+            acc = acc.reshape((-1, dim[1]) + acc.shape[1:])
+            low = acc.astype(bf16)
+            own = pick(acc, at, 1)
+            for k in range(1, dim[1]):
+                part = shift(pick(low, lax.rem(at + k, dim[1]), 1), dim, k)
+                own = own + (after(part, *gate) if gate else part).astype(f32)
+            acc = own
+        return acc[0]
+
+
+def spans_of(cols, most=512):
+    return [(s, min(most, cols - s)) for s in range(0, cols, most)]
+
+
+def ffn_body(count, index, x_ref, g_ref, *refs):
+    gate_up, down = refs[0], refs[1 : count + 1]
+    y_ref, act_ref, d_ref, dh_ref, w_gate_up, w_down, sem = refs[count + 1 :]
+    cols = w_down.shape[0]
+
+    @pl.when(pl.program_id(0) == 0)
+    def _():
+        copies = [pltpu.make_async_copy(gate_up, w_gate_up, sem.at[count])]
+        size = down[0].shape[0]
+        for i, block in enumerate(down):
+            at = pl.ds(pl.multiple_of(index[i] * size, 16), size)
+            copies.append(pltpu.make_async_copy(block, w_down.at[at], sem.at[i]))
+        for copy in copies:
+            copy.start()
+        for copy in copies:
+            copy.wait()
+
+    x, g = x_ref[...], g_ref[...]
+    for s, w in spans_of(cols):
+        gate, upper = dot(x, w_gate_up[:, s : s + w]), dot(x, w_gate_up[:, cols + s : cols + s + w])
+        d_act = dot_cols(g, w_down[s : s + w, :])
+        sigma = jax.nn.sigmoid(gate)
+        smooth = gate * sigma
+        act_ref[:, s : s + w] = (smooth * upper).astype(bf16)
+        d_ref[:, s : s + w] = (d_act * upper * sigma * (1.0 + gate * (1.0 - sigma))).astype(bf16)
+        d_ref[:, cols + s : cols + s + w] = (d_act * smooth).astype(bf16)
+    y_ref[...] = dot(act_ref[...], w_down[...]).astype(bf16)
+    dh_ref[...] = dot_cols(d_ref[...], w_gate_up[...]).astype(bf16)
+
+
+def ffn(x, g, gate_up, down, tile=256):
+    index = jnp.stack([i for i, _ in down]).astype(jnp.int32)
+    down = [b for _, b in down]
+    tokens, width = x.shape
+    count = len(down)
+    cols = count * down[0].shape[0]
+
+    def block(w):
+        return pl.BlockSpec((tile, w), lambda i, _: (i, 0))
+
+    return pl.pallas_call(
+        lambda *refs: ffn_body(count, *refs),
+        out_shape=[jax.ShapeDtypeStruct((tokens, w), bf16) for w in (width, cols, 2 * cols, width)],
+        grid_spec=pltpu.PrefetchScalarGridSpec(
+            num_scalar_prefetch=1,
+            grid=(tokens // tile,),
+            in_specs=[block(width), block(width)] + [pl.BlockSpec(memory_space=pl.ANY)] * (count + 1),
+            out_specs=[block(width), block(cols), block(2 * cols), block(width)],
+            scratch_shapes=[
+                pltpu.VMEM((width, 2 * cols), bf16),
+                pltpu.VMEM((cols, width), bf16),
+                pltpu.SemaphoreType.DMA((count + 1,)),
+            ],
+        ),
+        compiler_params=pltpu.CompilerParams(vmem_limit_bytes=VMEM),
+        cost_estimate=pl.CostEstimate(flops=0, bytes_accessed=0, transcendentals=0),
+    )(index, x, g, gate_up, *down)
+
+
+def product_body(count, index, *refs):
+    left, right, out = refs[:count], refs[count : 2 * count], refs[2 * count]
+    out[...] = sum(dot_rows(a[...], b[...]) for a, b in zip(left, right)).astype(out.dtype)
+
+
+def row_blocks(left, right, index, size):
+    count = index.shape[0]
+    cols = right[0].shape[1]
+    tokens = sum(a.shape[0] for a in left)
+    return pl.pallas_call(
+        lambda *refs: product_body(len(left), *refs),
+        out_shape=jax.ShapeDtypeStruct((count * size, cols), bf16),
+        grid_spec=pltpu.PrefetchScalarGridSpec(
+            num_scalar_prefetch=1,
+            grid=(count,),
+            in_specs=[pl.BlockSpec((a.shape[0], size), lambda i, at: (0, at[i])) for a in left]
+            + [pl.BlockSpec((b.shape[0], cols), lambda i, at: (0, 0)) for b in right],
+            out_specs=pl.BlockSpec((size, cols), lambda i, at: (i, 0)),
+        ),
+        compiler_params=pltpu.CompilerParams(vmem_limit_bytes=VMEM),
+        cost_estimate=pl.CostEstimate(flops=0, bytes_accessed=0, transcendentals=0),
+    )(index, x, g, gate_up, *down)
+
+
+def product_body(count, index, *refs):
+    left, right, out = refs[:count], refs[count : 2 * count], refs[2 * count]
+    out[...] = sum(dot_rows(a[...], b[...]) for a, b in zip(left, right)).astype(out.dtype)
+
+
+def row_blocks(left, right, index, size):
+    count = index.shape[0]
+    cols = right[0].shape[1]
+    tokens = sum(a.shape[0] for a in left)
+    return pl.pallas_call(
+        lambda *refs: product_body(len(left), *refs),
+        out_shape=jax.ShapeDtypeStruct((count * size, cols), bf16),
+        grid_spec=pltpu.PrefetchScalarGridSpec(
+            num_scalar_prefetch=1,
+            grid=(count,),
+            in_specs=[pl.BlockSpec((a.shape[0], size), lambda i, at: (0, at[i])) for a in left]
+            + [pl.BlockSpec((b.shape[0], cols), lambda i, at: (0, 0)) for b in right],
+            out_specs=pl.BlockSpec((size, cols), lambda i, at: (i, 0)),
+        ),
+        compiler_params=pltpu.CompilerParams(vmem_limit_bytes=VMEM),
+        cost_estimate=pl.CostEstimate(
+            flops=2 * tokens * count * size * cols,
+            bytes_accessed=2 * (tokens * cols + count * size * (tokens + cols)),
+            transcendentals=0,
+        ),
+    )(index.astype(jnp.int32), *left, *right)
+
+
+def part_maker(left, right, dims):
+    unit = min(d[0] for d in dims)
+    count = int(np.prod([d[1] for d in dims]))
+    size = left[0].shape[1] // count
+    cols = right[0].shape[1]
+    ids = np.zeros((), np.int32)
+    for stride, many in dims[:-1]:
+        ids = ids[..., None] + np.arange(many, dtype=np.int32) * (stride // unit)
+    ids = ids.reshape(-1)
+
+    def make(index):
+        index = jnp.asarray(ids) + index * (dims[-1][0] // unit)
+        if size % 128 == 0:
+            return row_blocks(left, right, index, size).reshape(-1, size, cols)
+        out = sum(dot_rows(a, b) for a, b in zip(left, right)).astype(bf16)
+        return out.reshape(count, size, cols)[index]
+
+    return make
 
 
 def feature_tables(heads):
@@ -331,7 +472,7 @@
             out_shape=shapes,
             scratch_shapes=scratch,
             compiler_params=pltpu.CompilerParams(vmem_limit_bytes=VMEM),
-            cost_estimate=pl.CostEstimate(flops=flops, bytes_accessed=size, transcendentals=0),
+            cost_estimate=pl.CostEstimate(flops=0, bytes_accessed=0, transcendentals=0),
         )(*args)
 
     def states(self):
@@ -388,7 +529,8 @@
         parts = lax.all_gather(state.astype(kind), "tok").astype(f32)
         index = jnp.arange(n)
         before = (sign * (me // 2 - index // 2) > 0) & (index % 2 == me % 2)
-        return jnp.sum(jnp.where(before.reshape((n,) + (1,) * state.ndim), parts, 0.0), axis=0)
+        out = jnp.sum(jnp.where(before.reshape((n,) + (1,) * state.ndim), parts, 0.0), axis=0)
+        return out, (state, out, out)
     plane = (me // 2) % 4
     slices = state.astype(kind).reshape((4, state.shape[0] // 4) + state.shape[1:])
     mine = [pick(slices, plane)]
@@ -405,7 +547,7 @@
                 before = before + jnp.where(sign * ((plane ^ k) - (plane ^ j)) > 0, mine[j], 0.0)
         before = before.astype(kind)
         pieces.append((plane ^ k, flip(before, 2 * k) if k else before))
-    return assemble(pieces).reshape(state.shape).astype(f32)
+    return assemble(pieces).reshape(state.shape).astype(f32), (slices, whole, beyond)
 
 
 def row_starts(positions, lengths, offsets):
@@ -413,8 +555,13 @@
     return jnp.sum(jnp.where(inside, offsets[None, :], 0), axis=1)
 
 
-def ordered(first, mine, theirs, axis=0):
-    return jnp.concatenate([jnp.where(first, mine, theirs), jnp.where(first, theirs, mine)], axis=axis)
+def side_by_side(core, mine, theirs, axis=0):
+    size = mine.shape[axis]
+    shape = list(mine.shape)
+    shape[axis] *= 2
+    out = jnp.zeros(shape, mine.dtype)
+    out = lax.dynamic_update_slice_in_dim(out, mine, core * size, axis)
+    return lax.dynamic_update_slice_in_dim(out, theirs, (1 - core) * size, axis)
 
 
 def shards(
@@ -435,7 +582,6 @@
     n = lax.axis_size("tok")
     me = lax.axis_index("tok")
     core, quad = me % 2, me % 4
-    even = core == 0
     cdims, qdims = chip_dims(n), quad_dims(n)
     chips, quads = n // 2, n // 4
     tokens, width = block_input.shape
@@ -443,7 +589,6 @@
     heads = w_query.shape[1] // QK // 2
     half = width // 2
     lanes = heads * QK
-    z_first = cdims
     x_last = [cdims[0]] + cdims[1:][::-1]
 
     def column_half(w, which):
@@ -453,24 +598,69 @@
         return lax.dynamic_slice_in_dim(w, which * (w.shape[0] // 2), w.shape[0] // 2, 0)
 
     gains = jnp.stack([norm1_gain, norm2_gain]).astype(f32)
-    gains = gather(gather(gains, [(1, 2)]), cdims).reshape(n, 2, rows).transpose(1, 0, 2).reshape(2, 1, width)
-    gain_one, gain_two = gains[0], gains[1]
+    gains = gather(gains, [(1, 2)])
 
     def by_core(which):
         return jnp.concatenate([column_half(w, which) for w in (w_query, w_key, w_value)], axis=1)
 
-    chip_qkv = ordered(even, by_core(core), flip(by_core(1 - core), 1))
+    chip_qkv = side_by_side(core, by_core(core), flip(by_core(1 - core), 1))
     cut = chip_qkv.shape[1] // 2
-    qkv_all = jnp.concatenate(
-        [gather(chip_qkv[:, :cut], z_first), gather(chip_qkv[:, cut:], x_last)], axis=2
-    ).reshape(width, 2 * cut)
+    chip_qkv = gather_stage(chip_qkv, cdims[0])
+    part_a, part_b = chip_qkv[..., :cut], chip_qkv[..., cut:]
+    marks = [(chip_qkv,)]
+    for dim_a, dim_b in zip(cdims[1:], x_last[1:]):
+        part_a, part_b = gather_stage(part_a, dim_a), gather_stage(part_b, dim_b)
+        marks.append((part_a, part_b))
+    for dim, mark in zip(cdims, [None] + marks):
+        gains = gather_stage(after(gains, *mark) if mark else gains, dim)
+    gains = in_order(gains, cdims[::-1]).reshape(n, 2, rows).transpose(1, 0, 2).reshape(2, 1, width)
+    gain_one, gain_two = gains[0], gains[1]
+    qkv_all = jnp.concatenate([in_order(part_a, cdims[::-1]), in_order(part_b, x_last[::-1])], axis=2)
+    qkv_all = qkv_all.reshape(width, 2 * cut)
+    early, late = marks[0], marks[-1]
 
     inputs32 = block_input.astype(f32)
     ratio_one = lax.rsqrt(jnp.mean(inputs32 * inputs32, axis=1, keepdims=True) + eps)
     normed_one = inputs32 * ratio_one
     hidden_one = (normed_one * gain_one).astype(bf16)
-    hidden_chip = ordered(even, hidden_one, flip(hidden_one, 1))
+    hidden_chip = side_by_side(core, hidden_one, flip(hidden_one, 1))
     qkv = dot(hidden_chip, qkv_all).astype(bf16)
+
+    unit = w_down.shape[0]
+    padded = -(-unit // 16) * 16
+    cols = quads * padded
+
+    def by_quad(w):
+        w = w.reshape(rows, quads, 4, unit)
+        w = jnp.pad(w, ((0, 0), (0, 0), (0, 0), (0, padded - unit)))
+        return w.transpose(2, 0, 1, 3).reshape(4, rows, cols)
+
+    gate_up = jnp.concatenate([by_quad(w_gate), by_quad(w_up)], axis=2)
+    pieces = [(quad, pick(gate_up, quad))]
+    for k in range(1, 4):
+        pieces.append((quad ^ k, flip(pick(gate_up, quad ^ k), k)))
+    gate_up = assemble(pieces).reshape(4 * rows, 2 * cols)
+    groups = [[q + 4 * i for i in range(quads)] for q in range(4)]
+    gate_up = lax.all_gather(gate_up, "tok", axis=0, tiled=True, axis_index_groups=groups)
+    down = jnp.pad(w_down, ((0, padded - unit), (0, 0)))
+
+    def step_of(dim, k):
+        return lax.rem(place(dim) + dim[1] - k, dim[1]) * (dim[0] // 4)
+
+    def first_stage(x, gates):
+        dim = qdims[0]
+        blocks = [(step_of(dim, 0), x)]
+        for k, gate in zip(shift_order(dim[1]), gates + gates[-1:] * dim[1]):
+            blocks.append((step_of(dim, k), shift(after(x, *gate), dim, k)))
+        return blocks
+
+    def next_stage(blocks, dim, gates):
+        out = []
+        for (i, x), gate in zip(blocks, gates + gates[-1:] * len(blocks)):
+            out.append((i + step_of(dim, 0), x))
+            x = after(x, *gate)
+            out += [(i + step_of(dim, k), shift(x, dim, k)) for k in range(1, dim[1])]
+        return out
 
     first = (me // 2) * 2 * tokens
     positions = first + jnp.arange(2 * tokens, dtype=jnp.int32)
@@ -479,107 +669,91 @@
     states = attention.states()
     fresh0 = (lo[tokens - 1] >= 0).astype(f32)
     fresh1 = (lo[2 * tokens - 1] >= tokens).astype(f32)
-    entering = others(states[:, 1] + (1.0 - fresh1) * states[:, 0], True, f32)
+    entering, scan = others(states[:, 1] + (1.0 - fresh1) * states[:, 0], True, f32)
     carry = jnp.stack([entering, states[:, 0] + (1.0 - fresh0) * entering], axis=1)
     y_heads, mixed_heads = attention.forward(carry)
-    mixed = ordered(even, row_half(mixed_heads, core), flip(row_half(mixed_heads, 1 - core), 1), 1)
-
-    chip_out = ordered(even, column_half(w_out, core), flip(column_half(w_out, 1 - core), 1))
-    out_half = gather(chip_out, z_first).reshape(width, half)
-    out_all = ordered(even, out_half, flip(out_half, 1), 1)
+    mixed = side_by_side(core, row_half(mixed_heads, core), flip(row_half(mixed_heads, 1 - core), 1), 1)
+
+    chip_out = side_by_side(core, column_half(w_out, core), flip(column_half(w_out, 1 - core), 1))
+    out_half = after(chip_out, *early)
+    for dim, gate in zip(cdims, [late, scan[1:2]] + [scan[2:3]] * len(cdims)):
+        out_half = after(gather_stage(out_half, dim), *gate)
+    out_half = in_order(out_half, cdims[::-1]).reshape(width, half)
+    out_all = side_by_side(core, out_half, flip(out_half, 1), 1)
     middle = inputs32 + dot(mixed, out_all)
     ratio_two = lax.rsqrt(jnp.mean(middle * middle, axis=1, keepdims=True) + eps)
     normed_two = middle * ratio_two
     hidden_two = (normed_two * gain_two).astype(bf16)
 
-    unit = w_down.shape[0]
-    padded = -(-unit // 16) * 16
-    cols = quads * padded
-
-    def by_quad(w):
-        w = w.reshape(rows, quads, 4, unit)
-        w = jnp.pad(w, ((0, 0), (0, 0), (0, 0), (0, padded - unit)))
-        return w.transpose(2, 0, 1, 3).reshape(4, rows, cols)
-
-    gate_up = jnp.concatenate([by_quad(w_gate), by_quad(w_up)], axis=2)
-    pieces = [(quad, pick(gate_up, quad))]
-    for k in range(1, 4):
-        pieces.append((quad ^ k, flip(pick(gate_up, quad ^ k), k)))
-    gate_up = assemble(pieces).reshape(4 * rows, 2 * cols)
-    gate_up = gather_blocks(gate_up, qdims).reshape(width, 2 * cols)
-    down = jnp.pad(w_down, ((0, padded - unit), (0, 0)))
-    down = gather_blocks(down, qdims).reshape(cols, width)
-
-    def to_quad(x):
-        near = jnp.concatenate([x, flip(x, 1)])
-        far = flip(x, 2)
-        return near, jnp.concatenate([far, flip(far, 1)])
-
-    def from_quad(near, far):
-        far_sum = far[:tokens] + flip(far[tokens:].astype(bf16), 1).astype(f32)
-        near_sum = near[:tokens] + flip(near[tokens:].astype(bf16), 1).astype(f32)
-        return near_sum + flip(far_sum.astype(bf16), 2).astype(f32)
-
-    hidden_quad = to_quad(hidden_two)
-    grad_quad = to_quad(out_grad)
-
-    def ffn(hidden, grad):
-        gate = dot(hidden, gate_up[:, :cols])
-        upper = dot(hidden, gate_up[:, cols:])
-        sigma = jax.nn.sigmoid(gate)
-        smooth = gate * sigma
-        activation = (smooth * upper).astype(bf16)
-        out = dot(activation, down)
-        d_act = dot_cols(grad, down)
-        d_gate = (d_act * upper * sigma * (1.0 + gate * (1.0 - sigma))).astype(bf16)
-        d_up = (d_act * smooth).astype(bf16)
-        d_hidden = dot_cols(d_gate, gate_up[:, :cols]) + dot_cols(d_up, gate_up[:, cols:])
-        return out, activation, d_gate, d_up, d_hidden
-
-    near, far = ffn(hidden_quad[0], grad_quad[0]), ffn(hidden_quad[1], grad_quad[1])
-    output = (middle + from_quad(near[0], far[0])).astype(bf16)
-    d_hidden_two = from_quad(near[4], far[4])
-    activation, d_gate, d_up = (jnp.concatenate([near[i], far[i]]) for i in (1, 2, 3))
-    hidden_quad = jnp.concatenate(hidden_quad)
-    grad_quad = jnp.concatenate(grad_quad)
+    down = first_stage(down, [early])
+    for dim in qdims[1:]:
+        down = next_stage(down, dim, [scan[1:2]])
+
+    far_grad = flip(after(out_grad, *late), 2)
+    grad_quad = [
+        jnp.concatenate([out_grad, flip(after(out_grad, *early), 1)]),
+        jnp.concatenate([far_grad, flip(after(far_grad, mixed_heads), 1)]),
+    ]
+    far_hidden = flip(hidden_two, 2)
+    near_hidden = jnp.concatenate([hidden_two, flip(hidden_two, 1)])
+    near = ffn(near_hidden, grad_quad[0], gate_up, down)
+    far_hidden = after(far_hidden, *near)
+    far_hidden = jnp.concatenate([far_hidden, flip(far_hidden, 1)])
+    far = ffn(far_hidden, grad_quad[1], gate_up, down)
+    hidden_quad = [near_hidden, far_hidden]
+
+    d_far = far[3][:tokens].astype(f32) + flip(far[3][tokens:], 1).astype(f32)
+    d_far_low = d_far.astype(bf16)
+    d_near = near[3][:tokens].astype(f32) + flip(near[3][tokens:], 1).astype(f32)
+    d_far = flip(d_far_low, 2)
 
     last = qdims[-1][1]
-
-    def hidden_part(index):
-        return pick(hidden_quad.reshape(4 * tokens, quads // last, last, width // quads), index, 2).reshape(
-            4 * tokens, width // last
-        )
-
-    def scatter_gate(d):
-        total = scatter(
-            lambda index: dot_rows(hidden_part(index), d).reshape(quads // last, width // quads, cols), qdims, None
-        )
-        total = total.reshape(4, rows, cols)
-        low = total.astype(bf16)
-        parts = [(quad, pick(total, quad))]
-        for k in range(1, 4):
-            parts.append((quad ^ k, flip(pick(low, quad ^ k), k).astype(f32)))
-        return assemble(parts).reshape(4, rows, quads, padded)[..., :unit].transpose(1, 2, 0, 3).reshape(rows, -1)
-
-    term_down = dot_rows(activation, grad_quad).reshape(quads // last, last, padded, width)
-    grad_down = scatter(lambda index: pick(term_down, index, 1), qdims, None)[:unit]
-    grad_gate = scatter_gate(d_gate)
-    grad_up = scatter_gate(d_up)
-
+    sent = row_blocks([after(near_hidden, d_far_low), far_hidden], [near[2], far[2]], jnp.arange(width // 128), 128)
+    gate_sum = lax.psum_scatter(sent, "tok", scatter_dimension=0, tiled=True, axis_index_groups=groups)
+    term = row_blocks([near[1], far[1]], [after(grad_quad[0], sent), grad_quad[1]], jnp.arange(cols // 128), 128)
+    kept = term
+    term = term.reshape(quads // last, last, padded, width)
+    sum_down = Scatter(lambda index: pick(term, index, 1), qdims)
+    sum_down.send()
+    sum_down.keep()
+
+    d_hidden_two = d_near + after(d_far, kept).astype(f32)
     term_norm_two = jnp.sum(d_hidden_two * normed_two, axis=0)
     scaled_two = d_hidden_two * gain_two
     d_middle = out_grad.astype(f32) + ratio_two * (
         scaled_two - normed_two * jnp.mean(scaled_two * normed_two, axis=1, keepdims=True)
     )
     d_mixed = d_middle.astype(bf16)
-    d_mixed_chip = ordered(even, d_mixed, flip(d_mixed, 1))
-
+    d_mixed_chip = side_by_side(core, d_mixed, flip(d_mixed, 1))
     d_heads = dot_cols(d_mixed_chip, row_half(out_all, core)).astype(bf16)
+    y_far = far[0][:tokens].astype(f32) + flip(far[0][tokens:], 1).astype(f32)
+    y_near = near[0][:tokens].astype(f32) + flip(near[0][tokens:], 1).astype(f32)
+    y_far_low = after(y_far.astype(bf16), d_mixed)
+    y_far = flip(y_far_low, 2)
+
+    d_heads = after(d_heads, y_far_low)
     dq, dk, dv, d_states = attention.backward(carry, y_heads, d_heads)
-    leaving = others(d_states[:, 0] + (1.0 - fresh0) * d_states[:, 1], False, bf16)
+    leaving, scan = others(d_states[:, 0] + (1.0 - fresh0) * d_states[:, 1], False, bf16)
+    grad_down = sum_down.finish((scan[0],), (dk,))[:unit]
+    mixed_chip = jnp.concatenate(
+        [
+            side_by_side(core, mixed_heads[:tokens], flip(mixed_heads[:tokens], 1), 1),
+            side_by_side(core, mixed_heads[tokens:], flip(mixed_heads[tokens:], 1), 1),
+        ]
+    )
+    sum_out = Scatter(part_maker([after(mixed_chip, scan[0])], [column_half(d_mixed_chip, core)], cdims), cdims)
+    sum_out.send()
+    sum_out.keep()
     d_states = jnp.stack([d_states[:, 1] + (1.0 - fresh1) * leaving, leaving], axis=1)
     dk, dv = attention.carried(d_states, dk, dv)
     d_qkv = jnp.concatenate([dq, dk, dv], axis=1)
+
+    sums = []
+    for d, dims in ((d_qkv[:, :cut], cdims), (d_qkv[:, cut:], x_last)):
+        sums.append(Scatter(part_maker([hidden_chip], [d], dims), dims))
+        sums[-1].send()
+    for part in sums:
+        part.keep()
 
     d_rows = row_half(d_qkv, 1 - core)
     theirs = flip(dot_cols(d_rows, qkv_all).astype(bf16), 1)
@@ -589,46 +763,36 @@
     input_grad = d_middle + ratio_one * (
         scaled_one - normed_one * jnp.mean(scaled_one * normed_one, axis=1, keepdims=True)
     )
-
-    last_chip = cdims[-1][1]
-
-    def chip_part(x, index):
-        return pick(x.reshape(2 * tokens, chips // last_chip, last_chip, 2 * rows), index, 2).reshape(
-            2 * tokens, width // last_chip
-        )
-
-    def scatter_rows(x, d):
-        total = scatter(
-            lambda index: dot_rows(chip_part(x, index), d).reshape(chips // last_chip, 2 * rows, d.shape[1]),
-            cdims,
-            None,
-        )
+    output = (middle + y_near + after(y_far, dk).astype(f32)).astype(bf16)
+
+    gate_sum = after(gate_sum, dk).reshape(4, rows, 2 * cols)
+    parts = [(quad, pick(gate_sum, quad).astype(f32))]
+    for k in range(1, 4):
+        parts.append((quad ^ k, flip(pick(gate_sum, quad ^ k), k).astype(f32)))
+    gate_sum = assemble(parts).reshape(4, rows, 2, quads, padded)[..., :unit]
+    gate_sum = gate_sum.transpose(2, 1, 3, 0, 4).reshape(2, rows, 4 * quads * unit)
+    grad_gate, grad_up = gate_sum[0], gate_sum[1]
+
+    def by_rows(total):
         return row_half(total, core), flip(row_half(total, 1 - core), 1)
 
-    mine, theirs = scatter_rows(hidden_chip, d_qkv)
+    grad_out = side_by_side(core, *by_rows(sum_out.finish()), 1)
+    mine, theirs = by_rows(jnp.concatenate([part.finish() for part in sums], axis=1))
     spans = [(0, lanes), (lanes, 2 * lanes), (2 * lanes, 2 * lanes + half)]
-    grad_query, grad_key, grad_value = (ordered(even, mine[:, a:b], theirs[:, a:b], 1) for a, b in spans)
-    mixed_chip = jnp.concatenate(
-        [
-            ordered(even, mixed_heads[:tokens], flip(mixed_heads[:tokens], 1), 1),
-            ordered(even, mixed_heads[tokens:], flip(mixed_heads[tokens:], 1), 1),
-        ]
-    )
-    grad_out = ordered(even, *scatter_rows(mixed_chip, column_half(d_mixed_chip, core)), 1)
-
-    def norm_shard(term):
-        term = total(term.reshape(1, width), [(1, 2)] + cdims).reshape(n, rows)
-        return pick(term, me)
+    grad_query, grad_key, grad_value = (side_by_side(core, mine[:, a:b], theirs[:, a:b], 1) for a, b in spans)
+
+    norms = total(jnp.stack([term_norm_one, term_norm_two]), [(1, 2)] + cdims).reshape(2, n, rows)
+    norms = pick(norms, me, 1)
 
     return (
         output,
         input_grad,
-        norm_shard(term_norm_one),
+        norms[0],
         grad_query,
         grad_key,
         grad_value,
         grad_out,
-        norm_shard(term_norm_two),
+        norms[1],
         grad_gate,
         grad_up,
         grad_down,

time: 1600 us -> 1100 us (0.69)
  waiting for transfers between devices: 679 us -> 375 us
  matrix products: 251 us -> 27.8 us
  Pallas kernels: 111 us -> 314 us
  local copies, waits for them, and re-layouts: 294 us -> 157 us
  other arithmetic: 104 us -> 71.1 us
  starting transfers between devices: 148 us -> 120 us
    ppermute x75 -> x56, waiting for transfers between devices: 587 us -> 292 us  [shift(): return lax.ppermute(x, 'tok', pairs)]
    pallas_call x0 -> x10, Pallas kernels: none -> 204 us  [the longest x8 105 us: row_blocks(): pl.pallas_call(lambda *refs: product_body(len(left), *refs), out_shape=ja...]
    dot_general x9 -> x0, matrix products: 80.6 us -> none  [dot_rows(): lax.dot_general(a, b, (((0,), (0,)), ((), ())), preferred_element_type=f32)]
    unnamed x178 -> x116, local copies, waits for them, and re-layouts: 103 us -> 22.1 us
    dot_general x8 -> x2, matrix products: 83 us -> 11.6 us  [dot(): lax.dot_general(a, b, (((1,), (0,)), ((), ())), preferred_element_type=f32)]
    dot_general x9 -> x3, matrix products: 87.1 us -> 16.3 us  [dot_cols(): lax.dot_general(a, b, (((1,), (1,)), ((), ())), preferred_element_type=f32)]
    dynamic_slice x3 -> x0, local copies, waits for them, and re-layouts: 41.3 us -> none  [pick(): return lax.dynamic_index_in_dim(x, index, axis, False)]
    reshape x9 -> x2, local copies, waits for them, and re-layouts: 40.8 us -> 4.88 us  [the longest x1 4.79 us: shards(): gate_sum = assemble(parts).reshape(4, rows, 2, quads, padded)[..., :unit]]
  transfers between devices with their start and end apart: 119 -> 99, of which waited for: 52 -> 41; matrix products, arithmetic and copies ran while one was open for 32% -> 20% of each run, Pallas kernels for 7% -> 21%
where the time goes in v2:
time: 1100 us; the launch traced here: 1080 us
  waiting for transfers between devices  375 us (34%)
  Pallas kernels  314 us (29%)
  local copies, waits for them, and re-layouts  157 us (14%)
  starting transfers between devices  120 us (11%)
  other arithmetic  71.1 us (6%)
  matrix products  27.8 us (3%)
  between operations  17.6 us (2%)
    ppermute x56, waiting for transfers between devices, shift(): return lax.ppermute(x, 'tok', pairs)  292 us
    pallas_call x4, Pallas kernels, call(): pl.pallas_call(body, grid=(2, self.heads), in_specs=ins, out_specs=outs,...  111 us
    pallas_call x8, Pallas kernels, row_blocks(): pl.pallas_call(lambda *refs: product_body(len(left), *refs), out_shape=ja...  105 us
    pallas_call x2, Pallas kernels, ffn(): pl.pallas_call(lambda *refs: ffn_body(count, *refs), out_shape=[jax.Shape...  98.6 us
    ppermute x56, starting transfers between devices, shift(): return lax.ppermute(x, 'tok', pairs)  96.9 us
    ppermute x41, waiting for transfers between devices, flip(): return lax.ppermute(x, 'tok', [(i, i ^ bits) for i in range(n)])  82.8 us
    dynamic_update_slice x39, local copies, waits for them, and re-layouts, assemble(): out = lax.dynamic_update_index_in_dim(out, block, index, 0)  28.8 us
    ppermute x41, starting transfers between devices, flip(): return lax.ppermute(x, 'tok', [(i, i ^ bits) for i in range(n)])  23.2 us
  transfers between devices with their start and end apart: 99, of which 41 were waited for; matrix products, arithmetic and copies ran while one was open for 20% of the time, Pallas kernels for 21%

profile of v2, /device:TPU:0, one launch (start us, length us, event | category | flops | bytes accessed | tf_op | source)
XLA Modules:
  0.0 1082.9 jit_solution(14688085870301789719)
XLA Ops:
  15.6 4.4 reshape.271
  22.0 4.4 reshape.273
  43.4 3.8 collective-permute-done.1
  58.5 4.2 collective-permute-start.6
  72.3 22.7 %collective-permute-done.6 = bf16[128,1280]{1,0:T(8,128)(2,1)} collective-permute-done((bf16[128,1280]{1,0:T(8,128)(2,1)}, bf16[128,1280]{1,0:T(8,128)(2,1)}, u32[]{:S(2)}, u32[]{:S(2)}) %collective-permute-start.6) | collective-permute-done | bytes 327712 | tf_op jit(solution)/shard_map/ppermute | solution.py:46
  97.0 29.8 %collective-permute-start.26 = (bf16[128,1024]{1,0:T(8,128)(2,1)}, bf16[128,1024]{1,0:T(8,128)(2,1)}, u32[]{:S(2)}, u32[]{:S(2)}) collective-permute-start(bf16[128,1024]{1,0:T(8,128)(2,1)} %constant_dynamic-update-slice_fusion.13), channel_id=1, source_target_pairs={{0,8},{1,9},{2,10},{3,11},{4,12},{5,13},{6,14},{7,15},{8,16},{9,17... | collective-permute-start | bytes 786440 | tf_op jit(solution)/shard_map/ppermute | solution.py:46
  133.4 10.5 collective-permute-done.8
  150.0 3.7 collective-permute-done.11
  166.0 25.7 %collective-permute-done.14 = bf16[2,4,128,640]{3,2,0,1:T(8,128)(2,1)S(1)} collective-permute-done((bf16[2,4,128,640]{3,2,0,1:T(8,128)(2,1)}, bf16[2,4,128,640]{3,2,0,1:T(8,128)(2,1)S(1)}, u32[]{:S(2)}, u32[]{:S(2)}) %collective-permute-start.14) | collective-permute-done | bytes 1310752 | tf_op jit(solution)/shard_map/ppermute | solution.py:46
  197.2 6.8 convolution_convert_fusion.k_ref.v_ref.q_ref
  204.0 14.0 %shard_map.266 = f32[8,2,168,128]{3,2,1,0:T(8,128)} custom-call(s32[2]{0:T(128)} %pad_add_fusion.scal, bf16[1024,1280]{1,0:T(8,128)(2,1)} %convolution_convert_fusion.k_ref.v_ref.q_ref, bf16[1024,1280]{1,0:T(8,128)(2,1)} %convolution_convert_fusion.k_ref.v_ref.q_ref, bf16[8,128,160]{2,1,0:T(8,128)(2,1)} %constant.558.clone.one, ...), custom_call_target="tpu_custom_call" | custom-call | tf_op jit(solution)/shard_map/pallas_call | solution.py:467
  225.7 25.1 %collective-permute-done.16 = f32[2,168,128]{2,1,0:T(8,128)S(1)} collective-permute-done((f32[2,168,128]{2,1,0:T(8,128)S(1)}, f32[2,168,128]{2,1,0:T(8,128)S(1)}, u32[]{:S(2)}, u32[]{:S(2)}) %collective-permute-start.16) | collective-permute-done | bytes 172064 | tf_op jit(solution)/shard_map/ppermute | solution.py:36
  263.8 5.2 collective-permute-done.19
  269.0 4.9 collective-permute-done.20
  274.7 21.3 %collective-permute-done.30 = bf16[2,4,128,1024]{3,2,0,1:T(8,128)(2,1)} collective-permute-done((bf16[2,4,128,1024]{3,2,0,1:T(8,128)(2,1)}, bf16[2,4,128,1024]{3,2,0,1:T(8,128)(2,1)}, u32[]{:S(2)}, u32[]{:S(2)}) %collective-permute-start.30) | collective-permute-done | bytes 2097184 | tf_op jit(solution)/shard_map/ppermute | solution.py:46
  309.5 4.6 collective-permute-done.22
  315.4 22.4 %shard_map.267 = (f32[1024,1024]{1,0:T(8,128)}, bf16[1024,1024]{1,0:T(8,128)(2,1)}) custom-call(bf16[1024,1280]{1,0:T(8,128)(2,1)} %convolution_convert_fusion.k_ref.v_ref.q_ref, bf16[1024,1280]{1,0:T(8,128)(2,1)} %convolution_convert_fusion.k_ref.v_ref.q_ref, bf16[1024,1280]{1,0:T(8,128)(2,1)} %convolution_convert_fusion.k_ref.v_ref.q_ref, ...), custom_call_target="tpu_custom_call" | custom-call | tf_op jit(solution)/shard_map/pallas_call | solution.py:467
  342.7 4.2 collective-permute-start.40
  357.7 4.7 multiply_reduce_fusion.2
  364.7 13.1 %collective-permute-done.40.refs_8_ = bf16[176,2048]{1,0:T(8,128)(2,1)} collective-permute-done((bf16[176,2048]{1,0:T(8,128)(2,1)S(1)}, bf16[176,2048]{1,0:T(8,128)(2,1)}, u32[]{:S(2)}, u32[]{:S(2)}) %collective-permute-start.40) | collective-permute-done | bytes 720928 | tf_op jit(solution)/shard_map/ppermute | solution.py:46
  377.8 30.6 %collective-permute-done.42.refs_10_ = bf16[176,2048]{1,0:T(8,128)(2,1)} collective-permute-done((bf16[176,2048]{1,0:T(8,128)(2,1)S(1)}, bf16[176,2048]{1,0:T(8,128)(2,1)}, u32[]{:S(2)}, u32[]{:S(2)}) %collective-permute-start.42) | collective-permute-done | bytes 720928 | tf_op jit(solution)/shard_map/ppermute | solution.py:46
  410.4 17.0 %collective-permute-done.39.refs_7_ = bf16[176,2048]{1,0:T(8,128)(2,1)S(1)} collective-permute-done((bf16[176,2048]{1,0:T(8,128)(2,1)S(1)}, bf16[176,2048]{1,0:T(8,128)(2,1)S(1)}, u32[]{:S(2)}, u32[]{:S(2)}) %collective-permute-start.39) | collective-permute-done | bytes 720928 | tf_op jit(solution)/shard_map/ppermute | solution.py:46
  436.8 4.1 pad_maximum_fusion.1.refs_1_
  443.0 15.4 %collective-permute-done.43.refs_11_ = bf16[176,2048]{1,0:T(8,128)(2,1)} collective-permute-done((bf16[176,2048]{1,0:T(8,128)(2,1)}, bf16[176,2048]{1,0:T(8,128)(2,1)}, u32[]{:S(2)}, u32[]{:S(2)}) %collective-permute-start.43) | collective-permute-done | bytes 720928 | tf_op jit(solution)/shard_map/ppermute | solution.py:46
  458.5 13.8 %collective-permute-done.37.refs_5_ = bf16[176,2048]{1,0:T(8,128)(2,1)} collective-permute-done((bf16[176,2048]{1,0:T(8,128)(2,1)S(1)}, bf16[176,2048]{1,0:T(8,128)(2,1)}, u32[]{:S(2)}, u32[]{:S(2)}) %collective-permute-start.37) | collective-permute-done | bytes 720928 | tf_op jit(solution)/shard_map/ppermute | solution.py:46
  472.3 49.3 %shard_map.268 = (bf16[1024,2048]{1,0:T(8,128)(2,1)}, bf16[1024,1408]{1,0:T(8,128)(2,1)}, bf16[1024,2816]{1,0:T(8,128)(2,1)}, bf16[1024,2048]{1,0:T(8,128)(2,1)}) custom-call(s32[8]{0:T(128)} %stack.88.refs_0_, bf16[1024,2048]{1,0:T(8,128)(2,1)} %pad_maximum_fusion.1.refs_1_, bf16[1024,2048]{1,0:T(8,128)(2,1)} %constant_dynamic-update-slice_fusion.26.refs_2_.refs_3_, ...), custom_call_target="tpu_custom_call" | custom-call | tf_op jit(solution)/shard_map/pallas_call | solution.py:171
  525.3 4.7 constant_dynamic-update-slice_fusion.31
  531.5 49.3 %shard_map.269 = (bf16[1024,2048]{1,0:T(8,128)(2,1)}, bf16[1024,1408]{1,0:T(8,128)(2,1)}, bf16[1024,2816]{1,0:T(8,128)(2,1)}, bf16[1024,2048]{1,0:T(8,128)(2,1)}) custom-call(s32[8]{0:T(128)} %stack.88.refs_0_, bf16[1024,2048]{1,0:T(8,128)(2,1)} %constant_dynamic-update-slice_fusion.30.refs_1_.refs_2_, bf16[1024,2048]{1,0:T(8,128)(2,1)} %copy-done.12, ...), custom_call_target="tpu_custom_call" | custom-call | tf_op jit(solution)/shard_map/pallas_call | solution.py:171
  583.3 3.8 collective-permute-done.51
  589.8 33.7 %shard_map.270 = bf16[2048,2816]{1,0:T(8,128)(2,1)} custom-call(s32[16]{0:T(128)} %iota.14.refs_0_, bf16[1024,2048]{1,0:T(8,128)(2,1)} %pad_maximum_fusion.1.refs_1_, bf16[1024,2048]{1,0:T(8,128)(2,1)} %constant_dynamic-update-slice_fusion.30.refs_1_.refs_2_, bf16[1024,2816]{1,0:T(8,128)(2,1)} %get-tuple-element.69.refs_3_, ...), custom_call_target="tpu_custom_call" | custom-call | flops 23622320128 | bytes 31457280 | tf_op jit(solution)/shard_map/pallas_call | solution.py:223
  633.7 20.3 %shard_map.271 = bf16[1408,2048]{1,0:T(8,128)(2,1)} custom-call(s32[11]{0:T(128)} %iota.13.refs_0_, bf16[1024,1408]{1,0:T(8,128)(2,1)} %get-tuple-element.68.refs_1_, bf16[1024,1408]{1,0:T(8,128)(2,1)} %get-tuple-element.76.refs_2_, bf16[1024,2048]{1,0:T(8,128)(2,1)} %constant_dynamic-update-slice_fusion.26.refs_2_.refs_3_, bf16[1024,2048]{1,0:T(8,128)(2,1)} %copy-done.12), custom_call_target="tpu_custom_call" | custom-call | flops 11811160064 | bytes 19922944 | tf_op jit(solution)/shard_map/pallas_call | solution.py:223
  654.0 17.7 %collective-permute-done.52 = bf16[512,2048]{1,0:T(8,128)(2,1)S(1)} collective-permute-done((bf16[512,2048]{1,0:T(8,128)(2,1)}, bf16[512,2048]{1,0:T(8,128)(2,1)S(1)}, u32[]{:S(2)}, u32[]{:S(2)}) %collective-permute-start.52) | collective-permute-done | bytes 2097184 | tf_op jit(solution)/shard_map/ppermute | solution.py:36
  677.4 6.0 constant_dynamic-update-slice_fusion.10
  691.1 3.9 slice.126
  695.5 3.8 add_convert_fusion.2
  702.9 5.8 fusion.13.d_ref
  708.7 45.9 %shard_map.272 = (bf16[1024,128]{1,0:T(8,128)(2,1)}, f32[1024,128]{1,0:T(8,128)}, f32[1024,1024]{1,0:T(8,128)}, f32[8,2,168,128]{3,2,1,0:T(8,128)}) custom-call(bf16[1024,1280]{1,0:T(8,128)(2,1)} %convolution_convert_fusion.k_ref.v_ref.q_ref, bf16[1024,1280]{1,0:T(8,128)(2,1)} %convolution_convert_fusion.k_ref.v_ref.q_ref, ...), custom_call_target="tpu_custom_call" | custom-call | tf_op jit(solution)/shard_map/pallas_call | solution.py:467
  756.0 21.5 %collective-permute-done.93 = bf16[4,176,2048]{2,1,0:T(8,128)(2,1)} collective-permute-done((bf16[4,176,2048]{2,1,0:T(8,128)(2,1)S(1)}, bf16[4,176,2048]{2,1,0:T(8,128)(2,1)}, u32[]{:S(2)}, u32[]{:S(2)}) %collective-permute-start.93) | collective-permute-done | bytes 2883616 | tf_op jit(solution)/shard_map/ppermute | solution.py:46
  784.2 9.1 shard_map.279
  793.2 6.7 fusion.70
  801.3 8.9 shard_map.278
  815.0 6.0 collective-permute-done.58
  821.9 13.7 %collective-permute-done.59 = bf16[2,168,128]{2,1,0:T(8,128)(2,1)S(1)} collective-permute-done((bf16[2,168,128]{2,1,0:T(8,128)(2,1)S(1)}, bf16[2,168,128]{2,1,0:T(8,128)(2,1)S(1)}, u32[]{:S(2)}, u32[]{:S(2)}) %collective-permute-start.59) | collective-permute-done | bytes 86048 | tf_op jit(solution)/shard_map/ppermute | solution.py:46
  836.0 4.8 collective-permute-done.61
  840.9 4.5 collective-permute-done.62
  845.4 5.4 collective-permute-done.63
  852.1 28.6 %shard_map.273 = (bf16[1024,128]{1,0:T(8,128)(2,1)}, bf16[1024,1024]{1,0:T(8,128)(2,1)}) custom-call(s32[2]{0:T(128)} %pad_add_fusion.scal, bf16[1024,1280]{1,0:T(8,128)(2,1)} %convolution_convert_fusion.k_ref.v_ref.q_ref, bf16[1024,1280]{1,0:T(8,128)(2,1)} %convolution_convert_fusion.k_ref.v_ref.q_ref, bf16[8,128,160]{2,1,0:T(8,128)(2,1)} %constant.558.clone.one, ...), custom_call_target="tpu_custom_call" | custom-call | tf_op jit(solution)/shard_map/pallas_call | solution.py:467
  888.0 8.1 shard_map.277
  896.8 5.8 add_convert_fusion
  902.6 8.6 shard_map.275
  912.7 5.5 convolution_convert_fusion.1
  918.1 8.1 shard_map.274
  926.2 8.1 shard_map.276
  940.4 20.7 %collective-permute-done.71 = bf16[8,128,640]{2,1,0:T(8,128)(2,1)} collective-permute-done((bf16[8,128,640]{2,1,0:T(8,128)(2,1)}, bf16[8,128,640]{2,1,0:T(8,128)(2,1)}, u32[]{:S(2)}, u32[]{:S(2)}) %collective-permute-start.71) | collective-permute-done | bytes 1310752 | tf_op jit(solution)/shard_map/ppermute | solution.py:46
  974.2 3.8 collective-permute-start.80
  978.3 5.0 fusion.9
  995.7 6.1 collective-permute-done.74
  1001.9 3.8 collective-permute-start.68
  1018.0 4.6 collective-permute-start.87
  1023.0 6.4 collective-permute-done.86
  1029.3 7.4 collective-permute-done.87
  1042.1 8.2 collective-permute-done.91
  1050.4 6.0 collective-permute-done.92
  1056.5 4.8 reshape.284
  (477 shorter events, 274.5 us)
Async XLA Ops:
  7.2 465.1 %all-gather.2.cloned.1.call-start = ((), (), s32[]{:S(2)}) async-start(), calls=%async_computation.1 | async-start | bytes 12976128 | tf_op jit(solution)/shard_map/all_gather | solution.py:644
  11.0 45.9 %collective-permute-start.4 = (bf16[64,1280]{1,0:T(8,128)(2,1)}, bf16[64,1280]{1,0:T(8,128)(2,1)}, u32[]{:S(2)}, u32[]{:S(2)}) collective-permute-start(bf16[64,1280]{1,0:T(8,128)(2,1)} %pad_maximum_fusion.8), channel_id=1, source_target_pairs={{0,1},{1,0},{2,3},{3,2},{4,5},{5,4},{6,7},{7,6},{8,9},{9,8},{10,11... | collective-permute-start | bytes 491528 | tf_op jit(solution)/shard_map/ppermute | solution.py:36
  12.7 28.5 %collective-permute-start = (f32[2,64]{1,0:T(2,128)}, f32[2,64]{1,0:T(2,128)}, u32[]{:S(2)}, u32[]{:S(2)}) collective-permute-start(f32[2,64]{1,0:T(2,128)} %maximum_convert_fusion.1), channel_id=1, source_target_pairs={{0,1},{1,0},{2,3},{3,2},{4,5},{5,4},{6,7},{7,6},{8,9},{9,8},{10,11... | collective-permute-start | bytes 1544 | tf_op jit(solution)/shard_map/ppermute | solution.py:46
  15.1 40.2 %collective-permute-start.25 = (bf16[64,1024]{1,0:T(8,128)(2,1)}, bf16[64,1024]{1,0:T(8,128)(2,1)}, u32[]{:S(2)}, u32[]{:S(2)}) collective-permute-start(bf16[64,1024]{1,0:T(8,128)(2,1)} %get-tuple-element.158), channel_id=1, source_target_pairs={{0,1},{1,0},{2,3},{3,2},{4,5},{5,4},{6,7},{7,6},{8,9},{9,8},{10,11... | collective-permute-start | bytes 393224 | tf_op jit(solution)/shard_map/ppermute | solution.py:36
  30.8 32.9 %collective-permute-start.34 = (bf16[64,2816]{1,0:T(8,128)(2,1)}, bf16[64,2816]{1,0:T(8,128)(2,1)}, u32[]{:S(2)}, u32[]{:S(2)}) collective-permute-start(bf16[64,2816]{1,0:T(8,128)(2,1)} %get-tuple-element.130), channel_id=1, source_target_pairs={{0,1},{1,0},{2,3},{3,2},{4,5},{5,4},{6,7},{7,6},{8,9},{9,8},{10,11... | collective-permute-start | bytes 1081352 | tf_op jit(solution)/shard_map/ppermute | solution.py:36
  30.9 34.7 %collective-permute-start.35 = (bf16[64,2816]{1,0:T(8,128)(2,1)}, bf16[64,2816]{1,0:T(8,128)(2,1)}, u32[]{:S(2)}, u32[]{:S(2)}) collective-permute-start(bf16[64,2816]{1,0:T(8,128)(2,1)} %get-tuple-element.129), channel_id=1, source_target_pairs={{0,2},{1,3},{2,0},{3,1},{4,6},{5,7},{6,4},{7,5},{8,10},{9,11},{10,... | collective-permute-start | bytes 1081352 | tf_op jit(solution)/shard_map/ppermute | solution.py:36
  58.5 36.5 %collective-permute-start.6 = (bf16[128,1280]{1,0:T(8,128)(2,1)}, bf16[128,1280]{1,0:T(8,128)(2,1)}, u32[]{:S(2)}, u32[]{:S(2)}) collective-permute-start(bf16[128,1280]{1,0:T(8,128)(2,1)} %constant_dynamic-update-slice_fusion.21), channel_id=1, source_target_pairs={{0,16},{1,17},{2,18},{3,19},{4,20},{5,21},{6,22},{7,23},{8,24},{9,... | collective-permute-start | bytes 983048 | tf_op jit(solution)/shard_map/ppermute | solution.py:46
  63.8 32.2 %collective-permute-start.7 = (bf16[128,1280]{1,0:T(8,128)(2,1)}, bf16[128,1280]{1,0:T(8,128)(2,1)}, u32[]{:S(2)}, u32[]{:S(2)}) collective-permute-start(bf16[128,1280]{1,0:T(8,128)(2,1)} %constant_dynamic-update-slice_fusion.21), channel_id=1, source_target_pairs={{0,24},{1,25},{2,26},{3,27},{4,28},{5,29},{6,30},{7,31},{8,0},{9,1... | collective-permute-start | bytes 983048 | tf_op jit(solution)/shard_map/ppermute | solution.py:46
  68.1 969.0 %reduce-scatter.2.cloned.1.call-start = ((), (), s32[]{:S(2)}) async-start(), calls=%async_computation.2 | async-start | bytes 12976128 | tf_op jit(solution)/shard_map/reduce_scatter | solution.py:712
  97.0 59.6 %collective-permute-start.26 = (bf16[128,1024]{1,0:T(8,128)(2,1)}, bf16[128,1024]{1,0:T(8,128)(2,1)}, u32[]{:S(2)}, u32[]{:S(2)}) collective-permute-start(bf16[128,1024]{1,0:T(8,128)(2,1)} %constant_dynamic-update-slice_fusion.13), channel_id=1, source_target_pairs={{0,8},{1,9},{2,10},{3,11},{4,12},{5,13},{6,14},{7,15},{8,16},{9,17... | collective-permute-start | bytes 786440 | tf_op jit(solution)/shard_map/ppermute | solution.py:46
  126.7 31.0 %collective-permute-start.27 = (bf16[128,1024]{1,0:T(8,128)(2,1)}, bf16[128,1024]{1,0:T(8,128)(2,1)}, u32[]{:S(2)}, u32[]{:S(2)}) collective-permute-start(bf16[128,1024]{1,0:T(8,128)(2,1)} %constant_dynamic-update-slice_fusion.13), channel_id=1, source_target_pairs={{0,16},{1,17},{2,18},{3,19},{4,20},{5,21},{6,22},{7,23},{8,24},{9,... | collective-permute-start | bytes 786440 | tf_op jit(solution)/shard_map/ppermute | solution.py:46
  126.9 22.1 %collective-permute-start.9 = (bf16[4,128,640]{2,1,0:T(8,128)(2,1)S(1)}, bf16[4,128,640]{2,1,0:T(8,128)(2,1)S(1)}, u32[]{:S(2)}, u32[]{:S(2)}) collective-permute-start(bf16[4,128,640]{2,1,0:T(8,128)(2,1)S(1)} %get-tuple-element.133), channel_id=1, source_target_pairs={{0,4},{1,5},{2,6},{3,7},{4,0},{5,1},{6,2},{7,3},{8,12},{9,13},{10,... | collective-permute-start | bytes 1966088 | tf_op jit(solution)/shard_map/ppermute | solution.py:46
  129.1 17.2 %collective-permute-start.10 = (bf16[4,128,640]{2,1,0:T(8,128)(2,1)S(1)}, bf16[4,128,640]{2,1,0:T(8,128)(2,1)S(1)}, u32[]{:S(2)}, u32[]{:S(2)}) collective-permute-start(bf16[4,128,640]{2,1,0:T(8,128)(2,1)S(1)} %get-tuple-element.132), channel_id=1, source_target_pairs={{0,2},{1,3},{2,0},{3,1},{4,6},{5,7},{6,4},{7,5},{8,10},{9,11},{10,... | collective-permute-start | bytes 1966088 | tf_op jit(solution)/shard_map/ppermute | solution.py:46
  143.9 17.0 %collective-permute-start.28 = (bf16[128,1024]{1,0:T(8,128)(2,1)}, bf16[128,1024]{1,0:T(8,128)(2,1)}, u32[]{:S(2)}, u32[]{:S(2)}) collective-permute-start(bf16[128,1024]{1,0:T(8,128)(2,1)} %constant_dynamic-update-slice_fusion.13), channel_id=1, source_target_pairs={{0,24},{1,25},{2,26},{3,27},{4,28},{5,29},{6,30},{7,31},{8,0},{9,1... | collective-permute-start | bytes 786440 | tf_op jit(solution)/shard_map/ppermute | solution.py:46
  147.3 44.4 %collective-permute-start.14 = (bf16[2,4,128,640]{3,2,0,1:T(8,128)(2,1)}, bf16[2,4,128,640]{3,2,0,1:T(8,128)(2,1)S(1)}, u32[]{:S(2)}, u32[]{:S(2)}) collective-permute-start(bf16[2,4,128,640]{3,2,0,1:T(8,128)(2,1)} %bitcast_dynamic-update-slice_fusion.8), channel_id=1, source_target_pairs={{0,4},{1,5},{2,6},{3,7},{4,0},{5,1},{6,2},{7,3},{8,12},{9,13},{10,... | collective-permute-start | bytes 3932168 | tf_op jit(solution)/shard_map/ppermute | solution.py:46
  155.4 39.4 %collective-permute-start.12 = (bf16[512,2048]{1,0:T(8,128)(2,1)S(1)}, bf16[512,2048]{1,0:T(8,128)(2,1)S(1)}, u32[]{:S(2)}, u32[]{:S(2)}) collective-permute-start(bf16[512,2048]{1,0:T(8,128)(2,1)S(1)} %get-tuple-element.115), channel_id=1, source_target_pairs={{0,1},{1,0},{2,3},{3,2},{4,5},{5,4},{6,7},{7,6},{8,9},{9,8},{10,11... | collective-permute-start | bytes 6291464 | tf_op jit(solution)/shard_map/ppermute | solution.py:36
  157.6 34.5 %collective-permute-start.13 = (bf16[2,4,128,640]{3,2,0,1:T(8,128)(2,1)}, bf16[2,4,128,640]{3,2,0,1:T(8,128)(2,1)S(1)}, u32[]{:S(2)}, u32[]{:S(2)}) collective-permute-start(bf16[2,4,128,640]{3,2,0,1:T(8,128)(2,1)} %bitcast_dynamic-update-slice_fusion.11), channel_id=1, source_target_pairs={{0,2},{1,3},{2,0},{3,1},{4,6},{5,7},{6,4},{7,5},{8,10},{9,11},{10,... | collective-permute-start | bytes 3932168 | tf_op jit(solution)/shard_map/ppermute | solution.py:46
  192.4 58.5 %collective-permute-start.29 = (bf16[4,128,1024]{2,1,0:T(8,128)(2,1)S(1)}, bf16[4,128,1024]{2,1,0:T(8,128)(2,1)S(1)}, u32[]{:S(2)}, u32[]{:S(2)}) collective-permute-start(bf16[4,128,1024]{2,1,0:T(8,128)(2,1)S(1)} %bitcast_dynamic-update-slice_fusion.20), channel_id=1, source_target_pairs={{0,4},{1,5},{2,6},{3,7},{4,0},{5,1},{6,2},{7,3},{8,12},{9,13},{10,... | collective-permute-start | bytes 3145736 | tf_op jit(solution)/shard_map/ppermute | solution.py:46
  219.6 31.2 %collective-permute-start.16 = (f32[2,168,128]{2,1,0:T(8,128)S(1)}, f32[2,168,128]{2,1,0:T(8,128)S(1)}, u32[]{:S(2)}, u32[]{:S(2)}) collective-permute-start(f32[2,168,128]{2,1,0:T(8,128)S(1)} %get-tuple-element.144), channel_id=1, source_target_pairs={{0,4},{1,5},{2,6},{3,7},{4,0},{5,1},{6,2},{7,3},{8,12},{9,13},{10,... | collective-permute-start | bytes 516104 | tf_op jit(solution)/shard_map/ppermute | solution.py:36
  220.7 30.1 %collective-permute-start.17 = (f32[2,168,128]{2,1,0:T(8,128)S(1)}, f32[2,168,128]{2,1,0:T(8,128)S(1)}, u32[]{:S(2)}, u32[]{:S(2)}) collective-permute-start(f32[2,168,128]{2,1,0:T(8,128)S(1)} %get-tuple-element.143), channel_id=1, source_target_pairs={{0,6},{1,7},{2,4},{3,5},{4,2},{5,3},{6,0},{7,1},{8,14},{9,15},{10,... | collective-permute-start | bytes 516104 | tf_op jit(solution)/shard_map/ppermute | solution.py:36
  252.6 43.5 %collective-permute-start.30 = (bf16[2,4,128,1024]{3,2,0,1:T(8,128)(2,1)}, bf16[2,4,128,1024]{3,2,0,1:T(8,128)(2,1)}, u32[]{:S(2)}, u32[]{:S(2)}) collective-permute-start(bf16[2,4,128,1024]{3,2,0,1:T(8,128)(2,1)} %bitcast_dynamic-update-slice_fusion.7), channel_id=1, source_target_pairs={{0,2},{1,3},{2,0},{3,1},{4,6},{5,7},{6,4},{7,5},{8,10},{9,11},{10,... | collective-permute-start | bytes 6291464 | tf_op jit(solution)/shard_map/ppermute | solution.py:46
  256.8 17.1 %collective-permute-start.20 = (f32[2,168,128]{2,1,0:T(8,128)S(1)}, f32[2,168,128]{2,1,0:T(8,128)S(1)}, u32[]{:S(2)}, u32[]{:S(2)}) collective-permute-start(f32[2,168,128]{2,1,0:T(8,128)S(1)} %fusion.47), channel_id=1, source_target_pairs={{0,24},{1,25},{2,26},{3,27},{4,28},{5,29},{6,30},{7,31}} | collective-permute-start | bytes 516104 | tf_op jit(solution)/shard_map/ppermute | solution.py:46
  299.2 55.8 %collective-permute-start.31 = (bf16[2048,1024]{1,0:T(8,128)(2,1)}, bf16[2048,1024]{1,0:T(8,128)(2,1)}, u32[]{:S(2)}, u32[]{:S(2)}) collective-permute-start(bf16[2048,1024]{1,0:T(8,128)(2,1)} %bitcast.69), channel_id=1, source_target_pairs={{0,1},{1,0},{2,3},{3,2},{4,5},{5,4},{6,7},{7,6},{8,9},{9,8},{10,11... | collective-permute-start | bytes 12582920 | tf_op jit(solution)/shard_map/ppermute | solution.py:36
  342.6 22.0 %collective-permute-start.38 = (bf16[176,2048]{1,0:T(8,128)(2,1)S(1)}, bf16[176,2048]{1,0:T(8,128)(2,1)S(1)}, u32[]{:S(2)}, u32[]{:S(2)}) collective-permute-start(bf16[176,2048]{1,0:T(8,128)(2,1)S(1)} %pad.13.refs_4_), channel_id=1, source_target_pairs={{0,8},{1,9},{2,10},{3,11},{4,12},{5,13},{6,14},{7,15},{8,16},{9,17... | collective-permute-start | bytes 2162696 | tf_op jit(solution)/shard_map/ppermute | solution.py:46
  342.7 35.0 %collective-permute-start.40 = (bf16[176,2048]{1,0:T(8,128)(2,1)S(1)}, bf16[176,2048]{1,0:T(8,128)(2,1)}, u32[]{:S(2)}, u32[]{:S(2)}) collective-permute-start(bf16[176,2048]{1,0:T(8,128)(2,1)S(1)} %pad.13.refs_4_), channel_id=1, source_target_pairs={{0,24},{1,25},{2,26},{3,27},{4,28},{5,29},{6,30},{7,31},{8,0},{9,1... | collective-permute-start | bytes 2162696 | tf_op jit(solution)/shard_map/ppermute | solution.py:46
  346.9 62.4 %collective-permute-start.33 = (bf16[512,2048]{1,0:T(8,128)(2,1)}, bf16[512,2048]{1,0:T(8,128)(2,1)}, u32[]{:S(2)}, u32[]{:S(2)}) collective-permute-start(bf16[512,2048]{1,0:T(8,128)(2,1)} %param.31), channel_id=1, source_target_pairs={{0,1},{1,0},{2,3},{3,2},{4,5},{5,4},{6,7},{7,6},{8,9},{9,8},{10,11... | collective-permute-start | bytes 6291464 | tf_op jit(solution)/shard_map/ppermute | solution.py:36
  349.4 78.9 %collective-permute-start.47 = (bf16[512,2048]{1,0:T(8,128)(2,1)}, bf16[512,2048]{1,0:T(8,128)(2,1)S(1)}, u32[]{:S(2)}, u32[]{:S(2)}) collective-permute-start(bf16[512,2048]{1,0:T(8,128)(2,1)} %param.31), channel_id=1, source_target_pairs={{0,2},{1,3},{2,0},{3,1},{4,6},{5,7},{6,4},{7,5},{8,10},{9,11},{10,... | collective-permute-start | bytes 6291464 | tf_op jit(solution)/shard_map/ppermute | solution.py:36
  364.5 69.1 %collective-permute-start.32 = (bf16[512,2048]{1,0:T(8,128)(2,1)S(1)}, bf16[512,2048]{1,0:T(8,128)(2,1)}, u32[]{:S(2)}, u32[]{:S(2)}) collective-permute-start(bf16[512,2048]{1,0:T(8,128)(2,1)S(1)} %multiply_convert_fusion), channel_id=1, source_target_pairs={{0,1},{1,0},{2,3},{3,2},{4,5},{5,4},{6,7},{7,6},{8,9},{9,8},{10,11... | collective-permute-start | bytes 6291464 | tf_op jit(solution)/shard_map/ppermute | solution.py:36
  364.7 43.7 %collective-permute-start.42 = (bf16[176,2048]{1,0:T(8,128)(2,1)S(1)}, bf16[176,2048]{1,0:T(8,128)(2,1)}, u32[]{:S(2)}, u32[]{:S(2)}) collective-permute-start(bf16[176,2048]{1,0:T(8,128)(2,1)S(1)} %pad.13.refs_4_), channel_id=1, source_target_pairs={{0,16},{1,17},{2,18},{3,19},{4,20},{5,21},{6,22},{7,23},{8,24},{9,... | collective-permute-start | bytes 2162696 | tf_op jit(solution)/shard_map/ppermute | solution.py:46
  377.8 143.8 %collective-permute-start.45 = (bf16[512,2048]{1,0:T(8,128)(2,1)S(1)}, bf16[512,2048]{1,0:T(8,128)(2,1)}, u32[]{:S(2)}, u32[]{:S(2)}) collective-permute-start(bf16[512,2048]{1,0:T(8,128)(2,1)S(1)} %multiply_convert_fusion), channel_id=1, source_target_pairs={{0,2},{1,3},{2,0},{3,1},{4,6},{5,7},{6,4},{7,5},{8,10},{9,11},{10,... | collective-permute-start | bytes 6291464 | tf_op jit(solution)/shard_map/ppermute | solution.py:36
  408.4 19.1 %collective-permute-start.39 = (bf16[176,2048]{1,0:T(8,128)(2,1)S(1)}, bf16[176,2048]{1,0:T(8,128)(2,1)S(1)}, u32[]{:S(2)}, u32[]{:S(2)}) collective-permute-start(bf16[176,2048]{1,0:T(8,128)(2,1)S(1)} %collective-permute-done.38.refs_6_), channel_id=1, source_target_pairs={{0,4},{1,5},{2,6},{3,7},{4,0},{5,1},{6,2},{7,3},{8,12},{9,13},{10,... | collective-permute-start | bytes 2162696 | tf_op jit(solution)/shard_map/ppermute | solution.py:46
  409.3 33.7 %collective-permute-start.41 = (bf16[176,2048]{1,0:T(8,128)(2,1)}, bf16[176,2048]{1,0:T(8,128)(2,1)}, u32[]{:S(2)}, u32[]{:S(2)}) collective-permute-start(bf16[176,2048]{1,0:T(8,128)(2,1)} %collective-permute-done.40.refs_8_), channel_id=1, source_target_pairs={{0,4},{1,5},{2,6},{3,7},{4,0},{5,1},{6,2},{7,3},{8,12},{9,13},{10,... | collective-permute-start | bytes 2162696 | tf_op jit(solution)/shard_map/ppermute | solution.py:46
  427.5 31.0 %collective-permute-start.43 = (bf16[176,2048]{1,0:T(8,128)(2,1)}, bf16[176,2048]{1,0:T(8,128)(2,1)}, u32[]{:S(2)}, u32[]{:S(2)}) collective-permute-start(bf16[176,2048]{1,0:T(8,128)(2,1)} %collective-permute-done.42.refs_10_), channel_id=1, source_target_pairs={{0,4},{1,5},{2,6},{3,7},{4,0},{5,1},{6,2},{7,3},{8,12},{9,13},{10,... | collective-permute-start | bytes 2162696 | tf_op jit(solution)/shard_map/ppermute | solution.py:46
  428.4 43.9 %collective-permute-start.37 = (bf16[176,2048]{1,0:T(8,128)(2,1)S(1)}, bf16[176,2048]{1,0:T(8,128)(2,1)}, u32[]{:S(2)}, u32[]{:S(2)}) collective-permute-start(bf16[176,2048]{1,0:T(8,128)(2,1)S(1)} %pad.13.refs_4_), channel_id=1, source_target_pairs={{0,4},{1,5},{2,6},{3,7},{4,0},{5,1},{6,2},{7,3},{8,12},{9,13},{10,... | collective-permute-start | bytes 2162696 | tf_op jit(solution)/shard_map/ppermute | solution.py:46
  433.6 89.9 %collective-permute-start.48 = (bf16[512,2048]{1,0:T(8,128)(2,1)}, bf16[512,2048]{1,0:T(8,128)(2,1)}, u32[]{:S(2)}, u32[]{:S(2)}) collective-permute-start(bf16[512,2048]{1,0:T(8,128)(2,1)} %copy-done.34), channel_id=1, source_target_pairs={{0,1},{1,0},{2,3},{3,2},{4,5},{5,4},{6,7},{7,6},{8,9},{9,8},{10,11... | collective-permute-start | bytes 6291464 | tf_op jit(solution)/shard_map/ppermute | solution.py:36
  623.5 48.2 %collective-permute-start.52 = (bf16[512,2048]{1,0:T(8,128)(2,1)}, bf16[512,2048]{1,0:T(8,128)(2,1)S(1)}, u32[]{:S(2)}, u32[]{:S(2)}) collective-permute-start(bf16[512,2048]{1,0:T(8,128)(2,1)} %add_convert_fusion.1), channel_id=1, source_target_pairs={{0,2},{1,3},{2,0},{3,1},{4,6},{5,7},{6,4},{7,5},{8,10},{9,11},{10,... | collective-permute-start | bytes 6291464 | tf_op jit(solution)/shard_map/ppermute | solution.py:36
  628.4 43.3 %collective-permute-start.50 = (bf16[512,2048]{1,0:T(8,128)(2,1)}, bf16[512,2048]{1,0:T(8,128)(2,1)}, u32[]{:S(2)}, u32[]{:S(2)}) collective-permute-start(bf16[512,2048]{1,0:T(8,128)(2,1)} %slice.130), channel_id=1, source_target_pairs={{0,1},{1,0},{2,3},{3,2},{4,5},{5,4},{6,7},{7,6},{8,9},{9,8},{10,11... | collective-permute-start | bytes 6291464 | tf_op jit(solution)/shard_map/ppermute | solution.py:36
  629.0 57.4 %collective-permute-start.82 = (bf16[512,1024]{1,0:T(8,128)(2,1)}, bf16[512,1024]{1,0:T(8,128)(2,1)}, u32[]{:S(2)}, u32[]{:S(2)}) collective-permute-start(bf16[512,1024]{1,0:T(8,128)(2,1)} %get-tuple-element.121), channel_id=1, source_target_pairs={{0,1},{1,0},{2,3},{3,2},{4,5},{5,4},{6,7},{7,6},{8,9},{9,8},{10,11... | collective-permute-start | bytes 3145736 | tf_op jit(solution)/shard_map/ppermute | solution.py:36
  629.4 58.8 %collective-permute-start.83 = (bf16[512,1024]{1,0:T(8,128)(2,1)}, bf16[512,1024]{1,0:T(8,128)(2,1)S(1)}, u32[]{:S(2)}, u32[]{:S(2)}) collective-permute-start(bf16[512,1024]{1,0:T(8,128)(2,1)} %get-tuple-element.123), channel_id=1, source_target_pairs={{0,1},{1,0},{2,3},{3,2},{4,5},{5,4},{6,7},{7,6},{8,9},{9,8},{10,11... | collective-permute-start | bytes 3145736 | tf_op jit(solution)/shard_map/ppermute | solution.py:36
  632.8 62.7 %collective-permute-start.49 = (bf16[512,2048]{1,0:T(8,128)(2,1)}, bf16[512,2048]{1,0:T(8,128)(2,1)}, u32[]{:S(2)}, u32[]{:S(2)}) collective-permute-start(bf16[512,2048]{1,0:T(8,128)(2,1)} %slice.128), channel_id=1, source_target_pairs={{0,1},{1,0},{2,3},{3,2},{4,5},{5,4},{6,7},{7,6},{8,9},{9,8},{10,11... | collective-permute-start | bytes 6291464 | tf_op jit(solution)/shard_map/ppermute | solution.py:36
  683.4 17.5 %collective-permute-start.54 = (bf16[512,2048]{1,0:T(8,128)(2,1)S(1)}, bf16[512,2048]{1,0:T(8,128)(2,1)}, u32[]{:S(2)}, u32[]{:S(2)}) collective-permute-start(bf16[512,2048]{1,0:T(8,128)(2,1)S(1)} %get-tuple-element.110), channel_id=1, source_target_pairs={{0,1},{1,0},{2,3},{3,2},{4,5},{5,4},{6,7},{7,6},{8,9},{9,8},{10,11... | collective-permute-start | bytes 6291464 | tf_op jit(solution)/shard_map/ppermute | solution.py:36
  684.8 92.7 %collective-permute-start.93 = (bf16[4,176,2048]{2,1,0:T(8,128)(2,1)S(1)}, bf16[4,176,2048]{2,1,0:T(8,128)(2,1)}, u32[]{:S(2)}, u32[]{:S(2)}) collective-permute-start(bf16[4,176,2048]{2,1,0:T(8,128)(2,1)S(1)} %dynamic-slice_bitcast_fusion), channel_id=1, source_target_pairs={{0,4},{1,5},{2,6},{3,7},{4,0},{5,1},{6,2},{7,3},{8,12},{9,13},{10,... | collective-permute-start | bytes 8650760 | tf_op jit(solution)/shard_map/ppermute | solution.py:46
  695.0 201.1 %collective-permute-start.44 = (bf16[512,2048]{1,0:T(8,128)(2,1)}, bf16[512,2048]{1,0:T(8,128)(2,1)}, u32[]{:S(2)}, u32[]{:S(2)}) collective-permute-start(bf16[512,2048]{1,0:T(8,128)(2,1)} %slice.126), channel_id=1, source_target_pairs={{0,1},{1,0},{2,3},{3,2},{4,5},{5,4},{6,7},{7,6},{8,9},{9,8},{10,11... | collective-permute-start | bytes 6291464 | tf_op jit(solution)/shard_map/ppermute | solution.py:36
  699.4 188.6 %collective-permute-start.53 = (bf16[512,2048]{1,0:T(8,128)(2,1)}, bf16[512,2048]{1,0:T(8,128)(2,1)}, u32[]{:S(2)}, u32[]{:S(2)}) collective-permute-start(bf16[512,2048]{1,0:T(8,128)(2,1)} %add_convert_fusion.2), channel_id=1, source_target_pairs={{0,2},{1,3},{2,0},{3,1},{4,6},{5,7},{6,4},{7,5},{8,10},{9,11},{10,... | collective-permute-start | bytes 6291464 | tf_op jit(solution)/shard_map/ppermute | solution.py:36
  777.5 32.7 %collective-permute-start.55 = (bf16[2,168,128]{2,1,0:T(8,128)(2,1)S(1)}, bf16[2,168,128]{2,1,0:T(8,128)(2,1)S(1)}, u32[]{:S(2)}, u32[]{:S(2)}) collective-permute-start(bf16[2,168,128]{2,1,0:T(8,128)(2,1)S(1)} %get-tuple-element.153), channel_id=1, source_target_pairs={{0,2},{1,3},{2,0},{3,1},{4,6},{5,7},{6,4},{7,5},{8,10},{9,11},{10,... | collective-permute-start | bytes 258056 | tf_op jit(solution)/shard_map/ppermute | solution.py:36
  779.3 30.9 %collective-permute-start.56 = (bf16[2,168,128]{2,1,0:T(8,128)(2,1)S(1)}, bf16[2,168,128]{2,1,0:T(8,128)(2,1)S(1)}, u32[]{:S(2)}, u32[]{:S(2)}) collective-permute-start(bf16[2,168,128]{2,1,0:T(8,128)(2,1)S(1)} %get-tuple-element.155), channel_id=1, source_target_pairs={{0,4},{1,5},{2,6},{3,7},{4,0},{5,1},{6,2},{7,3},{8,12},{9,13},{10,... | collective-permute-start | bytes 258056 | tf_op jit(solution)/shard_map/ppermute | solution.py:36
  779.6 30.6 %collective-permute-start.57 = (bf16[2,168,128]{2,1,0:T(8,128)(2,1)S(1)}, bf16[2,168,128]{2,1,0:T(8,128)(2,1)S(1)}, u32[]{:S(2)}, u32[]{:S(2)}) collective-permute-start(bf16[2,168,128]{2,1,0:T(8,128)(2,1)S(1)} %get-tuple-element.154), channel_id=1, source_target_pairs={{0,6},{1,7},{2,4},{3,5},{4,2},{5,3},{6,0},{7,1},{8,14},{9,15},{10,... | collective-permute-start | bytes 258056 | tf_op jit(solution)/shard_map/ppermute | solution.py:36
  811.7 23.9 %collective-permute-start.59 = (bf16[2,168,128]{2,1,0:T(8,128)(2,1)S(1)}, bf16[2,168,128]{2,1,0:T(8,128)(2,1)S(1)}, u32[]{:S(2)}, u32[]{:S(2)}) collective-permute-start(bf16[2,168,128]{2,1,0:T(8,128)(2,1)S(1)} %fusion.42), channel_id=1, source_target_pairs={{16,0},{17,1},{18,2},{19,3},{20,4},{21,5},{22,6},{23,7},{24,8},{25... | collective-permute-start | bytes 258056 | tf_op jit(solution)/shard_map/ppermute | solution.py:46
  813.0 22.6 %collective-permute-start.60 = (bf16[2,168,128]{2,1,0:T(8,128)(2,1)S(1)}, bf16[2,168,128]{2,1,0:T(8,128)(2,1)S(1)}, u32[]{:S(2)}, u32[]{:S(2)}) collective-permute-start(bf16[2,168,128]{2,1,0:T(8,128)(2,1)S(1)} %fusion.42), channel_id=1, source_target_pairs={{24,0},{25,1},{26,2},{27,3},{28,4},{29,5},{30,6},{31,7}} | collective-permute-start | bytes 258056 | tf_op jit(solution)/shard_map/ppermute | solution.py:46
  821.0 90.1 %collective-permute-start.94 = (bf16[1,176,2048]{2,1,0:T(8,128)(2,1)}, bf16[1,176,2048]{2,1,0:T(8,128)(2,1)}, u32[]{:S(2)}, u32[]{:S(2)}) collective-permute-start(bf16[1,176,2048]{2,1,0:T(8,128)(2,1)} %get-tuple-element.118), channel_id=1, source_target_pairs={{0,8},{1,9},{2,10},{3,11},{4,12},{5,13},{6,14},{7,15},{8,16},{9,17... | collective-permute-start | bytes 2162696 | tf_op jit(solution)/shard_map/ppermute | solution.py:46
  835.6 98.8 %collective-permute-start.95 = (bf16[1,176,2048]{2,1,0:T(8,128)(2,1)}, bf16[1,176,2048]{2,1,0:T(8,128)(2,1)}, u32[]{:S(2)}, u32[]{:S(2)}) collective-permute-start(bf16[1,176,2048]{2,1,0:T(8,128)(2,1)} %get-tuple-element.120), channel_id=1, source_target_pairs={{0,16},{1,17},{2,18},{3,19},{4,20},{5,21},{6,22},{7,23},{8,24},{9,... | collective-permute-start | bytes 2162696 | tf_op jit(solution)/shard_map/ppermute | solution.py:46
  850.7 83.6 %collective-permute-start.96 = (bf16[1,176,2048]{2,1,0:T(8,128)(2,1)S(1)}, bf16[1,176,2048]{2,1,0:T(8,128)(2,1)}, u32[]{:S(2)}, u32[]{:S(2)}) collective-permute-start(bf16[1,176,2048]{2,1,0:T(8,128)(2,1)S(1)} %get-tuple-element.119), channel_id=1, source_target_pairs={{0,24},{1,25},{2,26},{3,27},{4,28},{5,29},{6,30},{7,31},{8,0},{9,1... | collective-permute-start | bytes 2162696 | tf_op jit(solution)/shard_map/ppermute | solution.py:46
  888.0 76.2 %collective-permute-start.84 = (bf16[8,128,1024]{2,1,0:T(8,128)(2,1)S(1)}, bf16[8,128,1024]{2,1,0:T(8,128)(2,1)}, u32[]{:S(2)}, u32[]{:S(2)}) collective-permute-start(bf16[8,128,1024]{2,1,0:T(8,128)(2,1)S(1)} %bitcast.311), channel_id=1, source_target_pairs={{0,2},{1,3},{2,0},{3,1},{4,6},{5,7},{6,4},{7,5},{8,10},{9,11},{10,... | collective-permute-start | bytes 6291464 | tf_op jit(solution)/shard_map/ppermute | solution.py:46
  896.1 41.8 %collective-permute-start.76 = (bf16[8,128,640]{2,1,0:T(8,128)(2,1)}, bf16[8,128,640]{2,1,0:T(8,128)(2,1)}, u32[]{:S(2)}, u32[]{:S(2)}) collective-permute-start(bf16[8,128,640]{2,1,0:T(8,128)(2,1)} %bitcast.317), channel_id=1, source_target_pairs={{0,4},{1,5},{2,6},{3,7},{4,0},{5,1},{6,2},{7,3},{8,12},{9,13},{10,... | collective-permute-start | bytes 3932168 | tf_op jit(solution)/shard_map/ppermute | solution.py:46
  911.2 49.9 %collective-permute-start.71 = (bf16[8,128,640]{2,1,0:T(8,128)(2,1)}, bf16[8,128,640]{2,1,0:T(8,128)(2,1)}, u32[]{:S(2)}, u32[]{:S(2)}) collective-permute-start(bf16[8,128,640]{2,1,0:T(8,128)(2,1)} %bitcast.318), channel_id=1, source_target_pairs={{0,2},{1,3},{2,0},{3,1},{4,6},{5,7},{6,4},{7,5},{8,10},{9,11},{10,... | collective-permute-start | bytes 3932168 | tf_op jit(solution)/shard_map/ppermute | solution.py:46
  934.4 43.9 %collective-permute-start.64 = (bf16[512,2048]{1,0:T(8,128)(2,1)}, bf16[512,2048]{1,0:T(8,128)(2,1)S(1)}, u32[]{:S(2)}, u32[]{:S(2)}) collective-permute-start(bf16[512,2048]{1,0:T(8,128)(2,1)} %convolution_convert_fusion.1), channel_id=1, source_target_pairs={{0,1},{1,0},{2,3},{3,2},{4,5},{5,4},{6,7},{7,6},{8,9},{9,8},{10,11... | collective-permute-start | bytes 6291464 | tf_op jit(solution)/shard_map/ppermute | solution.py:36
  939.8 29.0 %collective-permute-start.77 = (bf16[4,128,640]{2,1,0:T(8,128)(2,1)S(1)}, bf16[4,128,640]{2,1,0:T(8,128)(2,1)S(1)}, u32[]{:S(2)}, u32[]{:S(2)}) collective-permute-start(bf16[4,128,640]{2,1,0:T(8,128)(2,1)S(1)} %fusion.26), channel_id=1, source_target_pairs={{0,2},{1,3},{2,0},{3,1},{4,6},{5,7},{6,4},{7,5},{8,10},{9,11},{10,... | collective-permute-start | bytes 1966088 | tf_op jit(solution)/shard_map/ppermute | solution.py:46
  968.0 47.9 %collective-permute-start.85 = (bf16[4,128,1024]{2,1,0:T(8,128)(2,1)}, bf16[4,128,1024]{2,1,0:T(8,128)(2,1)S(1)}, u32[]{:S(2)}, u32[]{:S(2)}) collective-permute-start(bf16[4,128,1024]{2,1,0:T(8,128)(2,1)} %fusion.24), channel_id=1, source_target_pairs={{0,4},{1,5},{2,6},{3,7},{4,0},{5,1},{6,2},{7,3},{8,12},{9,13},{10,... | collective-permute-start | bytes 3145736 | tf_op jit(solution)/shard_map/ppermute | solution.py:46
  969.1 17.7 %collective-permute-start.78 = (bf16[1,128,640]{2,1,0:T(8,128)(2,1)S(1)}, bf16[1,128,640]{2,1,0:T(8,128)(2,1)}, u32[]{:S(2)}, u32[]{:S(2)}) collective-permute-start(bf16[1,128,640]{2,1,0:T(8,128)(2,1)S(1)} %get-tuple-element.147), channel_id=1, source_target_pairs={{0,8},{1,9},{2,10},{3,11},{4,12},{5,13},{6,14},{7,15},{8,16},{9,17... | collective-permute-start | bytes 491528 | tf_op jit(solution)/shard_map/ppermute | solution.py:46
  970.9 17.1 %collective-permute-start.79 = (bf16[1,128,640]{2,1,0:T(8,128)(2,1)S(1)}, bf16[1,128,640]{2,1,0:T(8,128)(2,1)}, u32[]{:S(2)}, u32[]{:S(2)}) collective-permute-start(bf16[1,128,640]{2,1,0:T(8,128)(2,1)S(1)} %get-tuple-element.149), channel_id=1, source_target_pairs={{0,16},{1,17},{2,18},{3,19},{4,20},{5,21},{6,22},{7,23},{8,24},{9,... | collective-permute-start | bytes 491528 | tf_op jit(solution)/shard_map/ppermute | solution.py:46
  974.2 16.6 %collective-permute-start.80 = (bf16[1,128,640]{2,1,0:T(8,128)(2,1)S(1)}, bf16[1,128,640]{2,1,0:T(8,128)(2,1)}, u32[]{:S(2)}, u32[]{:S(2)}) collective-permute-start(bf16[1,128,640]{2,1,0:T(8,128)(2,1)S(1)} %get-tuple-element.148), channel_id=1, source_target_pairs={{0,24},{1,25},{2,26},{3,27},{4,28},{5,29},{6,30},{7,31},{8,0},{9,1... | collective-permute-start | bytes 491528 | tf_op jit(solution)/shard_map/ppermute | solution.py:46
  988.0 17.7 %collective-permute-start.75 = (bf16[1,128,640]{2,1,0:T(8,128)(2,1)S(1)}, bf16[1,128,640]{2,1,0:T(8,128)(2,1)S(1)}, u32[]{:S(2)}, u32[]{:S(2)}) collective-permute-start(bf16[1,128,640]{2,1,0:T(8,128)(2,1)S(1)} %get-tuple-element.151), channel_id=1, source_target_pairs={{0,24},{1,25},{2,26},{3,27},{4,28},{5,29},{6,30},{7,31},{8,0},{9,1... | collective-permute-start | bytes 491528 | tf_op jit(solution)/shard_map/ppermute | solution.py:46
  1005.8 17.1 %collective-permute-start.81 = (f32[64,1280]{1,0:T(8,128)S(1)}, f32[64,1280]{1,0:T(8,128)S(1)}, u32[]{:S(2)}, u32[]{:S(2)}) collective-permute-start(f32[64,1280]{1,0:T(8,128)S(1)} %get-tuple-element.145), channel_id=1, source_target_pairs={{0,1},{1,0},{2,3},{3,2},{4,5},{5,4},{6,7},{7,6},{8,9},{9,8},{10,11... | collective-permute-start | bytes 983048 | tf_op jit(solution)/shard_map/ppermute | solution.py:36
  1018.0 18.7 %collective-permute-start.87 = (bf16[1,128,1024]{2,1,0:T(8,128)(2,1)S(1)}, bf16[1,128,1024]{2,1,0:T(8,128)(2,1)S(1)}, u32[]{:S(2)}, u32[]{:S(2)}) collective-permute-start(bf16[1,128,1024]{2,1,0:T(8,128)(2,1)S(1)} %get-tuple-element.136), channel_id=1, source_target_pairs={{0,16},{1,17},{2,18},{3,19},{4,20},{5,21},{6,22},{7,23},{8,24},{9,... | collective-permute-start | bytes 786440 | tf_op jit(solution)/shard_map/ppermute | solution.py:46
  (90 other events, 1093.5 us)
Sparse Core Ops, SparseCore 0:
  68.2 234.2 all-gather.1
  623.6 267.1 reduce-scatter.1

commit v3 on v2

v3 whole, which is shorter than its diff:
```python
import jax
import jax.numpy as jnp
import numpy as np
from jax import lax
from jax.experimental import pallas as pl
from jax.experimental.pallas import tpu as pltpu
from jax.sharding import PartitionSpec as P

QK = 16
PAIR = 8
FEATS = 160
ROWS = 168
VMEM = 56 * 1024 * 1024
eps = 1e-06
f32 = jnp.float32
bf16 = jnp.bfloat16


def bits_from(n, low):
    bits = []
    while low < n:
        bits.insert(0, low)
        low *= 2
    return bits


def flip(x, bits):
    n = lax.axis_size("tok")
    return lax.ppermute(x, "tok", [(i, i ^ bits) for i in range(n)])


def side(bit):
    return (lax.axis_index("tok") // bit) % 2


def pick(x, index, axis=0):
    return lax.dynamic_index_in_dim(x, index, axis, False)


def assemble(pieces):
    out = jnp.broadcast_to(pieces[0][1][None], (len(pieces),) + pieces[0][1].shape)
    for index, block in pieces[1:]:
        out = lax.dynamic_update_index_in_dim(out, block, index, 0)
    return out


def assemble_all(pieces):
    out = jnp.zeros((len(pieces),) + pieces[0][1].shape, pieces[0][1].dtype)
    for index, block in pieces:
        out = lax.dynamic_update_index_in_dim(out, block, index, 0)
    return out


def after(x, *others):
    return lax.optimization_barrier((x,) + others)[0] if others else x


def move(x, bits, start=(), stop=()):
    return after(flip(after(x, *start), bits), *stop)


def grow(x, bit, start=(), stop=()):
    return assemble([(side(bit), x), (1 - side(bit), move(x, bit, start, stop))])


def in_order(x, bits):
    done = bits[::-1]
    axes = [done.index(b) for b in sorted(done, reverse=True)]
    x = x.transpose(axes + list(range(len(done), x.ndim)))
    return x.reshape((-1,) + x.shape[len(done) :])


def grown(bits):
    at = [0]
    for bit in bits[::-1]:
        at = [i + j for i in at for j in (0, bit)]
    return at


class Scatter:
    def __init__(self, make, bits):
        self.make, self.bits, self.bit = make, bits, bits[-1]

    def send(self, *start):
        self.sent = after(self.make(1 - side(self.bit)), *start)
        self.here = flip(self.sent, self.bit)

    def keep(self, *gate):
        self.kept = self.make(after(side(self.bit), *gate))
        return self.kept

    def hold(self, x, *gate):
        x, self.here = lax.optimization_barrier((x, after(self.here, *gate)))
        return x

    def step(self, *gate):
        acc = self.kept.astype(f32) + after(self.here, *gate).astype(f32)
        self.bits = self.bits[:-1]
        if not self.bits:
            return acc[0]
        bit = self.bits[-1]
        acc = acc.reshape((-1, 2) + acc.shape[1:])
        self.sent = pick(acc, 1 - side(bit), 1).astype(bf16)
        self.kept = pick(acc, side(bit), 1)
        self.here = flip(self.sent, bit)
        return self.sent

    def finish(self, *gate):
        while len(self.bits) > 1:
            self.step(*gate)
        return self.step(*gate)


MESH = pl.DeviceIdType.MESH
INV = pl.BlockSpec(memory_space=pltpu.VMEM)


def across(me, bits):
    for bit in (1, 2, 4, 8, 16):
        if bits & bit:
            me = me + bit - 2 * bit * ((me // bit) % 2)
    return me


def meet(me, partners):
    barrier = pltpu.get_barrier_semaphore()
    for bits in partners:
        pl.semaphore_signal(barrier, inc=1, device_id=(across(me, bits),), device_id_type=MESH)
    pl.semaphore_wait(barrier, len(partners))


class Mail:
    def __init__(self, me, sems):
        self.me, self.sems, self.count, self.open = me, sems, 0, []
    def send(self, source, target, bits):
        at = self.count
        self.count += 1
        copy = pltpu.make_async_remote_copy(src_ref=source, dst_ref=target, send_sem=self.sems.at[0, at],
            recv_sem=self.sems.at[1, at], device_id=(across(self.me, bits),), device_id_type=MESH)
        copy.start()
        self.open.append(copy)
        return copy
    def local(self, source, target):
        at = self.count
        self.count += 1
        copy = pltpu.make_async_copy(source, target, self.sems.at[0, at])
        copy.start()
        return copy
    def close(self):
        for copy in self.open:
            copy.wait_send()


def first_body(gains_in, gate_in, up_in, mine, theirs, gains, gate, up, z4, chip, sems):
    me = lax.axis_index("tok")
    core, z = me % 2, me // 8
    meet(me, (1, 2, 4, 8, 9, 16))
    mail = Mail(me, sems)
    size = mine.shape[0]
    swap = mail.send(theirs, chip.at[pl.ds(core * size, size)], 1)
    own = mail.local(mine, chip.at[pl.ds(core * size, size)])
    gains[pl.ds(me, 1)] = gains_in[...]

    def member(d):
        return ((d // 8) % 2) * 2 + d % 2

    to_gate = [mail.send(gate_in.at[member(across(me, k))], gate.at[member(me)], k) for k in (9, 8, 1)]
    own.wait()
    swap.wait_recv()
    high = mail.send(chip, z4.at[z], 16)
    low = mail.send(chip, z4.at[z], 8)
    to_up = [mail.send(up_in.at[member(across(me, k))], up.at[member(me)], k) for k in (9, 8, 1)]
    kept = [
        mail.local(chip, z4.at[z]),
        mail.local(gate_in.at[member(me)], gate.at[member(me)]),
        mail.local(up_in.at[member(me)], up.at[member(me)]),
    ]
    for bit in (1, 2, 4):
        at = pl.ds((me // bit) * bit, bit)
        mail.send(gains.at[at], gains.at[at], bit).wait_recv()
    high.wait_recv()
    zh = across(me, 16) // 8
    low2 = mail.send(z4.at[zh], z4.at[zh], 8)
    for bit in (8, 16):
        at = pl.ds((me // bit) * bit, bit)
        mail.send(gains.at[at], gains.at[at], bit).wait_recv()
    for c in to_gate + to_up + [low, low2]:
        c.wait_recv()
    for c in kept:
        c.wait()
    mail.close()


def spread_first(gains, gate, up, mine, theirs):
    rows, cols = mine.shape
    return pl.pallas_call(
        first_body,
        out_shape=[
            jax.ShapeDtypeStruct((32,) + gains.shape[1:], f32),
            jax.ShapeDtypeStruct(gate.shape, bf16),
            jax.ShapeDtypeStruct(up.shape, bf16),
            jax.ShapeDtypeStruct((4, 2 * rows, cols), bf16),
        ],
        in_specs=[INV] * 5,
        out_specs=[INV] * 4,
        scratch_shapes=[pltpu.VMEM((2 * rows, cols), bf16), pltpu.SemaphoreType.DMA((2, 20))],
        compiler_params=pltpu.CompilerParams(collective_id=1, has_side_effects=True, vmem_limit_bytes=40 * 2**20),
    )(gains, gate, up, mine, theirs)


def second_body(z4, out_mine, out_theirs, gate, whole, out4, gate2, chip, sems):
    me = lax.axis_index("tok")
    core, z, place = me % 2, me // 8, (me // 2) % 4
    across_y, across_x = across(place, 2), across(place, 1)
    meet(me, (1, 2, 4, 8, 16))
    mail = Mail(me, sems)
    size, cut = out_mine.shape[0], z4.shape[2] // 2
    a, b = pl.ds(0, cut), pl.ds(cut, cut)
    ya = mail.send(z4.at[:, :, a], whole.at[:, place, :, a], 4)
    xb = mail.send(z4.at[:, :, b], whole.at[:, place, :, b], 2)
    swap = mail.send(out_theirs, chip.at[pl.ds(core * size, size)], 1)
    own = mail.local(out_mine, chip.at[pl.ds(core * size, size)])
    kept = [mail.local(z4, whole.at[:, place]), mail.local(gate, gate2.at[z // 2])]
    xa = mail.send(z4.at[:, :, a], whole.at[:, place, :, a], 2)
    yb = mail.send(z4.at[:, :, b], whole.at[:, place, :, b], 4)
    own.wait()
    swap.wait_recv()
    high = mail.send(chip, out4.at[z], 16)
    low = mail.send(chip, out4.at[z], 8)
    kept.append(mail.local(chip, out4.at[z]))
    gate_high = mail.send(gate, gate2.at[z // 2], 16)
    ya.wait_recv()
    xa2 = mail.send(whole.at[:, across_y, :, a], whole.at[:, across_y, :, a], 2)
    xb.wait_recv()
    yb2 = mail.send(whole.at[:, across_x, :, b], whole.at[:, across_x, :, b], 4)
    high.wait_recv()
    zh = across(me, 16) // 8
    low2 = mail.send(out4.at[zh], out4.at[zh], 8)
    for c in (xa, yb, xa2, yb2, low, low2, gate_high):
        c.wait_recv()
    for c in kept:
        c.wait()
    mail.close()


def spread_second(z4, out_mine, out_theirs, gate):
    rows, cols = out_mine.shape
    return pl.pallas_call(
        second_body,
        out_shape=[
            jax.ShapeDtypeStruct((4, 4) + z4.shape[1:], bf16),
            jax.ShapeDtypeStruct((4, 2 * rows, cols), bf16),
            jax.ShapeDtypeStruct((2,) + gate.shape, bf16),
        ],
        in_specs=[INV] * 4,
        out_specs=[INV] * 3,
        scratch_shapes=[pltpu.VMEM((2 * rows, cols), bf16), pltpu.SemaphoreType.DMA((2, 16))],
        compiler_params=pltpu.CompilerParams(collective_id=2, has_side_effects=True, vmem_limit_bytes=40 * 2**20),
    )(z4, out_mine, out_theirs, gate)


def scan_body(sign, s_ref, o_ref, stage, here, whole, zhere, back, bhere, sems):
    me = lax.axis_index("tok")
    z, plane = me // 8, (me // 2) % 4
    barrier = pltpu.get_barrier_semaphore()
    for k in (1, 2, 3):
        for to in (across(me, 2 * k), lax.rem(me + 8 * k, 32)):
            pl.semaphore_signal(barrier, inc=1, device_id=(to,), device_id_type=MESH)
    pl.semaphore_wait(barrier, 6)

    def slot(k):
        return (across(me, 2 * k) // 2) % 4

    def copy(source, target, sem, i, to):
        return pltpu.make_async_remote_copy(
            src_ref=source,
            dst_ref=target,
            send_sem=sems.at[sem, 0, i],
            recv_sem=sems.at[sem, 1, i],
            device_id=(to,),
            device_id_type=MESH,
        )

    def receives(k):
        return z - k >= 0 if sign > 0 else z + k < 4

    def sends(k):
        return z + k < 4 if sign > 0 else z - k >= 0

    copies = []
    for k in (3, 1, 2):
        stage[k - 1] = s_ref[pl.ds(2 * slot(k), 2)].astype(stage.dtype)
        copies.append(copy(stage.at[k - 1], here.at[k - 1], 0, k - 1, across(me, 2 * k)))
        copies[-1].start()
    mine = [s_ref[pl.ds(2 * plane, 2)]]
    for c in copies:
        c.wait()
    mine += [here[k - 1].astype(f32) for k in (1, 2, 3)]
    whole[...] = sum(mine).astype(whole.dtype)
    for k in (2, 1, 3):

        @pl.when(sends(k))
        def _(k=k):
            copy(whole, zhere.at[k - 1], 1, k - 1, me + 8 * k * sign).start()

    for k in (1, 2, 3):

        @pl.when(receives(k))
        def _(k=k):
            copy(whole, zhere.at[k - 1], 1, k - 1, me).wait_recv()

        @pl.when(jnp.logical_not(receives(k)))
        def _(k=k):
            zhere[k - 1] = jnp.zeros_like(whole)

    for k in (1, 2, 3):

        @pl.when(sends(k))
        def _(k=k):
            copy(whole, zhere.at[k - 1], 1, k - 1, me).wait_send()

    beyond = sum(zhere[k].astype(f32) for k in range(3))
    copies = []
    for k in (3, 1, 2, 0):
        before = beyond
        for j in range(4):
            if j != k:
                before = before + (sign * (slot(k) - slot(j)) > 0).astype(f32) * mine[j]
        if k == 0:
            o_ref[pl.ds(2 * plane, 2)] = before
        else:
            back[k - 1] = before.astype(back.dtype)
            copies.append(copy(back.at[k - 1], bhere.at[k - 1], 2, k - 1, across(me, 2 * k)))
            copies[-1].start()
    for c in copies:
        c.wait()
    for k in (1, 2, 3):
        o_ref[pl.ds(2 * slot(k), 2)] = bhere[k - 1].astype(f32)


def spans_of(cols, most=512):
    return [(s, min(most, cols - s)) for s in range(0, cols, most)]


def ffn_body(order, sides, x_ref, g_ref, *refs):
    gates, ups, down = refs[0:4], refs[4:8], refs[8]
    y_ref, act_ref, d_ref, dh_ref, w_gate_up, w_down, sem = refs[9:]
    cols = w_down.shape[0]

    @pl.when(pl.program_id(0) == 0)
    def _():
        copies = [pltpu.make_async_copy(down, w_down, sem.at[0])]
        size = gates[0].shape[1]
        for j, pieces in enumerate((gates, ups)):
            for k, piece in enumerate(pieces):
                for i, at in enumerate(order):
                    rows = pl.ds(pl.multiple_of((at + sides[k]) * size, 16), size)
                    target = w_gate_up.at[rows, pl.ds(j * cols, cols)]
                    copies.append(pltpu.make_async_copy(piece.at[i], target, sem.at[len(copies)]))
        for copy in copies:
            copy.start()
        for copy in copies:
            copy.wait()

    x, g = x_ref[...], g_ref[...]
    for s, w in spans_of(cols):
        gate, upper = dot(x, w_gate_up[:, s : s + w]), dot(x, w_gate_up[:, cols + s : cols + s + w])
        d_act = dot_cols(g, w_down[s : s + w, :])
        sigma = jax.nn.sigmoid(gate)
        smooth = gate * sigma
        act_ref[:, s : s + w] = (smooth * upper).astype(bf16)
        d_ref[:, s : s + w] = (d_act * upper * sigma * (1.0 + gate * (1.0 - sigma))).astype(bf16)
        d_ref[:, cols + s : cols + s + w] = (d_act * smooth).astype(bf16)
    y_ref[...] = dot(act_ref[...], w_down[...]).astype(bf16)
    dh_ref[...] = dot_cols(d_ref[...], w_gate_up[...]).astype(bf16)


def ffn(x, g, gate, up, down, order, sides, tile=256):
    tokens, width = x.shape
    cols = down.shape[0]

    def block(w):
        return pl.BlockSpec((tile, w), lambda i: (i, 0))

    return pl.pallas_call(
        lambda *refs: ffn_body(order, *refs),
        out_shape=[jax.ShapeDtypeStruct((tokens, w), bf16) for w in (width, cols, 2 * cols, width)],
        grid=(tokens // tile,),
        in_specs=[pl.BlockSpec(memory_space=pltpu.SMEM), block(width), block(width)] + [pl.BlockSpec(memory_space=pl.ANY)] * 9,
        out_specs=[block(width), block(cols), block(2 * cols), block(width)],
        scratch_shapes=[
            pltpu.VMEM((width, 2 * cols), bf16),
            pltpu.VMEM((cols, width), bf16),
            pltpu.SemaphoreType.DMA((8 * len(order) + 1,)),
        ],
        compiler_params=pltpu.CompilerParams(vmem_limit_bytes=VMEM),
        cost_estimate=pl.CostEstimate(flops=0, bytes_accessed=0, transcendentals=0),
    )(sides, x, g, *gate, *up, down)


def product_body(count, index, *refs):
    left, right, out = refs[:count], refs[count : 2 * count], refs[2 * count]
    out[...] = sum(dot_rows(a[...], b[...]) for a, b in zip(left, right)).astype(out.dtype)


def row_blocks(left, right, index, size, half=None):
    count = index.shape[0]
    cols = right[0].shape[1] // (1 if half is None else 2)
    at_col = half or 0
    tokens = sum(a.shape[0] for a in left)
    return pl.pallas_call(
        lambda *refs: product_body(len(left), *refs),
        out_shape=jax.ShapeDtypeStruct((count * size, cols), bf16),
        grid_spec=pltpu.PrefetchScalarGridSpec(
            num_scalar_prefetch=1,
            grid=(count,),
            in_specs=[pl.BlockSpec((a.shape[0], size), lambda i, at: (0, at[i])) for a in left]
            + [pl.BlockSpec((b.shape[0], cols), lambda i, at: (0, at_col)) for b in right],
            out_specs=pl.BlockSpec((size, cols), lambda i, at: (i, 0)),
        ),
        compiler_params=pltpu.CompilerParams(vmem_limit_bytes=VMEM),
        cost_estimate=pl.CostEstimate(flops=0, bytes_accessed=0, transcendentals=0),
    )(index, x, g, gate_up, *down)


def product_body(count, index, *refs):
    left, right, out = refs[:count], refs[count : 2 * count], refs[2 * count]
    out[...] = sum(dot_rows(a[...], b[...]) for a, b in zip(left, right)).astype(out.dtype)


def row_blocks(left, right, index, size, half=None):
    count = index.shape[0]
    cols = right[0].shape[1] // (1 if half is None else 2)
    at_col = half or 0
    tokens = sum(a.shape[0] for a in left)
    return pl.pallas_call(
        lambda *refs: product_body(len(left), *refs),
        out_shape=jax.ShapeDtypeStruct((count * size, cols), bf16),
        grid_spec=pltpu.PrefetchScalarGridSpec(
            num_scalar_prefetch=1,
            grid=(count,),
            in_specs=[pl.BlockSpec((a.shape[0], size), lambda i, at: (0, at[i])) for a in left]
            + [pl.BlockSpec((b.shape[0], cols), lambda i, at: (0, at_col)) for b in right],
            out_specs=pl.BlockSpec((size, cols), lambda i, at: (i, 0)),
        ),
        compiler_params=pltpu.CompilerParams(vmem_limit_bytes=VMEM),
        cost_estimate=pl.CostEstimate(
            flops=2 * tokens * count * size * cols,
            bytes_accessed=2 * (tokens * cols + count * size * (tokens + cols)),
            transcendentals=0,
        ),
    )(index.astype(jnp.int32), *left, *right)


def part_maker(left, right, bits, within=(0,), half=None):
    n = lax.axis_size("tok")
    size = left[0].shape[1] * 2 // n
    cols = right[0].shape[1] // (1 if half is None else 2)
    ids = np.asarray([(at + more) // 2 for at in grown(bits[:-1][::-1]) for more in within], np.int32)

    def make(index):
        index = jnp.asarray(ids) + index * (bits[-1] // 2)
        if size % 128 == 0:
            out = row_blocks(left, right, index, size, half)
        else:
            out = sum(dot_rows(a, b) for a, b in zip(left, right)).astype(bf16).reshape(n // 2, size, -1)
            out = out[index][..., (half or 0) * cols : (half or 0) * cols + cols]
        return out.reshape(-1, size * len(within), cols)

    return make


def feature_tables(heads):
    pairs = [(a, b) for a in range(QK + 1) for b in range(a, QK + 1)]
    one = np.zeros((heads, heads * QK, FEATS), np.float32)
    two = np.zeros((heads, heads * QK, FEATS), np.float32)
    rows = np.zeros((8, FEATS), np.float32)
    for f, (a, b) in enumerate(pairs):
        for h in range(heads):
            if a < QK:
                one[h, h * QK + a, f] = 1
            if b < QK:
                two[h, h * QK + b, f] = 1
        rows[0, f] = a == QK
        rows[1, f] = b == QK
        if a == QK:
            rows[2, f] = 1.0
        elif b == QK:
            rows[2, f] = QK**-0.5
        else:
            rows[2, f] = (0.5 if a == b else 1.0) / QK
    return jnp.asarray(one, bf16), jnp.asarray(two, bf16), jnp.asarray(rows)


def dot(a, b):
    return lax.dot_general(a, b, (((1,), (0,)), ((), ())), preferred_element_type=f32)


def dot_rows(a, b):
    return lax.dot_general(a, b, (((0,), (0,)), ((), ())), preferred_element_type=f32)


def dot_cols(a, b):
    return lax.dot_general(a, b, (((1,), (1,)), ((), ())), preferred_element_type=f32)


def halves(x):
    high = x.astype(bf16)
    return high, (x - high.astype(f32)).astype(bf16)


def features(x, one, two, rows):
    return dot(x, one) + rows[0:1], dot(x, two) + rows[1:2]


def total_row(state):
    return jnp.concatenate([state[FEATS : FEATS + 1], state[FEATS + 1 : FEATS + 2, : FEATS - 128]], axis=1)


def store_state(ref, state, row):
    ref[0, 0, :FEATS, :] = state
    ref[0, 0, FEATS:, :] = jnp.zeros((ROWS - FEATS, state.shape[1]), f32)
    ref[0, 0, FEATS : FEATS + 1, :] = row[:, :128]
    ref[0, 0, FEATS + 1 : FEATS + 2, : FEATS - 128] = row[:, 128:]


def kept_rows(scal, tile, tokens):
    index = lax.broadcasted_iota(jnp.int32, (tokens, 1), 0) + tile * tokens
    return index >= scal[tile]


def state_body(scal, k_ref, v_ref, one, two, rows, out_ref):
    tile = pl.program_id(0)
    a, b = features(k_ref[...], one[0], two[0], rows)
    phi = jnp.where(kept_rows(scal, tile, a.shape[0]), a * b, 0.0)
    high, low = halves(phi)
    v = v_ref[...]
    store_state(out_ref, dot_rows(high, v) + dot_rows(low, v), jnp.sum(phi, axis=0, keepdims=True))


def weights(q_ref, k_ref, lo_ref, tile, head):
    tokens, lanes = q_ref.shape
    lane = lax.broadcasted_iota(jnp.int32, (tokens, lanes), 1) // QK == head
    q = jnp.where(lane, q_ref[...], jnp.zeros((), bf16))
    score = dot_cols(q, k_ref[...]) * QK**-0.5
    row = lax.broadcasted_iota(jnp.int32, score.shape, 0)
    col = lax.broadcasted_iota(jnp.int32, score.shape, 1)
    lo = lo_ref[...] - tile * tokens
    mask = (col <= row) & (col >= lo)
    weight = jnp.where(mask, 1.0 + score + 0.5 * score * score, 0.0)
    return lane, score, mask, weight, lo < 0


def forward_body(q_ref, k_ref, v_ref, lo_ref, carry_ref, one, two, rows, y_ref, mixed_ref):
    tile, head = pl.program_id(0), pl.program_id(1)
    _, _, _, weight, alive = weights(q_ref, k_ref, lo_ref, tile, head)
    a, b = features(q_ref[...], one[0], two[0], rows)
    phi = jnp.where(alive, a * b * rows[2:3], 0.0)
    high, low = halves(phi)
    carry = carry_ref[0, 0]
    s_high, s_low = halves(carry[:FEATS])
    numer = dot(weight.astype(bf16), v_ref[...])
    numer = numer + (dot(high, s_high) + dot(high, s_low) + dot(low, s_high))
    denom = jnp.sum(weight, axis=1, keepdims=True) + jnp.sum(phi * total_row(carry), axis=1, keepdims=True)
    y = numer / denom
    y_ref[...] = y
    mixed_ref[...] = y.astype(bf16)


def spread(t, a, b, one, two):
    first_high, first_low = halves(t * b)
    second_high, second_low = halves(t * a)
    return (
        dot_cols(first_high, one) + dot_cols(first_low, one) + dot_cols(second_high, two) + dot_cols(second_low, two)
    )


def backward_body(
    q_ref, k_ref, v_ref, lo_ref, carry_ref, one, two, rows, y_ref, d_ref, dq_ref, dk_ref, dv_ref, ds_ref, dq_acc, dk_acc
):
    tile, head = pl.program_id(0), pl.program_id(1)
    lane, score, mask, weight, alive = weights(q_ref, k_ref, lo_ref, tile, head)
    a, b = features(q_ref[...], one[0], two[0], rows)
    phi = jnp.where(alive, a * b * rows[2:3], 0.0)
    high, low = halves(phi)
    carry = carry_ref[0, 0]
    s_high, s_low = halves(carry[:FEATS])
    row = total_row(carry)
    denom = jnp.sum(weight, axis=1, keepdims=True) + jnp.sum(phi * row, axis=1, keepdims=True)
    d = d_ref[...].astype(f32)
    g = d / denom
    c = -jnp.sum(d * y_ref[...], axis=1, keepdims=True) / denom
    g_high, g_low = halves(g)
    v = v_ref[...]
    dk = dot_cols(g_high, v) + dot_cols(g_low, v) + c
    ds = jnp.where(mask, dk * (1.0 + score) * QK**-0.5, 0.0).astype(bf16)
    dv_ref[...] = dot_rows(weight.astype(bf16), g_high)
    dphi = dot_cols(g_high, s_high) + dot_cols(g_high, s_low) + dot_cols(g_low, s_high) + c * row
    t = jnp.where(alive, dphi * rows[2:3], 0.0)
    dq = jnp.where(lane, dot(ds, k_ref[...]), 0.0) + spread(t, a, b, one[0], two[0])
    dkeys = jnp.where(lane, dot_rows(ds, q_ref[...]), 0.0)

    @pl.when(head == 0)
    def _():
        dq_acc[...] = dq
        dk_acc[...] = dkeys

    @pl.when(head > 0)
    def _():
        dq_acc[...] += dq
        dk_acc[...] += dkeys

    @pl.when(head == pl.num_programs(1) - 1)
    def _():
        dq_ref[...] = dq_acc[...].astype(bf16)
        dk_ref[...] = dk_acc[...]

    state = dot_rows(high, g_high) + dot_rows(high, g_low) + dot_rows(low, g_high)
    store_state(ds_ref, state, jnp.sum(phi * c, axis=0, keepdims=True))


def carried_body(scal, k_ref, v_ref, one, two, rows, grad_ref, dk_in, dv_in, dk_ref, dv_ref, acc):
    tile, head = pl.program_id(0), pl.program_id(1)
    a, b = features(k_ref[...], one[0], two[0], rows)
    keep = kept_rows(scal, tile, a.shape[0])
    high, low = halves(jnp.where(keep, a * b, 0.0))
    grad = grad_ref[0, 0]
    g_high, g_low = halves(grad[:FEATS])
    v = v_ref[...]
    dv = dv_in[...] + dot(high, g_high) + dot(high, g_low) + dot(low, g_high)
    dv_ref[...] = dv.astype(bf16)
    t = jnp.where(keep, dot_cols(v, g_high) + dot_cols(v, g_low) + total_row(grad), 0.0)
    dk = spread(t, a, b, one[0], two[0])

    @pl.when(head == 0)
    def _():
        acc[...] = dk_in[...] + dk

    @pl.when(head > 0)
    def _():
        acc[...] += dk

    @pl.when(head == pl.num_programs(1) - 1)
    def _():
        dk_ref[...] = acc[...].astype(bf16)


class Attention:
    def __init__(self, qkv, lo, heads, tokens):
        self.qkv, self.heads, self.tokens = qkv, heads, tokens
        self.lo = lo[:, None]
        self.scal = jnp.stack([lo[tokens - 1], lo[2 * tokens - 1]])
        self.tables = feature_tables(heads)
        lanes = heads * QK
        self.value = (qkv.shape[1] - 2 * lanes) // heads
        skip = 2 * lanes // self.value
        self.q = pl.BlockSpec((tokens, lanes), lambda t, h: (t, 0))
        self.k = pl.BlockSpec((tokens, lanes), lambda t, h: (t, 1))
        self.v = pl.BlockSpec((tokens, self.value), lambda t, h: (t, h + skip))
        self.o = pl.BlockSpec((tokens, self.value), lambda t, h: (t, h))
        self.l = pl.BlockSpec((tokens, 1), lambda t, h: (t, 0))
        self.s = pl.BlockSpec((1, 1, ROWS, self.value), lambda t, h: (h, t, 0, 0))
        self.e = pl.BlockSpec((1, lanes, FEATS), lambda t, h: (h, 0, 0))
        self.r = pl.BlockSpec((8, FEATS), lambda t, h: (0, 0))
        self.m = pl.BlockSpec(memory_space=pltpu.SMEM)
        self.table_specs = [self.e, self.e, self.r]
        self.acc = pltpu.VMEM((tokens, lanes), f32)
        self.state_shape = jax.ShapeDtypeStruct((heads, 2, ROWS, self.value), f32)

    def wide(self, kind):
        return jax.ShapeDtypeStruct((2 * self.tokens, self.heads * self.value), kind)

    def narrow(self, kind):
        return jax.ShapeDtypeStruct((2 * self.tokens, self.heads * QK), kind)

    def call(self, body, ins, outs, shapes, scratch, flops, args):
        size = sum(int(np.prod(a.shape)) * a.dtype.itemsize for a in list(args) + list(shapes))
        return pl.pallas_call(
            body,
            grid=(2, self.heads),
            in_specs=ins,
            out_specs=outs,
            out_shape=shapes,
            scratch_shapes=scratch,
            compiler_params=pltpu.CompilerParams(vmem_limit_bytes=VMEM),
            cost_estimate=pl.CostEstimate(flops=0, bytes_accessed=0, transcendentals=0),
        )(*args)

    def states(self):
        (out,) = self.call(
            state_body,
            [self.m, self.k, self.v] + self.table_specs,
            [self.s],
            [self.state_shape],
            [],
            3 * 10**9,
            (self.scal, self.qkv, self.qkv, *self.tables),
        )
        return out

    def forward(self, carry):
        return self.call(
            forward_body,
            [self.q, self.k, self.v, self.l, self.s] + self.table_specs,
            [self.o, self.o],
            [self.wide(f32), self.wide(bf16)],
            [],
            10 * 10**9,
            (self.qkv, self.qkv, self.qkv, self.lo, carry, *self.tables),
        )

    def backward(self, carry, y, d_heads):
        return self.call(
            backward_body,
            [self.q, self.k, self.v, self.l, self.s] + self.table_specs + [self.o, self.o],
            [self.q, self.q, self.o, self.s],
            [self.narrow(bf16), self.narrow(f32), self.wide(f32), self.state_shape],
            [self.acc, self.acc],
            30 * 10**9,
            (self.qkv, self.qkv, self.qkv, self.lo, carry, *self.tables, y, d_heads),
        )

    def carried(self, grad, dk, dv):
        return self.call(
            carried_body,
            [self.m, self.k, self.v] + self.table_specs + [self.s, self.q, self.o],
            [self.q, self.o],
            [self.narrow(bf16), self.wide(bf16)],
            [self.acc],
            10 * 10**9,
            (self.scal, self.qkv, self.qkv, *self.tables, grad, dk, dv),
        )


def others(state, earlier, kind):
    n = lax.axis_size("tok")
    me = lax.axis_index("tok")
    sign = 1 if earlier else -1
    if n != 32:
        parts = lax.all_gather(state.astype(kind), "tok").astype(f32)
        index = jnp.arange(n)
        before = (sign * (me // 2 - index // 2) > 0) & (index % 2 == me % 2)
        out = jnp.sum(jnp.where(before.reshape((n,) + (1,) * state.ndim), parts, 0.0), axis=0)
        return out
    block = (state.shape[0] // 4,) + state.shape[1:]
    slots = pltpu.VMEM((3,) + block, kind)
    return pl.pallas_call(
        lambda *refs: scan_body(sign, *refs),
        out_shape=jax.ShapeDtypeStruct(state.shape, f32),
        in_specs=[INV],
        out_specs=INV,
        scratch_shapes=[slots, slots, pltpu.VMEM(block, kind), slots, slots, slots, pltpu.SemaphoreType.DMA((3, 2, 3))],
        compiler_params=pltpu.CompilerParams(
            collective_id=3 if earlier else 4, has_side_effects=True, vmem_limit_bytes=VMEM
        ),
        cost_estimate=pl.CostEstimate(flops=0, bytes_accessed=0, transcendentals=0),
    )(state)


def row_starts(positions, lengths, offsets):
    inside = (positions[:, None] >= offsets[None, :]) & (positions[:, None] < offsets[None, :] + lengths[None, :])
    return jnp.sum(jnp.where(inside, offsets[None, :], 0), axis=1)


def side_by_side(core, mine, theirs, axis=0):
    size = mine.shape[axis]
    shape = list(mine.shape)
    shape[axis] *= 2
    out = jnp.zeros(shape, mine.dtype)
    out = lax.dynamic_update_slice_in_dim(out, mine, core * size, axis)
    return lax.dynamic_update_slice_in_dim(out, theirs, (1 - core) * size, axis)


def shards(
    block_input,
    lengths,
    offsets,
    norm1_gain,
    w_query,
    w_key,
    w_value,
    w_out,
    norm2_gain,
    w_gate,
    w_up,
    w_down,
    out_grad,
):
    n = lax.axis_size("tok")
    me = lax.axis_index("tok")
    core, member = me % 2, side(PAIR) * 2 + me % 2
    cbits = bits_from(n, 2)
    qbits = [bit for bit in cbits if bit != PAIR]
    swapped = qbits[:-2] + [qbits[-1], qbits[-2]]
    chips, quads = n // 2, n // 4
    above, below = n // (2 * PAIR), PAIR // 2
    groups = [
        [i * 2 * PAIR + p * PAIR + j * 2 + c for i in range(above) for j in range(below)] for p in (0, 1) for c in (0, 1)
    ]
    to_member = {1: 1, 2: PAIR, 3: PAIR + 1}
    tokens, width = block_input.shape
    rows = w_query.shape[0]
    heads = w_query.shape[1] // QK // 2
    half = width // 2
    lanes = heads * QK
    def column_half(w, which):
        return lax.dynamic_slice_in_dim(w, which * (w.shape[1] // 2), w.shape[1] // 2, 1)

    def row_half(w, which):
        return lax.dynamic_slice_in_dim(w, which * (w.shape[0] // 2), w.shape[0] // 2, 0)

    unit = w_down.shape[0]
    padded = -(-unit // 16) * 16
    cols = quads * padded

    def by_quad(w):
        w = w.reshape(rows, above, 2, below, 2, unit)
        w = jnp.pad(w, ((0, 0),) * 5 + ((0, padded - unit),))
        return w.transpose(2, 4, 0, 1, 3, 5).reshape(4, rows, cols)

    gate, up = by_quad(w_gate), by_quad(w_up)
    down = jnp.pad(w_down, ((0, padded - unit), (0, 0)))
    near_grad = flip(out_grad, 1)

    def by_core(which):
        return jnp.concatenate([column_half(w, which) for w in (w_query, w_key, w_value)], axis=1)

    gains = jnp.stack([norm1_gain, norm2_gain]).astype(f32)
    if n == 32:
        gains = jnp.pad(gains, ((0, 6), (0, 128 - rows)))[None]
        gains = after(gains, near_grad)
        gains, gate, up, qkv_all = spread_first(gains, gate, up, by_core(core), by_core(1 - core))
        gains = gains[:, :2, :rows].transpose(1, 0, 2).reshape(2, 1, width)
        z4 = qkv_all
        qkv_all, out_half, gate = spread_second(z4, column_half(w_out, core), column_half(w_out, 1 - core), gate)
        qkv_all = qkv_all.reshape(width, -1)
    else:

        def to_group(x):
            pieces = [(member, pick(x, member))]
            for k in range(1, 4):
                pieces.append((member ^ k, flip(pick(x, member ^ k), to_member[k])))
            return assemble_all(pieces)

        gate, up = to_group(gate), to_group(up)
        qkv_all = side_by_side(core, by_core(core), flip(by_core(1 - core), 1))
        gains = grow(gains, 1)
        for bit in cbits:
            gains, qkv_all = grow(gains, bit), grow(qkv_all, bit)
        gains = in_order(gains, [1] + cbits).transpose(1, 0, 2).reshape(2, 1, width)
        qkv_all = in_order(qkv_all, cbits).reshape(width, -1)
        out_half = side_by_side(core, column_half(w_out, core), flip(column_half(w_out, 1 - core), 1))
        for bit in cbits[:-2]:
            out_half = grow(out_half, bit)
        out_half = in_order(out_half, cbits[:-2])
        gate = grow(gate, qbits[0])
    gain_one, gain_two = gains[0], gains[1]

    inputs32 = block_input.astype(f32)
    ratio_one = lax.rsqrt(jnp.mean(inputs32 * inputs32, axis=1, keepdims=True) + eps)
    normed_one = inputs32 * ratio_one
    hidden_one = (normed_one * gain_one).astype(bf16)
    hidden_chip = side_by_side(core, hidden_one, move(hidden_one, 1, (), (qkv_all,)))
    qkv = dot(hidden_chip, qkv_all).astype(bf16)

    first = (me // 2) * 2 * tokens
    positions = first + jnp.arange(2 * tokens, dtype=jnp.int32)
    lo = row_starts(positions, lengths, offsets) - first
    attention = Attention(qkv, lo, heads, tokens)
    states = attention.states()
    fresh0 = (lo[tokens - 1] >= 0).astype(f32)
    fresh1 = (lo[2 * tokens - 1] >= tokens).astype(f32)

    start, stop = (qkv_all,), (states,)
    down = lax.all_gather(after(down, qkv_all), "tok", axis=0, tiled=True, axis_index_groups=groups)
    for bit in qbits[1:-2]:
        gate = grow(gate, bit)
    gate_x = move(gate, 2, start, stop)
    up = grow(up, qbits[0], start, stop)
    for bit in qbits[1:-2]:
        up = grow(up, bit)
    out_y = move(out_half, 4, start, stop)
    leaving = states[:, 1] + (1.0 - fresh1) * states[:, 0]
    leaving, gate_x, up, out_y = lax.optimization_barrier((leaving, gate_x, up, out_y))
    entering = others(leaving, True, f32)
    start, stop = (leaving,), (entering,)
    flows = [(out_half, 2), (out_y, 2), (up, 4), (gate, 4), (up, 2)]
    flows = [move(w, bit, start, stop) for w, bit in flows]
    entering, out_x, out_xy, up_y, gate_y, up_x = lax.optimization_barrier((entering, *flows))
    carry = jnp.stack([entering, states[:, 0] + (1.0 - fresh0) * entering], axis=1)
    place = (me // 2) % 4
    out_pieces = [(place, out_half), (place ^ 1, out_x), (place ^ 2, out_y), (place ^ 3, out_xy)]
    out_half = jnp.zeros((chips // 4, 4, 2 * rows, half), bf16)
    for index, piece in out_pieces:
        out_half = lax.dynamic_update_index_in_dim(out_half, piece, index, 1)
    out_half = out_half.reshape(width, half)
    carry = after(carry, out_half)
    y_heads, mixed_heads = attention.forward(carry)
    start, stop = (carry,), (mixed_heads,)
    flows = [(gate_x, 4), (up_y, 2), (out_grad, PAIR), (out_half, 1)]
    flows = [move(w, bit, start, stop) for w, bit in flows]
    mixed_heads, gate_xy, up_xy, far_grad, out_there, down = lax.optimization_barrier((mixed_heads, *flows, down))
    out_all = side_by_side(core, out_half, out_there, 1)
    mixed_there = flip(mixed_heads, 1)
    mixed_chip = side_by_side(core, mixed_heads, mixed_there, 1)
    middle = inputs32 + dot(row_half(mixed_chip, core), out_all)
    ratio_two = lax.rsqrt(jnp.mean(middle * middle, axis=1, keepdims=True) + eps)
    normed_two = middle * ratio_two
    hidden_two = (normed_two * gain_two).astype(bf16)

    far_hidden = flip(hidden_two, PAIR)
    near_grad = jnp.concatenate([out_grad, near_grad])
    near_hidden = jnp.concatenate([hidden_two, flip(hidden_two, 1)])
    gate = [w.reshape(-1, 2 * rows, cols) for w in (gate, gate_x, gate_y, gate_xy)]
    up = [w.reshape(-1, 2 * rows, cols) for w in (up, up_x, up_y, up_xy)]
    order = [(at + more) // 2 for at in grown(qbits[:-2]) for more in (0, PAIR)]
    sides = jnp.stack([place, place ^ 1, place ^ 2, place ^ 3])
    near = ffn(near_hidden, near_grad, gate, up, down, order, sides)
    far_hidden, far_there = after(far_hidden, *near), move(far_grad, 1, (near_hidden,), (near[0],))
    far_grad = jnp.concatenate([far_grad, far_there])
    far_hidden = jnp.concatenate([far_hidden, flip(far_hidden, 1)])
    far = ffn(far_hidden, far_grad, gate, up, down, order, sides)
    start, stop = (near[0], far_hidden), (far[0],)
    near_parts = [move(near[i][tokens:], 1, start, stop) for i in (3, 0)]
    far, near_parts = lax.optimization_barrier((far, near_parts))

    right = [near[2], far[2]]
    sum_gate = Scatter(part_maker([near_hidden, far_hidden], right, qbits, (0, PAIR), 0), qbits)
    sum_gate.send()
    start, stop = (far[0],), (sum_gate.sent,)
    far_parts = [move(far[i][tokens:], 1, start, stop) for i in (3, 0)]
    sent, far_parts = lax.optimization_barrier((sum_gate.sent, far_parts))
    d_far = (far[3][:tokens].astype(f32) + far_parts[0].astype(f32)).astype(bf16)
    sum_up = Scatter(part_maker([after(near_hidden, sent, d_far), far_hidden], right, swapped, (0, PAIR), 1), swapped)
    sum_up.send()
    sum_gate.keep(sum_up.sent)
    sum_up.keep(sum_gate.kept)
    term = row_blocks([near[1], far[1]], [after(near_grad, sum_up.kept), far_grad], jnp.arange(cols // 128), 128)
    d_far = move(d_far, PAIR, (), (term,))
    d_far = sum_gate.hold(d_far, term)
    near_parts, far_parts = after(near_parts, d_far), after(far_parts, d_far)
    d_near = near[3][:tokens].astype(f32) + near_parts[0].astype(f32)
    y_near = near[0][:tokens].astype(f32) + near_parts[1].astype(f32)
    y_far = (far[0][:tokens].astype(f32) + far_parts[1].astype(f32)).astype(bf16)
    d_hidden_two = d_near + d_far.astype(f32)
    term_norm_two = jnp.sum(d_hidden_two * normed_two, axis=0)
    scaled_two = d_hidden_two * gain_two
    d_middle = out_grad.astype(f32) + ratio_two * (
        scaled_two - normed_two * jnp.mean(scaled_two * normed_two, axis=1, keepdims=True)
    )
    d_mixed = d_middle.astype(bf16)
    d_mixed_chip = side_by_side(core, d_mixed, flip(d_mixed, 1))
    d_heads = dot_cols(d_mixed_chip, row_half(out_all, core)).astype(bf16)

    d_heads = sum_up.hold(after(d_heads, y_far), d_mixed)
    d_heads = after(d_heads, sum_gate.step(), sum_up.step())

    def down_x(index):
        return pick(term.reshape(quads // 2, 2, padded, width)[..., :half], index, 1)

    def down_y(index):
        return pick(term.reshape(quads // 4, 2, 2, padded, width)[..., half:], index, 1).reshape(-1, padded, half)

    sum_down = [Scatter(down_x, qbits), Scatter(down_y, swapped)]
    for part in sum_down:
        part.send(d_heads)
        part.keep()
        d_heads = after(d_heads, part.sent, part.kept)
    dq, dk, dv, d_states = attention.backward(carry, y_heads, d_heads)
    y_far = move(y_far, PAIR, (d_heads,), (d_states,))
    for part in [sum_gate, sum_up] + sum_down:
        d_states = part.hold(d_states, d_states)
    d_states, y_far = lax.optimization_barrier((d_states, y_far))
    sent = [part.step() for part in [sum_gate, sum_up] + sum_down]
    d_mixed_half = column_half(d_mixed_chip, core)
    out_sums = []
    for h, bits in ((0, cbits), (1, cbits[:-2] + [cbits[-1], cbits[-2]])):
        out_sums.append(Scatter(part_maker([after(mixed_chip, *sent)], [d_mixed_half], bits, (0,), h), bits))
        out_sums[-1].send()
    leaving = d_states[:, 0] + (1.0 - fresh0) * d_states[:, 1]
    leaving = others(after(leaving, *(part.sent for part in out_sums)), False, bf16)
    for part in out_sums:
        leaving = after(leaving, part.keep(leaving))
    for part in sum_down:
        leaving = part.hold(leaving, leaving)
    leaving = after(leaving, *(part.step() for part in sum_down))
    d_states = jnp.stack([d_states[:, 1] + (1.0 - fresh1) * leaving, leaving], axis=1)
    dk, dv = attention.carried(d_states, dk, dv)
    for part in out_sums + [sum_gate, sum_up] + sum_down:
        dk = part.hold(dk, dk)
    sent = [part.step() for part in out_sums]
    gate_sum = jnp.stack([part.finish().reshape(4, rows, cols) for part in (sum_gate, sum_up)], axis=1)
    parts = [pick(gate_sum, member ^ k).astype(bf16) for k in range(1, 4)]
    d_qkv = after(jnp.concatenate([dq, dk, dv], axis=1), *sent, *parts)

    if (2 * rows) % 128 == 0:
        terms = row_blocks([hidden_chip], [d_qkv], jnp.arange(chips), 2 * rows)
    else:
        terms = dot_rows(hidden_chip, d_qkv).astype(bf16)
    parts = [move(part, to_member[k], (), (terms,)) for k, part in enumerate(parts, 1)]
    for part in out_sums:
        terms = part.hold(terms, terms)
    terms, parts = lax.optimization_barrier((terms, parts))
    terms = terms.reshape(chips // 4, 2, 2, 2 * rows, -1)
    cut = terms.shape[-1] // 2

    def along_x(index):
        return pick(terms[..., :cut], index, 2).reshape(chips // 2, 2 * rows, cut)

    def along_y(index):
        return pick(terms[..., cut:], index, 1).reshape(chips // 2, 2 * rows, cut)

    sums = [Scatter(along_x, cbits), Scatter(along_y, cbits[:-2] + [cbits[-1], cbits[-2]])]
    for part in sums:
        part.send()

    def join(both):
        out = Scatter(None, cbits[:-2] + [0])
        out.kept = jnp.concatenate([part.kept for part in both], axis=2)
        out.here = jnp.concatenate([part.here for part in both], axis=2)
        return out

    rest_out = join(out_sums)
    sent = rest_out.step()
    d_qkv = after(d_qkv, sent, *(part.sent for part in sums))
    theirs = flip(dot_cols(row_half(d_qkv, 1 - core), qkv_all).astype(bf16), 1)
    d_hidden_one = dot_cols(row_half(d_qkv, core), qkv_all) + theirs.astype(f32)
    term_norm_one = jnp.sum(d_hidden_one * normed_one, axis=0)
    scaled_one = d_hidden_one * gain_one
    mean_one = jnp.mean(scaled_one * normed_one, axis=1, keepdims=True)
    norms = jnp.stack([term_norm_one, term_norm_two])
    for part in sums:
        part.keep()
        norms = part.hold(norms, norms)
    norms = rest_out.hold(norms, norms)
    sent = [part.step() for part in sums] + [rest_out.step() for _ in rest_out.bits[1:]]
    norms = after(norms, *sent)
    norms = norms + flip(norms, 1)
    gate_sum = assemble_all([(member, pick(gate_sum, member))] + [(member ^ k, p.astype(f32)) for k, p in enumerate(parts, 1)])
    gate_sum = after(gate_sum, *sent).reshape(2, 2, 2, rows, above, below, padded)[..., :unit]
    norms = norms + flip(norms, cbits[-1])
    for part in sums:
        norms = part.hold(norms, gate_sum)
    rest = join(sums)
    sent = rest.step()
    norms = after(norms, sent)
    norms = norms + flip(norms, cbits[-2])
    gate_sum = after(gate_sum, sent).transpose(2, 3, 4, 0, 5, 1, 6).reshape(2, rows, n * unit)
    grad_gate, grad_up = gate_sum[0], gate_sum[1]
    norms = rest.hold(norms, norms)
    while len(rest.bits) > 1:
        sent = rest.step()
    norms = after(norms, sent)
    for bit in cbits[:-2]:
        norms = norms + flip(norms, bit)
    norms = pick(norms.reshape(2, n, rows), me, 1)
    input_grad = d_middle + ratio_one * (after(scaled_one, sent) - normed_one * mean_one)
    output = (after(middle, sent) + y_near + y_far.astype(f32)).astype(bf16)
    grad_down = jnp.concatenate([part.finish() for part in sum_down], axis=1)[:unit]
    rest.kept = jnp.concatenate([rest.kept, rest_out.kept], axis=2)
    rest.here = jnp.concatenate([rest.here, rest_out.here], axis=2)
    total = rest.step()
    mine, theirs = row_half(total, core), flip(row_half(total, 1 - core), 1)
    spans = [(0, lanes), (lanes, 2 * lanes), (2 * lanes, 2 * lanes + half), (2 * cut, 2 * cut + half)]
    grad_query, grad_key, grad_value, grad_out = (
        side_by_side(core, mine[:, a:b], theirs[:, a:b], 1) for a, b in spans
    )

    return (
        output,
        input_grad,
        norms[0],
        grad_query,
        grad_key,
        grad_value,
        grad_out,
        norms[1],
        grad_gate,
        grad_up,
        grad_down,
    )


def solution(mesh):
    return jax.shard_map(
        shards,
        mesh=mesh,
        in_specs=(
            P("tok", None),
            P(),
            P(),
            P("tok"),
            P("tok", None),
            P("tok", None),
            P("tok", None),
            P("tok", None),
            P("tok"),
            P("tok", None),
            P("tok", None),
            P("tok", None),
            P("tok", None),
        ),
        out_specs=(
            P("tok", None),
            P("tok", None),
            P("tok"),
            P("tok", None),
            P("tok", None),
            P("tok", None),
            P("tok", None),
            P("tok"),
            P("tok", None),
            P("tok", None),
            P("tok", None),
        ),
        check_vma=False,
    )
```

time: 1100 us -> 1040 us (0.945)
  Pallas kernels: 314 us -> 582 us
  waiting for transfers between devices: 375 us -> 113 us
  starting transfers between devices: 120 us -> 49.4 us
  other arithmetic: 71.1 us -> 88.9 us
    ppermute x56 -> x0, waiting for transfers between devices: 292 us -> none  [shift(): return lax.ppermute(x, 'tok', pairs)]
    pallas_call x2 -> x6, Pallas kernels: 98.6 us -> 351 us  [the longest x2 157 us: others(): pl.pallas_call(lambda *refs: scan_body(sign, *refs), out_shape=jax.ShapeD...]
    ppermute x56 -> x0, starting transfers between devices: 96.9 us -> none  [shift(): return lax.ppermute(x, 'tok', pairs)]
    ppermute x41 -> x60, waiting for transfers between devices: 82.8 us -> 113 us  [flip(): return lax.ppermute(x, 'tok', [(i, i ^ bits) for i in range(n)])]
    dynamic_update_slice x39 -> x1, local copies, waits for them, and re-layouts: 28.8 us -> 0.92 us  [assemble(): out = lax.dynamic_update_index_in_dim(out, block, index, 0)]
    ppermute x41 -> x60, starting transfers between devices: 23.2 us -> 49.3 us  [flip(): return lax.ppermute(x, 'tok', [(i, i ^ bits) for i in range(n)])]
    add x18 -> x35, other arithmetic: 14.7 us -> 40.8 us  [the longest x19 25.7 us: step(): acc = self.kept.astype(f32) + after(self.here, *gate).astype(f32)]
    pallas_call x8 -> x10, Pallas kernels: 105 us -> 120 us  [row_blocks(): pl.pallas_call(lambda *refs: product_body(len(left), *refs), out_shape=ja...]
  transfers between devices with their start and end apart: 99 -> 61, of which waited for: 41 -> 19; matrix products, arithmetic and copies ran while one was open for 20% -> 21% of each run, Pallas kernels for 21% -> 52%
where the time goes in v3:
time: 1040 us; the launch traced here: 1030 us
  Pallas kernels  582 us (56%)
  local copies, waits for them, and re-layouts  152 us (15%)
  waiting for transfers between devices  113 us (11%)
  other arithmetic  88.9 us (9%)
  starting transfers between devices  49.4 us (5%)
  matrix products  29.5 us (3%)
  between operations  17.6 us (2%)
    pallas_call x2, Pallas kernels, others(): pl.pallas_call(lambda *refs: scan_body(sign, *refs), out_shape=jax.ShapeD...  157 us
    pallas_call x10, Pallas kernels, row_blocks(): pl.pallas_call(lambda *refs: product_body(len(left), *refs), out_shape=ja...  120 us
    ppermute x60, waiting for transfers between devices, flip(): return lax.ppermute(x, 'tok', [(i, i ^ bits) for i in range(n)])  113 us
    pallas_call x4, Pallas kernels, call(): pl.pallas_call(body, grid=(2, self.heads), in_specs=ins, out_specs=outs,...  111 us
    pallas_call x2, Pallas kernels, ffn(): pl.pallas_call(lambda *refs: ffn_body(order, *refs), out_shape=[jax.Shape...  97.6 us
    ppermute x60, starting transfers between devices, flip(): return lax.ppermute(x, 'tok', [(i, i ^ bits) for i in range(n)])  49.3 us
    pallas_call x1, Pallas kernels, spread_first(): pl.pallas_call(first_body, out_shape=[jax.ShapeDtypeStruct((32,) + gains....  48.8 us
    pallas_call x1, Pallas kernels, spread_second(): pl.pallas_call(second_body, out_shape=[jax.ShapeDtypeStruct((4, 4) + z4.s...  47.6 us
  transfers between devices with their start and end apart: 61, of which 19 were waited for; matrix products, arithmetic and copies ran while one was open for 21% of the time, Pallas kernels for 52%

profile of v3, /device:TPU:0, one launch (start us, length us, event | category | flops | bytes accessed | tf_op | source)
XLA Modules:
  0.0 1032.1 jit_solution(17490630888489154031)
XLA Ops:
  7.7 4.8 reshape.347
  14.6 3.1 reshape.349
  19.7 2.8 reshape.350.up_in
  25.7 48.8 %shard_map.275 = (f32[32,8,128]{2,1,0:T(8,128)S(1)}, bf16[4,64,1408]{2,1,0:T(8,128)(2,1)S(1)}, bf16[4,64,1408]{2,1,0:T(8,128)(2,1)S(1)}, bf16[4,128,1280]{2,1,0:T(8,128)(2,1)S(1)}) custom-call(f32[1,8,128]{2,1,0:T(8,128)S(1)} %fusion.55.gains_in, bf16[4,64,1408]{2,1,0:T(8,128)(2,1)S(1)} %reshape.348.gate_in, bf16[4,64,1408]{2,1,0:T(8,128)(2,1)S(1)} %reshape.350.up_in, ...), custom_call_target="tpu_custom_call" | custom-call | tf_op jit(solution)/shard_map/pallas_call | solution.py:196
  84.9 47.6 %shard_map.276 = (bf16[4,4,128,1280]{3,2,1,0:T(8,128)(2,1)S(1)}, bf16[4,128,1024]{2,1,0:T(8,128)(2,1)S(1)}, bf16[2,4,64,1408]{3,2,1,0:T(8,128)(2,1)S(1)}) custom-call(bf16[4,128,1280]{2,1,0:T(8,128)(2,1)S(1)} %get-tuple-element.205.z4, bf16[64,1024]{1,0:T(8,128)(2,1)S(1)} %copy-done.6, bf16[64,1024]{1,0:T(8,128)(2,1)S(1)} %copy-done.5, ...), custom_call_target="tpu_custom_call" | custom-call | tf_op jit(solution)/shard_map/pallas_call | solution.py:248
  141.8 3.4 constant_dynamic-update-slice_fusion.6.refs_1_
  145.2 10.0 convolution_convert_fusion.k_ref.v_ref.q_ref
  155.2 14.0 %shard_map.277 = f32[8,2,168,128]{3,2,1,0:T(8,128)} custom-call(s32[2]{0:T(128)} %pad_add_fusion.scal, bf16[1024,1280]{1,0:T(8,128)(2,1)} %convolution_convert_fusion.k_ref.v_ref.q_ref, bf16[1024,1280]{1,0:T(8,128)(2,1)} %convolution_convert_fusion.k_ref.v_ref.q_ref, bf16[8,128,160]{2,1,0:T(8,128)(2,1)} %constant.484.clone.one, ...), custom_call_target="tpu_custom_call" | custom-call | tf_op jit(solution)/shard_map/pallas_call | solution.py:678
  169.7 28.1 %collective-permute-done.3 = bf16[4,64,1408]{2,1,0:T(8,128)(2,1)S(1)} collective-permute-done((bf16[4,64,1408]{2,1,0:T(8,128)(2,1)S(1)}, bf16[4,64,1408]{2,1,0:T(8,128)(2,1)S(1)}, u32[]{:S(2)}, u32[]{:S(2)}) %collective-permute-start.3) | collective-permute-done | bytes 720928 | tf_op jit(solution)/shard_map/ppermute | solution.py:29
  197.7 2.8 fusion.34.refs_0_
  208.4 2.5 broadcast_in_dim.84
  212.0 116.7 %shard_map.278 = f32[8,168,128]{2,1,0:T(8,128)} custom-call(f32[8,168,128]{2,1,0:T(8,128)} %fusion.34.refs_0_), custom_call_target="tpu_custom_call" | custom-call | tf_op jit(solution)/shard_map/pallas_call | solution.py:747
  344.2 2.5 copy.87.carry_ref
  346.7 22.4 %shard_map.279 = (f32[1024,1024]{1,0:T(8,128)}, bf16[1024,1024]{1,0:T(8,128)(2,1)}) custom-call(bf16[1024,1280]{1,0:T(8,128)(2,1)} %convolution_convert_fusion.k_ref.v_ref.q_ref, bf16[1024,1280]{1,0:T(8,128)(2,1)} %convolution_convert_fusion.k_ref.v_ref.q_ref, bf16[1024,1280]{1,0:T(8,128)(2,1)} %convolution_convert_fusion.k_ref.v_ref.q_ref, ...), custom_call_target="tpu_custom_call" | custom-call | tf_op jit(solution)/shard_map/pallas_call | solution.py:678
  369.1 5.4 collective-permute-done.11
  375.4 11.9 %collective-permute-done.12 = bf16[512,2048]{1,0:T(8,128)(2,1)} collective-permute-done((bf16[512,2048]{1,0:T(8,128)(2,1)S(1)}, bf16[512,2048]{1,0:T(8,128)(2,1)}, u32[]{:S(2)}, u32[]{:S(2)}) %collective-permute-start.12) | collective-permute-done | bytes 2097184 | tf_op jit(solution)/shard_map/ppermute | solution.py:29
  388.4 2.7 constant_dynamic-update-slice_fusion.3
  393.1 2.7 constant_dynamic-update-slice_fusion.2
  395.8 3.6 constant_dynamic-update-slice_fusion.4.refs_1_
  401.1 4.7 multiply_reduce_fusion.2
  413.0 5.6 pad_maximum_fusion.refs_1_
  418.6 48.8 %shard_map.280 = (bf16[1024,2048]{1,0:T(8,128)(2,1)}, bf16[1024,1408]{1,0:T(8,128)(2,1)}, bf16[1024,2816]{1,0:T(8,128)(2,1)}, bf16[1024,2048]{1,0:T(8,128)(2,1)}) custom-call(s32[4]{0:T(128)} %pad_add_fusion.1.refs_0_, bf16[1024,2048]{1,0:T(8,128)(2,1)} %pad_maximum_fusion.refs_1_, bf16[1024,2048]{1,0:T(8,128)(2,1)} %copy-done.27, ...), custom_call_target="tpu_custom_call" | custom-call | tf_op jit(solution)/shard_map/pallas_call | solution.py:385
  467.5 3.3 slice.128
  475.5 4.1 constant_dynamic-update-slice_fusion.13
  481.1 48.8 %shard_map.281 = (bf16[1024,2048]{1,0:T(8,128)(2,1)}, bf16[1024,1408]{1,0:T(8,128)(2,1)}, bf16[1024,2816]{1,0:T(8,128)(2,1)}, bf16[1024,2048]{1,0:T(8,128)(2,1)}) custom-call(s32[4]{0:T(128)} %pad_add_fusion.1.refs_0_, bf16[1024,2048]{1,0:T(8,128)(2,1)} %copy-done.8, bf16[1024,2048]{1,0:T(8,128)(2,1)} %constant_dynamic-update-slice_fusion.12.refs_2_.refs_4_, ...), custom_call_target="tpu_custom_call" | custom-call | tf_op jit(solution)/shard_map/pallas_call | solution.py:385
  529.9 3.3 slice.131
  536.2 13.5 %shard_map.282 = bf16[1024,1408]{1,0:T(8,128)(2,1)} custom-call(s32[8]{0:T(128)} %broadcast_add_fusion.5.refs_0_, bf16[1024,2048]{1,0:T(8,128)(2,1)} %pad_maximum_fusion.refs_1_, bf16[1024,2048]{1,0:T(8,128)(2,1)} %copy-done.8, bf16[1024,2816]{1,0:T(8,128)(2,1)} %get-tuple-element.257.refs_3_, bf16[1024,2816]{1,0:T(8,128)(2,1)} %get-tuple-element.273.refs_4_), custom_call_target="tpu_custom_call" | custom-call | flops 5905580032 | bytes 12845056 | tf_op jit(solution)/shard_map/pallas_call | solution.py:436
  551.2 3.8 add_convert_fusion.2
  555.3 13.1 %shard_map.283 = bf16[1024,1408]{1,0:T(8,128)(2,1)} custom-call(s32[8]{0:T(128)} %broadcast_add_fusion.4.refs_0_, bf16[1024,2048]{1,0:T(8,128)(2,1)} %pad_maximum_fusion.refs_1_, bf16[1024,2048]{1,0:T(8,128)(2,1)} %copy-done.8, bf16[1024,2816]{1,0:T(8,128)(2,1)} %get-tuple-element.257.refs_3_, bf16[1024,2816]{1,0:T(8,128)(2,1)} %get-tuple-element.273.refs_4_), custom_call_target="tpu_custom_call" | custom-call | flops 5905580032 | bytes 12845056 | tf_op jit(solution)/shard_map/pallas_call | solution.py:436
  569.9 13.5 %shard_map.284 = bf16[1024,1408]{1,0:T(8,128)(2,1)} custom-call(s32[8]{0:T(128)} %broadcast_add_fusion.2.refs_0_, bf16[1024,2048]{1,0:T(8,128)(2,1)} %pad_maximum_fusion.refs_1_, bf16[1024,2048]{1,0:T(8,128)(2,1)} %copy-done.8, bf16[1024,2816]{1,0:T(8,128)(2,1)} %get-tuple-element.257.refs_3_, bf16[1024,2816]{1,0:T(8,128)(2,1)} %get-tuple-element.273.refs_4_), custom_call_target="tpu_custom_call" | custom-call | flops 5905580032 | bytes 12845056 | tf_op jit(solution)/shard_map/pallas_call | solution.py:436
  583.9 13.1 %shard_map.285 = bf16[1024,1408]{1,0:T(8,128)(2,1)} custom-call(s32[8]{0:T(128)} %broadcast_add_fusion.1.refs_0_, bf16[1024,2048]{1,0:T(8,128)(2,1)} %pad_maximum_fusion.refs_1_, bf16[1024,2048]{1,0:T(8,128)(2,1)} %copy-done.8, bf16[1024,2816]{1,0:T(8,128)(2,1)} %get-tuple-element.257.refs_3_, bf16[1024,2816]{1,0:T(8,128)(2,1)} %get-tuple-element.273.refs_4_), custom_call_target="tpu_custom_call" | custom-call | flops 5905580032 | bytes 12845056 | tf_op jit(solution)/shard_map/pallas_call | solution.py:436
  597.5 19.7 %shard_map.286 = bf16[1408,2048]{1,0:T(8,128)(2,1)} custom-call(s32[11]{0:T(128)} %iota.14.refs_0_, bf16[1024,1408]{1,0:T(8,128)(2,1)} %get-tuple-element.256.refs_1_, bf16[1024,1408]{1,0:T(8,128)(2,1)} %get-tuple-element.280.refs_2_, bf16[1024,2048]{1,0:T(8,128)(2,1)} %copy-done.27, bf16[1024,2048]{1,0:T(8,128)(2,1)} %constant_dynamic-update-slice_fusion.12.refs_2_.refs_4_), custom_call_target="tpu_custom_call" | custom-call | flops 11811160064 | bytes 19922944 | tf_op jit(solution)/shard_map/pallas_call | solution.py:436
  622.7 3.2 multiply_reduce_fusion
  627.5 5.3 constant_dynamic-update-slice_fusion.1
  637.0 2.5 convert_add_fusion.2
  641.7 5.5 add_convert_fusion.1
  647.6 5.9 fusion.15.d_ref
  655.9 2.5 copy-done.17
  663.7 46.0 %shard_map.287 = (bf16[1024,128]{1,0:T(8,128)(2,1)}, f32[1024,128]{1,0:T(8,128)}, f32[1024,1024]{1,0:T(8,128)}, f32[8,2,168,128]{3,2,1,0:T(8,128)}) custom-call(bf16[1024,1280]{1,0:T(8,128)(2,1)} %convolution_convert_fusion.k_ref.v_ref.q_ref, bf16[1024,1280]{1,0:T(8,128)(2,1)} %convolution_convert_fusion.k_ref.v_ref.q_ref, ...), custom_call_target="tpu_custom_call" | custom-call | tf_op jit(solution)/shard_map/pallas_call | solution.py:678
  717.1 3.3 collective-permute-start.36
  720.4 4.4 collective-permute-done.29
  736.3 7.6 shard_map.288
  745.0 7.7 shard_map.289
  752.6 20.1 %collective-permute-done.31 = bf16[512,2048]{1,0:T(8,128)(2,1)} collective-permute-done((bf16[512,2048]{1,0:T(8,128)(2,1)}, bf16[512,2048]{1,0:T(8,128)(2,1)}, u32[]{:S(2)}, u32[]{:S(2)}) %collective-permute-start.31) | collective-permute-done | bytes 2097184 | tf_op jit(solution)/shard_map/ppermute | solution.py:29
  774.7 40.1 %shard_map.290 = f32[8,168,128]{2,1,0:T(8,128)} custom-call(f32[8,168,128]{2,1,0:T(8,128)} %fusion.33.refs_0_), custom_call_target="tpu_custom_call" | custom-call | tf_op jit(solution)/shard_map/pallas_call | solution.py:747
  815.3 7.9 shard_map.291
  823.7 7.8 shard_map.292
  833.9 2.8 collective-permute-start.38
  840.2 28.6 %shard_map.293 = (bf16[1024,128]{1,0:T(8,128)(2,1)}, bf16[1024,1024]{1,0:T(8,128)(2,1)}) custom-call(s32[2]{0:T(128)} %pad_add_fusion.scal, bf16[1024,1280]{1,0:T(8,128)(2,1)} %convolution_convert_fusion.k_ref.v_ref.q_ref, bf16[1024,1280]{1,0:T(8,128)(2,1)} %convolution_convert_fusion.k_ref.v_ref.q_ref, bf16[8,128,160]{2,1,0:T(8,128)(2,1)} %constant.484.clone.one, ...), custom_call_target="tpu_custom_call" | custom-call | tf_op jit(solution)/shard_map/pallas_call | solution.py:678
  880.7 3.5 collective-permute-done.38
  885.2 6.5 collective-permute-done.39
  895.0 16.0 %shard_map.294 = bf16[2048,1280]{1,0:T(8,128)(2,1)} custom-call(s32[16]{0:T(128)} %iota.13.refs_0_, bf16[1024,2048]{1,0:T(8,128)(2,1)} %constant_dynamic-update-slice_fusion.6.refs_1_, bf16[1024,1280]{1,0:T(8,128)(2,1)} %pad_maximum_fusion.1.refs_2_), custom_call_target="tpu_custom_call" | custom-call | flops 5368709120 | bytes 12058624 | tf_op jit(solution)/shard_map/pallas_call | solution.py:436
  911.0 3.2 fusion.62
  918.1 3.1 convolution_convert_fusion.1
  928.0 5.7 fusion.6
  933.7 21.2 %collective-permute-done.46 = bf16[8,128,640]{2,1,0:T(8,128)(2,1)S(1)} collective-permute-done((bf16[8,128,640]{2,1,0:T(8,128)(2,1)S(1)}, bf16[8,128,640]{2,1,0:T(8,128)(2,1)S(1)}, u32[]{:S(2)}, u32[]{:S(2)}) %collective-permute-start.46) | collective-permute-done | bytes 1310752 | tf_op jit(solution)/shard_map/ppermute | solution.py:29
  964.7 8.6 reshape.384
  983.4 3.0 copy.95
  986.3 3.9 squeeze.144
  990.3 4.6 copy.96
  994.9 4.2 squeeze.145
  1004.5 6.5 fusion.9
  1011.4 5.2 add_convert_fusion
  1017.2 3.7 collective-permute-done.56
  (446 shorter events, 183.4 us)
Async XLA Ops:
  7.2 380.1 %all-gather.2.cloned.1.call-start = ((), (), s32[]{:S(2)}) async-start(), calls=%async_computation | async-start | bytes 6488064 | tf_op jit(solution)/shard_map/all_gather | solution.py:875
  7.2 18.5 %collective-permute-start = (bf16[512,2048]{1,0:T(8,128)(2,1)}, bf16[512,2048]{1,0:T(8,128)(2,1)}, u32[]{:S(2)}, u32[]{:S(2)}) collective-permute-start(bf16[512,2048]{1,0:T(8,128)(2,1)} %param.32), channel_id=1, source_target_pairs={{0,1},{1,0},{2,3},{3,2},{4,5},{5,4},{6,7},{7,6},{8,9},{9,8},{10,11... | collective-permute-start | bytes 6291464 | tf_op jit(solution)/shard_map/ppermute | solution.py:29
  81.1 54.8 %copy-start.83 = (s32[3]{0:T(128)S(1)}, s32[3]{0:T(128)}, u32[]{:S(2)}) copy-start(s32[3]{0:T(128)} %param.21) | copy-start | bytes 40
  81.1 60.7 %collective-permute-start.1 = (bf16[512,2048]{1,0:T(8,128)(2,1)}, bf16[512,2048]{1,0:T(8,128)(2,1)}, u32[]{:S(2)}, u32[]{:S(2)}) collective-permute-start(bf16[512,2048]{1,0:T(8,128)(2,1)} %get-tuple-element.406), channel_id=1, source_target_pairs={{0,1},{1,0},{2,3},{3,2},{4,5},{5,4},{6,7},{7,6},{8,9},{9,8},{10,11... | collective-permute-start | bytes 6291464 | tf_op jit(solution)/shard_map/ppermute | solution.py:29
  135.8 67.9 %copy-start = (bf16[2,4,64,1408]{3,2,1,0:T(8,128)(2,1)}, bf16[2,4,64,1408]{3,2,1,0:T(8,128)(2,1)S(1)}, u32[]{:S(2)}) copy-start(bf16[2,4,64,1408]{3,2,1,0:T(8,128)(2,1)S(1)} %get-tuple-element.227) | copy-start | bytes 4325380
  139.3 30.3 %collective-permute-start.4 = (bf16[4,128,1024]{2,1,0:T(8,128)(2,1)}, bf16[4,128,1024]{2,1,0:T(8,128)(2,1)}, u32[]{:S(2)}, u32[]{:S(2)}) collective-permute-start(bf16[4,128,1024]{2,1,0:T(8,128)(2,1)} %copy-done.1), channel_id=1, source_target_pairs={{0,4},{1,5},{2,6},{3,7},{4,0},{5,1},{6,2},{7,3},{8,12},{9,13},{10,... | collective-permute-start | bytes 3145736 | tf_op jit(solution)/shard_map/ppermute | solution.py:29
  140.8 56.9 %collective-permute-start.3 = (bf16[4,64,1408]{2,1,0:T(8,128)(2,1)S(1)}, bf16[4,64,1408]{2,1,0:T(8,128)(2,1)S(1)}, u32[]{:S(2)}, u32[]{:S(2)}) collective-permute-start(bf16[4,64,1408]{2,1,0:T(8,128)(2,1)S(1)} %get-tuple-element.213), channel_id=1, source_target_pairs={{0,16},{1,17},{2,18},{3,19},{4,20},{5,21},{6,22},{7,23},{8,24},{9,... | collective-permute-start | bytes 2162696 | tf_op jit(solution)/shard_map/ppermute | solution.py:29
  140.9 56.9 %collective-permute-start.2 = (bf16[2,4,64,1408]{3,2,1,0:T(8,128)(2,1)S(1)}, bf16[2,4,64,1408]{3,2,1,0:T(8,128)(2,1)S(1)}, u32[]{:S(2)}, u32[]{:S(2)}) collective-permute-start(bf16[2,4,64,1408]{3,2,1,0:T(8,128)(2,1)S(1)} %get-tuple-element.227), channel_id=1, source_target_pairs={{0,2},{1,3},{2,0},{3,1},{4,6},{5,7},{6,4},{7,5},{8,10},{9,11},{10,... | collective-permute-start | bytes 4325384 | tf_op jit(solution)/shard_map/ppermute | solution.py:29
  202.7 126.0 %collective-permute-start.9 = (bf16[2,4,64,1408]{3,2,1,0:T(8,128)(2,1)}, bf16[2,4,64,1408]{3,2,1,0:T(8,128)(2,1)}, u32[]{:S(2)}, u32[]{:S(2)}) collective-permute-start(bf16[2,4,64,1408]{3,2,1,0:T(8,128)(2,1)} %bitcast_dynamic-update-slice_fusion.4), channel_id=1, source_target_pairs={{0,2},{1,3},{2,0},{3,1},{4,6},{5,7},{6,4},{7,5},{8,10},{9,11},{10,... | collective-permute-start | bytes 4325384 | tf_op jit(solution)/shard_map/ppermute | solution.py:29
  203.7 125.0 %collective-permute-start.8 = (bf16[2,4,64,1408]{3,2,1,0:T(8,128)(2,1)S(1)}, bf16[2,4,64,1408]{3,2,1,0:T(8,128)(2,1)}, u32[]{:S(2)}, u32[]{:S(2)}) collective-permute-start(bf16[2,4,64,1408]{3,2,1,0:T(8,128)(2,1)S(1)} %get-tuple-element.227), channel_id=1, source_target_pairs={{0,4},{1,5},{2,6},{3,7},{4,0},{5,1},{6,2},{7,3},{8,12},{9,13},{10,... | collective-permute-start | bytes 4325384 | tf_op jit(solution)/shard_map/ppermute | solution.py:29
  203.8 124.9 %collective-permute-start.7 = (bf16[2,4,64,1408]{3,2,1,0:T(8,128)(2,1)}, bf16[2,4,64,1408]{3,2,1,0:T(8,128)(2,1)}, u32[]{:S(2)}, u32[]{:S(2)}) collective-permute-start(bf16[2,4,64,1408]{3,2,1,0:T(8,128)(2,1)} %bitcast_dynamic-update-slice_fusion.4), channel_id=1, source_target_pairs={{0,4},{1,5},{2,6},{3,7},{4,0},{5,1},{6,2},{7,3},{8,12},{9,13},{10,... | collective-permute-start | bytes 4325384 | tf_op jit(solution)/shard_map/ppermute | solution.py:29
  205.7 123.0 %collective-permute-start.6 = (bf16[4,128,1024]{2,1,0:T(8,128)(2,1)}, bf16[4,128,1024]{2,1,0:T(8,128)(2,1)}, u32[]{:S(2)}, u32[]{:S(2)}) collective-permute-start(bf16[4,128,1024]{2,1,0:T(8,128)(2,1)} %collective-permute-done.4), channel_id=1, source_target_pairs={{0,2},{1,3},{2,0},{3,1},{4,6},{5,7},{6,4},{7,5},{8,10},{9,11},{10,... | collective-permute-start | bytes 3145736 | tf_op jit(solution)/shard_map/ppermute | solution.py:29
  206.7 122.0 %collective-permute-start.5 = (bf16[4,128,1024]{2,1,0:T(8,128)(2,1)S(1)}, bf16[4,128,1024]{2,1,0:T(8,128)(2,1)}, u32[]{:S(2)}, u32[]{:S(2)}) collective-permute-start(bf16[4,128,1024]{2,1,0:T(8,128)(2,1)S(1)} %copy-done.2), channel_id=1, source_target_pairs={{0,2},{1,3},{2,0},{3,1},{4,6},{5,7},{6,4},{7,5},{8,10},{9,11},{10,... | collective-permute-start | bytes 3145736 | tf_op jit(solution)/shard_map/ppermute | solution.py:29
  211.0 117.8 %copy-start.34 = (f32[8,2,168,128]{3,2,1,0:T(8,128)S(1)}, f32[8,2,168,128]{3,2,1,0:T(8,128)}, u32[]{:S(2)}) copy-start(f32[8,2,168,128]{3,2,1,0:T(8,128)} %shard_map.277) | copy-start | bytes 4128772
  339.1 48.2 %collective-permute-start.13 = (bf16[2048,1024]{1,0:T(8,128)(2,1)}, bf16[2048,1024]{1,0:T(8,128)(2,1)}, u32[]{:S(2)}, u32[]{:S(2)}) collective-permute-start(bf16[2048,1024]{1,0:T(8,128)(2,1)} %bitcast.23), channel_id=1, source_target_pairs={{0,1},{1,0},{2,3},{3,2},{4,5},{5,4},{6,7},{7,6},{8,9},{9,8},{10,11... | collective-permute-start | bytes 12582920 | tf_op jit(solution)/shard_map/ppermute | solution.py:29
  339.2 48.1 %collective-permute-start.12 = (bf16[512,2048]{1,0:T(8,128)(2,1)S(1)}, bf16[512,2048]{1,0:T(8,128)(2,1)}, u32[]{:S(2)}, u32[]{:S(2)}) collective-permute-start(bf16[512,2048]{1,0:T(8,128)(2,1)S(1)} %copy-done.35), channel_id=1, source_target_pairs={{0,8},{1,9},{2,10},{3,11},{4,12},{5,13},{6,14},{7,15},{8,0},{9,1},... | collective-permute-start | bytes 6291464 | tf_op jit(solution)/shard_map/ppermute | solution.py:29
  340.4 34.0 %collective-permute-start.11 = (bf16[2,4,64,1408]{3,2,1,0:T(8,128)(2,1)}, bf16[2,4,64,1408]{3,2,1,0:T(8,128)(2,1)}, u32[]{:S(2)}, u32[]{:S(2)}) collective-permute-start(bf16[2,4,64,1408]{3,2,1,0:T(8,128)(2,1)} %collective-permute-done.7), channel_id=1, source_target_pairs={{0,2},{1,3},{2,0},{3,1},{4,6},{5,7},{6,4},{7,5},{8,10},{9,11},{10,... | collective-permute-start | bytes 4325384 | tf_op jit(solution)/shard_map/ppermute | solution.py:29
  341.8 33.5 %collective-permute-start.10 = (bf16[2,4,64,1408]{3,2,1,0:T(8,128)(2,1)S(1)}, bf16[2,4,64,1408]{3,2,1,0:T(8,128)(2,1)}, u32[]{:S(2)}, u32[]{:S(2)}) collective-permute-start(bf16[2,4,64,1408]{3,2,1,0:T(8,128)(2,1)S(1)} %copy-done.41), channel_id=1, source_target_pairs={{0,4},{1,5},{2,6},{3,7},{4,0},{5,1},{6,2},{7,3},{8,12},{9,13},{10,... | collective-permute-start | bytes 4325384 | tf_op jit(solution)/shard_map/ppermute | solution.py:29
  387.3 8.5 collective-permute-start.14
  408.4 4.5 collective-permute-start.15
  409.0 58.5 %collective-permute-start.16 = (bf16[512,2048]{1,0:T(8,128)(2,1)}, bf16[512,2048]{1,0:T(8,128)(2,1)}, u32[]{:S(2)}, u32[]{:S(2)}) collective-permute-start(bf16[512,2048]{1,0:T(8,128)(2,1)} %multiply_convert_fusion), channel_id=1, source_target_pairs={{0,8},{1,9},{2,10},{3,11},{4,12},{5,13},{6,14},{7,15},{8,0},{9,1},... | collective-permute-start | bytes 6291464 | tf_op jit(solution)/shard_map/ppermute | solution.py:29
  467.4 7.4 collective-permute-start.17
  474.1 5.5 collective-permute-start.18
  475.0 54.9 %collective-permute-start.20 = (bf16[512,2048]{1,0:T(8,128)(2,1)}, bf16[512,2048]{1,0:T(8,128)(2,1)}, u32[]{:S(2)}, u32[]{:S(2)}) collective-permute-start(bf16[512,2048]{1,0:T(8,128)(2,1)} %slice.128), channel_id=1, source_target_pairs={{0,1},{1,0},{2,3},{3,2},{4,5},{5,4},{6,7},{7,6},{8,9},{9,8},{10,11... | collective-permute-start | bytes 6291464 | tf_op jit(solution)/shard_map/ppermute | solution.py:29
  475.1 54.8 %collective-permute-start.19 = (bf16[512,2048]{1,0:T(8,128)(2,1)}, bf16[512,2048]{1,0:T(8,128)(2,1)S(1)}, u32[]{:S(2)}, u32[]{:S(2)}) collective-permute-start(bf16[512,2048]{1,0:T(8,128)(2,1)} %slice.127), channel_id=1, source_target_pairs={{0,1},{1,0},{2,3},{3,2},{4,5},{5,4},{6,7},{7,6},{8,9},{9,8},{10,11... | collective-permute-start | bytes 6291464 | tf_op jit(solution)/shard_map/ppermute | solution.py:29
  533.2 18.0 %collective-permute-start.22 = (bf16[512,2048]{1,0:T(8,128)(2,1)}, bf16[512,2048]{1,0:T(8,128)(2,1)}, u32[]{:S(2)}, u32[]{:S(2)}) collective-permute-start(bf16[512,2048]{1,0:T(8,128)(2,1)} %slice.131), channel_id=1, source_target_pairs={{0,1},{1,0},{2,3},{3,2},{4,5},{5,4},{6,7},{7,6},{8,9},{9,8},{10,11... | collective-permute-start | bytes 6291464 | tf_op jit(solution)/shard_map/ppermute | solution.py:29
  534.8 16.4 %collective-permute-start.21 = (bf16[512,2048]{1,0:T(8,128)(2,1)}, bf16[512,2048]{1,0:T(8,128)(2,1)}, u32[]{:S(2)}, u32[]{:S(2)}) collective-permute-start(bf16[512,2048]{1,0:T(8,128)(2,1)} %slice.130), channel_id=1, source_target_pairs={{0,1},{1,0},{2,3},{3,2},{4,5},{5,4},{6,7},{7,6},{8,9},{9,8},{10,11... | collective-permute-start | bytes 6291464 | tf_op jit(solution)/shard_map/ppermute | solution.py:29
  549.8 72.0 %collective-permute-start.24 = (bf16[4,256,1408]{2,1,0:T(8,128)(2,1)}, bf16[4,256,1408]{2,1,0:T(8,128)(2,1)}, u32[]{:S(2)}, u32[]{:S(2)}) collective-permute-start(bf16[4,256,1408]{2,1,0:T(8,128)(2,1)} %bitcast.255), channel_id=1, source_target_pairs={{0,2},{1,3},{2,0},{3,1},{4,6},{5,7},{6,4},{7,5},{8,10},{9,11},{10,... | collective-permute-start | bytes 8650760 | tf_op jit(solution)/shard_map/ppermute | solution.py:29
  555.0 66.7 %collective-permute-start.23 = (bf16[512,2048]{1,0:T(8,128)(2,1)}, bf16[512,2048]{1,0:T(8,128)(2,1)}, u32[]{:S(2)}, u32[]{:S(2)}) collective-permute-start(bf16[512,2048]{1,0:T(8,128)(2,1)} %add_convert_fusion.2), channel_id=1, source_target_pairs={{0,8},{1,9},{2,10},{3,11},{4,12},{5,13},{6,14},{7,15},{8,0},{9,1},... | collective-permute-start | bytes 6291464 | tf_op jit(solution)/shard_map/ppermute | solution.py:29
  568.3 78.9 %collective-permute-start.26 = (bf16[4,256,1408]{2,1,0:T(8,128)(2,1)}, bf16[4,256,1408]{2,1,0:T(8,128)(2,1)}, u32[]{:S(2)}, u32[]{:S(2)}) collective-permute-start(bf16[4,256,1408]{2,1,0:T(8,128)(2,1)} %bitcast.254), channel_id=1, source_target_pairs={{0,4},{1,5},{2,6},{3,7},{4,0},{5,1},{6,2},{7,3},{8,12},{9,13},{10,... | collective-permute-start | bytes 8650760 | tf_op jit(solution)/shard_map/ppermute | solution.py:29
  632.8 14.4 %collective-permute-start.25 = (bf16[512,2048]{1,0:T(8,128)(2,1)S(1)}, bf16[512,2048]{1,0:T(8,128)(2,1)S(1)}, u32[]{:S(2)}, u32[]{:S(2)}) collective-permute-start(bf16[512,2048]{1,0:T(8,128)(2,1)S(1)} %get-tuple-element.403), channel_id=1, source_target_pairs={{0,1},{1,0},{2,3},{3,2},{4,5},{5,4},{6,7},{7,6},{8,9},{9,8},{10,11... | collective-permute-start | bytes 6291464 | tf_op jit(solution)/shard_map/ppermute | solution.py:29
  640.8 69.0 %collective-permute-start.27 = (bf16[2,256,1408]{2,1,0:T(8,128)(2,1)}, bf16[2,256,1408]{2,1,0:T(8,128)(2,1)}, u32[]{:S(2)}, u32[]{:S(2)}) collective-permute-start(bf16[2,256,1408]{2,1,0:T(8,128)(2,1)} %fusion.18), channel_id=1, source_target_pairs={{0,4},{1,5},{2,6},{3,7},{4,0},{5,1},{6,2},{7,3},{8,12},{9,13},{10,... | collective-permute-start | bytes 4325384 | tf_op jit(solution)/shard_map/ppermute | solution.py:29
  659.7 60.7 %collective-permute-start.28 = (bf16[2,256,1408]{2,1,0:T(8,128)(2,1)}, bf16[2,256,1408]{2,1,0:T(8,128)(2,1)}, u32[]{:S(2)}, u32[]{:S(2)}) collective-permute-start(bf16[2,256,1408]{2,1,0:T(8,128)(2,1)} %fusion.19), channel_id=1, source_target_pairs={{0,2},{1,3},{2,0},{3,1},{4,6},{5,7},{6,4},{7,5},{8,10},{9,11},{10,... | collective-permute-start | bytes 4325384 | tf_op jit(solution)/shard_map/ppermute | solution.py:29
  660.7 64.1 %collective-permute-start.29 = (bf16[4,176,1024]{2,1,0:T(8,128)(2,1)}, bf16[4,176,1024]{2,1,0:T(8,128)(2,1)}, u32[]{:S(2)}, u32[]{:S(2)}) collective-permute-start(bf16[4,176,1024]{2,1,0:T(8,128)(2,1)} %get-tuple-element.297), channel_id=1, source_target_pairs={{0,2},{1,3},{2,0},{3,1},{4,6},{5,7},{6,4},{7,5},{8,10},{9,11},{10,... | collective-permute-start | bytes 4325384 | tf_op jit(solution)/shard_map/ppermute | solution.py:29
  661.7 63.1 %collective-permute-start.30 = (bf16[4,176,1024]{2,1,0:T(8,128)(2,1)}, bf16[4,176,1024]{2,1,0:T(8,128)(2,1)}, u32[]{:S(2)}, u32[]{:S(2)}) collective-permute-start(bf16[4,176,1024]{2,1,0:T(8,128)(2,1)} %bitcast.48), channel_id=1, source_target_pairs={{0,4},{1,5},{2,6},{3,7},{4,0},{5,1},{6,2},{7,3},{8,12},{9,13},{10,... | collective-permute-start | bytes 4325384 | tf_op jit(solution)/shard_map/ppermute | solution.py:29
  709.8 63.0 %collective-permute-start.31 = (bf16[512,2048]{1,0:T(8,128)(2,1)}, bf16[512,2048]{1,0:T(8,128)(2,1)}, u32[]{:S(2)}, u32[]{:S(2)}) collective-permute-start(bf16[512,2048]{1,0:T(8,128)(2,1)} %add_convert_fusion.1), channel_id=1, source_target_pairs={{0,8},{1,9},{2,10},{3,11},{4,12},{5,13},{6,14},{7,15},{8,0},{9,1},... | collective-permute-start | bytes 6291464 | tf_op jit(solution)/shard_map/ppermute | solution.py:29
  717.1 152.2 %collective-permute-start.36 = (bf16[1,256,1408]{2,1,0:T(8,128)(2,1)}, bf16[1,256,1408]{2,1,0:T(8,128)(2,1)}, u32[]{:S(2)}, u32[]{:S(2)}) collective-permute-start(bf16[1,256,1408]{2,1,0:T(8,128)(2,1)} %dynamic-slice_convert_fusion.2), channel_id=1, source_target_pairs={{0,16},{1,17},{2,18},{3,19},{4,20},{5,21},{6,22},{7,23},{8,24},{9,... | collective-permute-start | bytes 2162696 | tf_op jit(solution)/shard_map/ppermute | solution.py:29
  727.8 103.7 %collective-permute-start.32 = (bf16[2,176,1024]{2,1,0:T(8,128)(2,1)}, bf16[2,176,1024]{2,1,0:T(8,128)(2,1)}, u32[]{:S(2)}, u32[]{:S(2)}) collective-permute-start(bf16[2,176,1024]{2,1,0:T(8,128)(2,1)} %fusion.23), channel_id=1, source_target_pairs={{0,4},{1,5},{2,6},{3,7},{4,0},{5,1},{6,2},{7,3},{8,12},{9,13},{10,... | collective-permute-start | bytes 2162696 | tf_op jit(solution)/shard_map/ppermute | solution.py:29
  732.6 100.5 %collective-permute-start.33 = (bf16[2,176,1024]{2,1,0:T(8,128)(2,1)}, bf16[2,176,1024]{2,1,0:T(8,128)(2,1)}, u32[]{:S(2)}, u32[]{:S(2)}) collective-permute-start(bf16[2,176,1024]{2,1,0:T(8,128)(2,1)} %fusion.24), channel_id=1, source_target_pairs={{0,2},{1,3},{2,0},{3,1},{4,6},{5,7},{6,4},{7,5},{8,10},{9,11},{10,... | collective-permute-start | bytes 2162696 | tf_op jit(solution)/shard_map/ppermute | solution.py:29
  744.0 124.9 %collective-permute-start.34 = (bf16[8,128,512]{2,1,0:T(8,128)(2,1)}, bf16[8,128,512]{2,1,0:T(8,128)(2,1)}, u32[]{:S(2)}, u32[]{:S(2)}) collective-permute-start(bf16[8,128,512]{2,1,0:T(8,128)(2,1)} %bitcast.259), channel_id=1, source_target_pairs={{0,2},{1,3},{2,0},{3,1},{4,6},{5,7},{6,4},{7,5},{8,10},{9,11},{10,... | collective-permute-start | bytes 3145736 | tf_op jit(solution)/shard_map/ppermute | solution.py:29
  772.7 96.6 %collective-permute-start.35 = (bf16[8,128,512]{2,1,0:T(8,128)(2,1)}, bf16[8,128,512]{2,1,0:T(8,128)(2,1)}, u32[]{:S(2)}, u32[]{:S(2)}) collective-permute-start(bf16[8,128,512]{2,1,0:T(8,128)(2,1)} %bitcast.258), channel_id=1, source_target_pairs={{0,4},{1,5},{2,6},{3,7},{4,0},{5,1},{6,2},{7,3},{8,12},{9,13},{10,... | collective-permute-start | bytes 3145736 | tf_op jit(solution)/shard_map/ppermute | solution.py:29
  831.5 41.0 %collective-permute-start.37 = (bf16[1,256,1408]{2,1,0:T(8,128)(2,1)}, bf16[1,256,1408]{2,1,0:T(8,128)(2,1)}, u32[]{:S(2)}, u32[]{:S(2)}) collective-permute-start(bf16[1,256,1408]{2,1,0:T(8,128)(2,1)} %dynamic-slice_convert_fusion.1), channel_id=1, source_target_pairs={{0,16},{1,17},{2,18},{3,19},{4,20},{5,21},{6,22},{7,23},{8,24},{9,... | collective-permute-start | bytes 2162696 | tf_op jit(solution)/shard_map/ppermute | solution.py:29
  833.9 50.3 %collective-permute-start.38 = (bf16[1,176,1024]{2,1,0:T(8,128)(2,1)}, bf16[1,176,1024]{2,1,0:T(8,128)(2,1)}, u32[]{:S(2)}, u32[]{:S(2)}) collective-permute-start(bf16[1,176,1024]{2,1,0:T(8,128)(2,1)} %dynamic-slice_convert_fusion.10), channel_id=1, source_target_pairs={{0,16},{1,17},{2,18},{3,19},{4,20},{5,21},{6,22},{7,23},{8,24},{9,... | collective-permute-start | bytes 1081352 | tf_op jit(solution)/shard_map/ppermute | solution.py:29
  868.8 22.9 %collective-permute-start.39 = (bf16[1,176,1024]{2,1,0:T(8,128)(2,1)}, bf16[1,176,1024]{2,1,0:T(8,128)(2,1)S(1)}, u32[]{:S(2)}, u32[]{:S(2)}) collective-permute-start(bf16[1,176,1024]{2,1,0:T(8,128)(2,1)} %dynamic-slice_convert_fusion.9), channel_id=1, source_target_pairs={{0,16},{1,17},{2,18},{3,19},{4,20},{5,21},{6,22},{7,23},{8,24},{9,... | collective-permute-start | bytes 1081352 | tf_op jit(solution)/shard_map/ppermute | solution.py:29
  878.3 32.6 %collective-permute-start.44 = (bf16[2,64,1408]{2,1,0:T(8,128)(2,1)}, bf16[2,64,1408]{2,1,0:T(8,128)(2,1)S(1)}, u32[]{:S(2)}, u32[]{:S(2)}) collective-permute-start(bf16[2,64,1408]{2,1,0:T(8,128)(2,1)} %get-tuple-element.411), channel_id=1, source_target_pairs={{0,9},{1,8},{2,11},{3,10},{4,13},{5,12},{6,15},{7,14},{8,1},{9,0},... | collective-permute-start | bytes 1081352 | tf_op jit(solution)/shard_map/ppermute | solution.py:29
  878.3 32.6 %collective-permute-start.43 = (bf16[2,64,1408]{2,1,0:T(8,128)(2,1)}, bf16[2,64,1408]{2,1,0:T(8,128)(2,1)}, u32[]{:S(2)}, u32[]{:S(2)}) collective-permute-start(bf16[2,64,1408]{2,1,0:T(8,128)(2,1)} %get-tuple-element.413), channel_id=1, source_target_pairs={{0,8},{1,9},{2,10},{3,11},{4,12},{5,13},{6,14},{7,15},{8,0},{9,1},... | collective-permute-start | bytes 1081352 | tf_op jit(solution)/shard_map/ppermute | solution.py:29
  879.3 31.7 %collective-permute-start.42 = (bf16[2,64,1408]{2,1,0:T(8,128)(2,1)}, bf16[2,64,1408]{2,1,0:T(8,128)(2,1)}, u32[]{:S(2)}, u32[]{:S(2)}) collective-permute-start(bf16[2,64,1408]{2,1,0:T(8,128)(2,1)} %get-tuple-element.412), channel_id=1, source_target_pairs={{0,1},{1,0},{2,3},{3,2},{4,5},{5,4},{6,7},{7,6},{8,9},{9,8},{10,11... | collective-permute-start | bytes 1081352 | tf_op jit(solution)/shard_map/ppermute | solution.py:29
  884.2 26.8 %collective-permute-start.40 = (bf16[4,128,512]{2,1,0:T(8,128)(2,1)S(1)}, bf16[4,128,512]{2,1,0:T(8,128)(2,1)S(1)}, u32[]{:S(2)}, u32[]{:S(2)}) collective-permute-start(bf16[4,128,512]{2,1,0:T(8,128)(2,1)S(1)} %fusion.38), channel_id=1, source_target_pairs={{0,4},{1,5},{2,6},{3,7},{4,0},{5,1},{6,2},{7,3},{8,12},{9,13},{10,... | collective-permute-start | bytes 1572872 | tf_op jit(solution)/shard_map/ppermute | solution.py:29
  891.7 19.3 %collective-permute-start.41 = (bf16[4,128,512]{2,1,0:T(8,128)(2,1)S(1)}, bf16[4,128,512]{2,1,0:T(8,128)(2,1)S(1)}, u32[]{:S(2)}, u32[]{:S(2)}) collective-permute-start(bf16[4,128,512]{2,1,0:T(8,128)(2,1)S(1)} %fusion.39), channel_id=1, source_target_pairs={{0,2},{1,3},{2,0},{3,1},{4,6},{5,7},{6,4},{7,5},{8,10},{9,11},{10,... | collective-permute-start | bytes 1572872 | tf_op jit(solution)/shard_map/ppermute | solution.py:29
  921.2 6.7 collective-permute-start.45
  923.8 31.2 %collective-permute-start.46 = (bf16[8,128,640]{2,1,0:T(8,128)(2,1)S(1)}, bf16[8,128,640]{2,1,0:T(8,128)(2,1)S(1)}, u32[]{:S(2)}, u32[]{:S(2)}) collective-permute-start(bf16[8,128,640]{2,1,0:T(8,128)(2,1)S(1)} %bitcast.257), channel_id=1, source_target_pairs={{0,2},{1,3},{2,0},{3,1},{4,6},{5,7},{6,4},{7,5},{8,10},{9,11},{10,... | collective-permute-start | bytes 3932168 | tf_op jit(solution)/shard_map/ppermute | solution.py:29
  924.8 30.9 %collective-permute-start.47 = (bf16[8,128,640]{2,1,0:T(8,128)(2,1)S(1)}, bf16[8,128,640]{2,1,0:T(8,128)(2,1)S(1)}, u32[]{:S(2)}, u32[]{:S(2)}) collective-permute-start(bf16[8,128,640]{2,1,0:T(8,128)(2,1)S(1)} %bitcast.256), channel_id=1, source_target_pairs={{0,4},{1,5},{2,6},{3,7},{4,0},{5,1},{6,2},{7,3},{8,12},{9,13},{10,... | collective-permute-start | bytes 3932168 | tf_op jit(solution)/shard_map/ppermute | solution.py:29
  925.8 29.9 %collective-permute-start.48 = (bf16[2,128,1024]{2,1,0:T(8,128)(2,1)S(1)}, bf16[2,128,1024]{2,1,0:T(8,128)(2,1)S(1)}, u32[]{:S(2)}, u32[]{:S(2)}) collective-permute-start(bf16[2,128,1024]{2,1,0:T(8,128)(2,1)S(1)} %fusion.40), channel_id=1, source_target_pairs={{0,8},{1,9},{2,10},{3,11},{4,12},{5,13},{6,14},{7,15},{8,0},{9,1},... | collective-permute-start | bytes 1572872 | tf_op jit(solution)/shard_map/ppermute | solution.py:29
  958.3 16.6 %collective-permute-start.52 = (bf16[4,128,640]{2,1,0:T(8,128)(2,1)}, bf16[4,128,640]{2,1,0:T(8,128)(2,1)}, u32[]{:S(2)}, u32[]{:S(2)}) collective-permute-start(bf16[4,128,640]{2,1,0:T(8,128)(2,1)} %fusion.36), channel_id=1, source_target_pairs={{0,2},{1,3},{2,0},{3,1},{4,6},{5,7},{6,4},{7,5},{8,10},{9,11},{10,... | collective-permute-start | bytes 1966088 | tf_op jit(solution)/shard_map/ppermute | solution.py:29
  959.3 16.1 %collective-permute-start.51 = (bf16[4,128,640]{2,1,0:T(8,128)(2,1)}, bf16[4,128,640]{2,1,0:T(8,128)(2,1)}, u32[]{:S(2)}, u32[]{:S(2)}) collective-permute-start(bf16[4,128,640]{2,1,0:T(8,128)(2,1)} %fusion.35), channel_id=1, source_target_pairs={{0,4},{1,5},{2,6},{3,7},{4,0},{5,1},{6,2},{7,3},{8,12},{9,13},{10,... | collective-permute-start | bytes 1966088 | tf_op jit(solution)/shard_map/ppermute | solution.py:29
  961.3 1.2 collective-permute-start.49
  962.5 12.4 %collective-permute-start.50 = (f32[2,2048]{1,0:T(2,128)S(1)}, f32[2,2048]{1,0:T(2,128)S(1)}, u32[]{:S(2)}, u32[]{:S(2)}) collective-permute-start(f32[2,2048]{1,0:T(2,128)S(1)} %add.520), channel_id=1, source_target_pairs={{0,2},{1,3},{2,0},{3,1},{4,6},{5,7},{6,4},{7,5},{8,10},{9,11},{10,... | collective-permute-start | bytes 49160 | tf_op jit(solution)/shard_map/ppermute | solution.py:29
  977.6 22.3 %collective-permute-start.54 = (bf16[2,128,1280]{2,1,0:T(8,128)(2,1)S(1)}, bf16[2,128,1280]{2,1,0:T(8,128)(2,1)}, u32[]{:S(2)}, u32[]{:S(2)}) collective-permute-start(bf16[2,128,1280]{2,1,0:T(8,128)(2,1)S(1)} %fusion.37), channel_id=1, source_target_pairs={{0,8},{1,9},{2,10},{3,11},{4,12},{5,13},{6,14},{7,15},{8,0},{9,1},... | collective-permute-start | bytes 1966088 | tf_op jit(solution)/shard_map/ppermute | solution.py:29
  977.7 43.7 %collective-permute-start.58 = (bf16[1,128,1024]{2,1,0:T(8,128)(2,1)}, bf16[1,128,1024]{2,1,0:T(8,128)(2,1)S(1)}, u32[]{:S(2)}, u32[]{:S(2)}) collective-permute-start(bf16[1,128,1024]{2,1,0:T(8,128)(2,1)} %dynamic-slice_convert_fusion.12), channel_id=1, source_target_pairs={{0,16},{1,17},{2,18},{3,19},{4,20},{5,21},{6,22},{7,23},{8,24},{9,... | collective-permute-start | bytes 786440 | tf_op jit(solution)/shard_map/ppermute | solution.py:29
  980.3 18.8 %collective-permute-start.53 = (f32[2,2048]{1,0:T(2,128)S(1)}, f32[2,2048]{1,0:T(2,128)}, u32[]{:S(2)}, u32[]{:S(2)}) collective-permute-start(f32[2,2048]{1,0:T(2,128)S(1)} %add.521), channel_id=1, source_target_pairs={{0,4},{1,5},{2,6},{3,7},{4,0},{5,1},{6,2},{7,3},{8,12},{9,13},{10,... | collective-permute-start | bytes 49160 | tf_op jit(solution)/shard_map/ppermute | solution.py:29
  1001.5 19.9 %collective-permute-start.57 = (bf16[1,128,1280]{2,1,0:T(8,128)(2,1)S(1)}, bf16[1,128,1280]{2,1,0:T(8,128)(2,1)S(1)}, u32[]{:S(2)}, u32[]{:S(2)}) collective-permute-start(bf16[1,128,1280]{2,1,0:T(8,128)(2,1)S(1)} %dynamic-slice_convert_fusion.11), channel_id=1, source_target_pairs={{0,16},{1,17},{2,18},{3,19},{4,20},{5,21},{6,22},{7,23},{8,24},{9,... | collective-permute-start | bytes 983048 | tf_op jit(solution)/shard_map/ppermute | solution.py:29
  1002.6 14.4 %collective-permute-start.55 = (f32[2,2048]{1,0:T(2,128)S(1)}, f32[2,2048]{1,0:T(2,128)S(1)}, u32[]{:S(2)}, u32[]{:S(2)}) collective-permute-start(f32[2,2048]{1,0:T(2,128)S(1)} %add.524), channel_id=1, source_target_pairs={{0,16},{1,17},{2,18},{3,19},{4,20},{5,21},{6,22},{7,23},{8,24},{9,... | collective-permute-start | bytes 49160 | tf_op jit(solution)/shard_map/ppermute | solution.py:29
  1017.0 3.8 collective-permute-start.56
  1021.7 2.1 collective-permute-start.59
  (92 other events, 692.1 us)
Sparse Core Ops, SparseCore 0:
  135.9 117.7 all-gather.1

commit v4 on v3

--- a/solution.py
+++ b/solution.py
@@ -10,7 +10,7 @@
 PAIR = 8
 FEATS = 160
 ROWS = 168
-VMEM = 56 * 1024 * 1024
+MIB = 1024 * 1024
 eps = 1e-06
 f32 = jnp.float32
 bf16 = jnp.bfloat16
@@ -94,14 +94,17 @@
         return x
 
     def step(self, *gate):
-        acc = self.kept.astype(f32) + after(self.here, *gate).astype(f32)
+        kept, here = self.kept, after(self.here, *gate)
         self.bits = self.bits[:-1]
         if not self.bits:
-            return acc[0]
+            return (kept.astype(f32) + here.astype(f32))[0]
         bit = self.bits[-1]
-        acc = acc.reshape((-1, 2) + acc.shape[1:])
-        self.sent = pick(acc, 1 - side(bit), 1).astype(bf16)
-        self.kept = pick(acc, side(bit), 1)
+
+        def half(index):
+            return sum(pick(a.reshape((-1, 2) + a.shape[1:]), index, 1).astype(f32) for a in (kept, here))
+
+        self.sent = half(1 - side(bit)).astype(bf16)
+        self.kept = half(side(bit))
         self.here = flip(self.sent, bit)
         return self.sent
 
@@ -109,6 +112,13 @@
         while len(self.bits) > 1:
             self.step(*gate)
         return self.step(*gate)
+
+
+def join(both):
+    out = Scatter(None, both[0].bits[:-1] + [0])
+    out.kept = jnp.concatenate([part.kept for part in both], axis=2)
+    out.here = jnp.concatenate([part.here for part in both], axis=2)
+    return out
 
 
 MESH = pl.DeviceIdType.MESH
@@ -151,7 +161,7 @@
             copy.wait_send()
 
 
-def first_body(gains_in, gate_in, up_in, mine, theirs, gains, gate, up, z4, chip, sems):
+def first_body(gains_in, gate_in, up_in, mine, theirs, down_in, gains, gate, up, z4, down, chip, sems):
     me = lax.axis_index("tok")
     core, z = me % 2, me // 8
     meet(me, (1, 2, 4, 8, 9, 16))
@@ -164,13 +174,21 @@
     def member(d):
         return ((d // 8) % 2) * 2 + d % 2
 
+    place = (me // 2) % 4
+    cut = down_in.shape[1] // 2
+    a, b = pl.ds(0, cut), pl.ds(cut, cut)
+    xa = mail.send(down_in.at[:, a], down.at[place, :, a], 2)
+    yb = mail.send(down_in.at[:, b], down.at[place, :, b], 4)
     to_gate = [mail.send(gate_in.at[member(across(me, k))], gate.at[member(me)], k) for k in (9, 8, 1)]
     own.wait()
     swap.wait_recv()
     high = mail.send(chip, z4.at[z], 16)
     low = mail.send(chip, z4.at[z], 8)
     to_up = [mail.send(up_in.at[member(across(me, k))], up.at[member(me)], k) for k in (9, 8, 1)]
+    ya = mail.send(down_in.at[:, a], down.at[place, :, a], 4)
+    xb = mail.send(down_in.at[:, b], down.at[place, :, b], 2)
     kept = [
+        mail.local(down_in, down.at[place]),
         mail.local(chip, z4.at[z]),
         mail.local(gate_in.at[member(me)], gate.at[member(me)]),
         mail.local(up_in.at[member(me)], up.at[member(me)]),
@@ -181,17 +199,22 @@
     high.wait_recv()
     zh = across(me, 16) // 8
     low2 = mail.send(z4.at[zh], z4.at[zh], 8)
+    across_x, across_y = across(place, 1), across(place, 2)
+    xa.wait_recv()
+    ya2 = mail.send(down.at[across_x, :, a], down.at[across_x, :, a], 4)
+    yb.wait_recv()
+    xb2 = mail.send(down.at[across_y, :, b], down.at[across_y, :, b], 2)
     for bit in (8, 16):
         at = pl.ds((me // bit) * bit, bit)
         mail.send(gains.at[at], gains.at[at], bit).wait_recv()
-    for c in to_gate + to_up + [low, low2]:
+    for c in to_gate + to_up + [low, low2, ya, xb, ya2, xb2]:
         c.wait_recv()
     for c in kept:
         c.wait()
     mail.close()
 
 
-def spread_first(gains, gate, up, mine, theirs):
+def spread_first(gains, gate, up, mine, theirs, down):
     rows, cols = mine.shape
     return pl.pallas_call(
         first_body,
@@ -200,12 +223,13 @@
             jax.ShapeDtypeStruct(gate.shape, bf16),
             jax.ShapeDtypeStruct(up.shape, bf16),
             jax.ShapeDtypeStruct((4, 2 * rows, cols), bf16),
+            jax.ShapeDtypeStruct((4,) + down.shape, bf16),
         ],
-        in_specs=[INV] * 5,
-        out_specs=[INV] * 4,
-        scratch_shapes=[pltpu.VMEM((2 * rows, cols), bf16), pltpu.SemaphoreType.DMA((2, 20))],
-        compiler_params=pltpu.CompilerParams(collective_id=1, has_side_effects=True, vmem_limit_bytes=40 * 2**20),
-    )(gains, gate, up, mine, theirs)
+        in_specs=[INV] * 6,
+        out_specs=[INV] * 5,
+        scratch_shapes=[pltpu.VMEM((2 * rows, cols), bf16), pltpu.SemaphoreType.DMA((2, 28))],
+        compiler_params=pltpu.CompilerParams(collective_id=1, has_side_effects=True, vmem_limit_bytes=20 * MIB),
+    )(gains, gate, up, mine, theirs, down)
 
 
 def second_body(z4, out_mine, out_theirs, gate, whole, out4, gate2, chip, sems):
@@ -255,7 +279,7 @@
         in_specs=[INV] * 4,
         out_specs=[INV] * 3,
         scratch_shapes=[pltpu.VMEM((2 * rows, cols), bf16), pltpu.SemaphoreType.DMA((2, 16))],
-        compiler_params=pltpu.CompilerParams(collective_id=2, has_side_effects=True, vmem_limit_bytes=40 * 2**20),
+        compiler_params=pltpu.CompilerParams(collective_id=2, has_side_effects=True, vmem_limit_bytes=20 * MIB),
     )(z4, out_mine, out_theirs, gate)
 
 
@@ -343,13 +367,20 @@
 
 
 def ffn_body(order, sides, x_ref, g_ref, *refs):
-    gates, ups, down = refs[0:4], refs[4:8], refs[8]
-    y_ref, act_ref, d_ref, dh_ref, w_gate_up, w_down, sem = refs[9:]
+    gates, ups, downs = refs[0:4], refs[4:8], refs[8:11]
+    y_ref, act_ref, d_ref, dh_ref, w_gate_up, w_down, sem = refs[11:]
     cols = w_down.shape[0]
 
     @pl.when(pl.program_id(0) == 0)
     def _():
-        copies = [pltpu.make_async_copy(down, w_down, sem.at[0])]
+        size, part, rest = downs[0].shape[0], downs[1].shape[1], downs[2].shape[1]
+        far = pl.ds(pl.multiple_of((1 - sides[4]) * size, 16), size)
+        targets = [
+            w_down.at[pl.ds(pl.multiple_of(sides[4] * size, 16), size)],
+            w_down.at[far, pl.ds(0, part)],
+            w_down.at[far, pl.ds(part, rest)],
+        ]
+        copies = [pltpu.make_async_copy(a, b, sem.at[i]) for i, (a, b) in enumerate(zip(downs, targets))]
         size = gates[0].shape[1]
         for j, pieces in enumerate((gates, ups)):
             for k, piece in enumerate(pieces):
@@ -377,7 +408,7 @@
 
 def ffn(x, g, gate, up, down, order, sides, tile=256):
     tokens, width = x.shape
-    cols = down.shape[0]
+    cols = 2 * down[0].shape[0]
 
     def block(w):
         return pl.BlockSpec((tile, w), lambda i: (i, 0))
@@ -386,70 +417,68 @@
         lambda *refs: ffn_body(order, *refs),
         out_shape=[jax.ShapeDtypeStruct((tokens, w), bf16) for w in (width, cols, 2 * cols, width)],
         grid=(tokens // tile,),
-        in_specs=[pl.BlockSpec(memory_space=pltpu.SMEM), block(width), block(width)] + [pl.BlockSpec(memory_space=pl.ANY)] * 9,
+        in_specs=[pl.BlockSpec(memory_space=pltpu.SMEM), block(width), block(width)] + [pl.BlockSpec(memory_space=pl.ANY)] * 11,
         out_specs=[block(width), block(cols), block(2 * cols), block(width)],
         scratch_shapes=[
             pltpu.VMEM((width, 2 * cols), bf16),
             pltpu.VMEM((cols, width), bf16),
-            pltpu.SemaphoreType.DMA((8 * len(order) + 1,)),
+            pltpu.SemaphoreType.DMA((8 * len(order) + 3,)),
         ],
-        compiler_params=pltpu.CompilerParams(vmem_limit_bytes=VMEM),
+        compiler_params=pltpu.CompilerParams(vmem_limit_bytes=48 * MIB),
         cost_estimate=pl.CostEstimate(flops=0, bytes_accessed=0, transcendentals=0),
-    )(sides, x, g, *gate, *up, down)
-
-
-def product_body(count, index, *refs):
-    left, right, out = refs[:count], refs[count : 2 * count], refs[2 * count]
-    out[...] = sum(dot_rows(a[...], b[...]) for a, b in zip(left, right)).astype(out.dtype)
+    )(sides, x, g, *gate, *up, *down)
+
+
+def product_body(count, group, index, *refs):
+    left, right, out = refs[: count * group], refs[count * group : -1], refs[-1]
+    acc = 0.0
+    for i in range(count):
+        rows = jnp.concatenate([a[...] for a in left[i * group : (i + 1) * group]], axis=1)
+        acc = acc + dot_rows(rows, right[i][...])
+    out[...] = acc.astype(out.dtype)
 
 
 def row_blocks(left, right, index, size, half=None):
     count = index.shape[0]
+    group = 4 if count % 4 == 0 else 1
     cols = right[0].shape[1] // (1 if half is None else 2)
     at_col = half or 0
-    tokens = sum(a.shape[0] for a in left)
+
+    def block(tokens, j):
+        return pl.BlockSpec((tokens, size), lambda i, at: (0, at[i * group + j]))
+
     return pl.pallas_call(
-        lambda *refs: product_body(len(left), *refs),
+        lambda *refs: product_body(len(left), group, *refs),
         out_shape=jax.ShapeDtypeStruct((count * size, cols), bf16),
         grid_spec=pltpu.PrefetchScalarGridSpec(
             num_scalar_prefetch=1,
-            grid=(count,),
-            in_specs=[pl.BlockSpec((a.shape[0], size), lambda i, at: (0, at[i])) for a in left]
+            grid=(count // group,),
+            in_specs=[block(a.shape[0], j) for a in left for j in range(group)]
             + [pl.BlockSpec((b.shape[0], cols), lambda i, at: (0, at_col)) for b in right],
-            out_specs=pl.BlockSpec((size, cols), lambda i, at: (i, 0)),
+            out_specs=pl.BlockSpec((group * size, cols), lambda i, at: (i, 0)),
         ),
-        compiler_params=pltpu.CompilerParams(vmem_limit_bytes=VMEM),
+        compiler_params=pltpu.CompilerParams(vmem_limit_bytes=56 * MIB),
         cost_estimate=pl.CostEstimate(flops=0, bytes_accessed=0, transcendentals=0),
-    )(index, x, g, gate_up, *down)
-
-
-def product_body(count, index, *refs):
-    left, right, out = refs[:count], refs[count : 2 * count], refs[2 * count]
-    out[...] = sum(dot_rows(a[...], b[...]) for a, b in zip(left, right)).astype(out.dtype)
-
-
-def row_blocks(left, right, index, size, half=None):
-    count = index.shape[0]
-    cols = right[0].shape[1] // (1 if half is None else 2)
-    at_col = half or 0
-    tokens = sum(a.shape[0] for a in left)
+    )(index.astype(jnp.int32), *[a for a in left for _ in range(group)], *right)
+
+
+def wide_body(d_ref, w_ref, out_ref):
+    out_ref[...] = dot_cols(d_ref[...], w_ref[...]).astype(bf16)
+
+
+def times_transposed(d, w, tile=256):
     return pl.pallas_call(
-        lambda *refs: product_body(len(left), *refs),
-        out_shape=jax.ShapeDtypeStruct((count * size, cols), bf16),
-        grid_spec=pltpu.PrefetchScalarGridSpec(
-            num_scalar_prefetch=1,
-            grid=(count,),
-            in_specs=[pl.BlockSpec((a.shape[0], size), lambda i, at: (0, at[i])) for a in left]
-            + [pl.BlockSpec((b.shape[0], cols), lambda i, at: (0, at_col)) for b in right],
-            out_specs=pl.BlockSpec((size, cols), lambda i, at: (i, 0)),
-        ),
-        compiler_params=pltpu.CompilerParams(vmem_limit_bytes=VMEM),
-        cost_estimate=pl.CostEstimate(
-            flops=2 * tokens * count * size * cols,
-            bytes_accessed=2 * (tokens * cols + count * size * (tokens + cols)),
-            transcendentals=0,
-        ),
-    )(index.astype(jnp.int32), *left, *right)
+        wide_body,
+        out_shape=jax.ShapeDtypeStruct((d.shape[0], w.shape[0]), bf16),
+        grid=(d.shape[0] // tile,),
+        in_specs=[
+            pl.BlockSpec((tile, d.shape[1]), lambda i: (i, 0)),
+            pl.BlockSpec(w.shape, lambda i: (0, 0)),
+        ],
+        out_specs=pl.BlockSpec((tile, w.shape[0]), lambda i: (i, 0)),
+        compiler_params=pltpu.CompilerParams(vmem_limit_bytes=48 * MIB),
+        cost_estimate=pl.CostEstimate(flops=0, bytes_accessed=0, transcendentals=0),
+    )(d, w)
 
 
 def part_maker(left, right, bits, within=(0,), half=None):
@@ -673,8 +702,7 @@
     def narrow(self, kind):
         return jax.ShapeDtypeStruct((2 * self.tokens, self.heads * QK), kind)
 
-    def call(self, body, ins, outs, shapes, scratch, flops, args):
-        size = sum(int(np.prod(a.shape)) * a.dtype.itemsize for a in list(args) + list(shapes))
+    def call(self, body, ins, outs, shapes, scratch, limit, args):
         return pl.pallas_call(
             body,
             grid=(2, self.heads),
@@ -682,7 +710,7 @@
             out_specs=outs,
             out_shape=shapes,
             scratch_shapes=scratch,
-            compiler_params=pltpu.CompilerParams(vmem_limit_bytes=VMEM),
+            compiler_params=pltpu.CompilerParams(vmem_limit_bytes=limit * MIB),
             cost_estimate=pl.CostEstimate(flops=0, bytes_accessed=0, transcendentals=0),
         )(*args)
 
@@ -693,7 +721,7 @@
             [self.s],
             [self.state_shape],
             [],
-            3 * 10**9,
+            24,
             (self.scal, self.qkv, self.qkv, *self.tables),
         )
         return out
@@ -705,7 +733,7 @@
             [self.o, self.o],
             [self.wide(f32), self.wide(bf16)],
             [],
-            10 * 10**9,
+            48,
             (self.qkv, self.qkv, self.qkv, self.lo, carry, *self.tables),
         )
 
@@ -716,7 +744,7 @@
             [self.q, self.q, self.o, self.s],
             [self.narrow(bf16), self.narrow(f32), self.wide(f32), self.state_shape],
             [self.acc, self.acc],
-            30 * 10**9,
+            48,
             (self.qkv, self.qkv, self.qkv, self.lo, carry, *self.tables, y, d_heads),
         )
 
@@ -727,7 +755,7 @@
             [self.q, self.o],
             [self.narrow(bf16), self.wide(bf16)],
             [self.acc],
-            10 * 10**9,
+            48,
             (self.scal, self.qkv, self.qkv, *self.tables, grad, dk, dv),
         )
 
@@ -751,7 +779,7 @@
         out_specs=INV,
         scratch_shapes=[slots, slots, pltpu.VMEM(block, kind), slots, slots, slots, pltpu.SemaphoreType.DMA((3, 2, 3))],
         compiler_params=pltpu.CompilerParams(
-            collective_id=3 if earlier else 4, has_side_effects=True, vmem_limit_bytes=VMEM
+            collective_id=3 if earlier else 4, has_side_effects=True, vmem_limit_bytes=16 * MIB
         ),
         cost_estimate=pl.CostEstimate(flops=0, bytes_accessed=0, transcendentals=0),
     )(state)
@@ -829,7 +857,7 @@
     if n == 32:
         gains = jnp.pad(gains, ((0, 6), (0, 128 - rows)))[None]
         gains = after(gains, near_grad)
-        gains, gate, up, qkv_all = spread_first(gains, gate, up, by_core(core), by_core(1 - core))
+        gains, gate, up, qkv_all, down = spread_first(gains, gate, up, by_core(core), by_core(1 - core), down)
         gains = gains[:, :2, :rows].transpose(1, 0, 2).reshape(2, 1, width)
         z4 = qkv_all
         qkv_all, out_half, gate = spread_second(z4, column_half(w_out, core), column_half(w_out, 1 - core), gate)
@@ -854,6 +882,9 @@
             out_half = grow(out_half, bit)
         out_half = in_order(out_half, cbits[:-2])
         gate = grow(gate, qbits[0])
+        for bit in qbits[1:]:
+            down = grow(down, bit)
+        down = in_order(down, qbits[1:])
     gain_one, gain_two = gains[0], gains[1]
 
     inputs32 = block_input.astype(f32)
@@ -872,7 +903,6 @@
     fresh1 = (lo[2 * tokens - 1] >= tokens).astype(f32)
 
     start, stop = (qkv_all,), (states,)
-    down = lax.all_gather(after(down, qkv_all), "tok", axis=0, tiled=True, axis_index_groups=groups)
     for bit in qbits[1:-2]:
         gate = grow(gate, bit)
     gate_x = move(gate, 2, start, stop)
@@ -884,12 +914,17 @@
     leaving, gate_x, up, out_y = lax.optimization_barrier((leaving, gate_x, up, out_y))
     entering = others(leaving, True, f32)
     start, stop = (leaving,), (entering,)
-    flows = [(out_half, 2), (out_y, 2), (up, 4), (gate, 4), (up, 2)]
+    down = down.reshape(cols // 2, width)
+    down_a, down_b = down[:, : width * 3 // 4], down[:, width * 3 // 4 :]
+    out_both = jnp.stack([out_half, out_y])
+    gate_up = jnp.concatenate([gate, up], axis=-1)
+    flows = [(out_both, 2), (gate_up, 4), (up, 2), (down_a, qbits[0]), (out_grad, PAIR)]
     flows = [move(w, bit, start, stop) for w, bit in flows]
-    entering, out_x, out_xy, up_y, gate_y, up_x = lax.optimization_barrier((entering, *flows))
+    entering, out_x, gate_up, up_x, down_a, far_grad = lax.optimization_barrier((entering, *flows))
+    gate_y, up_y = gate_up[..., :cols], gate_up[..., cols:]
     carry = jnp.stack([entering, states[:, 0] + (1.0 - fresh0) * entering], axis=1)
     place = (me // 2) % 4
-    out_pieces = [(place, out_half), (place ^ 1, out_x), (place ^ 2, out_y), (place ^ 3, out_xy)]
+    out_pieces = [(place, out_half), (place ^ 1, out_x[0]), (place ^ 2, out_y), (place ^ 3, out_x[1])]
     out_half = jnp.zeros((chips // 4, 4, 2 * rows, half), bf16)
     for index, piece in out_pieces:
         out_half = lax.dynamic_update_index_in_dim(out_half, piece, index, 1)
@@ -897,24 +932,25 @@
     carry = after(carry, out_half)
     y_heads, mixed_heads = attention.forward(carry)
     start, stop = (carry,), (mixed_heads,)
-    flows = [(gate_x, 4), (up_y, 2), (out_grad, PAIR), (out_half, 1)]
-    flows = [move(w, bit, start, stop) for w, bit in flows]
-    mixed_heads, gate_xy, up_xy, far_grad, out_there, down = lax.optimization_barrier((mixed_heads, *flows, down))
+    flows = [move(w, bit, start, stop) for w, bit in [(gate_x, 4), (up_y, 2), (down_b, qbits[0])]]
+    out_there = move(out_half, 1, start, stop)
+    mixed_heads, out_there, *flows = lax.optimization_barrier((mixed_heads, out_there, *flows))
+    gate_xy, up_xy, down_b = flows
+    down = [down, down_a, down_b]
+    near_grad = jnp.concatenate([out_grad, near_grad])
     out_all = side_by_side(core, out_half, out_there, 1)
-    mixed_there = flip(mixed_heads, 1)
-    mixed_chip = side_by_side(core, mixed_heads, mixed_there, 1)
+    mixed_chip = side_by_side(core, mixed_heads, flip(mixed_heads, 1), 1)
     middle = inputs32 + dot(row_half(mixed_chip, core), out_all)
     ratio_two = lax.rsqrt(jnp.mean(middle * middle, axis=1, keepdims=True) + eps)
     normed_two = middle * ratio_two
     hidden_two = (normed_two * gain_two).astype(bf16)
 
     far_hidden = flip(hidden_two, PAIR)
-    near_grad = jnp.concatenate([out_grad, near_grad])
     near_hidden = jnp.concatenate([hidden_two, flip(hidden_two, 1)])
     gate = [w.reshape(-1, 2 * rows, cols) for w in (gate, gate_x, gate_y, gate_xy)]
     up = [w.reshape(-1, 2 * rows, cols) for w in (up, up_x, up_y, up_xy)]
     order = [(at + more) // 2 for at in grown(qbits[:-2]) for more in (0, PAIR)]
-    sides = jnp.stack([place, place ^ 1, place ^ 2, place ^ 3])
+    sides = jnp.stack([place, place ^ 1, place ^ 2, place ^ 3, side(qbits[0])])
     near = ffn(near_hidden, near_grad, gate, up, down, order, sides)
     far_hidden, far_there = after(far_hidden, *near), move(far_grad, 1, (near_hidden,), (near[0],))
     far_grad = jnp.concatenate([far_grad, far_there])
@@ -931,17 +967,17 @@
     far_parts = [move(far[i][tokens:], 1, start, stop) for i in (3, 0)]
     sent, far_parts = lax.optimization_barrier((sum_gate.sent, far_parts))
     d_far = (far[3][:tokens].astype(f32) + far_parts[0].astype(f32)).astype(bf16)
-    sum_up = Scatter(part_maker([after(near_hidden, sent, d_far), far_hidden], right, swapped, (0, PAIR), 1), swapped)
+    y_far = (far[0][:tokens].astype(f32) + far_parts[1].astype(f32)).astype(bf16)
+    sum_up = Scatter(part_maker([after(near_hidden, sent, d_far, y_far), far_hidden], right, swapped, (0, PAIR), 1), swapped)
     sum_up.send()
     sum_gate.keep(sum_up.sent)
     sum_up.keep(sum_gate.kept)
     term = row_blocks([near[1], far[1]], [after(near_grad, sum_up.kept), far_grad], jnp.arange(cols // 128), 128)
     d_far = move(d_far, PAIR, (), (term,))
     d_far = sum_gate.hold(d_far, term)
-    near_parts, far_parts = after(near_parts, d_far), after(far_parts, d_far)
+    near_parts = after(near_parts, d_far)
     d_near = near[3][:tokens].astype(f32) + near_parts[0].astype(f32)
     y_near = near[0][:tokens].astype(f32) + near_parts[1].astype(f32)
-    y_far = (far[0][:tokens].astype(f32) + far_parts[1].astype(f32)).astype(bf16)
     d_hidden_two = d_near + d_far.astype(f32)
     term_norm_two = jnp.sum(d_hidden_two * normed_two, axis=0)
     scaled_two = d_hidden_two * gain_two
@@ -952,8 +988,14 @@
     d_mixed_chip = side_by_side(core, d_mixed, flip(d_mixed, 1))
     d_heads = dot_cols(d_mixed_chip, row_half(out_all, core)).astype(bf16)
 
-    d_heads = sum_up.hold(after(d_heads, y_far), d_mixed)
+    d_heads = sum_up.hold(d_heads, d_mixed)
     d_heads = after(d_heads, sum_gate.step(), sum_up.step())
+    dq, dk, dv, d_states = attention.backward(carry, y_heads, d_heads)
+    flows = (sum_gate.here, sum_up.here, move(y_far, PAIR, (d_heads,)))
+    flows = [after(flow, d_states) for flow in flows]
+    d_states, sum_gate.here, sum_up.here, y_far = lax.optimization_barrier((d_states, *flows))
+    sum_both = join([sum_gate, sum_up])
+    sent = [sum_both.step()]
 
     def down_x(index):
         return pick(term.reshape(quads // 2, 2, padded, width)[..., :half], index, 1)
@@ -963,15 +1005,9 @@
 
     sum_down = [Scatter(down_x, qbits), Scatter(down_y, swapped)]
     for part in sum_down:
-        part.send(d_heads)
+        part.send(d_states)
         part.keep()
-        d_heads = after(d_heads, part.sent, part.kept)
-    dq, dk, dv, d_states = attention.backward(carry, y_heads, d_heads)
-    y_far = move(y_far, PAIR, (d_heads,), (d_states,))
-    for part in [sum_gate, sum_up] + sum_down:
-        d_states = part.hold(d_states, d_states)
-    d_states, y_far = lax.optimization_barrier((d_states, y_far))
-    sent = [part.step() for part in [sum_gate, sum_up] + sum_down]
+    sent += [part.sent for part in sum_down]
     d_mixed_half = column_half(d_mixed_chip, core)
     out_sums = []
     for h, bits in ((0, cbits), (1, cbits[:-2] + [cbits[-1], cbits[-2]])):
@@ -981,82 +1017,64 @@
     leaving = others(after(leaving, *(part.sent for part in out_sums)), False, bf16)
     for part in out_sums:
         leaving = after(leaving, part.keep(leaving))
-    for part in sum_down:
+    for part in [sum_both] + sum_down + out_sums:
         leaving = part.hold(leaving, leaving)
-    leaving = after(leaving, *(part.step() for part in sum_down))
+    leaving = after(leaving, *(part.step() for part in sum_down + out_sums))
     d_states = jnp.stack([d_states[:, 1] + (1.0 - fresh1) * leaving, leaving], axis=1)
     dk, dv = attention.carried(d_states, dk, dv)
-    for part in out_sums + [sum_gate, sum_up] + sum_down:
+    for part in out_sums + sum_down:
         dk = part.hold(dk, dk)
-    sent = [part.step() for part in out_sums]
-    gate_sum = jnp.stack([part.finish().reshape(4, rows, cols) for part in (sum_gate, sum_up)], axis=1)
-    parts = [pick(gate_sum, member ^ k).astype(bf16) for k in range(1, 4)]
-    d_qkv = after(jnp.concatenate([dq, dk, dv], axis=1), *sent, *parts)
-
-    if (2 * rows) % 128 == 0:
-        terms = row_blocks([hidden_chip], [d_qkv], jnp.arange(chips), 2 * rows)
-    else:
-        terms = dot_rows(hidden_chip, d_qkv).astype(bf16)
-    parts = [move(part, to_member[k], (), (terms,)) for k, part in enumerate(parts, 1)]
-    for part in out_sums:
-        terms = part.hold(terms, terms)
-    terms, parts = lax.optimization_barrier((terms, parts))
-    terms = terms.reshape(chips // 4, 2, 2, 2 * rows, -1)
-    cut = terms.shape[-1] // 2
-
-    def along_x(index):
-        return pick(terms[..., :cut], index, 2).reshape(chips // 2, 2 * rows, cut)
-
-    def along_y(index):
-        return pick(terms[..., cut:], index, 1).reshape(chips // 2, 2 * rows, cut)
-
-    sums = [Scatter(along_x, cbits), Scatter(along_y, cbits[:-2] + [cbits[-1], cbits[-2]])]
+    sum_down = join(sum_down)
+    dk = after(dk, sum_down.step())
+    d_qkv = jnp.concatenate([dq, dk, dv], axis=1)
+
+    cut = d_qkv.shape[1] // 2
+    sums = []
+    for h, bits in ((0, cbits), (1, cbits[:-2] + [cbits[-1], cbits[-2]])):
+        sums.append(Scatter(part_maker([after(hidden_chip, *(p.sent for p in sums))], [d_qkv], bits, (0,), h), bits))
+        sums[-1].send()
+    start = tuple(part.sent for part in sums)
     for part in sums:
-        part.send()
-
-    def join(both):
-        out = Scatter(None, cbits[:-2] + [0])
-        out.kept = jnp.concatenate([part.kept for part in both], axis=2)
-        out.here = jnp.concatenate([part.here for part in both], axis=2)
-        return out
-
+        part.keep(*start)
+        start = (part.kept,)
+    d_hidden_one = times_transposed(after(d_qkv, *start), qkv_all)
     rest_out = join(out_sums)
-    sent = rest_out.step()
-    d_qkv = after(d_qkv, sent, *(part.sent for part in sums))
-    theirs = flip(dot_cols(row_half(d_qkv, 1 - core), qkv_all).astype(bf16), 1)
-    d_hidden_one = dot_cols(row_half(d_qkv, core), qkv_all) + theirs.astype(f32)
+    for part in [sum_down] + sums:
+        d_hidden_one = part.hold(d_hidden_one, d_hidden_one)
+    sent = [part.step() for part in sums] + [rest_out.step()]
+    d_hidden_one = after(d_hidden_one, *sent)
+    theirs = flip(row_half(d_hidden_one, 1 - core), 1)
+    gate_sum = after(sum_both.finish(), *sent).reshape(4, rows, 2, cols).transpose(0, 2, 1, 3)
+    parts = [flip(pick(gate_sum, member ^ k).astype(bf16), to_member[k]) for k in range(1, 4)]
+    d_hidden_one = row_half(d_hidden_one, core).astype(f32) + theirs.astype(f32)
     term_norm_one = jnp.sum(d_hidden_one * normed_one, axis=0)
     scaled_one = d_hidden_one * gain_one
     mean_one = jnp.mean(scaled_one * normed_one, axis=1, keepdims=True)
     norms = jnp.stack([term_norm_one, term_norm_two])
-    for part in sums:
-        part.keep()
-        norms = part.hold(norms, norms)
-    norms = rest_out.hold(norms, norms)
-    sent = [part.step() for part in sums] + [rest_out.step() for _ in rest_out.bits[1:]]
+    for part in sums + [rest_out]:
+        norms = part.hold(norms, theirs)
+    rest = join(sums)
+    sent = [rest.step()] + [rest_out.step() for _ in rest_out.bits[1:]]
     norms = after(norms, *sent)
     norms = norms + flip(norms, 1)
+    norms = norms + flip(norms, cbits[-1])
+    norms = norms + flip(norms, cbits[-2])
+    norms = norms + flip(norms, cbits[-3])
+    norms = rest.hold(norms, norms)
+    norms, parts = lax.optimization_barrier((norms, parts))
+    while len(rest.bits) > 1:
+        sent = [rest.step()]
+    norms = after(norms, *sent)
     gate_sum = assemble_all([(member, pick(gate_sum, member))] + [(member ^ k, p.astype(f32)) for k, p in enumerate(parts, 1)])
     gate_sum = after(gate_sum, *sent).reshape(2, 2, 2, rows, above, below, padded)[..., :unit]
-    norms = norms + flip(norms, cbits[-1])
-    for part in sums:
-        norms = part.hold(norms, gate_sum)
-    rest = join(sums)
-    sent = rest.step()
-    norms = after(norms, sent)
-    norms = norms + flip(norms, cbits[-2])
-    gate_sum = after(gate_sum, sent).transpose(2, 3, 4, 0, 5, 1, 6).reshape(2, rows, n * unit)
+    gate_sum = gate_sum.transpose(2, 3, 4, 0, 5, 1, 6).reshape(2, rows, n * unit)
     grad_gate, grad_up = gate_sum[0], gate_sum[1]
-    norms = rest.hold(norms, norms)
-    while len(rest.bits) > 1:
-        sent = rest.step()
-    norms = after(norms, sent)
-    for bit in cbits[:-2]:
+    for bit in cbits[:-3]:
         norms = norms + flip(norms, bit)
     norms = pick(norms.reshape(2, n, rows), me, 1)
-    input_grad = d_middle + ratio_one * (after(scaled_one, sent) - normed_one * mean_one)
-    output = (after(middle, sent) + y_near + y_far.astype(f32)).astype(bf16)
-    grad_down = jnp.concatenate([part.finish() for part in sum_down], axis=1)[:unit]
+    input_grad = d_middle + ratio_one * (after(scaled_one, *sent) - normed_one * mean_one)
+    output = (after(middle, *sent) + y_near + y_far.astype(f32)).astype(bf16)
+    grad_down = sum_down.finish()[:unit]
     rest.kept = jnp.concatenate([rest.kept, rest_out.kept], axis=2)
     rest.here = jnp.concatenate([rest.here, rest_out.here], axis=2)
     total = rest.step()

time: 1040 us -> 1000 us (0.962)
  waiting for transfers between devices: 113 us -> 77.3 us
  other arithmetic: 88.9 us -> 107 us
  between operations: 17.6 us -> 4.15 us
    ppermute x60 -> x58, waiting for transfers between devices: 113 us -> 77.3 us  [flip(): return lax.ppermute(x, 'tok', [(i, i ^ bits) for i in range(n)])]
    convert_element_type x2 -> x8, other arithmetic: 6.2 us -> 17.7 us  [the longest x7 12.5 us: step(): self.sent = half(1 - side(bit)).astype(bf16)]
    convert_element_type x16 -> x0, local copies, waits for them, and re-layouts: 11.3 us -> none  [step(): self.sent = pick(acc, 1 - side(bit), 1).astype(bf16)]
    add x20 -> x13, other arithmetic: 32.2 us -> 25.1 us  [the longest x10 20.1 us: half(): sum((pick(a.reshape((-1, 2) + a.shape[1:]), index, 1).astype(f32) for a i...]
    ppermute x60 -> x58, starting transfers between devices: 49.3 us -> 53.2 us  [flip(): return lax.ppermute(x, 'tok', [(i, i ^ bits) for i in range(n)])]
    unnamed x193 -> x210, local copies, waits for them, and re-layouts: 32.3 us -> 28.6 us
    pallas_call x10 -> x14, Pallas kernels: 120 us -> 123 us  [the longest x13 113 us: row_blocks(): pl.pallas_call(lambda *refs: product_body(len(left), group, *refs), out_s...]
  transfers between devices with their start and end apart: 61 -> 58, of which waited for: 19 -> 12; matrix products, arithmetic and copies ran while one was open for 21% -> 18% of each run, Pallas kernels for 52% -> 53%
where the time goes in v4:
time: 1000 us; the launch traced here: 991 us
  Pallas kernels  581 us (58%)
  local copies, waits for them, and re-layouts  146 us (15%)
  other arithmetic  107 us (11%)
  waiting for transfers between devices  77.3 us (8%)
  starting transfers between devices  53.2 us (5%)
  matrix products  21.8 us (2%)
    pallas_call x2, Pallas kernels, others(): pl.pallas_call(lambda *refs: scan_body(sign, *refs), out_shape=jax.ShapeD...  160 us
    pallas_call x13, Pallas kernels, row_blocks(): pl.pallas_call(lambda *refs: product_body(len(left), group, *refs), out_s...  113 us
    pallas_call x4, Pallas kernels, call(): pl.pallas_call(body, grid=(2, self.heads), in_specs=ins, out_specs=outs,...  105 us
    pallas_call x2, Pallas kernels, ffn(): pl.pallas_call(lambda *refs: ffn_body(order, *refs), out_shape=[jax.Shape...  95.7 us
    ppermute x58, waiting for transfers between devices, flip(): return lax.ppermute(x, 'tok', [(i, i ^ bits) for i in range(n)])  77.3 us
    ppermute x58, starting transfers between devices, flip(): return lax.ppermute(x, 'tok', [(i, i ^ bits) for i in range(n)])  53.2 us
    pallas_call x1, Pallas kernels, spread_first(): pl.pallas_call(first_body, out_shape=[jax.ShapeDtypeStruct((32,) + gains....  49.9 us
    pallas_call x1, Pallas kernels, spread_second(): pl.pallas_call(second_body, out_shape=[jax.ShapeDtypeStruct((4, 4) + z4.s...  47.6 us
  transfers between devices with their start and end apart: 58, of which 12 were waited for; matrix products, arithmetic and copies ran while one was open for 18% of the time, Pallas kernels for 53%

profile of v4, /device:TPU:0, one launch (start us, length us, event | category | flops | bytes accessed | tf_op | source)
XLA Modules:
  0.0 990.9 jit_solution(6913310350325504858)
XLA Ops:
  1.2 4.8 reshape.471
  8.0 3.1 reshape.473
  18.5 49.9 %shard_map.293 = (f32[32,8,128]{2,1,0:T(8,128)S(1)}, bf16[4,64,1408]{2,1,0:T(8,128)(2,1)S(1)}, bf16[4,64,1408]{2,1,0:T(8,128)(2,1)}, bf16[4,128,1280]{2,1,0:T(8,128)(2,1)S(1)}, bf16[4,176,2048]{2,1,0:T(8,128)(2,1)S(1)}) custom-call(f32[1,8,128]{2,1,0:T(8,128)S(1)} %fusion.69.gains_in, bf16[4,64,1408]{2,1,0:T(8,128)(2,1)S(1)} %reshape.472.gate_in, ...), custom_call_target="tpu_custom_call" | custom-call | tf_op jit(solution)/shard_map/pallas_call | solution.py:219
  73.5 4.3 constant_dynamic-update-slice_fusion.7
  80.6 47.6 %shard_map.294 = (bf16[4,4,128,1280]{3,2,1,0:T(8,128)(2,1)S(1)}, bf16[4,128,1024]{2,1,0:T(8,128)(2,1)S(1)}, bf16[2,4,64,1408]{3,2,1,0:T(8,128)(2,1)S(1)}) custom-call(bf16[4,128,1280]{2,1,0:T(8,128)(2,1)S(1)} %get-tuple-element.186.z4, bf16[64,1024]{1,0:T(8,128)(2,1)S(1)} %copy-done.27, bf16[64,1024]{1,0:T(8,128)(2,1)S(1)} %copy-done.26, ...), custom_call_target="tpu_custom_call" | custom-call | tf_op jit(solution)/shard_map/pallas_call | solution.py:272
  130.7 3.2 constant_dynamic-update-slice_fusion.6.refs_1_.refs_2_.refs_3_.refs_4_
  133.9 7.5 convolution_convert_fusion.k_ref.v_ref.q_ref
  141.5 10.5 %shard_map.295 = f32[8,2,168,128]{3,2,1,0:T(8,128)S(1)} custom-call(s32[2]{0:T(128)S(1)} %pad_add_fusion.scal, bf16[1024,1280]{1,0:T(8,128)(2,1)S(1)} %convolution_convert_fusion.k_ref.v_ref.q_ref, bf16[1024,1280]{1,0:T(8,128)(2,1)S(1)} %convolution_convert_fusion.k_ref.v_ref.q_ref, bf16[8,128,160]{2,1,0:T(8,128)(2,1)S(1)} %copy-done.10, ...), custom_call_target="tpu_custom_call" | custom-call | tf_op jit(solution)/shard_map/pallas_call | solution.py:706
  153.2 10.0 %collective-permute-done.3 = bf16[4,64,1408]{2,1,0:T(8,128)(2,1)S(1)} collective-permute-done((bf16[4,64,1408]{2,1,0:T(8,128)(2,1)}, bf16[4,64,1408]{2,1,0:T(8,128)(2,1)S(1)}, u32[]{:S(2)}, u32[]{:S(2)}) %collective-permute-start.3) | collective-permute-done | bytes 720928 | tf_op jit(solution)/shard_map/ppermute | solution.py:29
  167.5 3.3 pad_maximum_fusion.1
  183.3 100.1 %shard_map.296 = f32[8,168,128]{2,1,0:T(8,128)S(1)} custom-call(f32[8,168,128]{2,1,0:T(8,128)S(1)} %copy-done.21), custom_call_target="tpu_custom_call" | custom-call | tf_op jit(solution)/shard_map/pallas_call | solution.py:775
  290.4 3.6 fusion.78
  296.9 9.9 collective-permute-start.13
  309.5 21.8 %shard_map.297 = (f32[1024,1024]{1,0:T(8,128)}, bf16[1024,1024]{1,0:T(8,128)(2,1)}) custom-call(bf16[1024,1280]{1,0:T(8,128)(2,1)} %copy-done, bf16[1024,1280]{1,0:T(8,128)(2,1)} %copy-done, bf16[1024,1280]{1,0:T(8,128)(2,1)} %copy-done, s32[1024,1]{1,0:T(8,128)S(1)} %copy.142.lo_ref, f32[8,2,168,128]{3,2,1,0:T(8,128)S(1)} %copy.143.carry_ref, ...), custom_call_target="tpu_custom_call" | custom-call | tf_op jit(solution)/shard_map/pallas_call | solution.py:706
  331.3 7.4 collective-permute-done.13.refs_13_
  347.8 3.6 constant_dynamic-update-slice_fusion.4.refs_1_.refs_2_.refs_3_.refs_4_
  353.0 4.7 multiply_reduce_fusion.2
  365.1 6.5 pad_maximum_fusion.refs_1_.refs_2_.refs_3_.refs_4_
  371.6 48.0 %shard_map.298 = (bf16[1024,2048]{1,0:T(8,128)(2,1)}, bf16[1024,1408]{1,0:T(8,128)(2,1)}, bf16[1024,2816]{1,0:T(8,128)(2,1)}, bf16[1024,2048]{1,0:T(8,128)(2,1)}) custom-call(s32[5]{0:T(128)S(1)} %stack.81.refs_0_, bf16[1024,2048]{1,0:T(8,128)(2,1)} %pad_maximum_fusion.refs_1_.refs_2_.refs_3_.refs_4_, bf16[1024,2048]{1,0:T(8,128)(2,1)} %copy-done.39, ...), custom_call_target="tpu_custom_call" | custom-call | tf_op jit(solution)/shard_map/pallas_call | solution.py:416
  420.0 3.4 slice.147
  433.3 47.8 %shard_map.299 = (bf16[1024,2048]{1,0:T(8,128)(2,1)}, bf16[1024,1408]{1,0:T(8,128)(2,1)}, bf16[1024,2816]{1,0:T(8,128)(2,1)}, bf16[1024,2048]{1,0:T(8,128)(2,1)}) custom-call(s32[5]{0:T(128)S(1)} %stack.81.refs_0_, bf16[1024,2048]{1,0:T(8,128)(2,1)} %copy-done.31, bf16[1024,2048]{1,0:T(8,128)(2,1)} %copy-done.38, bf16[4,128,1408]{2,1,0:T(8,128)(2,1)S(1)} %bitcast.261, ...), custom_call_target="tpu_custom_call" | custom-call | tf_op jit(solution)/shard_map/pallas_call | solution.py:416
  481.1 3.3 slice.150
  486.9 13.0 %shard_map.300 = bf16[1024,1408]{1,0:T(8,128)(2,1)} custom-call(s32[8]{0:T(128)} %broadcast_add_fusion.5.refs_0_, bf16[1024,2048]{1,0:T(8,128)(2,1)} %pad_maximum_fusion.refs_1_.refs_2_.refs_3_.refs_4_, bf16[1024,2048]{1,0:T(8,128)(2,1)} %pad_maximum_fusion.refs_1_.refs_2_.refs_3_.refs_4_, ...), custom_call_target="tpu_custom_call" | custom-call | tf_op jit(solution)/shard_map/pallas_call | solution.py:450
  501.0 3.8 add_convert_fusion.2
  507.4 20.2 %shard_map.301 = bf16[1408,2048]{1,0:T(8,128)(2,1)} custom-call(s32[11]{0:T(128)} %iota.10.refs_0_, bf16[1024,1408]{1,0:T(8,128)(2,1)} %get-tuple-element.237.refs_1_, bf16[1024,1408]{1,0:T(8,128)(2,1)} %get-tuple-element.261.refs_2_, bf16[1024,2048]{1,0:T(8,128)(2,1)} %copy-done.39, bf16[1024,2048]{1,0:T(8,128)(2,1)} %copy-done.38), custom_call_target="tpu_custom_call" | custom-call | tf_op jit(solution)/shard_map/pallas_call | solution.py:450
  527.6 3.8 add_convert_fusion.1
  531.4 13.1 %shard_map.302 = bf16[1024,1408]{1,0:T(8,128)(2,1)} custom-call(s32[8]{0:T(128)} %get-tuple-element.417.refs_0_, bf16[1024,2048]{1,0:T(8,128)(2,1)} %pad_maximum_fusion.refs_1_.refs_2_.refs_3_.refs_4_, bf16[1024,2048]{1,0:T(8,128)(2,1)} %pad_maximum_fusion.refs_1_.refs_2_.refs_3_.refs_4_, bf16[1024,2048]{1,0:T(8,128)(2,1)} %pad_maximum_fusion.refs_1_.refs_2_.refs_3_.refs_4_, ...), custom_call_target="tpu_custom_call" | custom-call | tf_op jit(solution)/shard_map/pallas_call | solution.py:450
  545.6 19.3 %collective-permute-done.24 = bf16[4,256,1408]{2,1,0:T(8,128)(2,1)} collective-permute-done((bf16[4,256,1408]{2,1,0:T(8,128)(2,1)}, bf16[4,256,1408]{2,1,0:T(8,128)(2,1)}, u32[]{:S(2)}, u32[]{:S(2)}) %collective-permute-start.24) | collective-permute-done | bytes 2883616 | tf_op jit(solution)/shard_map/ppermute | solution.py:29
  564.9 3.8 multiply_reduce_fusion
  570.9 6.2 constant_dynamic-update-slice_fusion.1
  579.0 12.5 %shard_map.304 = bf16[1024,1408]{1,0:T(8,128)(2,1)} custom-call(s32[8]{0:T(128)} %get-tuple-element.416.refs_0_, bf16[1024,2048]{1,0:T(8,128)(2,1)} %pad_maximum_fusion.refs_1_.refs_2_.refs_3_.refs_4_, bf16[1024,2048]{1,0:T(8,128)(2,1)} %pad_maximum_fusion.refs_1_.refs_2_.refs_3_.refs_4_, bf16[1024,2048]{1,0:T(8,128)(2,1)} %pad_maximum_fusion.refs_1_.refs_2_.refs_3_.refs_4_, ...), custom_call_target="tpu_custom_call" | custom-call | tf_op jit(solution)/shard_map/pallas_call | solution.py:450
  592.1 12.9 %shard_map.303 = bf16[1024,1408]{1,0:T(8,128)(2,1)} custom-call(s32[8]{0:T(128)} %broadcast_add_fusion.2.refs_0_, bf16[1024,2048]{1,0:T(8,128)(2,1)} %pad_maximum_fusion.refs_1_.refs_2_.refs_3_.refs_4_, bf16[1024,2048]{1,0:T(8,128)(2,1)} %pad_maximum_fusion.refs_1_.refs_2_.refs_3_.refs_4_, ...), custom_call_target="tpu_custom_call" | custom-call | tf_op jit(solution)/shard_map/pallas_call | solution.py:450
  605.0 3.4 fusion.25
  610.9 9.6 fusion.22.d_ref
  620.5 4.5 add_bitcast_fusion
  630.5 3.3 slice.180
  639.7 45.4 %shard_map.305 = (bf16[1024,128]{1,0:T(8,128)(2,1)S(1)}, f32[1024,128]{1,0:T(8,128)S(1)}, f32[1024,1024]{1,0:T(8,128)}, f32[8,2,168,128]{3,2,1,0:T(8,128)S(1)}) custom-call(bf16[1024,1280]{1,0:T(8,128)(2,1)} %copy-done, bf16[1024,1280]{1,0:T(8,128)(2,1)} %copy-done, bf16[1024,1280]{1,0:T(8,128)(2,1)} %copy-done, s32[1024,1]{1,0:T(8,128)S(1)} %copy.142.lo_ref, ...), custom_call_target="tpu_custom_call" | custom-call | tf_op jit(solution)/shard_map/pallas_call | solution.py:706
  695.2 4.8 shard_map.306
  701.8 4.8 shard_map.307
  707.6 59.8 %shard_map.308 = f32[8,168,128]{2,1,0:T(8,128)S(1)} custom-call(f32[8,168,128]{2,1,0:T(8,128)S(1)} %fusion.47.refs_0_), custom_call_target="tpu_custom_call" | custom-call | tf_op jit(solution)/shard_map/pallas_call | solution.py:775
  767.3 4.9 shard_map.310
  772.7 4.7 shard_map.309
  777.5 3.1 convert_add_fusion.8
  781.7 2.8 add_bitcast_fusion.2
  791.1 27.5 %shard_map.311 = (bf16[1024,128]{1,0:T(8,128)(2,1)S(1)}, bf16[1024,1024]{1,0:T(8,128)(2,1)S(1)}) custom-call(s32[2]{0:T(128)S(1)} %copy-done.30, bf16[1024,1280]{1,0:T(8,128)(2,1)} %copy-done, bf16[1024,1280]{1,0:T(8,128)(2,1)} %copy-done, bf16[8,128,160]{2,1,0:T(8,128)(2,1)S(1)} %copy-done.10, bf16[8,128,160]{2,1,0:T(8,128)(2,1)S(1)} %copy-done.14, ...), custom_call_target="tpu_custom_call" | custom-call | tf_op jit(solution)/shard_map/pallas_call | solution.py:706
  822.7 5.4 shard_map.312
  829.1 5.4 shard_map.313
  840.9 5.5 shard_map.316
  846.5 9.7 shard_map.315
  856.7 5.7 shard_map.314
  862.4 6.0 collective-permute-done.39
  870.7 2.9 fusion.49
  877.2 4.2 fusion.17
  883.9 4.9 reshape.508
  890.1 5.4 collective-permute-done.45
  895.5 5.6 fusion.6
  916.4 24.3 %collective-permute-done.49 = f32[2,2048]{1,0:T(2,128)S(1)} collective-permute-done((f32[2,2048]{1,0:T(2,128)S(1)}, f32[2,2048]{1,0:T(2,128)S(1)}, u32[]{:S(2)}, u32[]{:S(2)}) %collective-permute-start.49) | collective-permute-done | bytes 16416 | tf_op jit(solution)/shard_map/ppermute | solution.py:29
  947.4 8.5 reshape.512
  956.0 3.1 slice_bitcast_fusion
  960.7 3.9 fusion.9
  965.7 5.2 add_convert_fusion
  974.5 3.5 squeeze.132
  978.0 3.2 copy.172
  981.2 3.5 squeeze.133
  (439 shorter events, 179.2 us)
Async XLA Ops:
  0.6 17.9 %collective-permute-start = (bf16[512,2048]{1,0:T(8,128)(2,1)}, bf16[512,2048]{1,0:T(8,128)(2,1)}, u32[]{:S(2)}, u32[]{:S(2)}) collective-permute-start(bf16[512,2048]{1,0:T(8,128)(2,1)} %param.34), channel_id=1, source_target_pairs={{0,1},{1,0},{2,3},{3,2},{4,5},{5,4},{6,7},{7,6},{8,9},{9,8},{10,11... | collective-permute-start | bytes 6291464 | tf_op jit(solution)/shard_map/ppermute | solution.py:29
  18.4 55.1 %copy-start.88 = (f32[512]{0:T(512)}, f32[512]{0:T(512)S(1)}, u32[]{:S(2)}) copy-start(f32[512]{0:T(512)S(1)} %add_rsqrt_fusion.1) | copy-start | bytes 6148
  77.8 53.0 %collective-permute-start.1 = (bf16[512,2048]{1,0:T(8,128)(2,1)}, bf16[512,2048]{1,0:T(8,128)(2,1)}, u32[]{:S(2)}, u32[]{:S(2)}) collective-permute-start(bf16[512,2048]{1,0:T(8,128)(2,1)} %get-tuple-element.368), channel_id=1, source_target_pairs={{0,1},{1,0},{2,3},{3,2},{4,5},{5,4},{6,7},{7,6},{8,9},{9,8},{10,11... | collective-permute-start | bytes 6291464 | tf_op jit(solution)/shard_map/ppermute | solution.py:29
  80.6 60.9 %copy-start.29 = (s32[2]{0:T(128)}, s32[2]{0:T(128)S(1)}, u32[]{:S(2)}) copy-start(s32[2]{0:T(128)S(1)} %pad_add_fusion.scal) | copy-start | bytes 28
  128.2 39.2 %copy-start.5 = (bf16[2,4,64,1408]{3,2,1,0:T(8,128)(2,1)}, bf16[2,4,64,1408]{3,2,1,0:T(8,128)(2,1)S(1)}, u32[]{:S(2)}) copy-start(bf16[2,4,64,1408]{3,2,1,0:T(8,128)(2,1)S(1)} %get-tuple-element.191) | copy-start | bytes 4325380
  128.2 47.2 %copy-start.16 = (bf16[4,128,1024]{2,1,0:T(8,128)(2,1)}, bf16[4,128,1024]{2,1,0:T(8,128)(2,1)S(1)}, u32[]{:S(2)}) copy-start(bf16[4,128,1024]{2,1,0:T(8,128)(2,1)S(1)} %get-tuple-element.197) | copy-start | bytes 3145732
  128.3 24.9 %collective-permute-start.4 = (bf16[4,128,1024]{2,1,0:T(8,128)(2,1)S(1)}, bf16[4,128,1024]{2,1,0:T(8,128)(2,1)S(1)}, u32[]{:S(2)}, u32[]{:S(2)}) collective-permute-start(bf16[4,128,1024]{2,1,0:T(8,128)(2,1)S(1)} %get-tuple-element.197), channel_id=1, source_target_pairs={{0,4},{1,5},{2,6},{3,7},{4,0},{5,1},{6,2},{7,3},{8,12},{9,13},{10,... | collective-permute-start | bytes 3145736 | tf_op jit(solution)/shard_map/ppermute | solution.py:29
  129.8 33.4 %collective-permute-start.3 = (bf16[4,64,1408]{2,1,0:T(8,128)(2,1)}, bf16[4,64,1408]{2,1,0:T(8,128)(2,1)S(1)}, u32[]{:S(2)}, u32[]{:S(2)}) collective-permute-start(bf16[4,64,1408]{2,1,0:T(8,128)(2,1)} %get-tuple-element.194), channel_id=1, source_target_pairs={{0,16},{1,17},{2,18},{3,19},{4,20},{5,21},{6,22},{7,23},{8,24},{9,... | collective-permute-start | bytes 2162696 | tf_op jit(solution)/shard_map/ppermute | solution.py:29
  129.8 33.4 %collective-permute-start.2 = (bf16[2,4,64,1408]{3,2,1,0:T(8,128)(2,1)S(1)}, bf16[2,4,64,1408]{3,2,1,0:T(8,128)(2,1)}, u32[]{:S(2)}, u32[]{:S(2)}) collective-permute-start(bf16[2,4,64,1408]{3,2,1,0:T(8,128)(2,1)S(1)} %get-tuple-element.191), channel_id=1, source_target_pairs={{0,2},{1,3},{2,0},{3,1},{4,6},{5,7},{6,4},{7,5},{8,10},{9,11},{10,... | collective-permute-start | bytes 4325384 | tf_op jit(solution)/shard_map/ppermute | solution.py:29
  170.8 112.7 %collective-permute-start.6 = (bf16[2,4,64,2816]{3,2,1,0:T(8,128)(2,1)}, bf16[2,4,64,2816]{3,2,1,0:T(8,128)(2,1)}, u32[]{:S(2)}, u32[]{:S(2)}) collective-permute-start(bf16[2,4,64,2816]{3,2,1,0:T(8,128)(2,1)} %pad_maximum_fusion.1), channel_id=1, source_target_pairs={{0,4},{1,5},{2,6},{3,7},{4,0},{5,1},{6,2},{7,3},{8,12},{9,13},{10,... | collective-permute-start | bytes 8650760 | tf_op jit(solution)/shard_map/ppermute | solution.py:29
  172.8 110.6 %collective-permute-start.9 = (bf16[512,2048]{1,0:T(8,128)(2,1)}, bf16[512,2048]{1,0:T(8,128)(2,1)}, u32[]{:S(2)}, u32[]{:S(2)}) collective-permute-start(bf16[512,2048]{1,0:T(8,128)(2,1)} %param.34), channel_id=1, source_target_pairs={{0,8},{1,9},{2,10},{3,11},{4,12},{5,13},{6,14},{7,15},{8,0},{9,1},... | collective-permute-start | bytes 6291464 | tf_op jit(solution)/shard_map/ppermute | solution.py:29
  174.7 108.7 %collective-permute-start.8 = (bf16[704,1536]{1,0:T(8,128)(2,1)}, bf16[704,1536]{1,0:T(8,128)(2,1)}, u32[]{:S(2)}, u32[]{:S(2)}) collective-permute-start(bf16[704,1536]{1,0:T(8,128)(2,1)} %slice.175), channel_id=1, source_target_pairs={{0,16},{1,17},{2,18},{3,19},{4,20},{5,21},{6,22},{7,23},{8,24},{9,... | collective-permute-start | bytes 6488072 | tf_op jit(solution)/shard_map/ppermute | solution.py:29
  176.9 106.5 %collective-permute-start.5 = (bf16[2,4,128,1024]{3,2,1,0:T(8,128)(2,1)}, bf16[2,4,128,1024]{3,2,1,0:T(8,128)(2,1)}, u32[]{:S(2)}, u32[]{:S(2)}) collective-permute-start(bf16[2,4,128,1024]{3,2,1,0:T(8,128)(2,1)} %pad_maximum_fusion.2), channel_id=1, source_target_pairs={{0,2},{1,3},{2,0},{3,1},{4,6},{5,7},{6,4},{7,5},{8,10},{9,11},{10,... | collective-permute-start | bytes 6291464 | tf_op jit(solution)/shard_map/ppermute | solution.py:29
  178.4 105.0 %collective-permute-start.7 = (bf16[2,4,64,1408]{3,2,1,0:T(8,128)(2,1)}, bf16[2,4,64,1408]{3,2,1,0:T(8,128)(2,1)}, u32[]{:S(2)}, u32[]{:S(2)}) collective-permute-start(bf16[2,4,64,1408]{3,2,1,0:T(8,128)(2,1)} %bitcast_dynamic-update-slice_fusion.4), channel_id=1, source_target_pairs={{0,2},{1,3},{2,0},{3,1},{4,6},{5,7},{6,4},{7,5},{8,10},{9,11},{10,... | collective-permute-start | bytes 4325384 | tf_op jit(solution)/shard_map/ppermute | solution.py:29
  182.2 103.6 %copy-start.75 = (bf16[4,128,1024]{2,1,0:T(8,128)(2,1)S(1)}, bf16[4,128,1024]{2,1,0:T(8,128)(2,1)}, u32[]{:S(2)}) copy-start(bf16[4,128,1024]{2,1,0:T(8,128)(2,1)} %copy-done.74) | copy-start | bytes 3145732
  290.4 48.3 %collective-permute-start.10 = (bf16[2048,1024]{1,0:T(8,128)(2,1)}, bf16[2048,1024]{1,0:T(8,128)(2,1)}, u32[]{:S(2)}, u32[]{:S(2)}) collective-permute-start(bf16[2048,1024]{1,0:T(8,128)(2,1)} %bitcast.26), channel_id=1, source_target_pairs={{0,1},{1,0},{2,3},{3,2},{4,5},{5,4},{6,7},{7,6},{8,9},{9,8},{10,11... | collective-permute-start | bytes 12582920 | tf_op jit(solution)/shard_map/ppermute | solution.py:29
  294.0 44.7 %collective-permute-start.12 = (bf16[2,4,64,1408]{3,2,1,0:T(8,128)(2,1)}, bf16[2,4,64,1408]{3,2,1,0:T(8,128)(2,1)}, u32[]{:S(2)}, u32[]{:S(2)}) collective-permute-start(bf16[2,4,64,1408]{3,2,1,0:T(8,128)(2,1)} %get-tuple-element.223), channel_id=1, source_target_pairs={{0,2},{1,3},{2,0},{3,1},{4,6},{5,7},{6,4},{7,5},{8,10},{9,11},{10,... | collective-permute-start | bytes 4325384 | tf_op jit(solution)/shard_map/ppermute | solution.py:29
  295.2 43.5 %collective-permute-start.11 = (bf16[2,4,64,1408]{3,2,1,0:T(8,128)(2,1)}, bf16[2,4,64,1408]{3,2,1,0:T(8,128)(2,1)}, u32[]{:S(2)}, u32[]{:S(2)}) collective-permute-start(bf16[2,4,64,1408]{3,2,1,0:T(8,128)(2,1)} %collective-permute-done.2), channel_id=1, source_target_pairs={{0,4},{1,5},{2,6},{3,7},{4,0},{5,1},{6,2},{7,3},{8,12},{9,13},{10,... | collective-permute-start | bytes 4325384 | tf_op jit(solution)/shard_map/ppermute | solution.py:29
  296.9 41.8 %collective-permute-start.13 = (bf16[704,512]{1,0:T(8,128)(2,1)}, bf16[704,512]{1,0:T(8,128)(2,1)S(1)}, u32[]{:S(2)}, u32[]{:S(2)}) collective-permute-start(bf16[704,512]{1,0:T(8,128)(2,1)} %slice.176), channel_id=1, source_target_pairs={{0,16},{1,17},{2,18},{3,19},{4,20},{5,21},{6,22},{7,23},{8,24},{9,... | collective-permute-start | bytes 2162696 | tf_op jit(solution)/shard_map/ppermute | solution.py:29
  338.7 9.1 collective-permute-start.14
  360.5 4.6 collective-permute-start.15
  361.0 58.6 %collective-permute-start.16 = (bf16[512,2048]{1,0:T(8,128)(2,1)}, bf16[512,2048]{1,0:T(8,128)(2,1)}, u32[]{:S(2)}, u32[]{:S(2)}) collective-permute-start(bf16[512,2048]{1,0:T(8,128)(2,1)} %multiply_convert_fusion), channel_id=1, source_target_pairs={{0,8},{1,9},{2,10},{3,11},{4,12},{5,13},{6,14},{7,15},{8,0},{9,1},... | collective-permute-start | bytes 6291464 | tf_op jit(solution)/shard_map/ppermute | solution.py:29
  419.6 7.4 collective-permute-start.17
  426.8 4.4 collective-permute-start.18
  427.2 53.9 %collective-permute-start.20 = (bf16[512,2048]{1,0:T(8,128)(2,1)}, bf16[512,2048]{1,0:T(8,128)(2,1)}, u32[]{:S(2)}, u32[]{:S(2)}) collective-permute-start(bf16[512,2048]{1,0:T(8,128)(2,1)} %slice.147), channel_id=1, source_target_pairs={{0,1},{1,0},{2,3},{3,2},{4,5},{5,4},{6,7},{7,6},{8,9},{9,8},{10,11... | collective-permute-start | bytes 6291464 | tf_op jit(solution)/shard_map/ppermute | solution.py:29
  427.7 53.4 %collective-permute-start.19 = (bf16[512,2048]{1,0:T(8,128)(2,1)}, bf16[512,2048]{1,0:T(8,128)(2,1)}, u32[]{:S(2)}, u32[]{:S(2)}) collective-permute-start(bf16[512,2048]{1,0:T(8,128)(2,1)} %slice.146), channel_id=1, source_target_pairs={{0,1},{1,0},{2,3},{3,2},{4,5},{5,4},{6,7},{7,6},{8,9},{9,8},{10,11... | collective-permute-start | bytes 6291464 | tf_op jit(solution)/shard_map/ppermute | solution.py:29
  484.4 16.5 %collective-permute-start.22 = (bf16[512,2048]{1,0:T(8,128)(2,1)}, bf16[512,2048]{1,0:T(8,128)(2,1)}, u32[]{:S(2)}, u32[]{:S(2)}) collective-permute-start(bf16[512,2048]{1,0:T(8,128)(2,1)} %slice.150), channel_id=1, source_target_pairs={{0,1},{1,0},{2,3},{3,2},{4,5},{5,4},{6,7},{7,6},{8,9},{9,8},{10,11... | collective-permute-start | bytes 6291464 | tf_op jit(solution)/shard_map/ppermute | solution.py:29
  486.0 14.9 %collective-permute-start.21 = (bf16[512,2048]{1,0:T(8,128)(2,1)}, bf16[512,2048]{1,0:T(8,128)(2,1)}, u32[]{:S(2)}, u32[]{:S(2)}) collective-permute-start(bf16[512,2048]{1,0:T(8,128)(2,1)} %slice.149), channel_id=1, source_target_pairs={{0,1},{1,0},{2,3},{3,2},{4,5},{5,4},{6,7},{7,6},{8,9},{9,8},{10,11... | collective-permute-start | bytes 6291464 | tf_op jit(solution)/shard_map/ppermute | solution.py:29
  500.0 64.9 %collective-permute-start.24 = (bf16[4,256,1408]{2,1,0:T(8,128)(2,1)}, bf16[4,256,1408]{2,1,0:T(8,128)(2,1)}, u32[]{:S(2)}, u32[]{:S(2)}) collective-permute-start(bf16[4,256,1408]{2,1,0:T(8,128)(2,1)} %bitcast.288), channel_id=1, source_target_pairs={{0,2},{1,3},{2,0},{3,1},{4,6},{5,7},{6,4},{7,5},{8,10},{9,11},{10,... | collective-permute-start | bytes 8650760 | tf_op jit(solution)/shard_map/ppermute | solution.py:29
  504.8 60.1 %collective-permute-start.23 = (bf16[512,2048]{1,0:T(8,128)(2,1)}, bf16[512,2048]{1,0:T(8,128)(2,1)}, u32[]{:S(2)}, u32[]{:S(2)}) collective-permute-start(bf16[512,2048]{1,0:T(8,128)(2,1)} %add_convert_fusion.2), channel_id=1, source_target_pairs={{0,8},{1,9},{2,10},{3,11},{4,12},{5,13},{6,14},{7,15},{8,0},{9,1},... | collective-permute-start | bytes 6291464 | tf_op jit(solution)/shard_map/ppermute | solution.py:29
  544.5 64.5 %collective-permute-start.26 = (bf16[4,256,1408]{2,1,0:T(8,128)(2,1)}, bf16[4,256,1408]{2,1,0:T(8,128)(2,1)}, u32[]{:S(2)}, u32[]{:S(2)}) collective-permute-start(bf16[4,256,1408]{2,1,0:T(8,128)(2,1)} %bitcast.289), channel_id=1, source_target_pairs={{0,4},{1,5},{2,6},{3,7},{4,0},{5,1},{6,2},{7,3},{8,12},{9,13},{10,... | collective-permute-start | bytes 8650760 | tf_op jit(solution)/shard_map/ppermute | solution.py:29
  579.0 30.0 %collective-permute-start.25 = (bf16[512,2048]{1,0:T(8,128)(2,1)}, bf16[512,2048]{1,0:T(8,128)(2,1)}, u32[]{:S(2)}, u32[]{:S(2)}) collective-permute-start(bf16[512,2048]{1,0:T(8,128)(2,1)} %get-tuple-element.365), channel_id=1, source_target_pairs={{0,1},{1,0},{2,3},{3,2},{4,5},{5,4},{6,7},{7,6},{8,9},{9,8},{10,11... | collective-permute-start | bytes 6291464 | tf_op jit(solution)/shard_map/ppermute | solution.py:29
  624.9 60.1 %collective-permute-start.29 = (bf16[512,2048]{1,0:T(8,128)(2,1)}, bf16[512,2048]{1,0:T(8,128)(2,1)}, u32[]{:S(2)}, u32[]{:S(2)}) collective-permute-start(bf16[512,2048]{1,0:T(8,128)(2,1)} %add_convert_fusion.1), channel_id=1, source_target_pairs={{0,8},{1,9},{2,10},{3,11},{4,12},{5,13},{6,14},{7,15},{8,0},{9,1},... | collective-permute-start | bytes 6291464 | tf_op jit(solution)/shard_map/ppermute | solution.py:29
  626.2 58.9 %collective-permute-start.27 = (bf16[2,256,1408]{2,1,0:T(8,128)(2,1)}, bf16[2,256,1408]{2,1,0:T(8,128)(2,1)}, u32[]{:S(2)}, u32[]{:S(2)}) collective-permute-start(bf16[2,256,1408]{2,1,0:T(8,128)(2,1)} %fusion.25), channel_id=1, source_target_pairs={{0,4},{1,5},{2,6},{3,7},{4,0},{5,1},{6,2},{7,3},{8,12},{9,13},{10,... | collective-permute-start | bytes 4325384 | tf_op jit(solution)/shard_map/ppermute | solution.py:29
  627.1 57.9 %collective-permute-start.28 = (bf16[2,256,1408]{2,1,0:T(8,128)(2,1)}, bf16[2,256,1408]{2,1,0:T(8,128)(2,1)}, u32[]{:S(2)}, u32[]{:S(2)}) collective-permute-start(bf16[2,256,1408]{2,1,0:T(8,128)(2,1)} %get-tuple-element.370), channel_id=1, source_target_pairs={{0,2},{1,3},{2,0},{3,1},{4,6},{5,7},{6,4},{7,5},{8,10},{9,11},{10,... | collective-permute-start | bytes 4325384 | tf_op jit(solution)/shard_map/ppermute | solution.py:29
  639.6 49.2 %copy-start.40 = (f32[2,256,1408]{2,1,0:T(8,128)}, f32[2,256,1408]{2,1,0:T(8,128)S(1)}, u32[]{:S(2)}) copy-start(f32[2,256,1408]{2,1,0:T(8,128)S(1)} %add_bitcast_fusion.1) | copy-start | bytes 8650756
  691.1 86.4 %collective-permute-start.30 = (bf16[1,256,2816]{2,1,0:T(8,128)(2,1)}, bf16[1,256,2816]{2,1,0:T(8,128)(2,1)}, u32[]{:S(2)}, u32[]{:S(2)}) collective-permute-start(bf16[1,256,2816]{2,1,0:T(8,128)(2,1)} %fusion.20), channel_id=1, source_target_pairs={{0,16},{1,17},{2,18},{3,19},{4,20},{5,21},{6,22},{7,23},{8,24},{9,... | collective-permute-start | bytes 4325384 | tf_op jit(solution)/shard_map/ppermute | solution.py:29
  691.1 86.4 %collective-permute-start.31 = (bf16[4,176,1024]{2,1,0:T(8,128)(2,1)}, bf16[4,176,1024]{2,1,0:T(8,128)(2,1)}, u32[]{:S(2)}, u32[]{:S(2)}) collective-permute-start(bf16[4,176,1024]{2,1,0:T(8,128)(2,1)} %get-tuple-element.283), channel_id=1, source_target_pairs={{0,2},{1,3},{2,0},{3,1},{4,6},{5,7},{6,4},{7,5},{8,10},{9,11},{10,... | collective-permute-start | bytes 4325384 | tf_op jit(solution)/shard_map/ppermute | solution.py:29
  692.2 85.3 %collective-permute-start.32 = (bf16[4,176,1024]{2,1,0:T(8,128)(2,1)}, bf16[4,176,1024]{2,1,0:T(8,128)(2,1)}, u32[]{:S(2)}, u32[]{:S(2)}) collective-permute-start(bf16[4,176,1024]{2,1,0:T(8,128)(2,1)} %bitcast.55), channel_id=1, source_target_pairs={{0,4},{1,5},{2,6},{3,7},{4,0},{5,1},{6,2},{7,3},{8,12},{9,13},{10,... | collective-permute-start | bytes 4325384 | tf_op jit(solution)/shard_map/ppermute | solution.py:29
  700.0 77.5 %collective-permute-start.33 = (bf16[8,128,512]{2,1,0:T(8,128)(2,1)}, bf16[8,128,512]{2,1,0:T(8,128)(2,1)}, u32[]{:S(2)}, u32[]{:S(2)}) collective-permute-start(bf16[8,128,512]{2,1,0:T(8,128)(2,1)} %bitcast.293), channel_id=1, source_target_pairs={{0,2},{1,3},{2,0},{3,1},{4,6},{5,7},{6,4},{7,5},{8,10},{9,11},{10,... | collective-permute-start | bytes 3145736 | tf_op jit(solution)/shard_map/ppermute | solution.py:29
  706.6 70.9 %collective-permute-start.34 = (bf16[8,128,512]{2,1,0:T(8,128)(2,1)}, bf16[8,128,512]{2,1,0:T(8,128)(2,1)}, u32[]{:S(2)}, u32[]{:S(2)}) collective-permute-start(bf16[8,128,512]{2,1,0:T(8,128)(2,1)} %bitcast.294), channel_id=1, source_target_pairs={{0,4},{1,5},{2,6},{3,7},{4,0},{5,1},{6,2},{7,3},{8,12},{9,13},{10,... | collective-permute-start | bytes 3145736 | tf_op jit(solution)/shard_map/ppermute | solution.py:29
  780.6 38.0 %collective-permute-start.35 = (bf16[4,128,512]{2,1,0:T(8,128)(2,1)}, bf16[4,128,512]{2,1,0:T(8,128)(2,1)}, u32[]{:S(2)}, u32[]{:S(2)}) collective-permute-start(bf16[4,128,512]{2,1,0:T(8,128)(2,1)} %get-tuple-element.391), channel_id=1, source_target_pairs={{0,4},{1,5},{2,6},{3,7},{4,0},{5,1},{6,2},{7,3},{8,12},{9,13},{10,... | collective-permute-start | bytes 1572872 | tf_op jit(solution)/shard_map/ppermute | solution.py:29
  784.5 35.0 %collective-permute-start.37 = (bf16[2,176,1024]{2,1,0:T(8,128)(2,1)}, bf16[2,176,1024]{2,1,0:T(8,128)(2,1)S(1)}, u32[]{:S(2)}, u32[]{:S(2)}) collective-permute-start(bf16[2,176,1024]{2,1,0:T(8,128)(2,1)} %get-tuple-element.383), channel_id=1, source_target_pairs={{0,4},{1,5},{2,6},{3,7},{4,0},{5,1},{6,2},{7,3},{8,12},{9,13},{10,... | collective-permute-start | bytes 2162696 | tf_op jit(solution)/shard_map/ppermute | solution.py:29
  787.4 32.1 %collective-permute-start.38 = (bf16[2,176,1024]{2,1,0:T(8,128)(2,1)S(1)}, bf16[2,176,1024]{2,1,0:T(8,128)(2,1)S(1)}, u32[]{:S(2)}, u32[]{:S(2)}) collective-permute-start(bf16[2,176,1024]{2,1,0:T(8,128)(2,1)S(1)} %get-tuple-element.372), channel_id=1, source_target_pairs={{0,2},{1,3},{2,0},{3,1},{4,6},{5,7},{6,4},{7,5},{8,10},{9,11},{10,... | collective-permute-start | bytes 2162696 | tf_op jit(solution)/shard_map/ppermute | solution.py:29
  789.8 28.9 %collective-permute-start.36 = (bf16[4,128,512]{2,1,0:T(8,128)(2,1)S(1)}, bf16[4,128,512]{2,1,0:T(8,128)(2,1)S(1)}, u32[]{:S(2)}, u32[]{:S(2)}) collective-permute-start(bf16[4,128,512]{2,1,0:T(8,128)(2,1)S(1)} %fusion.54), channel_id=1, source_target_pairs={{0,2},{1,3},{2,0},{3,1},{4,6},{5,7},{6,4},{7,5},{8,10},{9,11},{10,... | collective-permute-start | bytes 1572872 | tf_op jit(solution)/shard_map/ppermute | solution.py:29
  828.1 40.4 %collective-permute-start.40 = (bf16[8,128,640]{2,1,0:T(8,128)(2,1)}, bf16[8,128,640]{2,1,0:T(8,128)(2,1)S(1)}, u32[]{:S(2)}, u32[]{:S(2)}) collective-permute-start(bf16[8,128,640]{2,1,0:T(8,128)(2,1)} %bitcast.290), channel_id=1, source_target_pairs={{0,2},{1,3},{2,0},{3,1},{4,6},{5,7},{6,4},{7,5},{8,10},{9,11},{10,... | collective-permute-start | bytes 3932168 | tf_op jit(solution)/shard_map/ppermute | solution.py:29
  834.5 33.9 %collective-permute-start.41 = (bf16[8,128,640]{2,1,0:T(8,128)(2,1)}, bf16[8,128,640]{2,1,0:T(8,128)(2,1)}, u32[]{:S(2)}, u32[]{:S(2)}) collective-permute-start(bf16[8,128,640]{2,1,0:T(8,128)(2,1)} %bitcast.291), channel_id=1, source_target_pairs={{0,4},{1,5},{2,6},{3,7},{4,0},{5,1},{6,2},{7,3},{8,12},{9,13},{10,... | collective-permute-start | bytes 3932168 | tf_op jit(solution)/shard_map/ppermute | solution.py:29
  835.5 32.9 %collective-permute-start.39 = (bf16[1,176,2048]{2,1,0:T(8,128)(2,1)}, bf16[1,176,2048]{2,1,0:T(8,128)(2,1)}, u32[]{:S(2)}, u32[]{:S(2)}) collective-permute-start(bf16[1,176,2048]{2,1,0:T(8,128)(2,1)} %fusion.33), channel_id=1, source_target_pairs={{0,16},{1,17},{2,18},{3,19},{4,20},{5,21},{6,22},{7,23},{8,24},{9,... | collective-permute-start | bytes 2162696 | tf_op jit(solution)/shard_map/ppermute | solution.py:29
  875.1 20.4 %collective-permute-start.42 = (bf16[512,2048]{1,0:T(8,128)(2,1)}, bf16[512,2048]{1,0:T(8,128)(2,1)}, u32[]{:S(2)}, u32[]{:S(2)}) collective-permute-start(bf16[512,2048]{1,0:T(8,128)(2,1)} %constant_dynamic-slice_fusion.4), channel_id=1, source_target_pairs={{0,1},{1,0},{2,3},{3,2},{4,5},{5,4},{6,7},{7,6},{8,9},{9,8},{10,11... | collective-permute-start | bytes 6291464 | tf_op jit(solution)/shard_map/ppermute | solution.py:29
  875.1 20.3 %collective-permute-start.44 = (bf16[4,128,640]{2,1,0:T(8,128)(2,1)}, bf16[4,128,640]{2,1,0:T(8,128)(2,1)}, u32[]{:S(2)}, u32[]{:S(2)}) collective-permute-start(bf16[4,128,640]{2,1,0:T(8,128)(2,1)} %fusion.50), channel_id=1, source_target_pairs={{0,2},{1,3},{2,0},{3,1},{4,6},{5,7},{6,4},{7,5},{8,10},{9,11},{10,... | collective-permute-start | bytes 1966088 | tf_op jit(solution)/shard_map/ppermute | solution.py:29
  876.2 19.3 %collective-permute-start.43 = (bf16[4,128,640]{2,1,0:T(8,128)(2,1)}, bf16[4,128,640]{2,1,0:T(8,128)(2,1)}, u32[]{:S(2)}, u32[]{:S(2)}) collective-permute-start(bf16[4,128,640]{2,1,0:T(8,128)(2,1)} %get-tuple-element.388), channel_id=1, source_target_pairs={{0,4},{1,5},{2,6},{3,7},{4,0},{5,1},{6,2},{7,3},{8,12},{9,13},{10,... | collective-permute-start | bytes 1966088 | tf_op jit(solution)/shard_map/ppermute | solution.py:29
  881.4 14.0 %collective-permute-start.45 = (bf16[2,128,1024]{2,1,0:T(8,128)(2,1)}, bf16[2,128,1024]{2,1,0:T(8,128)(2,1)}, u32[]{:S(2)}, u32[]{:S(2)}) collective-permute-start(bf16[2,128,1024]{2,1,0:T(8,128)(2,1)} %get-tuple-element.378), channel_id=1, source_target_pairs={{0,8},{1,9},{2,10},{3,11},{4,12},{5,13},{6,14},{7,15},{8,0},{9,1},... | collective-permute-start | bytes 1572872 | tf_op jit(solution)/shard_map/ppermute | solution.py:29
  904.0 2.3 collective-permute-start.46
  906.4 3.8 collective-permute-start.47
  907.6 36.9 %collective-permute-start.51 = (bf16[2,64,1408]{2,1,0:T(8,128)(2,1)S(1)}, bf16[2,64,1408]{2,1,0:T(8,128)(2,1)S(1)}, u32[]{:S(2)}, u32[]{:S(2)}) collective-permute-start(bf16[2,64,1408]{2,1,0:T(8,128)(2,1)S(1)} %bitcast.295), channel_id=1, source_target_pairs={{0,1},{1,0},{2,3},{3,2},{4,5},{5,4},{6,7},{7,6},{8,9},{9,8},{10,11... | collective-permute-start | bytes 1081352 | tf_op jit(solution)/shard_map/ppermute | solution.py:29
  907.8 36.8 %collective-permute-start.52 = (bf16[2,64,1408]{2,1,0:T(8,128)(2,1)S(1)}, bf16[2,64,1408]{2,1,0:T(8,128)(2,1)S(1)}, u32[]{:S(2)}, u32[]{:S(2)}) collective-permute-start(bf16[2,64,1408]{2,1,0:T(8,128)(2,1)S(1)} %bitcast.296), channel_id=1, source_target_pairs={{0,8},{1,9},{2,10},{3,11},{4,12},{5,13},{6,14},{7,15},{8,0},{9,1},... | collective-permute-start | bytes 1081352 | tf_op jit(solution)/shard_map/ppermute | solution.py:29
  908.2 36.4 %collective-permute-start.53 = (bf16[2,64,1408]{2,1,0:T(8,128)(2,1)S(1)}, bf16[2,64,1408]{2,1,0:T(8,128)(2,1)S(1)}, u32[]{:S(2)}, u32[]{:S(2)}) collective-permute-start(bf16[2,64,1408]{2,1,0:T(8,128)(2,1)S(1)} %bitcast.297), channel_id=1, source_target_pairs={{0,9},{1,8},{2,11},{3,10},{4,13},{5,12},{6,15},{7,14},{8,1},{9,0},... | collective-permute-start | bytes 1081352 | tf_op jit(solution)/shard_map/ppermute | solution.py:29
  909.8 32.0 %collective-permute-start.50 = (bf16[2,128,1280]{2,1,0:T(8,128)(2,1)S(1)}, bf16[2,128,1280]{2,1,0:T(8,128)(2,1)S(1)}, u32[]{:S(2)}, u32[]{:S(2)}) collective-permute-start(bf16[2,128,1280]{2,1,0:T(8,128)(2,1)S(1)} %get-tuple-element.375), channel_id=1, source_target_pairs={{0,8},{1,9},{2,10},{3,11},{4,12},{5,13},{6,14},{7,15},{8,0},{9,1},... | collective-permute-start | bytes 1966088 | tf_op jit(solution)/shard_map/ppermute | solution.py:29
  910.2 3.9 collective-permute-start.48
  914.1 26.6 %collective-permute-start.49 = (f32[2,2048]{1,0:T(2,128)S(1)}, f32[2,2048]{1,0:T(2,128)S(1)}, u32[]{:S(2)}, u32[]{:S(2)}) collective-permute-start(f32[2,2048]{1,0:T(2,128)S(1)} %add.662), channel_id=1, source_target_pairs={{0,8},{1,9},{2,10},{3,11},{4,12},{5,13},{6,14},{7,15},{8,0},{9,1},... | collective-permute-start | bytes 49160 | tf_op jit(solution)/shard_map/ppermute | solution.py:29
  940.8 45.3 %collective-permute-start.56 = (bf16[1,128,1024]{2,1,0:T(8,128)(2,1)S(1)}, bf16[1,128,1024]{2,1,0:T(8,128)(2,1)}, u32[]{:S(2)}, u32[]{:S(2)}) collective-permute-start(bf16[1,128,1024]{2,1,0:T(8,128)(2,1)S(1)} %get-tuple-element.395), channel_id=1, source_target_pairs={{0,16},{1,17},{2,18},{3,19},{4,20},{5,21},{6,22},{7,23},{8,24},{9,... | collective-permute-start | bytes 786440 | tf_op jit(solution)/shard_map/ppermute | solution.py:29
  942.6 43.5 %collective-permute-start.55 = (bf16[1,128,1280]{2,1,0:T(8,128)(2,1)}, bf16[1,128,1280]{2,1,0:T(8,128)(2,1)}, u32[]{:S(2)}, u32[]{:S(2)}) collective-permute-start(bf16[1,128,1280]{2,1,0:T(8,128)(2,1)} %get-tuple-element.393), channel_id=1, source_target_pairs={{0,16},{1,17},{2,18},{3,19},{4,20},{5,21},{6,22},{7,23},{8,24},{9,... | collective-permute-start | bytes 983048 | tf_op jit(solution)/shard_map/ppermute | solution.py:29
  959.1 25.6 %collective-permute-start.54 = (f32[2,2048]{1,0:T(2,128)S(1)}, f32[2,2048]{1,0:T(2,128)}, u32[]{:S(2)}, u32[]{:S(2)}) collective-permute-start(f32[2,2048]{1,0:T(2,128)S(1)} %add.663), channel_id=1, source_target_pairs={{0,16},{1,17},{2,18},{3,19},{4,20},{5,21},{6,22},{7,23},{8,24},{9,... | collective-permute-start | bytes 49160 | tf_op jit(solution)/shard_map/ppermute | solution.py:29
  987.3 2.1 collective-permute-start.57
  (94 other events, 587.0 us)

commit v5 on v4

--- a/solution.py
+++ b/solution.py
@@ -82,12 +82,16 @@
         self.make, self.bits, self.bit = make, bits, bits[-1]
 
     def send(self, *start):
-        self.sent = after(self.make(1 - side(self.bit)), *start)
+        self.sent = after(self.make(1 - side(self.bit), *start), *start)
         self.here = flip(self.sent, self.bit)
 
     def keep(self, *gate):
-        self.kept = self.make(after(side(self.bit), *gate))
+        self.kept = self.make(side(self.bit), *gate)
         return self.kept
+
+    def gated(self, gate):
+        self.here = after(self.here, *gate)
+        return self
 
     def hold(self, x, *gate):
         x, self.here = lax.optimization_barrier((x, after(self.here, *gate)))
@@ -430,7 +434,7 @@
 
 
 def product_body(count, group, index, *refs):
-    left, right, out = refs[: count * group], refs[count * group : -1], refs[-1]
+    left, right, out = refs[: count * group], refs[count * group : count * (group + 1)], refs[-1]
     acc = 0.0
     for i in range(count):
         rows = jnp.concatenate([a[...] for a in left[i * group : (i + 1) * group]], axis=1)
@@ -438,7 +442,7 @@
     out[...] = acc.astype(out.dtype)
 
 
-def row_blocks(left, right, index, size, half=None):
+def row_blocks(left, right, index, size, half=None, deps=()):
     count = index.shape[0]
     group = 4 if count % 4 == 0 else 1
     cols = right[0].shape[1] // (1 if half is None else 2)
@@ -454,12 +458,64 @@
             num_scalar_prefetch=1,
             grid=(count // group,),
             in_specs=[block(a.shape[0], j) for a in left for j in range(group)]
-            + [pl.BlockSpec((b.shape[0], cols), lambda i, at: (0, at_col)) for b in right],
+            + [pl.BlockSpec((b.shape[0], cols), lambda i, at: (0, at_col)) for b in right]
+            + [pl.BlockSpec(memory_space=pl.ANY)] * len(deps),
             out_specs=pl.BlockSpec((group * size, cols), lambda i, at: (i, 0)),
         ),
         compiler_params=pltpu.CompilerParams(vmem_limit_bytes=56 * MIB),
         cost_estimate=pl.CostEstimate(flops=0, bytes_accessed=0, transcendentals=0),
-    )(index.astype(jnp.int32), *[a for a in left for _ in range(group)], *right)
+    )(index.astype(jnp.int32), *[a for a in left for _ in range(group)], *right, *deps)
+
+
+def apart_body(places, padded, w_ref, out_ref):
+    w = w_ref[...].astype(f32)
+    unit = w.shape[1] // sum(len(p) for p in places)
+    gap = [jnp.zeros((w.shape[0], padded - unit), f32)] if padded > unit else []
+    for q, place in enumerate(places):
+        blocks = []
+        for d in place:
+            blocks += [w[:, d * unit : (d + 1) * unit]] + gap
+        out_ref[q] = jnp.concatenate(blocks, axis=1).astype(bf16)
+
+
+def apart(w, places, padded):
+    rows, cols = w.shape[0], len(places[0]) * padded
+    return pl.pallas_call(
+        lambda *refs: apart_body(places, padded, *refs),
+        out_shape=jax.ShapeDtypeStruct((len(places), rows, cols), bf16),
+        in_specs=[INV],
+        out_specs=INV,
+        compiler_params=pltpu.CompilerParams(vmem_limit_bytes=24 * MIB),
+        cost_estimate=pl.CostEstimate(flops=0, bytes_accessed=0, transcendentals=0),
+    )(w)
+
+
+def together_body(places, padded, unit, member, *refs):
+    pieces, outs, held = refs[:4], refs[4:6], refs[6]
+    for k, piece in enumerate(pieces):
+        held[k] = piece[...].astype(f32)
+    cols = len(places[0]) * padded
+    for j, out in enumerate(outs):
+        blocks = {}
+        for q, place in enumerate(places):
+            for i, d in enumerate(place):
+                at = j * cols + i * padded
+                blocks[d] = held[member[0] ^ q][:, at : at + unit]
+        out[...] = jnp.concatenate([blocks[d] for d in sorted(blocks)], axis=1)
+
+
+def together(pieces, places, padded, unit, member):
+    rows = pieces[0].shape[0]
+    whole = jax.ShapeDtypeStruct((rows, unit * sum(len(p) for p in places)), f32)
+    return pl.pallas_call(
+        lambda *refs: together_body(places, padded, unit, *refs),
+        out_shape=[whole, whole],
+        in_specs=[pl.BlockSpec(memory_space=pltpu.SMEM)] + [INV] * 4,
+        out_specs=[INV, INV],
+        scratch_shapes=[pltpu.VMEM((4,) + pieces[0].shape, f32)],
+        compiler_params=pltpu.CompilerParams(vmem_limit_bytes=40 * MIB),
+        cost_estimate=pl.CostEstimate(flops=0, bytes_accessed=0, transcendentals=0),
+    )(jnp.reshape(member, (1,)).astype(jnp.int32), *pieces)
 
 
 def wide_body(d_ref, w_ref, out_ref):
@@ -487,10 +543,10 @@
     cols = right[0].shape[1] // (1 if half is None else 2)
     ids = np.asarray([(at + more) // 2 for at in grown(bits[:-1][::-1]) for more in within], np.int32)
 
-    def make(index):
+    def make(index, *deps):
         index = jnp.asarray(ids) + index * (bits[-1] // 2)
         if size % 128 == 0:
-            out = row_blocks(left, right, index, size, half)
+            out = row_blocks(left, right, index, size, half, deps)
         else:
             out = sum(dot_rows(a, b) for a, b in zip(left, right)).astype(bf16).reshape(n // 2, size, -1)
             out = out[index][..., (half or 0) * cols : (half or 0) * cols + cols]
@@ -841,14 +897,9 @@
     padded = -(-unit // 16) * 16
     cols = quads * padded
 
-    def by_quad(w):
-        w = w.reshape(rows, above, 2, below, 2, unit)
-        w = jnp.pad(w, ((0, 0),) * 5 + ((0, padded - unit),))
-        return w.transpose(2, 4, 0, 1, 3, 5).reshape(4, rows, cols)
-
-    gate, up = by_quad(w_gate), by_quad(w_up)
+    gate, up = apart(w_gate, groups, padded), apart(w_up, groups, padded)
     down = jnp.pad(w_down, ((0, padded - unit), (0, 0)))
-    near_grad = flip(out_grad, 1)
+    near_grad = side_by_side(core, out_grad, flip(out_grad, 1))
 
     def by_core(which):
         return jnp.concatenate([column_half(w, which) for w in (w_query, w_key, w_value)], axis=1)
@@ -937,7 +988,6 @@
     mixed_heads, out_there, *flows = lax.optimization_barrier((mixed_heads, out_there, *flows))
     gate_xy, up_xy, down_b = flows
     down = [down, down_a, down_b]
-    near_grad = jnp.concatenate([out_grad, near_grad])
     out_all = side_by_side(core, out_half, out_there, 1)
     mixed_chip = side_by_side(core, mixed_heads, flip(mixed_heads, 1), 1)
     middle = inputs32 + dot(row_half(mixed_chip, core), out_all)
@@ -946,38 +996,38 @@
     hidden_two = (normed_two * gain_two).astype(bf16)
 
     far_hidden = flip(hidden_two, PAIR)
-    near_hidden = jnp.concatenate([hidden_two, flip(hidden_two, 1)])
+    near_hidden = side_by_side(core, hidden_two, flip(hidden_two, 1))
     gate = [w.reshape(-1, 2 * rows, cols) for w in (gate, gate_x, gate_y, gate_xy)]
     up = [w.reshape(-1, 2 * rows, cols) for w in (up, up_x, up_y, up_xy)]
     order = [(at + more) // 2 for at in grown(qbits[:-2]) for more in (0, PAIR)]
     sides = jnp.stack([place, place ^ 1, place ^ 2, place ^ 3, side(qbits[0])])
     near = ffn(near_hidden, near_grad, gate, up, down, order, sides)
     far_hidden, far_there = after(far_hidden, *near), move(far_grad, 1, (near_hidden,), (near[0],))
-    far_grad = jnp.concatenate([far_grad, far_there])
-    far_hidden = jnp.concatenate([far_hidden, flip(far_hidden, 1)])
+    far_grad = side_by_side(core, far_grad, far_there)
+    far_hidden = side_by_side(core, far_hidden, flip(far_hidden, 1))
     far = ffn(far_hidden, far_grad, gate, up, down, order, sides)
     start, stop = (near[0], far_hidden), (far[0],)
-    near_parts = [move(near[i][tokens:], 1, start, stop) for i in (3, 0)]
+    near_parts = [move(row_half(near[i], 1 - core), 1, start, stop) for i in (3, 0)]
     far, near_parts = lax.optimization_barrier((far, near_parts))
 
     right = [near[2], far[2]]
     sum_gate = Scatter(part_maker([near_hidden, far_hidden], right, qbits, (0, PAIR), 0), qbits)
     sum_gate.send()
     start, stop = (far[0],), (sum_gate.sent,)
-    far_parts = [move(far[i][tokens:], 1, start, stop) for i in (3, 0)]
+    far_parts = [move(row_half(far[i], 1 - core), 1, start, stop) for i in (3, 0)]
     sent, far_parts = lax.optimization_barrier((sum_gate.sent, far_parts))
-    d_far = (far[3][:tokens].astype(f32) + far_parts[0].astype(f32)).astype(bf16)
-    y_far = (far[0][:tokens].astype(f32) + far_parts[1].astype(f32)).astype(bf16)
-    sum_up = Scatter(part_maker([after(near_hidden, sent, d_far, y_far), far_hidden], right, swapped, (0, PAIR), 1), swapped)
-    sum_up.send()
+    d_far = (row_half(far[3], core).astype(f32) + far_parts[0].astype(f32)).astype(bf16)
+    y_far = (row_half(far[0], core).astype(f32) + far_parts[1].astype(f32)).astype(bf16)
+    sum_up = Scatter(part_maker([near_hidden, far_hidden], right, swapped, (0, PAIR), 1), swapped)
+    sum_up.send(sent, d_far, y_far)
     sum_gate.keep(sum_up.sent)
     sum_up.keep(sum_gate.kept)
-    term = row_blocks([near[1], far[1]], [after(near_grad, sum_up.kept), far_grad], jnp.arange(cols // 128), 128)
+    term = row_blocks([near[1], far[1]], [near_grad, far_grad], jnp.arange(cols // 128), 128, None, (sum_up.kept,))
     d_far = move(d_far, PAIR, (), (term,))
     d_far = sum_gate.hold(d_far, term)
     near_parts = after(near_parts, d_far)
-    d_near = near[3][:tokens].astype(f32) + near_parts[0].astype(f32)
-    y_near = near[0][:tokens].astype(f32) + near_parts[1].astype(f32)
+    d_near = row_half(near[3], core).astype(f32) + near_parts[0].astype(f32)
+    y_near = row_half(near[0], core).astype(f32) + near_parts[1].astype(f32)
     d_hidden_two = d_near + d_far.astype(f32)
     term_norm_two = jnp.sum(d_hidden_two * normed_two, axis=0)
     scaled_two = d_hidden_two * gain_two
@@ -997,10 +1047,10 @@
     sum_both = join([sum_gate, sum_up])
     sent = [sum_both.step()]
 
-    def down_x(index):
+    def down_x(index, *_):
         return pick(term.reshape(quads // 2, 2, padded, width)[..., :half], index, 1)
 
-    def down_y(index):
+    def down_y(index, *_):
         return pick(term.reshape(quads // 4, 2, 2, padded, width)[..., half:], index, 1).reshape(-1, padded, half)
 
     sum_down = [Scatter(down_x, qbits), Scatter(down_y, swapped)]
@@ -1031,28 +1081,30 @@
     cut = d_qkv.shape[1] // 2
     sums = []
     for h, bits in ((0, cbits), (1, cbits[:-2] + [cbits[-1], cbits[-2]])):
-        sums.append(Scatter(part_maker([after(hidden_chip, *(p.sent for p in sums))], [d_qkv], bits, (0,), h), bits))
-        sums[-1].send()
+        sums.append(Scatter(part_maker([hidden_chip], [d_qkv], bits, (0,), h), bits))
+        sums[-1].send(*(p.sent for p in sums[:-1]))
     start = tuple(part.sent for part in sums)
     for part in sums:
         part.keep(*start)
         start = (part.kept,)
+    rest_out = join([part.gated(start) for part in out_sums])
+    start = start + (rest_out.step(),)
     d_hidden_one = times_transposed(after(d_qkv, *start), qkv_all)
-    rest_out = join(out_sums)
-    for part in [sum_down] + sums:
+    for part in [sum_down, rest_out] + sums:
         d_hidden_one = part.hold(d_hidden_one, d_hidden_one)
-    sent = [part.step() for part in sums] + [rest_out.step()]
+    sent = [part.step() for part in sums]
     d_hidden_one = after(d_hidden_one, *sent)
     theirs = flip(row_half(d_hidden_one, 1 - core), 1)
-    gate_sum = after(sum_both.finish(), *sent).reshape(4, rows, 2, cols).transpose(0, 2, 1, 3)
-    parts = [flip(pick(gate_sum, member ^ k).astype(bf16), to_member[k]) for k in range(1, 4)]
+    gate_sum = after(sum_both.finish(), *sent).astype(bf16).reshape(4, rows, 2 * cols)
+    parts = [flip(after(pick(gate_sum, member ^ k), theirs), to_member[k]) for k in range(1, 4)]
     d_hidden_one = row_half(d_hidden_one, core).astype(f32) + theirs.astype(f32)
     term_norm_one = jnp.sum(d_hidden_one * normed_one, axis=0)
     scaled_one = d_hidden_one * gain_one
     mean_one = jnp.mean(scaled_one * normed_one, axis=1, keepdims=True)
     norms = jnp.stack([term_norm_one, term_norm_two])
-    for part in sums + [rest_out]:
+    for part in sums:
         norms = part.hold(norms, theirs)
+    norms, parts = lax.optimization_barrier((norms, parts))
     rest = join(sums)
     sent = [rest.step()] + [rest_out.step() for _ in rest_out.bits[1:]]
     norms = after(norms, *sent)
@@ -1060,15 +1112,11 @@
     norms = norms + flip(norms, cbits[-1])
     norms = norms + flip(norms, cbits[-2])
     norms = norms + flip(norms, cbits[-3])
-    norms = rest.hold(norms, norms)
-    norms, parts = lax.optimization_barrier((norms, parts))
+    norms = rest_out.hold(rest.hold(norms, norms), norms)
     while len(rest.bits) > 1:
         sent = [rest.step()]
     norms = after(norms, *sent)
-    gate_sum = assemble_all([(member, pick(gate_sum, member))] + [(member ^ k, p.astype(f32)) for k, p in enumerate(parts, 1)])
-    gate_sum = after(gate_sum, *sent).reshape(2, 2, 2, rows, above, below, padded)[..., :unit]
-    gate_sum = gate_sum.transpose(2, 3, 4, 0, 5, 1, 6).reshape(2, rows, n * unit)
-    grad_gate, grad_up = gate_sum[0], gate_sum[1]
+    grad_gate, grad_up = together([pick(gate_sum, member), *parts], groups, padded, unit, member)
     for bit in cbits[:-3]:
         norms = norms + flip(norms, bit)
     norms = pick(norms.reshape(2, n, rows), me, 1)

time: 1000 us -> 933 us (0.933)
  local copies, waits for them, and re-layouts: 146 us -> 110 us
  other arithmetic: 107 us -> 87.2 us
  waiting for transfers between devices: 77.3 us -> 61.1 us
    reshape x8 -> x0, local copies, waits for them, and re-layouts: 24.5 us -> none  [the longest x4 8.74 us: by_quad(): w = w.reshape(rows, above, 2, below, 2, unit)]
    slice x7 -> x0, local copies, waits for them, and re-layouts: 16.6 us -> none  [the longest x3 6.88 us: shards(): grad_gate, grad_up = (gate_sum[0], gate_sum[1])]
    ppermute x58, waiting for transfers between devices: 77.3 us -> 61.1 us  [flip(): return lax.ppermute(x, 'tok', [(i, i ^ bits) for i in range(n)])]
    dynamic_slice x2 -> x5, local copies, waits for them, and re-layouts: 1.54 us -> 12.2 us  [row_half(): lax.dynamic_slice_in_dim(w, which * (w.shape[0] // 2), w.shape[0] // 2, 0)]
    unnamed x210 -> x236, local copies, waits for them, and re-layouts: 28.6 us -> 32 us
  transfers between devices with their start and end apart: 58 -> 58, of which waited for: 12 -> 13; matrix products, arithmetic and copies ran while one was open for 18% -> 14% of each run, Pallas kernels for 53% -> 57%
where the time goes in v5:
time: 933 us; the launch traced here: 924 us
  Pallas kernels  583 us (62%)
  local copies, waits for them, and re-layouts  110 us (12%)
  other arithmetic  87.2 us (9%)
  waiting for transfers between devices  61.1 us (7%)
  starting transfers between devices  57 us (6%)
  matrix products  21.7 us (2%)
    pallas_call x2, Pallas kernels, others(): pl.pallas_call(lambda *refs: scan_body(sign, *refs), out_shape=jax.ShapeD...  159 us
    pallas_call x13, Pallas kernels, row_blocks(): pl.pallas_call(lambda *refs: product_body(len(left), group, *refs), out_s...  112 us
    pallas_call x4, Pallas kernels, call(): pl.pallas_call(body, grid=(2, self.heads), in_specs=ins, out_specs=outs,...  105 us
    pallas_call x2, Pallas kernels, ffn(): pl.pallas_call(lambda *refs: ffn_body(order, *refs), out_shape=[jax.Shape...  95.5 us
    ppermute x58, waiting for transfers between devices, flip(): return lax.ppermute(x, 'tok', [(i, i ^ bits) for i in range(n)])  61.1 us
    ppermute x58, starting transfers between devices, flip(): return lax.ppermute(x, 'tok', [(i, i ^ bits) for i in range(n)])  57 us
    pallas_call x1, Pallas kernels, spread_first(): pl.pallas_call(first_body, out_shape=[jax.ShapeDtypeStruct((32,) + gains....  49.9 us
    pallas_call x1, Pallas kernels, spread_second(): pl.pallas_call(second_body, out_shape=[jax.ShapeDtypeStruct((4, 4) + z4.s...  47.6 us
  transfers between devices with their start and end apart: 58, of which 13 were waited for; matrix products, arithmetic and copies ran while one was open for 14% of the time, Pallas kernels for 57%

profile of v5, /device:TPU:0, one launch (start us, length us, event | category | flops | bytes accessed | tf_op | source)
XLA Modules:
  0.0 923.7 jit_solution(12640066875607047620)
XLA Ops:
  10.7 49.9 %shard_map.295 = (f32[32,8,128]{2,1,0:T(8,128)S(1)}, bf16[4,64,1408]{2,1,0:T(8,128)(2,1)S(1)}, bf16[4,64,1408]{2,1,0:T(8,128)(2,1)}, bf16[4,128,1280]{2,1,0:T(8,128)(2,1)S(1)}, bf16[4,176,2048]{2,1,0:T(8,128)(2,1)S(1)}) custom-call(f32[1,8,128]{2,1,0:T(8,128)S(1)} %fusion.67.gains_in, bf16[4,64,1408]{2,1,0:T(8,128)(2,1)S(1)} %shard_map.293.gate_in, ...), custom_call_target="tpu_custom_call" | custom-call | tf_op jit(solution)/shard_map/pallas_call | solution.py:223
  62.4 2.6 broadcast.80.clone
  65.0 2.6 constant_dynamic-update-slice_fusion.13
  70.4 47.6 %shard_map.296 = (bf16[4,4,128,1280]{3,2,1,0:T(8,128)(2,1)S(1)}, bf16[4,128,1024]{2,1,0:T(8,128)(2,1)S(1)}, bf16[2,4,64,1408]{3,2,1,0:T(8,128)(2,1)S(1)}) custom-call(bf16[4,128,1280]{2,1,0:T(8,128)(2,1)S(1)} %get-tuple-element.194.z4, bf16[64,1024]{1,0:T(8,128)(2,1)S(1)} %get-tuple-element.420.out_mine, bf16[64,1024]{1,0:T(8,128)(2,1)S(1)} %get-tuple-element.419.out_theirs, ...), custom_call_target="tpu_custom_call" | custom-call | tf_op jit(solution)/shard_map/pallas_call | solution.py:276
  120.5 3.2 constant_dynamic-update-slice_fusion.12.refs_1_.refs_2_.refs_3_.refs_4_
  123.7 7.5 convolution_convert_fusion.k_ref.v_ref.q_ref
  131.3 10.5 %shard_map.297 = f32[8,2,168,128]{3,2,1,0:T(8,128)S(1)} custom-call(s32[2]{0:T(128)S(1)} %pad_add_fusion.scal, bf16[1024,1280]{1,0:T(8,128)(2,1)S(1)} %convolution_convert_fusion.k_ref.v_ref.q_ref, bf16[1024,1280]{1,0:T(8,128)(2,1)S(1)} %convolution_convert_fusion.k_ref.v_ref.q_ref, bf16[8,128,160]{2,1,0:T(8,128)(2,1)S(1)} %copy-done.14, ...), custom_call_target="tpu_custom_call" | custom-call | tf_op jit(solution)/shard_map/pallas_call | solution.py:762
  143.0 10.0 %collective-permute-done.3 = bf16[4,64,1408]{2,1,0:T(8,128)(2,1)S(1)} collective-permute-done((bf16[4,64,1408]{2,1,0:T(8,128)(2,1)}, bf16[4,64,1408]{2,1,0:T(8,128)(2,1)S(1)}, u32[]{:S(2)}, u32[]{:S(2)}) %collective-permute-start.3) | collective-permute-done | bytes 720928 | tf_op jit(solution)/shard_map/ppermute | solution.py:29
  157.3 3.4 pad_maximum_fusion
  169.4 2.5 broadcast_in_dim.61
  173.0 100.2 %shard_map.298 = f32[8,168,128]{2,1,0:T(8,128)S(1)} custom-call(f32[8,168,128]{2,1,0:T(8,128)S(1)} %copy-done.28), custom_call_target="tpu_custom_call" | custom-call | tf_op jit(solution)/shard_map/pallas_call | solution.py:831
  280.1 3.6 fusion.74
  286.6 10.3 %collective-permute-start.13 = (bf16[704,512]{1,0:T(8,128)(2,1)}, bf16[704,512]{1,0:T(8,128)(2,1)S(1)}, u32[]{:S(2)}, u32[]{:S(2)}) collective-permute-start(bf16[704,512]{1,0:T(8,128)(2,1)} %slice.130), channel_id=1, source_target_pairs={{0,16},{1,17},{2,18},{3,19},{4,20},{5,21},{6,22},{7,23},{8,24},{9,... | collective-permute-start | bytes 2162696 | tf_op jit(solution)/shard_map/ppermute | solution.py:29
  299.8 22.1 %shard_map.299 = (f32[1024,1024]{1,0:T(8,128)}, bf16[1024,1024]{1,0:T(8,128)(2,1)}) custom-call(bf16[1024,1280]{1,0:T(8,128)(2,1)} %copy-done, bf16[1024,1280]{1,0:T(8,128)(2,1)} %copy-done, bf16[1024,1280]{1,0:T(8,128)(2,1)} %copy-done, s32[1024,1]{1,0:T(8,128)S(1)} %copy.134.lo_ref, f32[8,2,168,128]{3,2,1,0:T(8,128)S(1)} %copy.135.carry_ref, ...), custom_call_target="tpu_custom_call" | custom-call | tf_op jit(solution)/shard_map/pallas_call | solution.py:762
  321.9 6.6 collective-permute-done.13.refs_13_
  329.8 2.7 constant_dynamic-update-slice_fusion.9
  334.9 2.7 constant_dynamic-update-slice_fusion.8
  338.0 2.8 copy-done.46
  340.8 4.8 multiply_reduce_fusion.2
  353.0 3.2 constant_dynamic-update-slice_fusion.6.refs_1_.refs_2_.refs_3_.refs_4_
  356.2 47.8 %shard_map.300 = (bf16[1024,2048]{1,0:T(8,128)(2,1)}, bf16[1024,1408]{1,0:T(8,128)(2,1)}, bf16[1024,2816]{1,0:T(8,128)(2,1)}, bf16[1024,2048]{1,0:T(8,128)(2,1)}) custom-call(s32[5]{0:T(128)S(1)} %stack.81.refs_0_, bf16[1024,2048]{1,0:T(8,128)(2,1)} %constant_dynamic-update-slice_fusion.6.refs_1_.refs_2_.refs_3_.refs_4_, bf16[1024,2048]{1,0:T(8,128)(2,1)} %copy-done.42, ...), custom_call_target="tpu_custom_call" | custom-call | tf_op jit(solution)/shard_map/pallas_call | solution.py:420
  404.4 3.4 constant_dynamic-slice_fusion.8
  418.5 47.8 %shard_map.301 = (bf16[1024,2048]{1,0:T(8,128)(2,1)}, bf16[1024,1408]{1,0:T(8,128)(2,1)}, bf16[1024,2816]{1,0:T(8,128)(2,1)}, bf16[1024,2048]{1,0:T(8,128)(2,1)}) custom-call(s32[5]{0:T(128)S(1)} %stack.81.refs_0_, bf16[1024,2048]{1,0:T(8,128)(2,1)} %copy-done.37, bf16[1024,2048]{1,0:T(8,128)(2,1)} %copy-done.43, bf16[4,128,1408]{2,1,0:T(8,128)(2,1)S(1)} %bitcast.256, ...), custom_call_target="tpu_custom_call" | custom-call | tf_op jit(solution)/shard_map/pallas_call | solution.py:420
  466.3 5.6 constant_dynamic-slice_fusion.6
  472.9 13.4 %shard_map.302 = bf16[1024,1408]{1,0:T(8,128)(2,1)} custom-call(s32[8]{0:T(128)} %get-tuple-element.436.refs_0_, bf16[1024,2048]{1,0:T(8,128)(2,1)} %constant_dynamic-update-slice_fusion.6.refs_1_.refs_2_.refs_3_.refs_4_, bf16[1024,2048]{1,0:T(8,128)(2,1)} %constant_dynamic-update-slice_fusion.6.refs_1_.refs_2_.refs_3_.refs_4_, ...), custom_call_target="tpu_custom_call" | custom-call | tf_op jit(solution)/shard_map/pallas_call | solution.py:454
  487.6 3.8 add_convert_fusion.2.refs_12_
  492.0 3.7 add_convert_fusion.1.refs_13_
  495.7 12.5 %shard_map.303 = bf16[1024,1408]{1,0:T(8,128)(2,1)} custom-call(s32[8]{0:T(128)} %get-tuple-element.433.refs_0_, bf16[1024,2048]{1,0:T(8,128)(2,1)} %constant_dynamic-update-slice_fusion.6.refs_1_.refs_2_.refs_3_.refs_4_, bf16[1024,2048]{1,0:T(8,128)(2,1)} %constant_dynamic-update-slice_fusion.6.refs_1_.refs_2_.refs_3_.refs_4_, ...), custom_call_target="tpu_custom_call" | custom-call | tf_op jit(solution)/shard_map/pallas_call | solution.py:454
  509.0 12.5 %shard_map.304 = bf16[1024,1408]{1,0:T(8,128)(2,1)} custom-call(s32[8]{0:T(128)} %get-tuple-element.435.refs_0_, bf16[1024,2048]{1,0:T(8,128)(2,1)} %constant_dynamic-update-slice_fusion.6.refs_1_.refs_2_.refs_3_.refs_4_, bf16[1024,2048]{1,0:T(8,128)(2,1)} %constant_dynamic-update-slice_fusion.6.refs_1_.refs_2_.refs_3_.refs_4_, ...), custom_call_target="tpu_custom_call" | custom-call | tf_op jit(solution)/shard_map/pallas_call | solution.py:454
  521.5 12.5 %shard_map.305 = bf16[1024,1408]{1,0:T(8,128)(2,1)} custom-call(s32[8]{0:T(128)} %get-tuple-element.434.refs_0_, bf16[1024,2048]{1,0:T(8,128)(2,1)} %constant_dynamic-update-slice_fusion.6.refs_1_.refs_2_.refs_3_.refs_4_, bf16[1024,2048]{1,0:T(8,128)(2,1)} %constant_dynamic-update-slice_fusion.6.refs_1_.refs_2_.refs_3_.refs_4_, ...), custom_call_target="tpu_custom_call" | custom-call | tf_op jit(solution)/shard_map/pallas_call | solution.py:454
  534.6 20.2 %shard_map.306 = bf16[1408,2048]{1,0:T(8,128)(2,1)} custom-call(s32[11]{0:T(128)} %iota.10.refs_0_, bf16[1024,1408]{1,0:T(8,128)(2,1)} %get-tuple-element.245.refs_1_, bf16[1024,1408]{1,0:T(8,128)(2,1)} %get-tuple-element.269.refs_2_, bf16[1024,2048]{1,0:T(8,128)(2,1)} %copy-done.42, bf16[1024,2048]{1,0:T(8,128)(2,1)} %copy-done.43, ...), custom_call_target="tpu_custom_call" | custom-call | tf_op jit(solution)/shard_map/pallas_call | solution.py:454
  554.8 4.0 multiply_reduce_fusion
  561.0 6.2 constant_dynamic-update-slice_fusion.1
  569.2 4.6 add_bitcast_fusion.1
  575.7 9.5 %fusion.22.d_ref = bf16[1024,1024]{1,0:T(8,128)(2,1)} fusion(bf16[1024,2048]{1,0:T(8,128)(2,1)S(1)} %constant_dynamic-update-slice_fusion, bf16[2048,2048]{1,0:T(8,128)(2,1)} %copy-done.73, s32[]{:T(128)S(6)} %select_n.376), kind=kOutput, calls=%fused_computation.58 | convolution fusion | flops 4296015872 | bytes 10485764 | tf_op jit(solution)/shard_map/dot_general | solution.py:589
  585.2 2.9 fusion.26
  594.4 3.1 slice.134
  601.5 44.8 %shard_map.307 = (bf16[1024,128]{1,0:T(8,128)(2,1)S(1)}, f32[1024,128]{1,0:T(8,128)S(1)}, f32[1024,1024]{1,0:T(8,128)}, f32[8,2,168,128]{3,2,1,0:T(8,128)S(1)}) custom-call(bf16[1024,1280]{1,0:T(8,128)(2,1)} %copy-done, bf16[1024,1280]{1,0:T(8,128)(2,1)} %copy-done, bf16[1024,1280]{1,0:T(8,128)(2,1)} %copy-done, s32[1024,1]{1,0:T(8,128)S(1)} %copy-done.21, ...), custom_call_target="tpu_custom_call" | custom-call | tf_op jit(solution)/shard_map/pallas_call | solution.py:762
  659.7 4.8 shard_map.308
  665.9 4.7 shard_map.309
  672.5 59.1 %shard_map.310.refs_6_ = f32[8,168,128]{2,1,0:T(8,128)S(1)} custom-call(f32[8,168,128]{2,1,0:T(8,128)S(1)} %fusion.48.refs_0_), custom_call_target="tpu_custom_call" | custom-call | tf_op jit(solution)/shard_map/pallas_call | solution.py:831
  732.5 4.9 shard_map.312
  737.4 4.7 shard_map.311
  743.1 2.6 convert_add_fusion.8
  746.5 2.8 add_bitcast_fusion.2
  750.5 2.9 convert_add_fusion.3
  756.9 27.4 %shard_map.313 = (bf16[1024,128]{1,0:T(8,128)(2,1)S(1)}, bf16[1024,1024]{1,0:T(8,128)(2,1)S(1)}) custom-call(s32[2]{0:T(128)S(1)} %copy-done.35, bf16[1024,1280]{1,0:T(8,128)(2,1)} %copy-done, bf16[1024,1280]{1,0:T(8,128)(2,1)} %copy-done, bf16[8,128,160]{2,1,0:T(8,128)(2,1)S(1)} %copy-done.14, bf16[8,128,160]{2,1,0:T(8,128)(2,1)S(1)} %copy-done.18, ...), custom_call_target="tpu_custom_call" | custom-call | tf_op jit(solution)/shard_map/pallas_call | solution.py:762
  788.6 5.4 shard_map.314
  795.0 5.4 shard_map.315
  802.7 5.4 shard_map.316
  809.5 5.5 shard_map.317
  817.6 9.9 %shard_map.318 = bf16[1024,2048]{1,0:T(8,128)(2,1)} custom-call(bf16[1024,1280]{1,0:T(8,128)(2,1)S(1)} %copy-done.2, bf16[2048,1280]{1,0:T(8,128)(2,1)} %bitcast.261), custom_call_target="tpu_custom_call" | custom-call | tf_op jit(solution)/shard_map/pallas_call | solution.py:526
  827.5 13.2 %collective-permute-done.39 = bf16[1,176,2048]{2,1,0:T(8,128)(2,1)S(1)} collective-permute-done((bf16[1,176,2048]{2,1,0:T(8,128)(2,1)S(1)}, bf16[1,176,2048]{2,1,0:T(8,128)(2,1)S(1)}, u32[]{:S(2)}, u32[]{:S(2)}) %collective-permute-start.39) | collective-permute-done | bytes 720928 | tf_op jit(solution)/shard_map/ppermute | solution.py:29
  843.9 3.0 fusion.51
  850.4 2.6 fusion.17
  858.3 7.5 collective-permute-done.45
  866.5 5.7 fusion.6
  877.5 3.3 collective-permute-start.54
  885.0 3.3 fusion.30
  888.4 2.9 shard_map.319
  891.3 10.5 %collective-permute-done.52 = f32[2,2048]{1,0:T(2,128)S(1)} collective-permute-done((f32[2,2048]{1,0:T(2,128)S(1)}, f32[2,2048]{1,0:T(2,128)S(1)}, u32[]{:S(2)}, u32[]{:S(2)}) %collective-permute-start.52) | collective-permute-done | bytes 16416 | tf_op jit(solution)/shard_map/ppermute | solution.py:29
  905.0 3.0 fusion.9
  910.0 5.2 add_convert_fusion
  915.2 4.1 collective-permute-done.55
  (452 shorter events, 152.2 us)
Async XLA Ops:
  0.7 8.2 collective-permute-start
  6.4 58.5 %copy-start.103 = (f32[512]{0:T(512)}, f32[512]{0:T(512)S(1)}, u32[]{:S(2)}) copy-start(f32[512]{0:T(512)S(1)} %add_rsqrt_fusion.1) | copy-start | bytes 6148
  10.7 51.5 %copy-start.42 = (bf16[1024,2048]{1,0:T(8,128)(2,1)}, bf16[1024,2048]{1,0:T(8,128)(2,1)S(1)}, u32[]{:S(2)}) copy-start(bf16[1024,2048]{1,0:T(8,128)(2,1)S(1)} %constant_dynamic-update-slice_fusion.14.refs_2_.refs_3_) | copy-start | bytes 12582916
  67.6 53.0 %collective-permute-start.1 = (bf16[512,2048]{1,0:T(8,128)(2,1)}, bf16[512,2048]{1,0:T(8,128)(2,1)}, u32[]{:S(2)}, u32[]{:S(2)}) collective-permute-start(bf16[512,2048]{1,0:T(8,128)(2,1)} %get-tuple-element.386), channel_id=1, source_target_pairs={{0,1},{1,0},{2,3},{3,2},{4,5},{5,4},{6,7},{7,6},{8,9},{9,8},{10,11... | collective-permute-start | bytes 6291464 | tf_op jit(solution)/shard_map/ppermute | solution.py:29
  70.3 60.9 %copy-start.34 = (s32[2]{0:T(128)}, s32[2]{0:T(128)S(1)}, u32[]{:S(2)}) copy-start(s32[2]{0:T(128)S(1)} %pad_add_fusion.scal) | copy-start | bytes 28
  118.0 47.1 %copy-start.22 = (bf16[4,128,1024]{2,1,0:T(8,128)(2,1)}, bf16[4,128,1024]{2,1,0:T(8,128)(2,1)S(1)}, u32[]{:S(2)}) copy-start(bf16[4,128,1024]{2,1,0:T(8,128)(2,1)S(1)} %get-tuple-element.205) | copy-start | bytes 3145732
  118.0 24.9 %collective-permute-start.4 = (bf16[4,128,1024]{2,1,0:T(8,128)(2,1)S(1)}, bf16[4,128,1024]{2,1,0:T(8,128)(2,1)S(1)}, u32[]{:S(2)}, u32[]{:S(2)}) collective-permute-start(bf16[4,128,1024]{2,1,0:T(8,128)(2,1)S(1)} %get-tuple-element.205), channel_id=1, source_target_pairs={{0,4},{1,5},{2,6},{3,7},{4,0},{5,1},{6,2},{7,3},{8,12},{9,13},{10,... | collective-permute-start | bytes 3145736 | tf_op jit(solution)/shard_map/ppermute | solution.py:29
  119.6 33.4 %collective-permute-start.3 = (bf16[4,64,1408]{2,1,0:T(8,128)(2,1)}, bf16[4,64,1408]{2,1,0:T(8,128)(2,1)S(1)}, u32[]{:S(2)}, u32[]{:S(2)}) collective-permute-start(bf16[4,64,1408]{2,1,0:T(8,128)(2,1)} %get-tuple-element.202), channel_id=1, source_target_pairs={{0,16},{1,17},{2,18},{3,19},{4,20},{5,21},{6,22},{7,23},{8,24},{9,... | collective-permute-start | bytes 2162696 | tf_op jit(solution)/shard_map/ppermute | solution.py:29
  119.6 33.4 %collective-permute-start.2 = (bf16[2,4,64,1408]{3,2,1,0:T(8,128)(2,1)S(1)}, bf16[2,4,64,1408]{3,2,1,0:T(8,128)(2,1)}, u32[]{:S(2)}, u32[]{:S(2)}) collective-permute-start(bf16[2,4,64,1408]{3,2,1,0:T(8,128)(2,1)S(1)} %get-tuple-element.199), channel_id=1, source_target_pairs={{0,2},{1,3},{2,0},{3,1},{4,6},{5,7},{6,4},{7,5},{8,10},{9,11},{10,... | collective-permute-start | bytes 4325384 | tf_op jit(solution)/shard_map/ppermute | solution.py:29
  160.7 112.5 %collective-permute-start.6 = (bf16[2,4,64,2816]{3,2,1,0:T(8,128)(2,1)}, bf16[2,4,64,2816]{3,2,1,0:T(8,128)(2,1)}, u32[]{:S(2)}, u32[]{:S(2)}) collective-permute-start(bf16[2,4,64,2816]{3,2,1,0:T(8,128)(2,1)} %pad_maximum_fusion), channel_id=1, source_target_pairs={{0,4},{1,5},{2,6},{3,7},{4,0},{5,1},{6,2},{7,3},{8,12},{9,13},{10,... | collective-permute-start | bytes 8650760 | tf_op jit(solution)/shard_map/ppermute | solution.py:29
  162.6 110.6 %collective-permute-start.9 = (bf16[512,2048]{1,0:T(8,128)(2,1)}, bf16[512,2048]{1,0:T(8,128)(2,1)}, u32[]{:S(2)}, u32[]{:S(2)}) collective-permute-start(bf16[512,2048]{1,0:T(8,128)(2,1)} %param.34), channel_id=1, source_target_pairs={{0,8},{1,9},{2,10},{3,11},{4,12},{5,13},{6,14},{7,15},{8,0},{9,1},... | collective-permute-start | bytes 6291464 | tf_op jit(solution)/shard_map/ppermute | solution.py:29
  164.5 108.7 %collective-permute-start.8 = (bf16[704,1536]{1,0:T(8,128)(2,1)}, bf16[704,1536]{1,0:T(8,128)(2,1)}, u32[]{:S(2)}, u32[]{:S(2)}) collective-permute-start(bf16[704,1536]{1,0:T(8,128)(2,1)} %slice.129), channel_id=1, source_target_pairs={{0,16},{1,17},{2,18},{3,19},{4,20},{5,21},{6,22},{7,23},{8,24},{9,... | collective-permute-start | bytes 6488072 | tf_op jit(solution)/shard_map/ppermute | solution.py:29
  166.7 106.6 %collective-permute-start.5 = (bf16[2,4,128,1024]{3,2,1,0:T(8,128)(2,1)}, bf16[2,4,128,1024]{3,2,1,0:T(8,128)(2,1)}, u32[]{:S(2)}, u32[]{:S(2)}) collective-permute-start(bf16[2,4,128,1024]{3,2,1,0:T(8,128)(2,1)} %pad_maximum_fusion.1), channel_id=1, source_target_pairs={{0,2},{1,3},{2,0},{3,1},{4,6},{5,7},{6,4},{7,5},{8,10},{9,11},{10,... | collective-permute-start | bytes 6291464 | tf_op jit(solution)/shard_map/ppermute | solution.py:29
  168.1 105.1 %collective-permute-start.7 = (bf16[2,4,64,1408]{3,2,1,0:T(8,128)(2,1)}, bf16[2,4,64,1408]{3,2,1,0:T(8,128)(2,1)}, u32[]{:S(2)}, u32[]{:S(2)}) collective-permute-start(bf16[2,4,64,1408]{3,2,1,0:T(8,128)(2,1)} %bitcast_dynamic-update-slice_fusion.4), channel_id=1, source_target_pairs={{0,2},{1,3},{2,0},{3,1},{4,6},{5,7},{6,4},{7,5},{8,10},{9,11},{10,... | collective-permute-start | bytes 4325384 | tf_op jit(solution)/shard_map/ppermute | solution.py:29
  171.9 103.6 %copy-start.84 = (bf16[4,128,1024]{2,1,0:T(8,128)(2,1)S(1)}, bf16[4,128,1024]{2,1,0:T(8,128)(2,1)}, u32[]{:S(2)}) copy-start(bf16[4,128,1024]{2,1,0:T(8,128)(2,1)} %copy-done.83) | copy-start | bytes 3145732
  280.1 48.5 %collective-permute-start.10 = (bf16[2048,1024]{1,0:T(8,128)(2,1)}, bf16[2048,1024]{1,0:T(8,128)(2,1)}, u32[]{:S(2)}, u32[]{:S(2)}) collective-permute-start(bf16[2048,1024]{1,0:T(8,128)(2,1)} %bitcast.24), channel_id=1, source_target_pairs={{0,1},{1,0},{2,3},{3,2},{4,5},{5,4},{6,7},{7,6},{8,9},{9,8},{10,11... | collective-permute-start | bytes 12582920 | tf_op jit(solution)/shard_map/ppermute | solution.py:29
  283.7 44.9 %collective-permute-start.12 = (bf16[2,4,64,1408]{3,2,1,0:T(8,128)(2,1)}, bf16[2,4,64,1408]{3,2,1,0:T(8,128)(2,1)}, u32[]{:S(2)}, u32[]{:S(2)}) collective-permute-start(bf16[2,4,64,1408]{3,2,1,0:T(8,128)(2,1)} %get-tuple-element.231), channel_id=1, source_target_pairs={{0,2},{1,3},{2,0},{3,1},{4,6},{5,7},{6,4},{7,5},{8,10},{9,11},{10,... | collective-permute-start | bytes 4325384 | tf_op jit(solution)/shard_map/ppermute | solution.py:29
  284.9 43.7 %collective-permute-start.11 = (bf16[2,4,64,1408]{3,2,1,0:T(8,128)(2,1)}, bf16[2,4,64,1408]{3,2,1,0:T(8,128)(2,1)}, u32[]{:S(2)}, u32[]{:S(2)}) collective-permute-start(bf16[2,4,64,1408]{3,2,1,0:T(8,128)(2,1)} %collective-permute-done.2), channel_id=1, source_target_pairs={{0,4},{1,5},{2,6},{3,7},{4,0},{5,1},{6,2},{7,3},{8,12},{9,13},{10,... | collective-permute-start | bytes 4325384 | tf_op jit(solution)/shard_map/ppermute | solution.py:29
  286.6 41.9 %collective-permute-start.13 = (bf16[704,512]{1,0:T(8,128)(2,1)}, bf16[704,512]{1,0:T(8,128)(2,1)S(1)}, u32[]{:S(2)}, u32[]{:S(2)}) collective-permute-start(bf16[704,512]{1,0:T(8,128)(2,1)} %slice.130), channel_id=1, source_target_pairs={{0,16},{1,17},{2,18},{3,19},{4,20},{5,21},{6,22},{7,23},{8,24},{9,... | collective-permute-start | bytes 2162696 | tf_op jit(solution)/shard_map/ppermute | solution.py:29
  328.6 9.1 collective-permute-start.14
  348.3 4.7 collective-permute-start.15
  348.8 55.1 %collective-permute-start.16 = (bf16[512,2048]{1,0:T(8,128)(2,1)}, bf16[512,2048]{1,0:T(8,128)(2,1)}, u32[]{:S(2)}, u32[]{:S(2)}) collective-permute-start(bf16[512,2048]{1,0:T(8,128)(2,1)} %get-tuple-element.384), channel_id=1, source_target_pairs={{0,8},{1,9},{2,10},{3,11},{4,12},{5,13},{6,14},{7,15},{8,0},{9,1},... | collective-permute-start | bytes 6291464 | tf_op jit(solution)/shard_map/ppermute | solution.py:29
  403.9 8.0 collective-permute-start.17
  411.7 4.4 collective-permute-start.18
  412.2 54.0 %collective-permute-start.20 = (bf16[512,2048]{1,0:T(8,128)(2,1)}, bf16[512,2048]{1,0:T(8,128)(2,1)}, u32[]{:S(2)}, u32[]{:S(2)}) collective-permute-start(bf16[512,2048]{1,0:T(8,128)(2,1)} %constant_dynamic-slice_fusion.8), channel_id=1, source_target_pairs={{0,1},{1,0},{2,3},{3,2},{4,5},{5,4},{6,7},{7,6},{8,9},{9,8},{10,11... | collective-permute-start | bytes 6291464 | tf_op jit(solution)/shard_map/ppermute | solution.py:29
  412.7 53.6 %collective-permute-start.19 = (bf16[512,2048]{1,0:T(8,128)(2,1)}, bf16[512,2048]{1,0:T(8,128)(2,1)S(1)}, u32[]{:S(2)}, u32[]{:S(2)}) collective-permute-start(bf16[512,2048]{1,0:T(8,128)(2,1)} %constant_dynamic-slice_fusion.9), channel_id=1, source_target_pairs={{0,1},{1,0},{2,3},{3,2},{4,5},{5,4},{6,7},{7,6},{8,9},{9,8},{10,11... | collective-permute-start | bytes 6291464 | tf_op jit(solution)/shard_map/ppermute | solution.py:29
  471.9 15.7 %collective-permute-start.22 = (bf16[512,2048]{1,0:T(8,128)(2,1)}, bf16[512,2048]{1,0:T(8,128)(2,1)S(1)}, u32[]{:S(2)}, u32[]{:S(2)}) collective-permute-start(bf16[512,2048]{1,0:T(8,128)(2,1)} %get-tuple-element.266), channel_id=1, source_target_pairs={{0,1},{1,0},{2,3},{3,2},{4,5},{5,4},{6,7},{7,6},{8,9},{9,8},{10,11... | collective-permute-start | bytes 6291464 | tf_op jit(solution)/shard_map/ppermute | solution.py:29
  472.1 15.6 %collective-permute-start.21 = (bf16[512,2048]{1,0:T(8,128)(2,1)}, bf16[512,2048]{1,0:T(8,128)(2,1)}, u32[]{:S(2)}, u32[]{:S(2)}) collective-permute-start(bf16[512,2048]{1,0:T(8,128)(2,1)} %get-tuple-element.264), channel_id=1, source_target_pairs={{0,1},{1,0},{2,3},{3,2},{4,5},{5,4},{6,7},{7,6},{8,9},{9,8},{10,11... | collective-permute-start | bytes 6291464 | tf_op jit(solution)/shard_map/ppermute | solution.py:29
  486.4 68.4 %collective-permute-start.24 = (bf16[4,256,1408]{2,1,0:T(8,128)(2,1)}, bf16[4,256,1408]{2,1,0:T(8,128)(2,1)}, u32[]{:S(2)}, u32[]{:S(2)}) collective-permute-start(bf16[4,256,1408]{2,1,0:T(8,128)(2,1)} %bitcast.276), channel_id=1, source_target_pairs={{0,2},{1,3},{2,0},{3,1},{4,6},{5,7},{6,4},{7,5},{8,10},{9,11},{10,... | collective-permute-start | bytes 8650760 | tf_op jit(solution)/shard_map/ppermute | solution.py:29
  491.4 63.3 %collective-permute-start.23 = (bf16[512,2048]{1,0:T(8,128)(2,1)}, bf16[512,2048]{1,0:T(8,128)(2,1)}, u32[]{:S(2)}, u32[]{:S(2)}) collective-permute-start(bf16[512,2048]{1,0:T(8,128)(2,1)} %add_convert_fusion.2.refs_12_), channel_id=1, source_target_pairs={{0,8},{1,9},{2,10},{3,11},{4,12},{5,13},{6,14},{7,15},{8,0},{9,1},... | collective-permute-start | bytes 6291464 | tf_op jit(solution)/shard_map/ppermute | solution.py:29
  508.2 65.7 %collective-permute-start.26 = (bf16[4,256,1408]{2,1,0:T(8,128)(2,1)}, bf16[4,256,1408]{2,1,0:T(8,128)(2,1)}, u32[]{:S(2)}, u32[]{:S(2)}) collective-permute-start(bf16[4,256,1408]{2,1,0:T(8,128)(2,1)} %bitcast.278), channel_id=1, source_target_pairs={{0,4},{1,5},{2,6},{3,7},{4,0},{5,1},{6,2},{7,3},{8,12},{9,13},{10,... | collective-permute-start | bytes 8650760 | tf_op jit(solution)/shard_map/ppermute | solution.py:29
  569.2 4.6 collective-permute-start.25
  588.1 60.6 %collective-permute-start.29 = (bf16[512,2048]{1,0:T(8,128)(2,1)}, bf16[512,2048]{1,0:T(8,128)(2,1)}, u32[]{:S(2)}, u32[]{:S(2)}) collective-permute-start(bf16[512,2048]{1,0:T(8,128)(2,1)} %add_convert_fusion.1.refs_13_), channel_id=1, source_target_pairs={{0,8},{1,9},{2,10},{3,11},{4,12},{5,13},{6,14},{7,15},{8,0},{9,1},... | collective-permute-start | bytes 6291464 | tf_op jit(solution)/shard_map/ppermute | solution.py:29
  590.1 56.1 %collective-permute-start.27 = (bf16[2,256,1408]{2,1,0:T(8,128)(2,1)}, bf16[2,256,1408]{2,1,0:T(8,128)(2,1)}, u32[]{:S(2)}, u32[]{:S(2)}) collective-permute-start(bf16[2,256,1408]{2,1,0:T(8,128)(2,1)} %get-tuple-element.388), channel_id=1, source_target_pairs={{0,4},{1,5},{2,6},{3,7},{4,0},{5,1},{6,2},{7,3},{8,12},{9,13},{10,... | collective-permute-start | bytes 4325384 | tf_op jit(solution)/shard_map/ppermute | solution.py:29
  591.4 57.3 %collective-permute-start.28 = (bf16[2,256,1408]{2,1,0:T(8,128)(2,1)}, bf16[2,256,1408]{2,1,0:T(8,128)(2,1)}, u32[]{:S(2)}, u32[]{:S(2)}) collective-permute-start(bf16[2,256,1408]{2,1,0:T(8,128)(2,1)} %fusion.26), channel_id=1, source_target_pairs={{0,2},{1,3},{2,0},{3,1},{4,6},{5,7},{6,4},{7,5},{8,10},{9,11},{10,... | collective-permute-start | bytes 4325384 | tf_op jit(solution)/shard_map/ppermute | solution.py:29
  601.5 44.8 %copy-start.49 = (bf16[1024,1408]{1,0:T(8,128)(2,1)S(1)}, bf16[1024,1408]{1,0:T(8,128)(2,1)}, u32[]{:S(2)}) copy-start(bf16[1024,1408]{1,0:T(8,128)(2,1)} %shard_map.305) | copy-start | bytes 8650756
  655.0 87.1 %collective-permute-start.30 = (bf16[1,256,2816]{2,1,0:T(8,128)(2,1)}, bf16[1,256,2816]{2,1,0:T(8,128)(2,1)}, u32[]{:S(2)}, u32[]{:S(2)}) collective-permute-start(bf16[1,256,2816]{2,1,0:T(8,128)(2,1)} %fusion.20), channel_id=1, source_target_pairs={{0,16},{1,17},{2,18},{3,19},{4,20},{5,21},{6,22},{7,23},{8,24},{9,... | collective-permute-start | bytes 4325384 | tf_op jit(solution)/shard_map/ppermute | solution.py:29
  655.6 86.5 %collective-permute-start.31 = (bf16[4,176,1024]{2,1,0:T(8,128)(2,1)}, bf16[4,176,1024]{2,1,0:T(8,128)(2,1)}, u32[]{:S(2)}, u32[]{:S(2)}) collective-permute-start(bf16[4,176,1024]{2,1,0:T(8,128)(2,1)} %get-tuple-element.291), channel_id=1, source_target_pairs={{0,2},{1,3},{2,0},{3,1},{4,6},{5,7},{6,4},{7,5},{8,10},{9,11},{10,... | collective-permute-start | bytes 4325384 | tf_op jit(solution)/shard_map/ppermute | solution.py:29
  656.4 85.7 %collective-permute-start.32 = (bf16[4,176,1024]{2,1,0:T(8,128)(2,1)}, bf16[4,176,1024]{2,1,0:T(8,128)(2,1)}, u32[]{:S(2)}, u32[]{:S(2)}) collective-permute-start(bf16[4,176,1024]{2,1,0:T(8,128)(2,1)} %bitcast.55), channel_id=1, source_target_pairs={{0,4},{1,5},{2,6},{3,7},{4,0},{5,1},{6,2},{7,3},{8,12},{9,13},{10,... | collective-permute-start | bytes 4325384 | tf_op jit(solution)/shard_map/ppermute | solution.py:29
  664.6 77.5 %collective-permute-start.33 = (bf16[8,128,512]{2,1,0:T(8,128)(2,1)}, bf16[8,128,512]{2,1,0:T(8,128)(2,1)}, u32[]{:S(2)}, u32[]{:S(2)}) collective-permute-start(bf16[8,128,512]{2,1,0:T(8,128)(2,1)} %bitcast.295), channel_id=1, source_target_pairs={{0,2},{1,3},{2,0},{3,1},{4,6},{5,7},{6,4},{7,5},{8,10},{9,11},{10,... | collective-permute-start | bytes 3145736 | tf_op jit(solution)/shard_map/ppermute | solution.py:29
  670.6 71.5 %collective-permute-start.34 = (bf16[8,128,512]{2,1,0:T(8,128)(2,1)}, bf16[8,128,512]{2,1,0:T(8,128)(2,1)S(1)}, u32[]{:S(2)}, u32[]{:S(2)}) collective-permute-start(bf16[8,128,512]{2,1,0:T(8,128)(2,1)} %bitcast.296), channel_id=1, source_target_pairs={{0,4},{1,5},{2,6},{3,7},{4,0},{5,1},{6,2},{7,3},{8,12},{9,13},{10,... | collective-permute-start | bytes 3145736 | tf_op jit(solution)/shard_map/ppermute | solution.py:29
  745.7 38.6 %collective-permute-start.35 = (bf16[4,128,512]{2,1,0:T(8,128)(2,1)}, bf16[4,128,512]{2,1,0:T(8,128)(2,1)S(1)}, u32[]{:S(2)}, u32[]{:S(2)}) collective-permute-start(bf16[4,128,512]{2,1,0:T(8,128)(2,1)} %get-tuple-element.404), channel_id=1, source_target_pairs={{0,4},{1,5},{2,6},{3,7},{4,0},{5,1},{6,2},{7,3},{8,12},{9,13},{10,... | collective-permute-start | bytes 1572872 | tf_op jit(solution)/shard_map/ppermute | solution.py:29
  749.4 35.0 %collective-permute-start.37 = (bf16[2,176,1024]{2,1,0:T(8,128)(2,1)}, bf16[2,176,1024]{2,1,0:T(8,128)(2,1)}, u32[]{:S(2)}, u32[]{:S(2)}) collective-permute-start(bf16[2,176,1024]{2,1,0:T(8,128)(2,1)} %get-tuple-element.396), channel_id=1, source_target_pairs={{0,4},{1,5},{2,6},{3,7},{4,0},{5,1},{6,2},{7,3},{8,12},{9,13},{10,... | collective-permute-start | bytes 2162696 | tf_op jit(solution)/shard_map/ppermute | solution.py:29
  753.4 32.3 %collective-permute-start.38 = (bf16[2,176,1024]{2,1,0:T(8,128)(2,1)}, bf16[2,176,1024]{2,1,0:T(8,128)(2,1)S(1)}, u32[]{:S(2)}, u32[]{:S(2)}) collective-permute-start(bf16[2,176,1024]{2,1,0:T(8,128)(2,1)} %get-tuple-element.390), channel_id=1, source_target_pairs={{0,2},{1,3},{2,0},{3,1},{4,6},{5,7},{6,4},{7,5},{8,10},{9,11},{10,... | collective-permute-start | bytes 2162696 | tf_op jit(solution)/shard_map/ppermute | solution.py:29
  754.6 29.8 %collective-permute-start.36 = (bf16[4,128,512]{2,1,0:T(8,128)(2,1)S(1)}, bf16[4,128,512]{2,1,0:T(8,128)(2,1)S(1)}, u32[]{:S(2)}, u32[]{:S(2)}) collective-permute-start(bf16[4,128,512]{2,1,0:T(8,128)(2,1)S(1)} %fusion.55), channel_id=1, source_target_pairs={{0,2},{1,3},{2,0},{3,1},{4,6},{5,7},{6,4},{7,5},{8,10},{9,11},{10,... | collective-permute-start | bytes 1572872 | tf_op jit(solution)/shard_map/ppermute | solution.py:29
  794.0 47.8 %collective-permute-start.41 = (bf16[8,128,640]{2,1,0:T(8,128)(2,1)}, bf16[8,128,640]{2,1,0:T(8,128)(2,1)}, u32[]{:S(2)}, u32[]{:S(2)}) collective-permute-start(bf16[8,128,640]{2,1,0:T(8,128)(2,1)} %bitcast.270), channel_id=1, source_target_pairs={{0,2},{1,3},{2,0},{3,1},{4,6},{5,7},{6,4},{7,5},{8,10},{9,11},{10,... | collective-permute-start | bytes 3932168 | tf_op jit(solution)/shard_map/ppermute | solution.py:29
  800.4 41.4 %collective-permute-start.42 = (bf16[8,128,640]{2,1,0:T(8,128)(2,1)}, bf16[8,128,640]{2,1,0:T(8,128)(2,1)}, u32[]{:S(2)}, u32[]{:S(2)}) collective-permute-start(bf16[8,128,640]{2,1,0:T(8,128)(2,1)} %bitcast.282), channel_id=1, source_target_pairs={{0,4},{1,5},{2,6},{3,7},{4,0},{5,1},{6,2},{7,3},{8,12},{9,13},{10,... | collective-permute-start | bytes 3932168 | tf_op jit(solution)/shard_map/ppermute | solution.py:29
  808.1 32.7 %collective-permute-start.39 = (bf16[1,176,2048]{2,1,0:T(8,128)(2,1)S(1)}, bf16[1,176,2048]{2,1,0:T(8,128)(2,1)S(1)}, u32[]{:S(2)}, u32[]{:S(2)}) collective-permute-start(bf16[1,176,2048]{2,1,0:T(8,128)(2,1)S(1)} %fusion.33), channel_id=1, source_target_pairs={{0,16},{1,17},{2,18},{3,19},{4,20},{5,21},{6,22},{7,23},{8,24},{9,... | collective-permute-start | bytes 2162696 | tf_op jit(solution)/shard_map/ppermute | solution.py:29
  816.5 25.3 %collective-permute-start.40 = (bf16[2,128,1024]{2,1,0:T(8,128)(2,1)S(1)}, bf16[2,128,1024]{2,1,0:T(8,128)(2,1)S(1)}, u32[]{:S(2)}, u32[]{:S(2)}) collective-permute-start(bf16[2,128,1024]{2,1,0:T(8,128)(2,1)S(1)} %get-tuple-element.394), channel_id=1, source_target_pairs={{0,8},{1,9},{2,10},{3,11},{4,12},{5,13},{6,14},{7,15},{8,0},{9,1},... | collective-permute-start | bytes 1572872 | tf_op jit(solution)/shard_map/ppermute | solution.py:29
  848.4 7.9 collective-permute-start.43
  848.4 17.4 %collective-permute-start.45 = (bf16[4,128,640]{2,1,0:T(8,128)(2,1)}, bf16[4,128,640]{2,1,0:T(8,128)(2,1)S(1)}, u32[]{:S(2)}, u32[]{:S(2)}) collective-permute-start(bf16[4,128,640]{2,1,0:T(8,128)(2,1)} %get-tuple-element.401), channel_id=1, source_target_pairs={{0,2},{1,3},{2,0},{3,1},{4,6},{5,7},{6,4},{7,5},{8,10},{9,11},{10,... | collective-permute-start | bytes 1966088 | tf_op jit(solution)/shard_map/ppermute | solution.py:29
  849.4 17.1 %collective-permute-start.44 = (bf16[4,128,640]{2,1,0:T(8,128)(2,1)}, bf16[4,128,640]{2,1,0:T(8,128)(2,1)S(1)}, u32[]{:S(2)}, u32[]{:S(2)}) collective-permute-start(bf16[4,128,640]{2,1,0:T(8,128)(2,1)} %fusion.50), channel_id=1, source_target_pairs={{0,4},{1,5},{2,6},{3,7},{4,0},{5,1},{6,2},{7,3},{8,12},{9,13},{10,... | collective-permute-start | bytes 1966088 | tf_op jit(solution)/shard_map/ppermute | solution.py:29
  856.3 18.7 %collective-permute-start.48 = (bf16[64,2816]{1,0:T(8,128)(2,1)S(1)}, bf16[64,2816]{1,0:T(8,128)(2,1)S(1)}, u32[]{:S(2)}, u32[]{:S(2)}) collective-permute-start(bf16[64,2816]{1,0:T(8,128)(2,1)S(1)} %get-tuple-element.352), channel_id=1, source_target_pairs={{0,9},{1,8},{2,11},{3,10},{4,13},{5,12},{6,15},{7,14},{8,1},{9,0},... | collective-permute-start | bytes 1081352 | tf_op jit(solution)/shard_map/ppermute | solution.py:29
  856.4 18.6 %collective-permute-start.47 = (bf16[64,2816]{1,0:T(8,128)(2,1)S(1)}, bf16[64,2816]{1,0:T(8,128)(2,1)S(1)}, u32[]{:S(2)}, u32[]{:S(2)}) collective-permute-start(bf16[64,2816]{1,0:T(8,128)(2,1)S(1)} %get-tuple-element.351), channel_id=1, source_target_pairs={{0,8},{1,9},{2,10},{3,11},{4,12},{5,13},{6,14},{7,15},{8,0},{9,1},... | collective-permute-start | bytes 1081352 | tf_op jit(solution)/shard_map/ppermute | solution.py:29
  858.0 17.0 %collective-permute-start.46 = (bf16[64,2816]{1,0:T(8,128)(2,1)S(1)}, bf16[64,2816]{1,0:T(8,128)(2,1)S(1)}, u32[]{:S(2)}, u32[]{:S(2)}) collective-permute-start(bf16[64,2816]{1,0:T(8,128)(2,1)S(1)} %get-tuple-element.350), channel_id=1, source_target_pairs={{0,1},{1,0},{2,3},{3,2},{4,5},{5,4},{6,7},{7,6},{8,9},{9,8},{10,11... | collective-permute-start | bytes 1081352 | tf_op jit(solution)/shard_map/ppermute | solution.py:29
  875.0 1.2 collective-permute-start.49
  876.3 6.8 collective-permute-start.50
  877.5 24.4 %collective-permute-start.54 = (bf16[1,128,1024]{2,1,0:T(8,128)(2,1)}, bf16[1,128,1024]{2,1,0:T(8,128)(2,1)S(1)}, u32[]{:S(2)}, u32[]{:S(2)}) collective-permute-start(bf16[1,128,1024]{2,1,0:T(8,128)(2,1)} %get-tuple-element.408), channel_id=1, source_target_pairs={{0,16},{1,17},{2,18},{3,19},{4,20},{5,21},{6,22},{7,23},{8,24},{9,... | collective-permute-start | bytes 786440 | tf_op jit(solution)/shard_map/ppermute | solution.py:29
  880.7 21.2 %collective-permute-start.53 = (bf16[2,128,1280]{2,1,0:T(8,128)(2,1)}, bf16[2,128,1280]{2,1,0:T(8,128)(2,1)S(1)}, u32[]{:S(2)}, u32[]{:S(2)}) collective-permute-start(bf16[2,128,1280]{2,1,0:T(8,128)(2,1)} %get-tuple-element.391), channel_id=1, source_target_pairs={{0,8},{1,9},{2,10},{3,11},{4,12},{5,13},{6,14},{7,15},{8,0},{9,1},... | collective-permute-start | bytes 1966088 | tf_op jit(solution)/shard_map/ppermute | solution.py:29
  883.9 4.5 collective-permute-start.51
  888.3 13.5 %collective-permute-start.52 = (f32[2,2048]{1,0:T(2,128)S(1)}, f32[2,2048]{1,0:T(2,128)S(1)}, u32[]{:S(2)}, u32[]{:S(2)}) collective-permute-start(f32[2,2048]{1,0:T(2,128)S(1)} %add.670), channel_id=1, source_target_pairs={{0,8},{1,9},{2,10},{3,11},{4,12},{5,13},{6,14},{7,15},{8,0},{9,1},... | collective-permute-start | bytes 49160 | tf_op jit(solution)/shard_map/ppermute | solution.py:29
  902.0 17.9 %collective-permute-start.56 = (bf16[1,128,1280]{2,1,0:T(8,128)(2,1)S(1)}, bf16[1,128,1280]{2,1,0:T(8,128)(2,1)S(1)}, u32[]{:S(2)}, u32[]{:S(2)}) collective-permute-start(bf16[1,128,1280]{2,1,0:T(8,128)(2,1)S(1)} %get-tuple-element.406), channel_id=1, source_target_pairs={{0,16},{1,17},{2,18},{3,19},{4,20},{5,21},{6,22},{7,23},{8,24},{9,... | collective-permute-start | bytes 983048 | tf_op jit(solution)/shard_map/ppermute | solution.py:29
  904.4 15.0 %collective-permute-start.55 = (f32[2,2048]{1,0:T(2,128)S(1)}, f32[2,2048]{1,0:T(2,128)S(1)}, u32[]{:S(2)}, u32[]{:S(2)}) collective-permute-start(f32[2,2048]{1,0:T(2,128)S(1)} %add.671), channel_id=1, source_target_pairs={{0,16},{1,17},{2,18},{3,19},{4,20},{5,21},{6,22},{7,23},{8,24},{9,... | collective-permute-start | bytes 49160 | tf_op jit(solution)/shard_map/ppermute | solution.py:29
  920.2 2.1 collective-permute-start.57
  (110 other events, 787.4 us)

commit v6 on v5

--- a/solution.py
+++ b/solution.py
@@ -627,26 +627,35 @@
     tokens, lanes = q_ref.shape
     lane = lax.broadcasted_iota(jnp.int32, (tokens, lanes), 1) // QK == head
     q = jnp.where(lane, q_ref[...], jnp.zeros((), bf16))
-    score = dot_cols(q, k_ref[...]) * QK**-0.5
-    row = lax.broadcasted_iota(jnp.int32, score.shape, 0)
-    col = lax.broadcasted_iota(jnp.int32, score.shape, 1)
     lo = lo_ref[...] - tile * tokens
-    mask = (col <= row) & (col >= lo)
-    weight = jnp.where(mask, 1.0 + score + 0.5 * score * score, 0.0)
-    return lane, score, mask, weight, lo < 0
+    parts = []
+    for start in (0, tokens // 2):
+        end = start + tokens // 2
+        score = dot_cols(q[start:end], k_ref[:end]) * QK**-0.5
+        row = lax.broadcasted_iota(jnp.int32, score.shape, 0) + start
+        col = lax.broadcasted_iota(jnp.int32, score.shape, 1)
+        mask = (col <= row) & (col >= lo[start:end])
+        parts.append((start, end, score, mask, jnp.where(mask, 1.0 + score + 0.5 * score * score, 0.0)))
+    return lane, parts, lo < 0
+
+
+def over_halves(first, second):
+    size = first.shape[0]
+    return jnp.concatenate([first + second[:size], second[size:]], axis=0)
 
 
 def forward_body(q_ref, k_ref, v_ref, lo_ref, carry_ref, one, two, rows, y_ref, mixed_ref):
     tile, head = pl.program_id(0), pl.program_id(1)
-    _, _, _, weight, alive = weights(q_ref, k_ref, lo_ref, tile, head)
+    _, parts, alive = weights(q_ref, k_ref, lo_ref, tile, head)
     a, b = features(q_ref[...], one[0], two[0], rows)
     phi = jnp.where(alive, a * b * rows[2:3], 0.0)
     high, low = halves(phi)
     carry = carry_ref[0, 0]
     s_high, s_low = halves(carry[:FEATS])
-    numer = dot(weight.astype(bf16), v_ref[...])
+    numer = jnp.concatenate([dot(weight.astype(bf16), v_ref[:end]) for _, end, _, _, weight in parts], axis=0)
     numer = numer + (dot(high, s_high) + dot(high, s_low) + dot(low, s_high))
-    denom = jnp.sum(weight, axis=1, keepdims=True) + jnp.sum(phi * total_row(carry), axis=1, keepdims=True)
+    denom = jnp.concatenate([jnp.sum(part[4], axis=1, keepdims=True) for part in parts], axis=0)
+    denom = denom + jnp.sum(phi * total_row(carry), axis=1, keepdims=True)
     y = numer / denom
     y_ref[...] = y
     mixed_ref[...] = y.astype(bf16)
@@ -664,26 +673,32 @@
     q_ref, k_ref, v_ref, lo_ref, carry_ref, one, two, rows, y_ref, d_ref, dq_ref, dk_ref, dv_ref, ds_ref, dq_acc, dk_acc
 ):
     tile, head = pl.program_id(0), pl.program_id(1)
-    lane, score, mask, weight, alive = weights(q_ref, k_ref, lo_ref, tile, head)
+    lane, parts, alive = weights(q_ref, k_ref, lo_ref, tile, head)
     a, b = features(q_ref[...], one[0], two[0], rows)
     phi = jnp.where(alive, a * b * rows[2:3], 0.0)
     high, low = halves(phi)
     carry = carry_ref[0, 0]
     s_high, s_low = halves(carry[:FEATS])
     row = total_row(carry)
-    denom = jnp.sum(weight, axis=1, keepdims=True) + jnp.sum(phi * row, axis=1, keepdims=True)
+    denom = jnp.concatenate([jnp.sum(part[4], axis=1, keepdims=True) for part in parts], axis=0)
+    denom = denom + jnp.sum(phi * row, axis=1, keepdims=True)
     d = d_ref[...].astype(f32)
     g = d / denom
     c = -jnp.sum(d * y_ref[...], axis=1, keepdims=True) / denom
     g_high, g_low = halves(g)
-    v = v_ref[...]
-    dk = dot_cols(g_high, v) + dot_cols(g_low, v) + c
-    ds = jnp.where(mask, dk * (1.0 + score) * QK**-0.5, 0.0).astype(bf16)
-    dv_ref[...] = dot_rows(weight.astype(bf16), g_high)
+    dq, dkeys, dv = [], [], []
+    for start, end, score, mask, weight in parts:
+        v = v_ref[:end]
+        dk = dot_cols(g_high[start:end], v) + dot_cols(g_low[start:end], v) + c[start:end]
+        ds = jnp.where(mask, dk * (1.0 + score) * QK**-0.5, 0.0).astype(bf16)
+        dv.append(dot_rows(weight.astype(bf16), g_high[start:end]))
+        dq.append(dot(ds, k_ref[:end]))
+        dkeys.append(dot_rows(ds, q_ref[start:end]))
+    dv_ref[...] = over_halves(*dv)
     dphi = dot_cols(g_high, s_high) + dot_cols(g_high, s_low) + dot_cols(g_low, s_high) + c * row
     t = jnp.where(alive, dphi * rows[2:3], 0.0)
-    dq = jnp.where(lane, dot(ds, k_ref[...]), 0.0) + spread(t, a, b, one[0], two[0])
-    dkeys = jnp.where(lane, dot_rows(ds, q_ref[...]), 0.0)
+    dq = jnp.where(lane, jnp.concatenate(dq, axis=0), 0.0) + spread(t, a, b, one[0], two[0])
+    dkeys = jnp.where(lane, over_halves(*dkeys), 0.0)
 
     @pl.when(head == 0)
     def _():

time: 933 us -> 939 us (level)
  no operation moved by 1% of the time
where the time goes in v6:
time: 939 us; the launch traced here: 930 us
  Pallas kernels  587 us (63%)
  local copies, waits for them, and re-layouts  110 us (12%)
  other arithmetic  87.3 us (9%)
  waiting for transfers between devices  62.5 us (7%)
  starting transfers between devices  57.3 us (6%)
  matrix products  21.7 us (2%)
    pallas_call x2, Pallas kernels, others(): pl.pallas_call(lambda *refs: scan_body(sign, *refs), out_shape=jax.ShapeD...  160 us
    pallas_call x13, Pallas kernels, row_blocks(): pl.pallas_call(lambda *refs: product_body(len(left), group, *refs), out_s...  112 us
    pallas_call x4, Pallas kernels, call(): pl.pallas_call(body, grid=(2, self.heads), in_specs=ins, out_specs=outs,...  109 us
    pallas_call x2, Pallas kernels, ffn(): pl.pallas_call(lambda *refs: ffn_body(order, *refs), out_shape=[jax.Shape...  95.5 us
    ppermute x58, waiting for transfers between devices, flip(): return lax.ppermute(x, 'tok', [(i, i ^ bits) for i in range(n)])  62.5 us
    ppermute x58, starting transfers between devices, flip(): return lax.ppermute(x, 'tok', [(i, i ^ bits) for i in range(n)])  57.3 us
    pallas_call x1, Pallas kernels, spread_first(): pl.pallas_call(first_body, out_shape=[jax.ShapeDtypeStruct((32,) + gains....  49.9 us
    pallas_call x1, Pallas kernels, spread_second(): pl.pallas_call(second_body, out_shape=[jax.ShapeDtypeStruct((4, 4) + z4.s...  47.6 us
  transfers between devices with their start and end apart: 58, of which 13 were waited for; matrix products, arithmetic and copies ran while one was open for 14% of the time, Pallas kernels for 57%

profile of v6, /device:TPU:0, one launch (start us, length us, event | category | flops | bytes accessed | tf_op | source)
XLA Modules:
  0.0 929.8 jit_solution(16948599439627149593)
XLA Ops:
  10.7 49.9 %shard_map.295 = (f32[32,8,128]{2,1,0:T(8,128)S(1)}, bf16[4,64,1408]{2,1,0:T(8,128)(2,1)S(1)}, bf16[4,64,1408]{2,1,0:T(8,128)(2,1)}, bf16[4,128,1280]{2,1,0:T(8,128)(2,1)S(1)}, bf16[4,176,2048]{2,1,0:T(8,128)(2,1)S(1)}) custom-call(f32[1,8,128]{2,1,0:T(8,128)S(1)} %fusion.67.gains_in, bf16[4,64,1408]{2,1,0:T(8,128)(2,1)S(1)} %shard_map.293.gate_in, ...), custom_call_target="tpu_custom_call" | custom-call | tf_op jit(solution)/shard_map/pallas_call | solution.py:223
  62.4 2.6 broadcast.80.clone
  65.0 2.6 constant_dynamic-update-slice_fusion.13
  70.4 47.6 %shard_map.296 = (bf16[4,4,128,1280]{3,2,1,0:T(8,128)(2,1)S(1)}, bf16[4,128,1024]{2,1,0:T(8,128)(2,1)S(1)}, bf16[2,4,64,1408]{3,2,1,0:T(8,128)(2,1)S(1)}) custom-call(bf16[4,128,1280]{2,1,0:T(8,128)(2,1)S(1)} %get-tuple-element.194.z4, bf16[64,1024]{1,0:T(8,128)(2,1)S(1)} %get-tuple-element.420.out_mine, bf16[64,1024]{1,0:T(8,128)(2,1)S(1)} %get-tuple-element.419.out_theirs, ...), custom_call_target="tpu_custom_call" | custom-call | tf_op jit(solution)/shard_map/pallas_call | solution.py:276
  120.5 3.2 constant_dynamic-update-slice_fusion.12.refs_1_.refs_2_.refs_3_.refs_4_
  123.7 7.5 convolution_convert_fusion.k_ref.v_ref.q_ref
  131.3 10.5 %shard_map.297 = f32[8,2,168,128]{3,2,1,0:T(8,128)S(1)} custom-call(s32[2]{0:T(128)S(1)} %pad_add_fusion.scal, bf16[1024,1280]{1,0:T(8,128)(2,1)S(1)} %convolution_convert_fusion.k_ref.v_ref.q_ref, bf16[1024,1280]{1,0:T(8,128)(2,1)S(1)} %convolution_convert_fusion.k_ref.v_ref.q_ref, bf16[8,128,160]{2,1,0:T(8,128)(2,1)S(1)} %copy-done.14, ...), custom_call_target="tpu_custom_call" | custom-call | tf_op jit(solution)/shard_map/pallas_call | solution.py:777
  143.0 10.0 %collective-permute-done.3 = bf16[4,64,1408]{2,1,0:T(8,128)(2,1)S(1)} collective-permute-done((bf16[4,64,1408]{2,1,0:T(8,128)(2,1)}, bf16[4,64,1408]{2,1,0:T(8,128)(2,1)S(1)}, u32[]{:S(2)}, u32[]{:S(2)}) %collective-permute-start.3) | collective-permute-done | bytes 720928 | tf_op jit(solution)/shard_map/ppermute | solution.py:29
  157.3 3.4 pad_maximum_fusion
  169.4 2.5 broadcast_in_dim.61
  173.0 100.2 %shard_map.298 = f32[8,168,128]{2,1,0:T(8,128)S(1)} custom-call(f32[8,168,128]{2,1,0:T(8,128)S(1)} %copy-done.28), custom_call_target="tpu_custom_call" | custom-call | tf_op jit(solution)/shard_map/pallas_call | solution.py:846
  280.1 3.6 fusion.74
  286.6 10.3 %collective-permute-start.13 = (bf16[704,512]{1,0:T(8,128)(2,1)}, bf16[704,512]{1,0:T(8,128)(2,1)S(1)}, u32[]{:S(2)}, u32[]{:S(2)}) collective-permute-start(bf16[704,512]{1,0:T(8,128)(2,1)} %slice.130), channel_id=1, source_target_pairs={{0,16},{1,17},{2,18},{3,19},{4,20},{5,21},{6,22},{7,23},{8,24},{9,... | collective-permute-start | bytes 2162696 | tf_op jit(solution)/shard_map/ppermute | solution.py:29
  299.8 20.3 %shard_map.299 = (f32[1024,1024]{1,0:T(8,128)}, bf16[1024,1024]{1,0:T(8,128)(2,1)}) custom-call(bf16[1024,1280]{1,0:T(8,128)(2,1)} %copy-done, bf16[1024,1280]{1,0:T(8,128)(2,1)} %copy-done, bf16[1024,1280]{1,0:T(8,128)(2,1)} %copy-done, s32[1024,1]{1,0:T(8,128)S(1)} %copy.134.lo_ref, f32[8,2,168,128]{3,2,1,0:T(8,128)S(1)} %copy.135.carry_ref, ...), custom_call_target="tpu_custom_call" | custom-call | tf_op jit(solution)/shard_map/pallas_call | solution.py:777
  320.2 8.3 collective-permute-done.13.refs_13_
  329.8 2.7 constant_dynamic-update-slice_fusion.9
  334.9 2.7 constant_dynamic-update-slice_fusion.8
  338.0 2.8 copy-done.46
  340.8 4.8 multiply_reduce_fusion.2
  353.0 3.2 constant_dynamic-update-slice_fusion.6.refs_1_.refs_2_.refs_3_.refs_4_
  356.2 47.8 %shard_map.300 = (bf16[1024,2048]{1,0:T(8,128)(2,1)}, bf16[1024,1408]{1,0:T(8,128)(2,1)}, bf16[1024,2816]{1,0:T(8,128)(2,1)}, bf16[1024,2048]{1,0:T(8,128)(2,1)}) custom-call(s32[5]{0:T(128)S(1)} %stack.81.refs_0_, bf16[1024,2048]{1,0:T(8,128)(2,1)} %constant_dynamic-update-slice_fusion.6.refs_1_.refs_2_.refs_3_.refs_4_, bf16[1024,2048]{1,0:T(8,128)(2,1)} %copy-done.42, ...), custom_call_target="tpu_custom_call" | custom-call | tf_op jit(solution)/shard_map/pallas_call | solution.py:420
  404.4 3.4 constant_dynamic-slice_fusion.8
  418.5 47.8 %shard_map.301 = (bf16[1024,2048]{1,0:T(8,128)(2,1)}, bf16[1024,1408]{1,0:T(8,128)(2,1)}, bf16[1024,2816]{1,0:T(8,128)(2,1)}, bf16[1024,2048]{1,0:T(8,128)(2,1)}) custom-call(s32[5]{0:T(128)S(1)} %stack.81.refs_0_, bf16[1024,2048]{1,0:T(8,128)(2,1)} %copy-done.37, bf16[1024,2048]{1,0:T(8,128)(2,1)} %copy-done.43, bf16[4,128,1408]{2,1,0:T(8,128)(2,1)S(1)} %bitcast.256, ...), custom_call_target="tpu_custom_call" | custom-call | tf_op jit(solution)/shard_map/pallas_call | solution.py:420
  466.3 5.6 constant_dynamic-slice_fusion.6
  472.9 13.4 %shard_map.302 = bf16[1024,1408]{1,0:T(8,128)(2,1)} custom-call(s32[8]{0:T(128)} %get-tuple-element.436.refs_0_, bf16[1024,2048]{1,0:T(8,128)(2,1)} %constant_dynamic-update-slice_fusion.6.refs_1_.refs_2_.refs_3_.refs_4_, bf16[1024,2048]{1,0:T(8,128)(2,1)} %constant_dynamic-update-slice_fusion.6.refs_1_.refs_2_.refs_3_.refs_4_, ...), custom_call_target="tpu_custom_call" | custom-call | tf_op jit(solution)/shard_map/pallas_call | solution.py:454
  487.6 3.8 add_convert_fusion.2.refs_12_
  492.0 3.7 add_convert_fusion.1.refs_13_
  495.7 12.5 %shard_map.303 = bf16[1024,1408]{1,0:T(8,128)(2,1)} custom-call(s32[8]{0:T(128)} %get-tuple-element.433.refs_0_, bf16[1024,2048]{1,0:T(8,128)(2,1)} %constant_dynamic-update-slice_fusion.6.refs_1_.refs_2_.refs_3_.refs_4_, bf16[1024,2048]{1,0:T(8,128)(2,1)} %constant_dynamic-update-slice_fusion.6.refs_1_.refs_2_.refs_3_.refs_4_, ...), custom_call_target="tpu_custom_call" | custom-call | tf_op jit(solution)/shard_map/pallas_call | solution.py:454
  509.0 12.5 %shard_map.304 = bf16[1024,1408]{1,0:T(8,128)(2,1)} custom-call(s32[8]{0:T(128)} %get-tuple-element.435.refs_0_, bf16[1024,2048]{1,0:T(8,128)(2,1)} %constant_dynamic-update-slice_fusion.6.refs_1_.refs_2_.refs_3_.refs_4_, bf16[1024,2048]{1,0:T(8,128)(2,1)} %constant_dynamic-update-slice_fusion.6.refs_1_.refs_2_.refs_3_.refs_4_, ...), custom_call_target="tpu_custom_call" | custom-call | tf_op jit(solution)/shard_map/pallas_call | solution.py:454
  521.5 12.5 %shard_map.305 = bf16[1024,1408]{1,0:T(8,128)(2,1)} custom-call(s32[8]{0:T(128)} %get-tuple-element.434.refs_0_, bf16[1024,2048]{1,0:T(8,128)(2,1)} %constant_dynamic-update-slice_fusion.6.refs_1_.refs_2_.refs_3_.refs_4_, bf16[1024,2048]{1,0:T(8,128)(2,1)} %constant_dynamic-update-slice_fusion.6.refs_1_.refs_2_.refs_3_.refs_4_, ...), custom_call_target="tpu_custom_call" | custom-call | tf_op jit(solution)/shard_map/pallas_call | solution.py:454
  534.6 20.2 %shard_map.306 = bf16[1408,2048]{1,0:T(8,128)(2,1)} custom-call(s32[11]{0:T(128)} %iota.10.refs_0_, bf16[1024,1408]{1,0:T(8,128)(2,1)} %get-tuple-element.245.refs_1_, bf16[1024,1408]{1,0:T(8,128)(2,1)} %get-tuple-element.269.refs_2_, bf16[1024,2048]{1,0:T(8,128)(2,1)} %copy-done.42, bf16[1024,2048]{1,0:T(8,128)(2,1)} %copy-done.43, ...), custom_call_target="tpu_custom_call" | custom-call | tf_op jit(solution)/shard_map/pallas_call | solution.py:454
  554.8 4.0 multiply_reduce_fusion
  561.0 6.2 constant_dynamic-update-slice_fusion.1
  569.2 4.6 add_bitcast_fusion.1
  575.7 9.5 %fusion.22.d_ref = bf16[1024,1024]{1,0:T(8,128)(2,1)} fusion(bf16[1024,2048]{1,0:T(8,128)(2,1)S(1)} %constant_dynamic-update-slice_fusion, bf16[2048,2048]{1,0:T(8,128)(2,1)} %copy-done.73, s32[]{:T(128)S(6)} %select_n.376), kind=kOutput, calls=%fused_computation.58 | convolution fusion | flops 4296015872 | bytes 10485764 | tf_op jit(solution)/shard_map/dot_general | solution.py:589
  585.2 2.9 fusion.26
  594.4 3.1 slice.134
  601.5 50.7 %shard_map.307 = (bf16[1024,128]{1,0:T(8,128)(2,1)S(1)}, f32[1024,128]{1,0:T(8,128)S(1)}, f32[1024,1024]{1,0:T(8,128)}, f32[8,2,168,128]{3,2,1,0:T(8,128)S(1)}) custom-call(bf16[1024,1280]{1,0:T(8,128)(2,1)} %copy-done, bf16[1024,1280]{1,0:T(8,128)(2,1)} %copy-done, bf16[1024,1280]{1,0:T(8,128)(2,1)} %copy-done, s32[1024,1]{1,0:T(8,128)S(1)} %copy-done.21, ...), custom_call_target="tpu_custom_call" | custom-call | tf_op jit(solution)/shard_map/pallas_call | solution.py:777
  665.7 4.8 shard_map.308
  671.9 4.7 shard_map.309
  678.4 59.3 %shard_map.310.refs_6_ = f32[8,168,128]{2,1,0:T(8,128)S(1)} custom-call(f32[8,168,128]{2,1,0:T(8,128)S(1)} %fusion.48.refs_0_), custom_call_target="tpu_custom_call" | custom-call | tf_op jit(solution)/shard_map/pallas_call | solution.py:846
  738.6 4.7 shard_map.312
  743.3 4.7 shard_map.311
  749.1 2.6 convert_add_fusion.8
  752.4 2.9 add_bitcast_fusion.2
  756.5 2.9 convert_add_fusion.3
  762.8 27.4 %shard_map.313 = (bf16[1024,128]{1,0:T(8,128)(2,1)S(1)}, bf16[1024,1024]{1,0:T(8,128)(2,1)S(1)}) custom-call(s32[2]{0:T(128)S(1)} %copy-done.35, bf16[1024,1280]{1,0:T(8,128)(2,1)} %copy-done, bf16[1024,1280]{1,0:T(8,128)(2,1)} %copy-done, bf16[8,128,160]{2,1,0:T(8,128)(2,1)S(1)} %copy-done.14, bf16[8,128,160]{2,1,0:T(8,128)(2,1)S(1)} %copy-done.18, ...), custom_call_target="tpu_custom_call" | custom-call | tf_op jit(solution)/shard_map/pallas_call | solution.py:777
  794.6 5.4 shard_map.314
  801.0 5.4 shard_map.315
  808.6 5.4 shard_map.316
  815.2 5.5 shard_map.317
  823.5 9.9 %shard_map.318 = bf16[1024,2048]{1,0:T(8,128)(2,1)} custom-call(bf16[1024,1280]{1,0:T(8,128)(2,1)S(1)} %copy-done.2, bf16[2048,1280]{1,0:T(8,128)(2,1)} %bitcast.261), custom_call_target="tpu_custom_call" | custom-call | tf_op jit(solution)/shard_map/pallas_call | solution.py:526
  833.5 13.2 %collective-permute-done.39 = bf16[1,176,2048]{2,1,0:T(8,128)(2,1)S(1)} collective-permute-done((bf16[1,176,2048]{2,1,0:T(8,128)(2,1)S(1)}, bf16[1,176,2048]{2,1,0:T(8,128)(2,1)S(1)}, u32[]{:S(2)}, u32[]{:S(2)}) %collective-permute-start.39) | collective-permute-done | bytes 720928 | tf_op jit(solution)/shard_map/ppermute | solution.py:29
  849.7 3.0 fusion.51
  856.2 2.6 fusion.17
  864.0 7.5 collective-permute-done.45
  872.2 5.7 fusion.6
  883.2 3.6 collective-permute-start.54
  891.0 3.3 fusion.30
  894.5 2.9 shard_map.319
  897.3 10.5 %collective-permute-done.52 = f32[2,2048]{1,0:T(2,128)S(1)} collective-permute-done((f32[2,2048]{1,0:T(2,128)S(1)}, f32[2,2048]{1,0:T(2,128)S(1)}, u32[]{:S(2)}, u32[]{:S(2)}) %collective-permute-start.52) | collective-permute-done | bytes 16416 | tf_op jit(solution)/shard_map/ppermute | solution.py:29
  911.1 3.0 fusion.9
  916.0 5.2 add_convert_fusion
  921.3 4.1 collective-permute-done.55
  (452 shorter events, 152.1 us)
Async XLA Ops:
  0.7 8.2 collective-permute-start
  6.4 58.5 %copy-start.103 = (f32[512]{0:T(512)}, f32[512]{0:T(512)S(1)}, u32[]{:S(2)}) copy-start(f32[512]{0:T(512)S(1)} %add_rsqrt_fusion.1) | copy-start | bytes 6148
  10.7 51.5 %copy-start.42 = (bf16[1024,2048]{1,0:T(8,128)(2,1)}, bf16[1024,2048]{1,0:T(8,128)(2,1)S(1)}, u32[]{:S(2)}) copy-start(bf16[1024,2048]{1,0:T(8,128)(2,1)S(1)} %constant_dynamic-update-slice_fusion.14.refs_2_.refs_3_) | copy-start | bytes 12582916
  67.6 53.0 %collective-permute-start.1 = (bf16[512,2048]{1,0:T(8,128)(2,1)}, bf16[512,2048]{1,0:T(8,128)(2,1)}, u32[]{:S(2)}, u32[]{:S(2)}) collective-permute-start(bf16[512,2048]{1,0:T(8,128)(2,1)} %get-tuple-element.386), channel_id=1, source_target_pairs={{0,1},{1,0},{2,3},{3,2},{4,5},{5,4},{6,7},{7,6},{8,9},{9,8},{10,11... | collective-permute-start | bytes 6291464 | tf_op jit(solution)/shard_map/ppermute | solution.py:29
  70.3 60.9 %copy-start.34 = (s32[2]{0:T(128)}, s32[2]{0:T(128)S(1)}, u32[]{:S(2)}) copy-start(s32[2]{0:T(128)S(1)} %pad_add_fusion.scal) | copy-start | bytes 28
  118.0 47.1 %copy-start.22 = (bf16[4,128,1024]{2,1,0:T(8,128)(2,1)}, bf16[4,128,1024]{2,1,0:T(8,128)(2,1)S(1)}, u32[]{:S(2)}) copy-start(bf16[4,128,1024]{2,1,0:T(8,128)(2,1)S(1)} %get-tuple-element.205) | copy-start | bytes 3145732
  118.0 24.9 %collective-permute-start.4 = (bf16[4,128,1024]{2,1,0:T(8,128)(2,1)S(1)}, bf16[4,128,1024]{2,1,0:T(8,128)(2,1)S(1)}, u32[]{:S(2)}, u32[]{:S(2)}) collective-permute-start(bf16[4,128,1024]{2,1,0:T(8,128)(2,1)S(1)} %get-tuple-element.205), channel_id=1, source_target_pairs={{0,4},{1,5},{2,6},{3,7},{4,0},{5,1},{6,2},{7,3},{8,12},{9,13},{10,... | collective-permute-start | bytes 3145736 | tf_op jit(solution)/shard_map/ppermute | solution.py:29
  119.6 33.4 %collective-permute-start.3 = (bf16[4,64,1408]{2,1,0:T(8,128)(2,1)}, bf16[4,64,1408]{2,1,0:T(8,128)(2,1)S(1)}, u32[]{:S(2)}, u32[]{:S(2)}) collective-permute-start(bf16[4,64,1408]{2,1,0:T(8,128)(2,1)} %get-tuple-element.202), channel_id=1, source_target_pairs={{0,16},{1,17},{2,18},{3,19},{4,20},{5,21},{6,22},{7,23},{8,24},{9,... | collective-permute-start | bytes 2162696 | tf_op jit(solution)/shard_map/ppermute | solution.py:29
  119.6 33.4 %collective-permute-start.2 = (bf16[2,4,64,1408]{3,2,1,0:T(8,128)(2,1)S(1)}, bf16[2,4,64,1408]{3,2,1,0:T(8,128)(2,1)}, u32[]{:S(2)}, u32[]{:S(2)}) collective-permute-start(bf16[2,4,64,1408]{3,2,1,0:T(8,128)(2,1)S(1)} %get-tuple-element.199), channel_id=1, source_target_pairs={{0,2},{1,3},{2,0},{3,1},{4,6},{5,7},{6,4},{7,5},{8,10},{9,11},{10,... | collective-permute-start | bytes 4325384 | tf_op jit(solution)/shard_map/ppermute | solution.py:29
  160.7 112.5 %collective-permute-start.6 = (bf16[2,4,64,2816]{3,2,1,0:T(8,128)(2,1)}, bf16[2,4,64,2816]{3,2,1,0:T(8,128)(2,1)}, u32[]{:S(2)}, u32[]{:S(2)}) collective-permute-start(bf16[2,4,64,2816]{3,2,1,0:T(8,128)(2,1)} %pad_maximum_fusion), channel_id=1, source_target_pairs={{0,4},{1,5},{2,6},{3,7},{4,0},{5,1},{6,2},{7,3},{8,12},{9,13},{10,... | collective-permute-start | bytes 8650760 | tf_op jit(solution)/shard_map/ppermute | solution.py:29
  162.6 110.6 %collective-permute-start.9 = (bf16[512,2048]{1,0:T(8,128)(2,1)}, bf16[512,2048]{1,0:T(8,128)(2,1)}, u32[]{:S(2)}, u32[]{:S(2)}) collective-permute-start(bf16[512,2048]{1,0:T(8,128)(2,1)} %param.34), channel_id=1, source_target_pairs={{0,8},{1,9},{2,10},{3,11},{4,12},{5,13},{6,14},{7,15},{8,0},{9,1},... | collective-permute-start | bytes 6291464 | tf_op jit(solution)/shard_map/ppermute | solution.py:29
  164.5 108.7 %collective-permute-start.8 = (bf16[704,1536]{1,0:T(8,128)(2,1)}, bf16[704,1536]{1,0:T(8,128)(2,1)}, u32[]{:S(2)}, u32[]{:S(2)}) collective-permute-start(bf16[704,1536]{1,0:T(8,128)(2,1)} %slice.129), channel_id=1, source_target_pairs={{0,16},{1,17},{2,18},{3,19},{4,20},{5,21},{6,22},{7,23},{8,24},{9,... | collective-permute-start | bytes 6488072 | tf_op jit(solution)/shard_map/ppermute | solution.py:29
  166.7 106.6 %collective-permute-start.5 = (bf16[2,4,128,1024]{3,2,1,0:T(8,128)(2,1)}, bf16[2,4,128,1024]{3,2,1,0:T(8,128)(2,1)}, u32[]{:S(2)}, u32[]{:S(2)}) collective-permute-start(bf16[2,4,128,1024]{3,2,1,0:T(8,128)(2,1)} %pad_maximum_fusion.1), channel_id=1, source_target_pairs={{0,2},{1,3},{2,0},{3,1},{4,6},{5,7},{6,4},{7,5},{8,10},{9,11},{10,... | collective-permute-start | bytes 6291464 | tf_op jit(solution)/shard_map/ppermute | solution.py:29
  168.1 105.1 %collective-permute-start.7 = (bf16[2,4,64,1408]{3,2,1,0:T(8,128)(2,1)}, bf16[2,4,64,1408]{3,2,1,0:T(8,128)(2,1)}, u32[]{:S(2)}, u32[]{:S(2)}) collective-permute-start(bf16[2,4,64,1408]{3,2,1,0:T(8,128)(2,1)} %bitcast_dynamic-update-slice_fusion.4), channel_id=1, source_target_pairs={{0,2},{1,3},{2,0},{3,1},{4,6},{5,7},{6,4},{7,5},{8,10},{9,11},{10,... | collective-permute-start | bytes 4325384 | tf_op jit(solution)/shard_map/ppermute | solution.py:29
  171.9 103.6 %copy-start.84 = (bf16[4,128,1024]{2,1,0:T(8,128)(2,1)S(1)}, bf16[4,128,1024]{2,1,0:T(8,128)(2,1)}, u32[]{:S(2)}) copy-start(bf16[4,128,1024]{2,1,0:T(8,128)(2,1)} %copy-done.83) | copy-start | bytes 3145732
  280.1 48.5 %collective-permute-start.10 = (bf16[2048,1024]{1,0:T(8,128)(2,1)}, bf16[2048,1024]{1,0:T(8,128)(2,1)}, u32[]{:S(2)}, u32[]{:S(2)}) collective-permute-start(bf16[2048,1024]{1,0:T(8,128)(2,1)} %bitcast.24), channel_id=1, source_target_pairs={{0,1},{1,0},{2,3},{3,2},{4,5},{5,4},{6,7},{7,6},{8,9},{9,8},{10,11... | collective-permute-start | bytes 12582920 | tf_op jit(solution)/shard_map/ppermute | solution.py:29
  283.7 44.9 %collective-permute-start.12 = (bf16[2,4,64,1408]{3,2,1,0:T(8,128)(2,1)}, bf16[2,4,64,1408]{3,2,1,0:T(8,128)(2,1)}, u32[]{:S(2)}, u32[]{:S(2)}) collective-permute-start(bf16[2,4,64,1408]{3,2,1,0:T(8,128)(2,1)} %get-tuple-element.231), channel_id=1, source_target_pairs={{0,2},{1,3},{2,0},{3,1},{4,6},{5,7},{6,4},{7,5},{8,10},{9,11},{10,... | collective-permute-start | bytes 4325384 | tf_op jit(solution)/shard_map/ppermute | solution.py:29
  284.9 43.7 %collective-permute-start.11 = (bf16[2,4,64,1408]{3,2,1,0:T(8,128)(2,1)}, bf16[2,4,64,1408]{3,2,1,0:T(8,128)(2,1)}, u32[]{:S(2)}, u32[]{:S(2)}) collective-permute-start(bf16[2,4,64,1408]{3,2,1,0:T(8,128)(2,1)} %collective-permute-done.2), channel_id=1, source_target_pairs={{0,4},{1,5},{2,6},{3,7},{4,0},{5,1},{6,2},{7,3},{8,12},{9,13},{10,... | collective-permute-start | bytes 4325384 | tf_op jit(solution)/shard_map/ppermute | solution.py:29
  286.6 41.9 %collective-permute-start.13 = (bf16[704,512]{1,0:T(8,128)(2,1)}, bf16[704,512]{1,0:T(8,128)(2,1)S(1)}, u32[]{:S(2)}, u32[]{:S(2)}) collective-permute-start(bf16[704,512]{1,0:T(8,128)(2,1)} %slice.130), channel_id=1, source_target_pairs={{0,16},{1,17},{2,18},{3,19},{4,20},{5,21},{6,22},{7,23},{8,24},{9,... | collective-permute-start | bytes 2162696 | tf_op jit(solution)/shard_map/ppermute | solution.py:29
  328.6 9.1 collective-permute-start.14
  348.3 4.7 collective-permute-start.15
  348.8 55.1 %collective-permute-start.16 = (bf16[512,2048]{1,0:T(8,128)(2,1)}, bf16[512,2048]{1,0:T(8,128)(2,1)}, u32[]{:S(2)}, u32[]{:S(2)}) collective-permute-start(bf16[512,2048]{1,0:T(8,128)(2,1)} %get-tuple-element.384), channel_id=1, source_target_pairs={{0,8},{1,9},{2,10},{3,11},{4,12},{5,13},{6,14},{7,15},{8,0},{9,1},... | collective-permute-start | bytes 6291464 | tf_op jit(solution)/shard_map/ppermute | solution.py:29
  403.9 8.0 collective-permute-start.17
  411.7 4.4 collective-permute-start.18
  412.2 54.0 %collective-permute-start.20 = (bf16[512,2048]{1,0:T(8,128)(2,1)}, bf16[512,2048]{1,0:T(8,128)(2,1)}, u32[]{:S(2)}, u32[]{:S(2)}) collective-permute-start(bf16[512,2048]{1,0:T(8,128)(2,1)} %constant_dynamic-slice_fusion.8), channel_id=1, source_target_pairs={{0,1},{1,0},{2,3},{3,2},{4,5},{5,4},{6,7},{7,6},{8,9},{9,8},{10,11... | collective-permute-start | bytes 6291464 | tf_op jit(solution)/shard_map/ppermute | solution.py:29
  412.7 53.6 %collective-permute-start.19 = (bf16[512,2048]{1,0:T(8,128)(2,1)}, bf16[512,2048]{1,0:T(8,128)(2,1)S(1)}, u32[]{:S(2)}, u32[]{:S(2)}) collective-permute-start(bf16[512,2048]{1,0:T(8,128)(2,1)} %constant_dynamic-slice_fusion.9), channel_id=1, source_target_pairs={{0,1},{1,0},{2,3},{3,2},{4,5},{5,4},{6,7},{7,6},{8,9},{9,8},{10,11... | collective-permute-start | bytes 6291464 | tf_op jit(solution)/shard_map/ppermute | solution.py:29
  471.9 15.7 %collective-permute-start.22 = (bf16[512,2048]{1,0:T(8,128)(2,1)}, bf16[512,2048]{1,0:T(8,128)(2,1)S(1)}, u32[]{:S(2)}, u32[]{:S(2)}) collective-permute-start(bf16[512,2048]{1,0:T(8,128)(2,1)} %get-tuple-element.266), channel_id=1, source_target_pairs={{0,1},{1,0},{2,3},{3,2},{4,5},{5,4},{6,7},{7,6},{8,9},{9,8},{10,11... | collective-permute-start | bytes 6291464 | tf_op jit(solution)/shard_map/ppermute | solution.py:29
  472.1 15.6 %collective-permute-start.21 = (bf16[512,2048]{1,0:T(8,128)(2,1)}, bf16[512,2048]{1,0:T(8,128)(2,1)}, u32[]{:S(2)}, u32[]{:S(2)}) collective-permute-start(bf16[512,2048]{1,0:T(8,128)(2,1)} %get-tuple-element.264), channel_id=1, source_target_pairs={{0,1},{1,0},{2,3},{3,2},{4,5},{5,4},{6,7},{7,6},{8,9},{9,8},{10,11... | collective-permute-start | bytes 6291464 | tf_op jit(solution)/shard_map/ppermute | solution.py:29
  486.4 68.4 %collective-permute-start.24 = (bf16[4,256,1408]{2,1,0:T(8,128)(2,1)}, bf16[4,256,1408]{2,1,0:T(8,128)(2,1)}, u32[]{:S(2)}, u32[]{:S(2)}) collective-permute-start(bf16[4,256,1408]{2,1,0:T(8,128)(2,1)} %bitcast.276), channel_id=1, source_target_pairs={{0,2},{1,3},{2,0},{3,1},{4,6},{5,7},{6,4},{7,5},{8,10},{9,11},{10,... | collective-permute-start | bytes 8650760 | tf_op jit(solution)/shard_map/ppermute | solution.py:29
  491.4 63.3 %collective-permute-start.23 = (bf16[512,2048]{1,0:T(8,128)(2,1)}, bf16[512,2048]{1,0:T(8,128)(2,1)}, u32[]{:S(2)}, u32[]{:S(2)}) collective-permute-start(bf16[512,2048]{1,0:T(8,128)(2,1)} %add_convert_fusion.2.refs_12_), channel_id=1, source_target_pairs={{0,8},{1,9},{2,10},{3,11},{4,12},{5,13},{6,14},{7,15},{8,0},{9,1},... | collective-permute-start | bytes 6291464 | tf_op jit(solution)/shard_map/ppermute | solution.py:29
  508.2 65.7 %collective-permute-start.26 = (bf16[4,256,1408]{2,1,0:T(8,128)(2,1)}, bf16[4,256,1408]{2,1,0:T(8,128)(2,1)}, u32[]{:S(2)}, u32[]{:S(2)}) collective-permute-start(bf16[4,256,1408]{2,1,0:T(8,128)(2,1)} %bitcast.278), channel_id=1, source_target_pairs={{0,4},{1,5},{2,6},{3,7},{4,0},{5,1},{6,2},{7,3},{8,12},{9,13},{10,... | collective-permute-start | bytes 8650760 | tf_op jit(solution)/shard_map/ppermute | solution.py:29
  569.2 4.6 collective-permute-start.25
  588.1 66.5 %collective-permute-start.29 = (bf16[512,2048]{1,0:T(8,128)(2,1)}, bf16[512,2048]{1,0:T(8,128)(2,1)}, u32[]{:S(2)}, u32[]{:S(2)}) collective-permute-start(bf16[512,2048]{1,0:T(8,128)(2,1)} %add_convert_fusion.1.refs_13_), channel_id=1, source_target_pairs={{0,8},{1,9},{2,10},{3,11},{4,12},{5,13},{6,14},{7,15},{8,0},{9,1},... | collective-permute-start | bytes 6291464 | tf_op jit(solution)/shard_map/ppermute | solution.py:29
  590.1 62.0 %collective-permute-start.27 = (bf16[2,256,1408]{2,1,0:T(8,128)(2,1)}, bf16[2,256,1408]{2,1,0:T(8,128)(2,1)}, u32[]{:S(2)}, u32[]{:S(2)}) collective-permute-start(bf16[2,256,1408]{2,1,0:T(8,128)(2,1)} %get-tuple-element.388), channel_id=1, source_target_pairs={{0,4},{1,5},{2,6},{3,7},{4,0},{5,1},{6,2},{7,3},{8,12},{9,13},{10,... | collective-permute-start | bytes 4325384 | tf_op jit(solution)/shard_map/ppermute | solution.py:29
  591.4 63.2 %collective-permute-start.28 = (bf16[2,256,1408]{2,1,0:T(8,128)(2,1)}, bf16[2,256,1408]{2,1,0:T(8,128)(2,1)}, u32[]{:S(2)}, u32[]{:S(2)}) collective-permute-start(bf16[2,256,1408]{2,1,0:T(8,128)(2,1)} %fusion.26), channel_id=1, source_target_pairs={{0,2},{1,3},{2,0},{3,1},{4,6},{5,7},{6,4},{7,5},{8,10},{9,11},{10,... | collective-permute-start | bytes 4325384 | tf_op jit(solution)/shard_map/ppermute | solution.py:29
  601.5 50.7 %copy-start.49 = (bf16[1024,1408]{1,0:T(8,128)(2,1)S(1)}, bf16[1024,1408]{1,0:T(8,128)(2,1)}, u32[]{:S(2)}) copy-start(bf16[1024,1408]{1,0:T(8,128)(2,1)} %shard_map.305) | copy-start | bytes 8650756
  660.9 87.1 %collective-permute-start.30 = (bf16[1,256,2816]{2,1,0:T(8,128)(2,1)}, bf16[1,256,2816]{2,1,0:T(8,128)(2,1)}, u32[]{:S(2)}, u32[]{:S(2)}) collective-permute-start(bf16[1,256,2816]{2,1,0:T(8,128)(2,1)} %fusion.20), channel_id=1, source_target_pairs={{0,16},{1,17},{2,18},{3,19},{4,20},{5,21},{6,22},{7,23},{8,24},{9,... | collective-permute-start | bytes 4325384 | tf_op jit(solution)/shard_map/ppermute | solution.py:29
  661.6 86.5 %collective-permute-start.31 = (bf16[4,176,1024]{2,1,0:T(8,128)(2,1)}, bf16[4,176,1024]{2,1,0:T(8,128)(2,1)}, u32[]{:S(2)}, u32[]{:S(2)}) collective-permute-start(bf16[4,176,1024]{2,1,0:T(8,128)(2,1)} %get-tuple-element.291), channel_id=1, source_target_pairs={{0,2},{1,3},{2,0},{3,1},{4,6},{5,7},{6,4},{7,5},{8,10},{9,11},{10,... | collective-permute-start | bytes 4325384 | tf_op jit(solution)/shard_map/ppermute | solution.py:29
  662.4 85.7 %collective-permute-start.32 = (bf16[4,176,1024]{2,1,0:T(8,128)(2,1)}, bf16[4,176,1024]{2,1,0:T(8,128)(2,1)}, u32[]{:S(2)}, u32[]{:S(2)}) collective-permute-start(bf16[4,176,1024]{2,1,0:T(8,128)(2,1)} %bitcast.55), channel_id=1, source_target_pairs={{0,4},{1,5},{2,6},{3,7},{4,0},{5,1},{6,2},{7,3},{8,12},{9,13},{10,... | collective-permute-start | bytes 4325384 | tf_op jit(solution)/shard_map/ppermute | solution.py:29
  670.5 77.6 %collective-permute-start.33 = (bf16[8,128,512]{2,1,0:T(8,128)(2,1)}, bf16[8,128,512]{2,1,0:T(8,128)(2,1)}, u32[]{:S(2)}, u32[]{:S(2)}) collective-permute-start(bf16[8,128,512]{2,1,0:T(8,128)(2,1)} %bitcast.295), channel_id=1, source_target_pairs={{0,2},{1,3},{2,0},{3,1},{4,6},{5,7},{6,4},{7,5},{8,10},{9,11},{10,... | collective-permute-start | bytes 3145736 | tf_op jit(solution)/shard_map/ppermute | solution.py:29
  676.6 71.5 %collective-permute-start.34 = (bf16[8,128,512]{2,1,0:T(8,128)(2,1)}, bf16[8,128,512]{2,1,0:T(8,128)(2,1)S(1)}, u32[]{:S(2)}, u32[]{:S(2)}) collective-permute-start(bf16[8,128,512]{2,1,0:T(8,128)(2,1)} %bitcast.296), channel_id=1, source_target_pairs={{0,4},{1,5},{2,6},{3,7},{4,0},{5,1},{6,2},{7,3},{8,12},{9,13},{10,... | collective-permute-start | bytes 3145736 | tf_op jit(solution)/shard_map/ppermute | solution.py:29
  751.7 38.6 %collective-permute-start.35 = (bf16[4,128,512]{2,1,0:T(8,128)(2,1)}, bf16[4,128,512]{2,1,0:T(8,128)(2,1)S(1)}, u32[]{:S(2)}, u32[]{:S(2)}) collective-permute-start(bf16[4,128,512]{2,1,0:T(8,128)(2,1)} %get-tuple-element.404), channel_id=1, source_target_pairs={{0,4},{1,5},{2,6},{3,7},{4,0},{5,1},{6,2},{7,3},{8,12},{9,13},{10,... | collective-permute-start | bytes 1572872 | tf_op jit(solution)/shard_map/ppermute | solution.py:29
  755.3 35.0 %collective-permute-start.37 = (bf16[2,176,1024]{2,1,0:T(8,128)(2,1)}, bf16[2,176,1024]{2,1,0:T(8,128)(2,1)}, u32[]{:S(2)}, u32[]{:S(2)}) collective-permute-start(bf16[2,176,1024]{2,1,0:T(8,128)(2,1)} %get-tuple-element.396), channel_id=1, source_target_pairs={{0,4},{1,5},{2,6},{3,7},{4,0},{5,1},{6,2},{7,3},{8,12},{9,13},{10,... | collective-permute-start | bytes 2162696 | tf_op jit(solution)/shard_map/ppermute | solution.py:29
  759.4 32.3 %collective-permute-start.38 = (bf16[2,176,1024]{2,1,0:T(8,128)(2,1)}, bf16[2,176,1024]{2,1,0:T(8,128)(2,1)S(1)}, u32[]{:S(2)}, u32[]{:S(2)}) collective-permute-start(bf16[2,176,1024]{2,1,0:T(8,128)(2,1)} %get-tuple-element.390), channel_id=1, source_target_pairs={{0,2},{1,3},{2,0},{3,1},{4,6},{5,7},{6,4},{7,5},{8,10},{9,11},{10,... | collective-permute-start | bytes 2162696 | tf_op jit(solution)/shard_map/ppermute | solution.py:29
  760.5 29.8 %collective-permute-start.36 = (bf16[4,128,512]{2,1,0:T(8,128)(2,1)S(1)}, bf16[4,128,512]{2,1,0:T(8,128)(2,1)S(1)}, u32[]{:S(2)}, u32[]{:S(2)}) collective-permute-start(bf16[4,128,512]{2,1,0:T(8,128)(2,1)S(1)} %fusion.55), channel_id=1, source_target_pairs={{0,2},{1,3},{2,0},{3,1},{4,6},{5,7},{6,4},{7,5},{8,10},{9,11},{10,... | collective-permute-start | bytes 1572872 | tf_op jit(solution)/shard_map/ppermute | solution.py:29
  800.0 47.5 %collective-permute-start.41 = (bf16[8,128,640]{2,1,0:T(8,128)(2,1)}, bf16[8,128,640]{2,1,0:T(8,128)(2,1)}, u32[]{:S(2)}, u32[]{:S(2)}) collective-permute-start(bf16[8,128,640]{2,1,0:T(8,128)(2,1)} %bitcast.270), channel_id=1, source_target_pairs={{0,2},{1,3},{2,0},{3,1},{4,6},{5,7},{6,4},{7,5},{8,10},{9,11},{10,... | collective-permute-start | bytes 3932168 | tf_op jit(solution)/shard_map/ppermute | solution.py:29
  806.4 41.1 %collective-permute-start.42 = (bf16[8,128,640]{2,1,0:T(8,128)(2,1)}, bf16[8,128,640]{2,1,0:T(8,128)(2,1)}, u32[]{:S(2)}, u32[]{:S(2)}) collective-permute-start(bf16[8,128,640]{2,1,0:T(8,128)(2,1)} %bitcast.282), channel_id=1, source_target_pairs={{0,4},{1,5},{2,6},{3,7},{4,0},{5,1},{6,2},{7,3},{8,12},{9,13},{10,... | collective-permute-start | bytes 3932168 | tf_op jit(solution)/shard_map/ppermute | solution.py:29
  814.0 32.7 %collective-permute-start.39 = (bf16[1,176,2048]{2,1,0:T(8,128)(2,1)S(1)}, bf16[1,176,2048]{2,1,0:T(8,128)(2,1)S(1)}, u32[]{:S(2)}, u32[]{:S(2)}) collective-permute-start(bf16[1,176,2048]{2,1,0:T(8,128)(2,1)S(1)} %fusion.33), channel_id=1, source_target_pairs={{0,16},{1,17},{2,18},{3,19},{4,20},{5,21},{6,22},{7,23},{8,24},{9,... | collective-permute-start | bytes 2162696 | tf_op jit(solution)/shard_map/ppermute | solution.py:29
  822.3 25.2 %collective-permute-start.40 = (bf16[2,128,1024]{2,1,0:T(8,128)(2,1)S(1)}, bf16[2,128,1024]{2,1,0:T(8,128)(2,1)S(1)}, u32[]{:S(2)}, u32[]{:S(2)}) collective-permute-start(bf16[2,128,1024]{2,1,0:T(8,128)(2,1)S(1)} %get-tuple-element.394), channel_id=1, source_target_pairs={{0,8},{1,9},{2,10},{3,11},{4,12},{5,13},{6,14},{7,15},{8,0},{9,1},... | collective-permute-start | bytes 1572872 | tf_op jit(solution)/shard_map/ppermute | solution.py:29
  854.1 7.9 collective-permute-start.43
  854.2 17.4 %collective-permute-start.45 = (bf16[4,128,640]{2,1,0:T(8,128)(2,1)}, bf16[4,128,640]{2,1,0:T(8,128)(2,1)S(1)}, u32[]{:S(2)}, u32[]{:S(2)}) collective-permute-start(bf16[4,128,640]{2,1,0:T(8,128)(2,1)} %get-tuple-element.401), channel_id=1, source_target_pairs={{0,2},{1,3},{2,0},{3,1},{4,6},{5,7},{6,4},{7,5},{8,10},{9,11},{10,... | collective-permute-start | bytes 1966088 | tf_op jit(solution)/shard_map/ppermute | solution.py:29
  855.1 17.1 %collective-permute-start.44 = (bf16[4,128,640]{2,1,0:T(8,128)(2,1)}, bf16[4,128,640]{2,1,0:T(8,128)(2,1)S(1)}, u32[]{:S(2)}, u32[]{:S(2)}) collective-permute-start(bf16[4,128,640]{2,1,0:T(8,128)(2,1)} %fusion.50), channel_id=1, source_target_pairs={{0,4},{1,5},{2,6},{3,7},{4,0},{5,1},{6,2},{7,3},{8,12},{9,13},{10,... | collective-permute-start | bytes 1966088 | tf_op jit(solution)/shard_map/ppermute | solution.py:29
  862.1 18.6 %collective-permute-start.48 = (bf16[64,2816]{1,0:T(8,128)(2,1)S(1)}, bf16[64,2816]{1,0:T(8,128)(2,1)S(1)}, u32[]{:S(2)}, u32[]{:S(2)}) collective-permute-start(bf16[64,2816]{1,0:T(8,128)(2,1)S(1)} %get-tuple-element.352), channel_id=1, source_target_pairs={{0,9},{1,8},{2,11},{3,10},{4,13},{5,12},{6,15},{7,14},{8,1},{9,0},... | collective-permute-start | bytes 1081352 | tf_op jit(solution)/shard_map/ppermute | solution.py:29
  862.2 18.6 %collective-permute-start.47 = (bf16[64,2816]{1,0:T(8,128)(2,1)S(1)}, bf16[64,2816]{1,0:T(8,128)(2,1)S(1)}, u32[]{:S(2)}, u32[]{:S(2)}) collective-permute-start(bf16[64,2816]{1,0:T(8,128)(2,1)S(1)} %get-tuple-element.351), channel_id=1, source_target_pairs={{0,8},{1,9},{2,10},{3,11},{4,12},{5,13},{6,14},{7,15},{8,0},{9,1},... | collective-permute-start | bytes 1081352 | tf_op jit(solution)/shard_map/ppermute | solution.py:29
  863.7 17.0 %collective-permute-start.46 = (bf16[64,2816]{1,0:T(8,128)(2,1)S(1)}, bf16[64,2816]{1,0:T(8,128)(2,1)S(1)}, u32[]{:S(2)}, u32[]{:S(2)}) collective-permute-start(bf16[64,2816]{1,0:T(8,128)(2,1)S(1)} %get-tuple-element.350), channel_id=1, source_target_pairs={{0,1},{1,0},{2,3},{3,2},{4,5},{5,4},{6,7},{7,6},{8,9},{9,8},{10,11... | collective-permute-start | bytes 1081352 | tf_op jit(solution)/shard_map/ppermute | solution.py:29
  880.7 1.2 collective-permute-start.49
  882.0 7.2 collective-permute-start.50
  883.2 24.7 %collective-permute-start.54 = (bf16[1,128,1024]{2,1,0:T(8,128)(2,1)}, bf16[1,128,1024]{2,1,0:T(8,128)(2,1)S(1)}, u32[]{:S(2)}, u32[]{:S(2)}) collective-permute-start(bf16[1,128,1024]{2,1,0:T(8,128)(2,1)} %get-tuple-element.408), channel_id=1, source_target_pairs={{0,16},{1,17},{2,18},{3,19},{4,20},{5,21},{6,22},{7,23},{8,24},{9,... | collective-permute-start | bytes 786440 | tf_op jit(solution)/shard_map/ppermute | solution.py:29
  886.7 21.2 %collective-permute-start.53 = (bf16[2,128,1280]{2,1,0:T(8,128)(2,1)}, bf16[2,128,1280]{2,1,0:T(8,128)(2,1)S(1)}, u32[]{:S(2)}, u32[]{:S(2)}) collective-permute-start(bf16[2,128,1280]{2,1,0:T(8,128)(2,1)} %get-tuple-element.391), channel_id=1, source_target_pairs={{0,8},{1,9},{2,10},{3,11},{4,12},{5,13},{6,14},{7,15},{8,0},{9,1},... | collective-permute-start | bytes 1966088 | tf_op jit(solution)/shard_map/ppermute | solution.py:29
  890.0 4.4 collective-permute-start.51
  894.4 13.5 %collective-permute-start.52 = (f32[2,2048]{1,0:T(2,128)S(1)}, f32[2,2048]{1,0:T(2,128)S(1)}, u32[]{:S(2)}, u32[]{:S(2)}) collective-permute-start(f32[2,2048]{1,0:T(2,128)S(1)} %add.670), channel_id=1, source_target_pairs={{0,8},{1,9},{2,10},{3,11},{4,12},{5,13},{6,14},{7,15},{8,0},{9,1},... | collective-permute-start | bytes 49160 | tf_op jit(solution)/shard_map/ppermute | solution.py:29
  908.1 18.0 %collective-permute-start.56 = (bf16[1,128,1280]{2,1,0:T(8,128)(2,1)S(1)}, bf16[1,128,1280]{2,1,0:T(8,128)(2,1)S(1)}, u32[]{:S(2)}, u32[]{:S(2)}) collective-permute-start(bf16[1,128,1280]{2,1,0:T(8,128)(2,1)S(1)} %get-tuple-element.406), channel_id=1, source_target_pairs={{0,16},{1,17},{2,18},{3,19},{4,20},{5,21},{6,22},{7,23},{8,24},{9,... | collective-permute-start | bytes 983048 | tf_op jit(solution)/shard_map/ppermute | solution.py:29
  910.5 14.9 %collective-permute-start.55 = (f32[2,2048]{1,0:T(2,128)S(1)}, f32[2,2048]{1,0:T(2,128)S(1)}, u32[]{:S(2)}, u32[]{:S(2)}) collective-permute-start(f32[2,2048]{1,0:T(2,128)S(1)} %add.671), channel_id=1, source_target_pairs={{0,16},{1,17},{2,18},{3,19},{4,20},{5,21},{6,22},{7,23},{8,24},{9,... | collective-permute-start | bytes 49160 | tf_op jit(solution)/shard_map/ppermute | solution.py:29
  926.2 2.1 collective-permute-start.57
  (110 other events, 783.5 us)

commit v7 on v5

--- a/solution.py
+++ b/solution.py
@@ -372,7 +372,7 @@
 
 def ffn_body(order, sides, x_ref, g_ref, *refs):
     gates, ups, downs = refs[0:4], refs[4:8], refs[8:11]
-    y_ref, act_ref, d_ref, dh_ref, w_gate_up, w_down, sem = refs[11:]
+    y_ref, act_ref, d_ref, dh_ref, y_there, dh_there, w_gate_up, w_down, sem = refs[11:]
     cols = w_down.shape[0]
 
     @pl.when(pl.program_id(0) == 0)
@@ -406,29 +406,52 @@
         act_ref[:, s : s + w] = (smooth * upper).astype(bf16)
         d_ref[:, s : s + w] = (d_act * upper * sigma * (1.0 + gate * (1.0 - sigma))).astype(bf16)
         d_ref[:, cols + s : cols + s + w] = (d_act * smooth).astype(bf16)
-    y_ref[...] = dot(act_ref[...], w_down[...]).astype(bf16)
-    dh_ref[...] = dot_cols(d_ref[...], w_gate_up[...]).astype(bf16)
+    mine = pl.program_id(0) // (pl.num_programs(0) // 2) == sides[5]
+    y = dot(act_ref[...], w_down[...]).astype(bf16)
+    dh = dot_cols(d_ref[...], w_gate_up[...]).astype(bf16)
+
+    @pl.when(mine)
+    def _():
+        y_ref[...] = y
+        dh_ref[...] = dh
+
+    @pl.when(jnp.logical_not(mine))
+    def _():
+        y_there[...] = y
+        dh_there[...] = dh
 
 
 def ffn(x, g, gate, up, down, order, sides, tile=256):
     tokens, width = x.shape
     cols = 2 * down[0].shape[0]
 
+    steps = tokens // tile // 2
+
     def block(w):
-        return pl.BlockSpec((tile, w), lambda i: (i, 0))
-
+        return pl.BlockSpec((tile, w), lambda i, s: (i, 0))
+
+    def half(of_mine):
+        def at(i, s):
+            return jnp.clip(i - steps * (s[5] if of_mine else 1 - s[5]), 0, steps - 1), 0
+
+        return pl.BlockSpec((tile, width), at)
+
+    shapes = [(tokens // 2, width), (tokens, cols), (tokens, 2 * cols)] + [(tokens // 2, width)] * 3
     return pl.pallas_call(
         lambda *refs: ffn_body(order, *refs),
-        out_shape=[jax.ShapeDtypeStruct((tokens, w), bf16) for w in (width, cols, 2 * cols, width)],
-        grid=(tokens // tile,),
-        in_specs=[pl.BlockSpec(memory_space=pltpu.SMEM), block(width), block(width)] + [pl.BlockSpec(memory_space=pl.ANY)] * 11,
-        out_specs=[block(width), block(cols), block(2 * cols), block(width)],
-        scratch_shapes=[
-            pltpu.VMEM((width, 2 * cols), bf16),
-            pltpu.VMEM((cols, width), bf16),
-            pltpu.SemaphoreType.DMA((8 * len(order) + 3,)),
-        ],
-        compiler_params=pltpu.CompilerParams(vmem_limit_bytes=48 * MIB),
+        out_shape=[jax.ShapeDtypeStruct(shape, bf16) for shape in shapes],
+        grid_spec=pltpu.PrefetchScalarGridSpec(
+            num_scalar_prefetch=1,
+            grid=(tokens // tile,),
+            in_specs=[block(width), block(width)] + [pl.BlockSpec(memory_space=pl.ANY)] * 11,
+            out_specs=[half(True), block(cols), block(2 * cols), half(True), half(False), half(False)],
+            scratch_shapes=[
+                pltpu.VMEM((width, 2 * cols), bf16),
+                pltpu.VMEM((cols, width), bf16),
+                pltpu.SemaphoreType.DMA((8 * len(order) + 3,)),
+            ],
+        ),
+        compiler_params=pltpu.CompilerParams(vmem_limit_bytes=52 * MIB),
         cost_estimate=pl.CostEstimate(flops=0, bytes_accessed=0, transcendentals=0),
     )(sides, x, g, *gate, *up, *down)
 
@@ -1000,24 +1023,24 @@
     gate = [w.reshape(-1, 2 * rows, cols) for w in (gate, gate_x, gate_y, gate_xy)]
     up = [w.reshape(-1, 2 * rows, cols) for w in (up, up_x, up_y, up_xy)]
     order = [(at + more) // 2 for at in grown(qbits[:-2]) for more in (0, PAIR)]
-    sides = jnp.stack([place, place ^ 1, place ^ 2, place ^ 3, side(qbits[0])])
+    sides = jnp.stack([place, place ^ 1, place ^ 2, place ^ 3, side(qbits[0]), core]).astype(jnp.int32)
     near = ffn(near_hidden, near_grad, gate, up, down, order, sides)
     far_hidden, far_there = after(far_hidden, *near), move(far_grad, 1, (near_hidden,), (near[0],))
     far_grad = side_by_side(core, far_grad, far_there)
     far_hidden = side_by_side(core, far_hidden, flip(far_hidden, 1))
     far = ffn(far_hidden, far_grad, gate, up, down, order, sides)
     start, stop = (near[0], far_hidden), (far[0],)
-    near_parts = [move(row_half(near[i], 1 - core), 1, start, stop) for i in (3, 0)]
+    near_parts = [move(near[i], 1, start, stop) for i in (5, 4)]
     far, near_parts = lax.optimization_barrier((far, near_parts))
 
     right = [near[2], far[2]]
     sum_gate = Scatter(part_maker([near_hidden, far_hidden], right, qbits, (0, PAIR), 0), qbits)
     sum_gate.send()
     start, stop = (far[0],), (sum_gate.sent,)
-    far_parts = [move(row_half(far[i], 1 - core), 1, start, stop) for i in (3, 0)]
+    far_parts = [move(far[i], 1, start, stop) for i in (5, 4)]
     sent, far_parts = lax.optimization_barrier((sum_gate.sent, far_parts))
-    d_far = (row_half(far[3], core).astype(f32) + far_parts[0].astype(f32)).astype(bf16)
-    y_far = (row_half(far[0], core).astype(f32) + far_parts[1].astype(f32)).astype(bf16)
+    d_far = (far[3].astype(f32) + far_parts[0].astype(f32)).astype(bf16)
+    y_far = (far[0].astype(f32) + far_parts[1].astype(f32)).astype(bf16)
     sum_up = Scatter(part_maker([near_hidden, far_hidden], right, swapped, (0, PAIR), 1), swapped)
     sum_up.send(sent, d_far, y_far)
     sum_gate.keep(sum_up.sent)
@@ -1026,8 +1049,8 @@
     d_far = move(d_far, PAIR, (), (term,))
     d_far = sum_gate.hold(d_far, term)
     near_parts = after(near_parts, d_far)
-    d_near = row_half(near[3], core).astype(f32) + near_parts[0].astype(f32)
-    y_near = row_half(near[0], core).astype(f32) + near_parts[1].astype(f32)
+    d_near = near[3].astype(f32) + near_parts[0].astype(f32)
+    y_near = near[0].astype(f32) + near_parts[1].astype(f32)
     d_hidden_two = d_near + d_far.astype(f32)
     term_norm_two = jnp.sum(d_hidden_two * normed_two, axis=0)
     scaled_two = d_hidden_two * gain_two

time: 933 us -> 935 us (level)
  local copies, waits for them, and re-layouts: 110 us -> 98.3 us
    dynamic_slice x5 -> x2, local copies, waits for them, and re-layouts: 12.2 us -> 1.54 us  [row_half(): lax.dynamic_slice_in_dim(w, which * (w.shape[0] // 2), w.shape[0] // 2, 0)]
    unnamed x236 -> x218, local copies, waits for them, and re-layouts: 32 us -> 27.4 us
  transfers between devices with their start and end apart: 58 -> 58, of which waited for: 13 -> 13; matrix products, arithmetic and copies ran while one was open for 14% -> 14% of each run, Pallas kernels for 57% -> 58%
where the time goes in v7:
time: 935 us; the launch traced here: 926 us
  Pallas kernels  590 us (63%)
  local copies, waits for them, and re-layouts  98.3 us (11%)
  other arithmetic  91.5 us (10%)
  waiting for transfers between devices  63.2 us (7%)
  starting transfers between devices  56.8 us (6%)
  matrix products  21.7 us (2%)
    pallas_call x2, Pallas kernels, others(): pl.pallas_call(lambda *refs: scan_body(sign, *refs), out_shape=jax.ShapeD...  159 us
    pallas_call x13, Pallas kernels, row_blocks(): pl.pallas_call(lambda *refs: product_body(len(left), group, *refs), out_s...  112 us
    pallas_call x4, Pallas kernels, call(): pl.pallas_call(body, grid=(2, self.heads), in_specs=ins, out_specs=outs,...  104 us
    pallas_call x2, Pallas kernels, ffn(): pl.pallas_call(lambda *refs: ffn_body(order, *refs), out_shape=[jax.Shape...  104 us
    ppermute x58, waiting for transfers between devices, flip(): return lax.ppermute(x, 'tok', [(i, i ^ bits) for i in range(n)])  63.2 us
    ppermute x58, starting transfers between devices, flip(): return lax.ppermute(x, 'tok', [(i, i ^ bits) for i in range(n)])  56.8 us
    pallas_call x1, Pallas kernels, spread_first(): pl.pallas_call(first_body, out_shape=[jax.ShapeDtypeStruct((32,) + gains....  49.9 us
    pallas_call x1, Pallas kernels, spread_second(): pl.pallas_call(second_body, out_shape=[jax.ShapeDtypeStruct((4, 4) + z4.s...  47.6 us
  transfers between devices with their start and end apart: 58, of which 13 were waited for; matrix products, arithmetic and copies ran while one was open for 14% of the time, Pallas kernels for 58%

profile of v7, /device:TPU:0, one launch (start us, length us, event | category | flops | bytes accessed | tf_op | source)
XLA Modules:
  0.0 926.0 jit_solution(15476849747535676520)
XLA Ops:
  11.7 49.9 %shard_map.295 = (f32[32,8,128]{2,1,0:T(8,128)S(1)}, bf16[4,64,1408]{2,1,0:T(8,128)(2,1)S(1)}, bf16[4,64,1408]{2,1,0:T(8,128)(2,1)}, bf16[4,128,1280]{2,1,0:T(8,128)(2,1)S(1)}, bf16[4,176,2048]{2,1,0:T(8,128)(2,1)S(1)}) custom-call(f32[1,8,128]{2,1,0:T(8,128)S(1)} %fusion.67.gains_in, bf16[4,64,1408]{2,1,0:T(8,128)(2,1)S(1)} %shard_map.293.gate_in, ...), custom_call_target="tpu_custom_call" | custom-call | tf_op jit(solution)/shard_map/pallas_call | solution.py:223
  63.4 2.5 broadcast.80.clone
  66.0 2.6 constant_dynamic-update-slice_fusion.13
  71.4 47.6 %shard_map.296 = (bf16[4,4,128,1280]{3,2,1,0:T(8,128)(2,1)S(1)}, bf16[4,128,1024]{2,1,0:T(8,128)(2,1)S(1)}, bf16[2,4,64,1408]{3,2,1,0:T(8,128)(2,1)S(1)}) custom-call(bf16[4,128,1280]{2,1,0:T(8,128)(2,1)S(1)} %get-tuple-element.200.z4, bf16[64,1024]{1,0:T(8,128)(2,1)S(1)} %copy-done.27, bf16[64,1024]{1,0:T(8,128)(2,1)S(1)} %copy-done.26, ...), custom_call_target="tpu_custom_call" | custom-call | tf_op jit(solution)/shard_map/pallas_call | solution.py:276
  121.5 3.1 constant_dynamic-update-slice_fusion.12.refs_1_.refs_2_.refs_3_.refs_4_
  124.7 7.5 convolution_convert_fusion.k_ref.v_ref.q_ref
  132.3 10.5 %shard_map.297 = f32[8,2,168,128]{3,2,1,0:T(8,128)S(1)} custom-call(s32[2]{0:T(128)S(1)} %pad_add_fusion.scal, bf16[1024,1280]{1,0:T(8,128)(2,1)S(1)} %convolution_convert_fusion.k_ref.v_ref.q_ref, bf16[1024,1280]{1,0:T(8,128)(2,1)S(1)} %convolution_convert_fusion.k_ref.v_ref.q_ref, bf16[8,128,160]{2,1,0:T(8,128)(2,1)S(1)} %copy-done.10, ...), custom_call_target="tpu_custom_call" | custom-call | tf_op jit(solution)/shard_map/pallas_call | solution.py:785
  144.0 10.0 %collective-permute-done.3 = bf16[4,64,1408]{2,1,0:T(8,128)(2,1)S(1)} collective-permute-done((bf16[4,64,1408]{2,1,0:T(8,128)(2,1)}, bf16[4,64,1408]{2,1,0:T(8,128)(2,1)S(1)}, u32[]{:S(2)}, u32[]{:S(2)}) %collective-permute-start.3) | collective-permute-done | bytes 720928 | tf_op jit(solution)/shard_map/ppermute | solution.py:29
  158.3 3.3 pad_maximum_fusion
  170.4 2.5 broadcast_in_dim.61
  174.0 100.2 %shard_map.298 = f32[8,168,128]{2,1,0:T(8,128)S(1)} custom-call(f32[8,168,128]{2,1,0:T(8,128)S(1)} %copy-done.21), custom_call_target="tpu_custom_call" | custom-call | tf_op jit(solution)/shard_map/pallas_call | solution.py:854
  281.1 3.6 fusion.74
  287.6 10.3 %collective-permute-start.13 = (bf16[704,512]{1,0:T(8,128)(2,1)}, bf16[704,512]{1,0:T(8,128)(2,1)S(1)}, u32[]{:S(2)}, u32[]{:S(2)}) collective-permute-start(bf16[704,512]{1,0:T(8,128)(2,1)} %slice.130), channel_id=1, source_target_pairs={{0,16},{1,17},{2,18},{3,19},{4,20},{5,21},{6,22},{7,23},{8,24},{9,... | collective-permute-start | bytes 2162696 | tf_op jit(solution)/shard_map/ppermute | solution.py:29
  300.7 21.6 %shard_map.299 = (f32[1024,1024]{1,0:T(8,128)}, bf16[1024,1024]{1,0:T(8,128)(2,1)}) custom-call(bf16[1024,1280]{1,0:T(8,128)(2,1)} %copy-done, bf16[1024,1280]{1,0:T(8,128)(2,1)} %copy-done, bf16[1024,1280]{1,0:T(8,128)(2,1)} %copy-done, s32[1024,1]{1,0:T(8,128)S(1)} %copy.134.lo_ref, f32[8,2,168,128]{3,2,1,0:T(8,128)S(1)} %copy.135.carry_ref, ...), custom_call_target="tpu_custom_call" | custom-call | tf_op jit(solution)/shard_map/pallas_call | solution.py:785
  322.3 7.3 collective-permute-done.13.refs_13_
  330.8 2.7 constant_dynamic-update-slice_fusion.9
  335.9 2.7 constant_dynamic-update-slice_fusion.8
  338.7 3.6 constant_dynamic-update-slice_fusion.10.refs_1_.refs_2_.refs_3_.refs_4_
  343.9 4.8 multiply_reduce_fusion.2
  353.5 2.5 collective-permute-done.15
  356.0 3.2 constant_dynamic-update-slice_fusion.6.refs_1_.refs_2_.refs_3_.refs_4_
  359.2 51.8 %shard_map.300 = (bf16[512,2048]{1,0:T(8,128)(2,1)}, bf16[1024,1408]{1,0:T(8,128)(2,1)}, bf16[1024,2816]{1,0:T(8,128)(2,1)}, bf16[512,2048]{1,0:T(8,128)(2,1)}, ...) custom-call(s32[6]{0:T(128)S(1)} %stack.85.refs_0_, ...), custom_call_target="tpu_custom_call" | custom-call | tf_op jit(solution)/shard_map/pallas_call | solution.py:440
  421.4 51.9 %shard_map.301 = (bf16[512,2048]{1,0:T(8,128)(2,1)}, bf16[1024,1408]{1,0:T(8,128)(2,1)}, bf16[1024,2816]{1,0:T(8,128)(2,1)}, bf16[512,2048]{1,0:T(8,128)(2,1)}, ...) custom-call(s32[6]{0:T(128)S(1)} %stack.85.refs_0_, bf16[1024,2048]{1,0:T(8,128)(2,1)} %copy-done.32, ...), custom_call_target="tpu_custom_call" | custom-call | tf_op jit(solution)/shard_map/pallas_call | solution.py:440
  474.4 13.0 %shard_map.302 = bf16[1024,1408]{1,0:T(8,128)(2,1)} custom-call(s32[8]{0:T(128)} %get-tuple-element.448.refs_0_, bf16[1024,2048]{1,0:T(8,128)(2,1)} %constant_dynamic-update-slice_fusion.6.refs_1_.refs_2_.refs_3_.refs_4_, bf16[1024,2048]{1,0:T(8,128)(2,1)} %constant_dynamic-update-slice_fusion.6.refs_1_.refs_2_.refs_3_.refs_4_, ...), custom_call_target="tpu_custom_call" | custom-call | tf_op jit(solution)/shard_map/pallas_call | solution.py:477
  488.7 3.9 add_convert_fusion.2.refs_12_
  493.1 4.4 add_convert_fusion.1.refs_13_
  497.6 12.5 %shard_map.303 = bf16[1024,1408]{1,0:T(8,128)(2,1)} custom-call(s32[8]{0:T(128)} %get-tuple-element.445.refs_0_, bf16[1024,2048]{1,0:T(8,128)(2,1)} %constant_dynamic-update-slice_fusion.6.refs_1_.refs_2_.refs_3_.refs_4_, bf16[1024,2048]{1,0:T(8,128)(2,1)} %constant_dynamic-update-slice_fusion.6.refs_1_.refs_2_.refs_3_.refs_4_, ...), custom_call_target="tpu_custom_call" | custom-call | tf_op jit(solution)/shard_map/pallas_call | solution.py:477
  510.9 12.5 %shard_map.304 = bf16[1024,1408]{1,0:T(8,128)(2,1)} custom-call(s32[8]{0:T(128)} %get-tuple-element.447.refs_0_, bf16[1024,2048]{1,0:T(8,128)(2,1)} %constant_dynamic-update-slice_fusion.6.refs_1_.refs_2_.refs_3_.refs_4_, bf16[1024,2048]{1,0:T(8,128)(2,1)} %constant_dynamic-update-slice_fusion.6.refs_1_.refs_2_.refs_3_.refs_4_, ...), custom_call_target="tpu_custom_call" | custom-call | tf_op jit(solution)/shard_map/pallas_call | solution.py:477
  523.4 12.5 %shard_map.305 = bf16[1024,1408]{1,0:T(8,128)(2,1)} custom-call(s32[8]{0:T(128)} %get-tuple-element.446.refs_0_, bf16[1024,2048]{1,0:T(8,128)(2,1)} %constant_dynamic-update-slice_fusion.6.refs_1_.refs_2_.refs_3_.refs_4_, bf16[1024,2048]{1,0:T(8,128)(2,1)} %constant_dynamic-update-slice_fusion.6.refs_1_.refs_2_.refs_3_.refs_4_, ...), custom_call_target="tpu_custom_call" | custom-call | tf_op jit(solution)/shard_map/pallas_call | solution.py:477
  536.5 20.2 %shard_map.306 = bf16[1408,2048]{1,0:T(8,128)(2,1)} custom-call(s32[11]{0:T(128)} %iota.10.refs_0_, bf16[1024,1408]{1,0:T(8,128)(2,1)} %get-tuple-element.251.refs_1_, bf16[1024,1408]{1,0:T(8,128)(2,1)} %get-tuple-element.281.refs_2_, bf16[1024,2048]{1,0:T(8,128)(2,1)} %copy-done.37, bf16[1024,2048]{1,0:T(8,128)(2,1)} %copy-done.38, ...), custom_call_target="tpu_custom_call" | custom-call | tf_op jit(solution)/shard_map/pallas_call | solution.py:477
  556.7 4.5 multiply_reduce_fusion
  562.8 6.4 constant_dynamic-update-slice_fusion.1
  571.2 5.5 add_bitcast_fusion.1
  578.6 9.5 %fusion.22.d_ref = bf16[1024,1024]{1,0:T(8,128)(2,1)} fusion(bf16[1024,2048]{1,0:T(8,128)(2,1)S(1)} %constant_dynamic-update-slice_fusion, bf16[2048,2048]{1,0:T(8,128)(2,1)} %copy-done.62, s32[]{:T(128)S(6)} %select_n.368), kind=kOutput, calls=%fused_computation.58 | convolution fusion | flops 4296015872 | bytes 10485764 | tf_op jit(solution)/shard_map/dot_general | solution.py:612
  588.1 2.8 fusion.26
  597.2 3.1 slice.134
  603.4 44.8 %shard_map.307 = (bf16[1024,128]{1,0:T(8,128)(2,1)S(1)}, f32[1024,128]{1,0:T(8,128)S(1)}, f32[1024,1024]{1,0:T(8,128)}, f32[8,2,168,128]{3,2,1,0:T(8,128)S(1)}) custom-call(bf16[1024,1280]{1,0:T(8,128)(2,1)} %copy-done, bf16[1024,1280]{1,0:T(8,128)(2,1)} %copy-done, bf16[1024,1280]{1,0:T(8,128)(2,1)} %copy-done, s32[1024,1]{1,0:T(8,128)S(1)} %copy.134.lo_ref, ...), custom_call_target="tpu_custom_call" | custom-call | tf_op jit(solution)/shard_map/pallas_call | solution.py:785
  650.6 2.5 constant_dynamic-update-slice_fusion.17
  661.4 4.8 shard_map.308
  667.9 4.8 shard_map.309
  674.3 59.2 %shard_map.310.refs_6_ = f32[8,168,128]{2,1,0:T(8,128)S(1)} custom-call(f32[8,168,128]{2,1,0:T(8,128)S(1)} %fusion.48.refs_0_), custom_call_target="tpu_custom_call" | custom-call | tf_op jit(solution)/shard_map/pallas_call | solution.py:854
  734.4 4.9 shard_map.312
  739.3 4.7 shard_map.311
  744.1 3.1 convert_add_fusion.8
  747.9 2.9 add_bitcast_fusion.2
  758.6 27.5 %shard_map.313 = (bf16[1024,128]{1,0:T(8,128)(2,1)S(1)}, bf16[1024,1024]{1,0:T(8,128)(2,1)S(1)}) custom-call(s32[2]{0:T(128)S(1)} %copy-done.30, bf16[1024,1280]{1,0:T(8,128)(2,1)} %copy-done, bf16[1024,1280]{1,0:T(8,128)(2,1)} %copy-done, bf16[8,128,160]{2,1,0:T(8,128)(2,1)S(1)} %copy-done.10, bf16[8,128,160]{2,1,0:T(8,128)(2,1)S(1)} %copy-done.14, ...), custom_call_target="tpu_custom_call" | custom-call | tf_op jit(solution)/shard_map/pallas_call | solution.py:785
  789.8 5.4 shard_map.314
  796.1 5.4 shard_map.315
  803.8 5.4 shard_map.316
  810.6 5.5 shard_map.317
  819.9 9.9 %shard_map.318 = bf16[1024,2048]{1,0:T(8,128)(2,1)} custom-call(bf16[1024,1280]{1,0:T(8,128)(2,1)S(1)} %copy-done.2, bf16[2048,1280]{1,0:T(8,128)(2,1)} %bitcast.260), custom_call_target="tpu_custom_call" | custom-call | tf_op jit(solution)/shard_map/pallas_call | solution.py:549
  829.8 12.1 %collective-permute-done.39 = bf16[1,176,2048]{2,1,0:T(8,128)(2,1)S(1)} collective-permute-done((bf16[1,176,2048]{2,1,0:T(8,128)(2,1)S(1)}, bf16[1,176,2048]{2,1,0:T(8,128)(2,1)S(1)}, u32[]{:S(2)}, u32[]{:S(2)}) %collective-permute-start.39) | collective-permute-done | bytes 720928 | tf_op jit(solution)/shard_map/ppermute | solution.py:29
  852.8 2.6 fusion.17
  860.6 7.5 collective-permute-done.45
  868.7 5.7 fusion.6
  879.8 3.2 collective-permute-start.54
  882.9 2.5 collective-permute-start.53
  887.2 3.3 fusion.30
  890.6 2.9 shard_map.319
  893.5 10.6 %collective-permute-done.52 = f32[2,2048]{1,0:T(2,128)S(1)} collective-permute-done((f32[2,2048]{1,0:T(2,128)S(1)}, f32[2,2048]{1,0:T(2,128)S(1)}, u32[]{:S(2)}, u32[]{:S(2)}) %collective-permute-start.52) | collective-permute-done | bytes 16416 | tf_op jit(solution)/shard_map/ppermute | solution.py:29
  904.3 2.4 collective-permute-start.56
  907.3 3.0 fusion.9
  911.7 5.2 add_convert_fusion
  916.9 4.7 collective-permute-done.55
  (429 shorter events, 148.4 us)
Async XLA Ops:
  0.7 9.2 collective-permute-start
  7.4 58.6 %copy-start.94 = (f32[512]{0:T(512)}, f32[512]{0:T(512)S(1)}, u32[]{:S(2)}) copy-start(f32[512]{0:T(512)S(1)} %add_rsqrt_fusion.1) | copy-start | bytes 6148
  11.7 51.5 %copy-start.37 = (bf16[1024,2048]{1,0:T(8,128)(2,1)}, bf16[1024,2048]{1,0:T(8,128)(2,1)S(1)}, u32[]{:S(2)}) copy-start(bf16[1024,2048]{1,0:T(8,128)(2,1)S(1)} %constant_dynamic-update-slice_fusion.14.refs_2_.refs_3_) | copy-start | bytes 12582916
  68.6 52.9 %collective-permute-start.1 = (bf16[512,2048]{1,0:T(8,128)(2,1)}, bf16[512,2048]{1,0:T(8,128)(2,1)}, u32[]{:S(2)}, u32[]{:S(2)}) collective-permute-start(bf16[512,2048]{1,0:T(8,128)(2,1)} %get-tuple-element.398), channel_id=1, source_target_pairs={{0,1},{1,0},{2,3},{3,2},{4,5},{5,4},{6,7},{7,6},{8,9},{9,8},{10,11... | collective-permute-start | bytes 6291464 | tf_op jit(solution)/shard_map/ppermute | solution.py:29
  71.4 60.8 %copy-start.29 = (s32[2]{0:T(128)}, s32[2]{0:T(128)S(1)}, u32[]{:S(2)}) copy-start(s32[2]{0:T(128)S(1)} %pad_add_fusion.scal) | copy-start | bytes 28
  119.1 47.1 %copy-start.16 = (bf16[4,128,1024]{2,1,0:T(8,128)(2,1)}, bf16[4,128,1024]{2,1,0:T(8,128)(2,1)S(1)}, u32[]{:S(2)}) copy-start(bf16[4,128,1024]{2,1,0:T(8,128)(2,1)S(1)} %get-tuple-element.211) | copy-start | bytes 3145732
  119.1 24.9 %collective-permute-start.4 = (bf16[4,128,1024]{2,1,0:T(8,128)(2,1)S(1)}, bf16[4,128,1024]{2,1,0:T(8,128)(2,1)S(1)}, u32[]{:S(2)}, u32[]{:S(2)}) collective-permute-start(bf16[4,128,1024]{2,1,0:T(8,128)(2,1)S(1)} %get-tuple-element.211), channel_id=1, source_target_pairs={{0,4},{1,5},{2,6},{3,7},{4,0},{5,1},{6,2},{7,3},{8,12},{9,13},{10,... | collective-permute-start | bytes 3145736 | tf_op jit(solution)/shard_map/ppermute | solution.py:29
  120.7 33.4 %collective-permute-start.3 = (bf16[4,64,1408]{2,1,0:T(8,128)(2,1)}, bf16[4,64,1408]{2,1,0:T(8,128)(2,1)S(1)}, u32[]{:S(2)}, u32[]{:S(2)}) collective-permute-start(bf16[4,64,1408]{2,1,0:T(8,128)(2,1)} %get-tuple-element.208), channel_id=1, source_target_pairs={{0,16},{1,17},{2,18},{3,19},{4,20},{5,21},{6,22},{7,23},{8,24},{9,... | collective-permute-start | bytes 2162696 | tf_op jit(solution)/shard_map/ppermute | solution.py:29
  120.7 33.4 %collective-permute-start.2 = (bf16[2,4,64,1408]{3,2,1,0:T(8,128)(2,1)S(1)}, bf16[2,4,64,1408]{3,2,1,0:T(8,128)(2,1)}, u32[]{:S(2)}, u32[]{:S(2)}) collective-permute-start(bf16[2,4,64,1408]{3,2,1,0:T(8,128)(2,1)S(1)} %get-tuple-element.205), channel_id=1, source_target_pairs={{0,2},{1,3},{2,0},{3,1},{4,6},{5,7},{6,4},{7,5},{8,10},{9,11},{10,... | collective-permute-start | bytes 4325384 | tf_op jit(solution)/shard_map/ppermute | solution.py:29
  161.6 112.6 %collective-permute-start.6 = (bf16[2,4,64,2816]{3,2,1,0:T(8,128)(2,1)}, bf16[2,4,64,2816]{3,2,1,0:T(8,128)(2,1)}, u32[]{:S(2)}, u32[]{:S(2)}) collective-permute-start(bf16[2,4,64,2816]{3,2,1,0:T(8,128)(2,1)} %pad_maximum_fusion), channel_id=1, source_target_pairs={{0,4},{1,5},{2,6},{3,7},{4,0},{5,1},{6,2},{7,3},{8,12},{9,13},{10,... | collective-permute-start | bytes 8650760 | tf_op jit(solution)/shard_map/ppermute | solution.py:29
  163.6 110.6 %collective-permute-start.9 = (bf16[512,2048]{1,0:T(8,128)(2,1)}, bf16[512,2048]{1,0:T(8,128)(2,1)}, u32[]{:S(2)}, u32[]{:S(2)}) collective-permute-start(bf16[512,2048]{1,0:T(8,128)(2,1)} %param.34), channel_id=1, source_target_pairs={{0,8},{1,9},{2,10},{3,11},{4,12},{5,13},{6,14},{7,15},{8,0},{9,1},... | collective-permute-start | bytes 6291464 | tf_op jit(solution)/shard_map/ppermute | solution.py:29
  165.5 108.7 %collective-permute-start.8 = (bf16[704,1536]{1,0:T(8,128)(2,1)}, bf16[704,1536]{1,0:T(8,128)(2,1)}, u32[]{:S(2)}, u32[]{:S(2)}) collective-permute-start(bf16[704,1536]{1,0:T(8,128)(2,1)} %slice.129), channel_id=1, source_target_pairs={{0,16},{1,17},{2,18},{3,19},{4,20},{5,21},{6,22},{7,23},{8,24},{9,... | collective-permute-start | bytes 6488072 | tf_op jit(solution)/shard_map/ppermute | solution.py:29
  167.7 106.5 %collective-permute-start.5 = (bf16[2,4,128,1024]{3,2,1,0:T(8,128)(2,1)}, bf16[2,4,128,1024]{3,2,1,0:T(8,128)(2,1)}, u32[]{:S(2)}, u32[]{:S(2)}) collective-permute-start(bf16[2,4,128,1024]{3,2,1,0:T(8,128)(2,1)} %pad_maximum_fusion.1), channel_id=1, source_target_pairs={{0,2},{1,3},{2,0},{3,1},{4,6},{5,7},{6,4},{7,5},{8,10},{9,11},{10,... | collective-permute-start | bytes 6291464 | tf_op jit(solution)/shard_map/ppermute | solution.py:29
  169.2 105.0 %collective-permute-start.7 = (bf16[2,4,64,1408]{3,2,1,0:T(8,128)(2,1)}, bf16[2,4,64,1408]{3,2,1,0:T(8,128)(2,1)}, u32[]{:S(2)}, u32[]{:S(2)}) collective-permute-start(bf16[2,4,64,1408]{3,2,1,0:T(8,128)(2,1)} %bitcast_dynamic-update-slice_fusion.4), channel_id=1, source_target_pairs={{0,2},{1,3},{2,0},{3,1},{4,6},{5,7},{6,4},{7,5},{8,10},{9,11},{10,... | collective-permute-start | bytes 4325384 | tf_op jit(solution)/shard_map/ppermute | solution.py:29
  173.0 103.5 %copy-start.73 = (bf16[4,128,1024]{2,1,0:T(8,128)(2,1)S(1)}, bf16[4,128,1024]{2,1,0:T(8,128)(2,1)}, u32[]{:S(2)}) copy-start(bf16[4,128,1024]{2,1,0:T(8,128)(2,1)} %copy-done.72) | copy-start | bytes 3145732
  281.1 48.5 %collective-permute-start.10 = (bf16[2048,1024]{1,0:T(8,128)(2,1)}, bf16[2048,1024]{1,0:T(8,128)(2,1)}, u32[]{:S(2)}, u32[]{:S(2)}) collective-permute-start(bf16[2048,1024]{1,0:T(8,128)(2,1)} %bitcast.24), channel_id=1, source_target_pairs={{0,1},{1,0},{2,3},{3,2},{4,5},{5,4},{6,7},{7,6},{8,9},{9,8},{10,11... | collective-permute-start | bytes 12582920 | tf_op jit(solution)/shard_map/ppermute | solution.py:29
  284.7 44.9 %collective-permute-start.12 = (bf16[2,4,64,1408]{3,2,1,0:T(8,128)(2,1)}, bf16[2,4,64,1408]{3,2,1,0:T(8,128)(2,1)}, u32[]{:S(2)}, u32[]{:S(2)}) collective-permute-start(bf16[2,4,64,1408]{3,2,1,0:T(8,128)(2,1)} %get-tuple-element.237), channel_id=1, source_target_pairs={{0,2},{1,3},{2,0},{3,1},{4,6},{5,7},{6,4},{7,5},{8,10},{9,11},{10,... | collective-permute-start | bytes 4325384 | tf_op jit(solution)/shard_map/ppermute | solution.py:29
  285.9 43.7 %collective-permute-start.11 = (bf16[2,4,64,1408]{3,2,1,0:T(8,128)(2,1)}, bf16[2,4,64,1408]{3,2,1,0:T(8,128)(2,1)}, u32[]{:S(2)}, u32[]{:S(2)}) collective-permute-start(bf16[2,4,64,1408]{3,2,1,0:T(8,128)(2,1)} %collective-permute-done.2), channel_id=1, source_target_pairs={{0,4},{1,5},{2,6},{3,7},{4,0},{5,1},{6,2},{7,3},{8,12},{9,13},{10,... | collective-permute-start | bytes 4325384 | tf_op jit(solution)/shard_map/ppermute | solution.py:29
  287.6 41.9 %collective-permute-start.13 = (bf16[704,512]{1,0:T(8,128)(2,1)}, bf16[704,512]{1,0:T(8,128)(2,1)S(1)}, u32[]{:S(2)}, u32[]{:S(2)}) collective-permute-start(bf16[704,512]{1,0:T(8,128)(2,1)} %slice.130), channel_id=1, source_target_pairs={{0,16},{1,17},{2,18},{3,19},{4,20},{5,21},{6,22},{7,23},{8,24},{9,... | collective-permute-start | bytes 2162696 | tf_op jit(solution)/shard_map/ppermute | solution.py:29
  329.6 9.1 collective-permute-start.14
  351.4 4.6 collective-permute-start.15
  351.8 59.2 %collective-permute-start.16 = (bf16[512,2048]{1,0:T(8,128)(2,1)}, bf16[512,2048]{1,0:T(8,128)(2,1)}, u32[]{:S(2)}, u32[]{:S(2)}) collective-permute-start(bf16[512,2048]{1,0:T(8,128)(2,1)} %get-tuple-element.396), channel_id=1, source_target_pairs={{0,8},{1,9},{2,10},{3,11},{4,12},{5,13},{6,14},{7,15},{8,0},{9,1},... | collective-permute-start | bytes 6291464 | tf_op jit(solution)/shard_map/ppermute | solution.py:29
  411.0 4.4 collective-permute-start.17
  413.8 5.3 collective-permute-start.18
  415.7 57.5 %collective-permute-start.20 = (bf16[512,2048]{1,0:T(8,128)(2,1)}, bf16[512,2048]{1,0:T(8,128)(2,1)}, u32[]{:S(2)}, u32[]{:S(2)}) collective-permute-start(bf16[512,2048]{1,0:T(8,128)(2,1)} %get-tuple-element.267), channel_id=1, source_target_pairs={{0,1},{1,0},{2,3},{3,2},{4,5},{5,4},{6,7},{7,6},{8,9},{9,8},{10,11... | collective-permute-start | bytes 6291464 | tf_op jit(solution)/shard_map/ppermute | solution.py:29
  416.1 57.1 %collective-permute-start.19 = (bf16[512,2048]{1,0:T(8,128)(2,1)}, bf16[512,2048]{1,0:T(8,128)(2,1)}, u32[]{:S(2)}, u32[]{:S(2)}) collective-permute-start(bf16[512,2048]{1,0:T(8,128)(2,1)} %get-tuple-element.265), channel_id=1, source_target_pairs={{0,1},{1,0},{2,3},{3,2},{4,5},{5,4},{6,7},{7,6},{8,9},{9,8},{10,11... | collective-permute-start | bytes 6291464 | tf_op jit(solution)/shard_map/ppermute | solution.py:29
  421.4 52.5 %copy-start.105 = (s32[8]{0:T(128)S(1)}, s32[8]{0:T(128)}, u32[]{:S(2)}) copy-start(s32[8]{0:T(128)} %constant.564.clone) | copy-start | bytes 100
  473.3 15.4 %collective-permute-start.22 = (bf16[512,2048]{1,0:T(8,128)(2,1)}, bf16[512,2048]{1,0:T(8,128)(2,1)}, u32[]{:S(2)}, u32[]{:S(2)}) collective-permute-start(bf16[512,2048]{1,0:T(8,128)(2,1)} %get-tuple-element.278), channel_id=1, source_target_pairs={{0,1},{1,0},{2,3},{3,2},{4,5},{5,4},{6,7},{7,6},{8,9},{9,8},{10,11... | collective-permute-start | bytes 6291464 | tf_op jit(solution)/shard_map/ppermute | solution.py:29
  473.6 15.0 %collective-permute-start.21 = (bf16[512,2048]{1,0:T(8,128)(2,1)}, bf16[512,2048]{1,0:T(8,128)(2,1)}, u32[]{:S(2)}, u32[]{:S(2)}) collective-permute-start(bf16[512,2048]{1,0:T(8,128)(2,1)} %get-tuple-element.275), channel_id=1, source_target_pairs={{0,1},{1,0},{2,3},{3,2},{4,5},{5,4},{6,7},{7,6},{8,9},{9,8},{10,11... | collective-permute-start | bytes 6291464 | tf_op jit(solution)/shard_map/ppermute | solution.py:29
  487.4 69.3 %collective-permute-start.24 = (bf16[4,256,1408]{2,1,0:T(8,128)(2,1)}, bf16[4,256,1408]{2,1,0:T(8,128)(2,1)}, u32[]{:S(2)}, u32[]{:S(2)}) collective-permute-start(bf16[4,256,1408]{2,1,0:T(8,128)(2,1)} %bitcast.277), channel_id=1, source_target_pairs={{0,2},{1,3},{2,0},{3,1},{4,6},{5,7},{6,4},{7,5},{8,10},{9,11},{10,... | collective-permute-start | bytes 8650760 | tf_op jit(solution)/shard_map/ppermute | solution.py:29
  492.6 64.0 %collective-permute-start.23 = (bf16[512,2048]{1,0:T(8,128)(2,1)}, bf16[512,2048]{1,0:T(8,128)(2,1)}, u32[]{:S(2)}, u32[]{:S(2)}) collective-permute-start(bf16[512,2048]{1,0:T(8,128)(2,1)} %add_convert_fusion.2.refs_12_), channel_id=1, source_target_pairs={{0,8},{1,9},{2,10},{3,11},{4,12},{5,13},{6,14},{7,15},{8,0},{9,1},... | collective-permute-start | bytes 6291464 | tf_op jit(solution)/shard_map/ppermute | solution.py:29
  510.1 66.6 %collective-permute-start.26 = (bf16[4,256,1408]{2,1,0:T(8,128)(2,1)}, bf16[4,256,1408]{2,1,0:T(8,128)(2,1)}, u32[]{:S(2)}, u32[]{:S(2)}) collective-permute-start(bf16[4,256,1408]{2,1,0:T(8,128)(2,1)} %bitcast.279), channel_id=1, source_target_pairs={{0,4},{1,5},{2,6},{3,7},{4,0},{5,1},{6,2},{7,3},{8,12},{9,13},{10,... | collective-permute-start | bytes 8650760 | tf_op jit(solution)/shard_map/ppermute | solution.py:29
  571.2 5.5 collective-permute-start.25
  590.9 59.7 %collective-permute-start.29 = (bf16[512,2048]{1,0:T(8,128)(2,1)}, bf16[512,2048]{1,0:T(8,128)(2,1)}, u32[]{:S(2)}, u32[]{:S(2)}) collective-permute-start(bf16[512,2048]{1,0:T(8,128)(2,1)} %add_convert_fusion.1.refs_13_), channel_id=1, source_target_pairs={{0,8},{1,9},{2,10},{3,11},{4,12},{5,13},{6,14},{7,15},{8,0},{9,1},... | collective-permute-start | bytes 6291464 | tf_op jit(solution)/shard_map/ppermute | solution.py:29
  592.9 55.3 %collective-permute-start.27 = (bf16[2,256,1408]{2,1,0:T(8,128)(2,1)}, bf16[2,256,1408]{2,1,0:T(8,128)(2,1)}, u32[]{:S(2)}, u32[]{:S(2)}) collective-permute-start(bf16[2,256,1408]{2,1,0:T(8,128)(2,1)} %get-tuple-element.400), channel_id=1, source_target_pairs={{0,4},{1,5},{2,6},{3,7},{4,0},{5,1},{6,2},{7,3},{8,12},{9,13},{10,... | collective-permute-start | bytes 4325384 | tf_op jit(solution)/shard_map/ppermute | solution.py:29
  594.1 56.5 %collective-permute-start.28 = (bf16[2,256,1408]{2,1,0:T(8,128)(2,1)}, bf16[2,256,1408]{2,1,0:T(8,128)(2,1)}, u32[]{:S(2)}, u32[]{:S(2)}) collective-permute-start(bf16[2,256,1408]{2,1,0:T(8,128)(2,1)} %fusion.26), channel_id=1, source_target_pairs={{0,2},{1,3},{2,0},{3,1},{4,6},{5,7},{6,4},{7,5},{8,10},{9,11},{10,... | collective-permute-start | bytes 4325384 | tf_op jit(solution)/shard_map/ppermute | solution.py:29
  656.9 87.1 %collective-permute-start.30 = (bf16[1,256,2816]{2,1,0:T(8,128)(2,1)}, bf16[1,256,2816]{2,1,0:T(8,128)(2,1)}, u32[]{:S(2)}, u32[]{:S(2)}) collective-permute-start(bf16[1,256,2816]{2,1,0:T(8,128)(2,1)} %fusion.20), channel_id=1, source_target_pairs={{0,16},{1,17},{2,18},{3,19},{4,20},{5,21},{6,22},{7,23},{8,24},{9,... | collective-permute-start | bytes 4325384 | tf_op jit(solution)/shard_map/ppermute | solution.py:29
  657.3 86.7 %collective-permute-start.31 = (bf16[4,176,1024]{2,1,0:T(8,128)(2,1)}, bf16[4,176,1024]{2,1,0:T(8,128)(2,1)}, u32[]{:S(2)}, u32[]{:S(2)}) collective-permute-start(bf16[4,176,1024]{2,1,0:T(8,128)(2,1)} %get-tuple-element.303), channel_id=1, source_target_pairs={{0,2},{1,3},{2,0},{3,1},{4,6},{5,7},{6,4},{7,5},{8,10},{9,11},{10,... | collective-permute-start | bytes 4325384 | tf_op jit(solution)/shard_map/ppermute | solution.py:29
  658.4 85.7 %collective-permute-start.32 = (bf16[4,176,1024]{2,1,0:T(8,128)(2,1)}, bf16[4,176,1024]{2,1,0:T(8,128)(2,1)}, u32[]{:S(2)}, u32[]{:S(2)}) collective-permute-start(bf16[4,176,1024]{2,1,0:T(8,128)(2,1)} %bitcast.56), channel_id=1, source_target_pairs={{0,4},{1,5},{2,6},{3,7},{4,0},{5,1},{6,2},{7,3},{8,12},{9,13},{10,... | collective-permute-start | bytes 4325384 | tf_op jit(solution)/shard_map/ppermute | solution.py:29
  666.3 77.8 %collective-permute-start.33 = (bf16[8,128,512]{2,1,0:T(8,128)(2,1)}, bf16[8,128,512]{2,1,0:T(8,128)(2,1)}, u32[]{:S(2)}, u32[]{:S(2)}) collective-permute-start(bf16[8,128,512]{2,1,0:T(8,128)(2,1)} %bitcast.297), channel_id=1, source_target_pairs={{0,2},{1,3},{2,0},{3,1},{4,6},{5,7},{6,4},{7,5},{8,10},{9,11},{10,... | collective-permute-start | bytes 3145736 | tf_op jit(solution)/shard_map/ppermute | solution.py:29
  672.8 71.3 %collective-permute-start.34 = (bf16[8,128,512]{2,1,0:T(8,128)(2,1)}, bf16[8,128,512]{2,1,0:T(8,128)(2,1)}, u32[]{:S(2)}, u32[]{:S(2)}) collective-permute-start(bf16[8,128,512]{2,1,0:T(8,128)(2,1)} %bitcast.298), channel_id=1, source_target_pairs={{0,4},{1,5},{2,6},{3,7},{4,0},{5,1},{6,2},{7,3},{8,12},{9,13},{10,... | collective-permute-start | bytes 3145736 | tf_op jit(solution)/shard_map/ppermute | solution.py:29
  747.2 38.9 %collective-permute-start.35 = (bf16[4,128,512]{2,1,0:T(8,128)(2,1)}, bf16[4,128,512]{2,1,0:T(8,128)(2,1)}, u32[]{:S(2)}, u32[]{:S(2)}) collective-permute-start(bf16[4,128,512]{2,1,0:T(8,128)(2,1)} %get-tuple-element.416), channel_id=1, source_target_pairs={{0,4},{1,5},{2,6},{3,7},{4,0},{5,1},{6,2},{7,3},{8,12},{9,13},{10,... | collective-permute-start | bytes 1572872 | tf_op jit(solution)/shard_map/ppermute | solution.py:29
  750.8 36.1 %collective-permute-start.37 = (bf16[2,176,1024]{2,1,0:T(8,128)(2,1)}, bf16[2,176,1024]{2,1,0:T(8,128)(2,1)S(1)}, u32[]{:S(2)}, u32[]{:S(2)}) collective-permute-start(bf16[2,176,1024]{2,1,0:T(8,128)(2,1)} %get-tuple-element.408), channel_id=1, source_target_pairs={{0,4},{1,5},{2,6},{3,7},{4,0},{5,1},{6,2},{7,3},{8,12},{9,13},{10,... | collective-permute-start | bytes 2162696 | tf_op jit(solution)/shard_map/ppermute | solution.py:29
  754.0 32.9 %collective-permute-start.38 = (bf16[2,176,1024]{2,1,0:T(8,128)(2,1)S(1)}, bf16[2,176,1024]{2,1,0:T(8,128)(2,1)S(1)}, u32[]{:S(2)}, u32[]{:S(2)}) collective-permute-start(bf16[2,176,1024]{2,1,0:T(8,128)(2,1)S(1)} %get-tuple-element.402), channel_id=1, source_target_pairs={{0,2},{1,3},{2,0},{3,1},{4,6},{5,7},{6,4},{7,5},{8,10},{9,11},{10,... | collective-permute-start | bytes 2162696 | tf_op jit(solution)/shard_map/ppermute | solution.py:29
  756.1 29.9 %collective-permute-start.36 = (bf16[4,128,512]{2,1,0:T(8,128)(2,1)S(1)}, bf16[4,128,512]{2,1,0:T(8,128)(2,1)S(1)}, u32[]{:S(2)}, u32[]{:S(2)}) collective-permute-start(bf16[4,128,512]{2,1,0:T(8,128)(2,1)S(1)} %fusion.55), channel_id=1, source_target_pairs={{0,2},{1,3},{2,0},{3,1},{4,6},{5,7},{6,4},{7,5},{8,10},{9,11},{10,... | collective-permute-start | bytes 1572872 | tf_op jit(solution)/shard_map/ppermute | solution.py:29
  795.2 48.9 %collective-permute-start.41 = (bf16[8,128,640]{2,1,0:T(8,128)(2,1)}, bf16[8,128,640]{2,1,0:T(8,128)(2,1)}, u32[]{:S(2)}, u32[]{:S(2)}) collective-permute-start(bf16[8,128,640]{2,1,0:T(8,128)(2,1)} %bitcast.271), channel_id=1, source_target_pairs={{0,2},{1,3},{2,0},{3,1},{4,6},{5,7},{6,4},{7,5},{8,10},{9,11},{10,... | collective-permute-start | bytes 3932168 | tf_op jit(solution)/shard_map/ppermute | solution.py:29
  801.5 42.6 %collective-permute-start.42 = (bf16[8,128,640]{2,1,0:T(8,128)(2,1)}, bf16[8,128,640]{2,1,0:T(8,128)(2,1)S(1)}, u32[]{:S(2)}, u32[]{:S(2)}) collective-permute-start(bf16[8,128,640]{2,1,0:T(8,128)(2,1)} %bitcast.283), channel_id=1, source_target_pairs={{0,4},{1,5},{2,6},{3,7},{4,0},{5,1},{6,2},{7,3},{8,12},{9,13},{10,... | collective-permute-start | bytes 3932168 | tf_op jit(solution)/shard_map/ppermute | solution.py:29
  809.3 32.7 %collective-permute-start.39 = (bf16[1,176,2048]{2,1,0:T(8,128)(2,1)S(1)}, bf16[1,176,2048]{2,1,0:T(8,128)(2,1)S(1)}, u32[]{:S(2)}, u32[]{:S(2)}) collective-permute-start(bf16[1,176,2048]{2,1,0:T(8,128)(2,1)S(1)} %fusion.33), channel_id=1, source_target_pairs={{0,16},{1,17},{2,18},{3,19},{4,20},{5,21},{6,22},{7,23},{8,24},{9,... | collective-permute-start | bytes 2162696 | tf_op jit(solution)/shard_map/ppermute | solution.py:29
  818.8 25.3 %collective-permute-start.40 = (bf16[2,128,1024]{2,1,0:T(8,128)(2,1)S(1)}, bf16[2,128,1024]{2,1,0:T(8,128)(2,1)S(1)}, u32[]{:S(2)}, u32[]{:S(2)}) collective-permute-start(bf16[2,128,1024]{2,1,0:T(8,128)(2,1)S(1)} %get-tuple-element.406), channel_id=1, source_target_pairs={{0,8},{1,9},{2,10},{3,11},{4,12},{5,13},{6,14},{7,15},{8,0},{9,1},... | collective-permute-start | bytes 1572872 | tf_op jit(solution)/shard_map/ppermute | solution.py:29
  850.8 7.9 collective-permute-start.43
  850.8 17.4 %collective-permute-start.45 = (bf16[4,128,640]{2,1,0:T(8,128)(2,1)}, bf16[4,128,640]{2,1,0:T(8,128)(2,1)S(1)}, u32[]{:S(2)}, u32[]{:S(2)}) collective-permute-start(bf16[4,128,640]{2,1,0:T(8,128)(2,1)} %get-tuple-element.413), channel_id=1, source_target_pairs={{0,2},{1,3},{2,0},{3,1},{4,6},{5,7},{6,4},{7,5},{8,10},{9,11},{10,... | collective-permute-start | bytes 1966088 | tf_op jit(solution)/shard_map/ppermute | solution.py:29
  851.7 17.1 %collective-permute-start.44 = (bf16[4,128,640]{2,1,0:T(8,128)(2,1)}, bf16[4,128,640]{2,1,0:T(8,128)(2,1)S(1)}, u32[]{:S(2)}, u32[]{:S(2)}) collective-permute-start(bf16[4,128,640]{2,1,0:T(8,128)(2,1)} %fusion.50), channel_id=1, source_target_pairs={{0,4},{1,5},{2,6},{3,7},{4,0},{5,1},{6,2},{7,3},{8,12},{9,13},{10,... | collective-permute-start | bytes 1966088 | tf_op jit(solution)/shard_map/ppermute | solution.py:29
  858.7 18.6 %collective-permute-start.48 = (bf16[64,2816]{1,0:T(8,128)(2,1)S(1)}, bf16[64,2816]{1,0:T(8,128)(2,1)S(1)}, u32[]{:S(2)}, u32[]{:S(2)}) collective-permute-start(bf16[64,2816]{1,0:T(8,128)(2,1)S(1)} %get-tuple-element.364), channel_id=1, source_target_pairs={{0,9},{1,8},{2,11},{3,10},{4,13},{5,12},{6,15},{7,14},{8,1},{9,0},... | collective-permute-start | bytes 1081352 | tf_op jit(solution)/shard_map/ppermute | solution.py:29
  858.8 18.5 %collective-permute-start.47 = (bf16[64,2816]{1,0:T(8,128)(2,1)S(1)}, bf16[64,2816]{1,0:T(8,128)(2,1)S(1)}, u32[]{:S(2)}, u32[]{:S(2)}) collective-permute-start(bf16[64,2816]{1,0:T(8,128)(2,1)S(1)} %get-tuple-element.363), channel_id=1, source_target_pairs={{0,8},{1,9},{2,10},{3,11},{4,12},{5,13},{6,14},{7,15},{8,0},{9,1},... | collective-permute-start | bytes 1081352 | tf_op jit(solution)/shard_map/ppermute | solution.py:29
  860.3 16.9 %collective-permute-start.46 = (bf16[64,2816]{1,0:T(8,128)(2,1)S(1)}, bf16[64,2816]{1,0:T(8,128)(2,1)S(1)}, u32[]{:S(2)}, u32[]{:S(2)}) collective-permute-start(bf16[64,2816]{1,0:T(8,128)(2,1)S(1)} %get-tuple-element.362), channel_id=1, source_target_pairs={{0,1},{1,0},{2,3},{3,2},{4,5},{5,4},{6,7},{7,6},{8,9},{9,8},{10,11... | collective-permute-start | bytes 1081352 | tf_op jit(solution)/shard_map/ppermute | solution.py:29
  877.3 1.2 collective-permute-start.49
  878.5 6.9 collective-permute-start.50
  879.8 24.3 %collective-permute-start.54 = (bf16[1,128,1024]{2,1,0:T(8,128)(2,1)}, bf16[1,128,1024]{2,1,0:T(8,128)(2,1)S(1)}, u32[]{:S(2)}, u32[]{:S(2)}) collective-permute-start(bf16[1,128,1024]{2,1,0:T(8,128)(2,1)} %get-tuple-element.420), channel_id=1, source_target_pairs={{0,16},{1,17},{2,18},{3,19},{4,20},{5,21},{6,22},{7,23},{8,24},{9,... | collective-permute-start | bytes 786440 | tf_op jit(solution)/shard_map/ppermute | solution.py:29
  882.9 21.2 %collective-permute-start.53 = (bf16[2,128,1280]{2,1,0:T(8,128)(2,1)}, bf16[2,128,1280]{2,1,0:T(8,128)(2,1)S(1)}, u32[]{:S(2)}, u32[]{:S(2)}) collective-permute-start(bf16[2,128,1280]{2,1,0:T(8,128)(2,1)} %get-tuple-element.403), channel_id=1, source_target_pairs={{0,8},{1,9},{2,10},{3,11},{4,12},{5,13},{6,14},{7,15},{8,0},{9,1},... | collective-permute-start | bytes 1966088 | tf_op jit(solution)/shard_map/ppermute | solution.py:29
  886.2 4.3 collective-permute-start.51
  890.5 13.5 %collective-permute-start.52 = (f32[2,2048]{1,0:T(2,128)S(1)}, f32[2,2048]{1,0:T(2,128)S(1)}, u32[]{:S(2)}, u32[]{:S(2)}) collective-permute-start(f32[2,2048]{1,0:T(2,128)S(1)} %add.662), channel_id=1, source_target_pairs={{0,8},{1,9},{2,10},{3,11},{4,12},{5,13},{6,14},{7,15},{8,0},{9,1},... | collective-permute-start | bytes 49160 | tf_op jit(solution)/shard_map/ppermute | solution.py:29
  904.3 18.0 %collective-permute-start.56 = (bf16[1,128,1280]{2,1,0:T(8,128)(2,1)S(1)}, bf16[1,128,1280]{2,1,0:T(8,128)(2,1)S(1)}, u32[]{:S(2)}, u32[]{:S(2)}) collective-permute-start(bf16[1,128,1280]{2,1,0:T(8,128)(2,1)S(1)} %get-tuple-element.418), channel_id=1, source_target_pairs={{0,16},{1,17},{2,18},{3,19},{4,20},{5,21},{6,22},{7,23},{8,24},{9,... | collective-permute-start | bytes 983048 | tf_op jit(solution)/shard_map/ppermute | solution.py:29
  906.7 14.9 %collective-permute-start.55 = (f32[2,2048]{1,0:T(2,128)S(1)}, f32[2,2048]{1,0:T(2,128)S(1)}, u32[]{:S(2)}, u32[]{:S(2)}) collective-permute-start(f32[2,2048]{1,0:T(2,128)S(1)} %add.663), channel_id=1, source_target_pairs={{0,16},{1,17},{2,18},{3,19},{4,20},{5,21},{6,22},{7,23},{8,24},{9,... | collective-permute-start | bytes 49160 | tf_op jit(solution)/shard_map/ppermute | solution.py:29
  922.5 2.1 collective-permute-start.57
  (101 other events, 714.0 us)
